TPU v7x, 32 devices: a whole 2x2x4 slice. The times are simulated.
32 devices in a mesh: section: 2 (over core), dp: 4 (over z), seq: 4 (over y, x).
Axes of the slice: x: 2, y: 2, z: 4, core: 2. Of those that a mesh axis runs over, the one named last changes fastest.
Arguments:
- layer_in: bfloat16 [2, 4, 1024, 767], P(None, 'dp', 'seq'), may hold values from -12 to 12
- cotangent: bfloat16 [2, 4, 1024, 767], P(None, 'dp', 'seq'), may hold values from -6 to 6
- lengths: int32 [2, 4, 4], P(None, 'dp'), may hold values from 1 to 896, 1024 in all within a row
- w_qkv: bfloat16 [2, 767, 2304], P('section'), may hold values from -0.21875 to 0.21875
- bias_qv: float32 [2, 1536], P('section'), may hold values from -3 to 3
- w_out: bfloat16 [2, 768, 767], P('section'), may hold values from -1.5 to 1.5
- bias_out: float32 [2, 767], P('section'), may hold values from -2 to 2
- gain_attn: float32 [2, 767], P('section'), may hold values from 0.5 to 1.5
- gain_mlp: float32 [2, 767], P('section'), may hold values from 0.5 to 1.5
- w_up: bfloat16 [2, 767, 3072], P('section'), may hold values from -0.21875 to 0.21875
- bias_up: float32 [2, 3072], P('section'), may hold values from -3 to 3
- w_down: bfloat16 [2, 3072, 767], P('section'), may hold values from -0.109375 to 0.109375
- bias_down: float32 [2, 767], P('section'), may hold values from -2 to 2
Outputs:
- layer_out: bfloat16 [2, 2, 4, 1024, 767], P('section', None, 'dp', 'seq')
- input_grad: bfloat16 [2, 2, 4, 1024, 767], P('section', None, 'dp', 'seq')
- grad_w_qkv: float32 [2, 767, 2304], P('section')
- grad_bias_qv: float32 [2, 1536], P('section')
- grad_w_out: float32 [2, 768, 767], P('section')
- grad_bias_out: float32 [2, 767], P('section')
- grad_gain_attn: float32 [2, 767], P('section')
- grad_gain_mlp: float32 [2, 767], P('section')
- grad_w_up: float32 [2, 767, 3072], P('section')
- grad_bias_up: float32 [2, 3072], P('section')
- grad_w_down: float32 [2, 3072, 767], P('section')
- grad_bias_down: float32 [2, 767], P('section')
- rms_log: float32 [2], P('section')
Inputs may be any that keep to these rules, and one draw needn't show every extreme that they name: The lengths of each row sum to 1024, and the longest in every row is 896.
All inputs are finite; a program needn't handle non-finite values.
Results may differ from a plain program's by a relative error of at most 0.015.
Values may be sent and summed in bfloat16 or wider, within the bound.
No kernel may reach another device: no remote copies, remote signals or barrier semaphores. Data moves between devices by JAX's collectives and lax.ppermute only.
A program may use at most 320 MiB of HBM per device.

v0:
```python
import jax
import jax.numpy as jnp
from jax import lax
from jax.sharding import PartitionSpec as P

HEADS = 12


epsilon = 1e-06
masked_fill = -1e30


def shifted(value, axis, steps):
    count = lax.axis_size(axis)
    first, last = (max(0, -steps), min(count, count - steps))
    return lax.ppermute(value, axis, [(source, source + steps) for source in range(first, last)])


def crms_norm(values, gain_vec):
    full_width = values.shape[-1] + 1
    squares = jnp.sum(values * values, axis=-1, keepdims=True)
    column_sum = jnp.sum(values, axis=-1, keepdims=True)
    scale_inv = lax.rsqrt((squares + column_sum * column_sum) / full_width + epsilon)
    return values * scale_inv * gain_vec


def mean_square(values):
    full_width = values.shape[-1] + 1
    column_sum = jnp.sum(values, axis=-1)
    return (jnp.sum(values * values, axis=-1) + column_sum * column_sum) / full_width


def segments(doc_lengths, positions):
    doc_ends = jnp.cumsum(doc_lengths, axis=-1)
    return jnp.sum((doc_ends[..., None, :] <= positions[:, None]).astype(jnp.int32), axis=-1)


def softmax_parts(queries, key_heads, visible, score_scale):
    raw_scores = jnp.einsum(
        "rqhd,rkhd->rhqk", queries, key_heads, preferred_element_type=jnp.float32
    )
    scores = jnp.where(visible[:, None], raw_scores * score_scale, masked_fill)
    row_max = jnp.max(scores, axis=-1, keepdims=True)
    exps = jnp.exp(scores - row_max)
    row_total = jnp.sum(exps, axis=-1, keepdims=True)
    return (exps / row_total, row_max, row_total)


def on_device(
    layer_in,
    cotangent,
    lengths,
    w_qkv,
    bias_qv,
    w_out,
    bias_out,
    gain_attn,
    gain_mlp,
    w_up,
    bias_up,
    w_down,
    bias_down,
):
    micro_count, row_count, span_len, compact = layer_in.shape
    model_width = w_out.shape[1]
    head_count = HEADS
    head_size = model_width // head_count
    score_scale = head_size ** (-0.5)
    section_index = lax.axis_index("section")
    dp_count = lax.axis_size("dp")
    seq_len = span_len * lax.axis_size("seq")
    own_start = lax.axis_index("seq") * span_len
    query_pos = own_start + jnp.arange(span_len, dtype=jnp.int32)
    key_pos = jnp.arange(seq_len, dtype=jnp.int32)
    wqkv_local = w_qkv[0]
    wout_local = w_out[0]
    wup_local = w_up[0]
    wdown_local = w_down[0]
    gain_a = gain_attn[0]
    gain_m = gain_mlp[0]
    bias_o = bias_out[0]
    bias_u = bias_up[0]
    bias_d = bias_down[0]
    bias_full = jnp.concatenate(
        [bias_qv[0, :model_width], jnp.zeros((model_width,), jnp.float32), bias_qv[0, model_width:]]
    )
    heads_local = (row_count, span_len, head_count, head_size)
    heads_all = (row_count, seq_len, head_count, head_size)
    received = jnp.zeros((row_count, span_len, compact), jnp.bfloat16)
    outputs = jnp.zeros_like(layer_in)
    saved_list = []
    square_sum = jnp.zeros((), jnp.float32)
    for turn_index in range(micro_count + 1):
        slot_raw = turn_index - section_index
        is_live = (slot_raw >= 0) & (slot_raw < micro_count)
        slot_index = jnp.clip(slot_raw, 0, micro_count - 1)
        first_input = layer_in[min(turn_index, micro_count - 1)]
        layer_input = jnp.where(section_index == 0, first_input, received)
        doc_lengths = lax.dynamic_index_in_dim(lengths, slot_index, 0, keepdims=False)
        input_f = layer_input.astype(jnp.float32)
        q_segments = segments(doc_lengths, query_pos)
        k_segments = segments(doc_lengths, key_pos)
        forward_visible = (q_segments[:, :, None] == k_segments[:, None, :]) & (
            key_pos[None, None, :] <= query_pos[None, :, None]
        )
        forward_normed = crms_norm(input_f, gain_a).astype(jnp.bfloat16)
        qkv = (
            jnp.einsum(
                "rtc,cf->rtf", forward_normed, wqkv_local, preferred_element_type=jnp.float32
            )
            + bias_full
        ).astype(jnp.bfloat16)
        key_rows = lax.all_gather(
            qkv[..., model_width : 2 * model_width], "seq", axis=1, tiled=True
        )
        value_rows = lax.all_gather(qkv[..., 2 * model_width :], "seq", axis=1, tiled=True)
        forward_queries = qkv[..., :model_width].reshape(heads_local)
        forward_key_heads = key_rows.reshape(heads_all)
        forward_value_heads = value_rows.reshape(heads_all)
        forward_attn_probs = softmax_parts(
            forward_queries, forward_key_heads, forward_visible, score_scale
        )[0]
        attended = jnp.einsum(
            "rhqk,rkhd->rqhd",
            forward_attn_probs.astype(jnp.bfloat16),
            forward_value_heads,
            preferred_element_type=jnp.float32,
        )
        forward_attended_low = attended.reshape(row_count, span_len, model_width).astype(
            jnp.bfloat16
        )
        forward_middle = (
            input_f
            + jnp.einsum(
                "rtd,dc->rtc", forward_attended_low, wout_local, preferred_element_type=jnp.float32
            )
            + bias_o
        )
        forward_normed_mlp = crms_norm(forward_middle, gain_m).astype(jnp.bfloat16)
        forward_up_proj = (
            jnp.einsum(
                "rtc,cf->rtf", forward_normed_mlp, wup_local, preferred_element_type=jnp.float32
            )
            + bias_u
        )
        forward_activated = jax.nn.gelu(forward_up_proj).astype(jnp.bfloat16)
        final_sum = (
            forward_middle
            + jnp.einsum(
                "rtf,fc->rtc", forward_activated, wdown_local, preferred_element_type=jnp.float32
            )
            + bias_d
        )
        forward_kept_state = (
            layer_input,
            forward_queries,
            forward_key_heads,
            forward_value_heads,
            forward_visible,
            forward_attended_low,
            forward_middle,
            forward_up_proj,
            doc_lengths,
        )
        final_sum, kept_state = (final_sum, forward_kept_state)
        result = final_sum.astype(jnp.bfloat16)
        current = lax.dynamic_index_in_dim(outputs, slot_index, 0, keepdims=False)
        outputs = lax.dynamic_update_index_in_dim(
            outputs, jnp.where(is_live, result, current), slot_index, 0
        )
        square_sum = square_sum + jnp.where(is_live, jnp.sum(mean_square(final_sum)), 0.0)
        saved_list.append(kept_state)
        if turn_index < micro_count:
            received = shifted(result, "section", 1)
    attn_totals = (
        jnp.zeros(wqkv_local.shape, jnp.float32),
        jnp.zeros((2 * model_width,), jnp.float32),
        jnp.zeros(wout_local.shape, jnp.float32),
        jnp.zeros((compact,), jnp.float32),
        jnp.zeros((compact,), jnp.float32),
    )
    mlp_totals = (
        jnp.zeros((compact,), jnp.float32),
        jnp.zeros(wup_local.shape, jnp.float32),
        jnp.zeros(bias_u.shape, jnp.float32),
        jnp.zeros(wdown_local.shape, jnp.float32),
        jnp.zeros((compact,), jnp.float32),
    )
    back_grad = jnp.zeros((row_count, span_len, compact), jnp.bfloat16)
    input_grads = jnp.zeros_like(layer_in)
    for turn_index in range(micro_count + 1):
        slot_raw = turn_index - 1 + section_index
        is_live = (slot_raw >= 0) & (slot_raw < micro_count)
        slot_index = jnp.clip(slot_raw, 0, micro_count - 1)
        incoming = jnp.where(
            section_index == 1, cotangent[min(turn_index, micro_count - 1)], back_grad
        )
        incoming = jnp.where(is_live, incoming, jnp.zeros_like(incoming))
        kept_state = jax.tree.map(
            lambda higher, lower: jnp.where(section_index == 1, higher, lower),
            saved_list[min(turn_index + 1, micro_count)],
            saved_list[max(turn_index - 1, 0)],
        )
        mlp_middle = kept_state[6]
        mlp_up_proj = kept_state[7]
        final_grad = incoming.astype(jnp.float32)
        activated, gelu_back = jax.vjp(jax.nn.gelu, mlp_up_proj)
        mlp_grad_down = jnp.einsum(
            "rtf,rtc->fc",
            activated.astype(jnp.bfloat16),
            incoming,
            preferred_element_type=jnp.float32,
        )
        mlp_grad_bdown = jnp.sum(final_grad, axis=(0, 1))
        act_grad = jnp.einsum(
            "rtc,fc->rtf", incoming, wdown_local, preferred_element_type=jnp.float32
        )
        up_grad = gelu_back(act_grad)[0].astype(jnp.bfloat16)
        normed_mlp, mlp_norm_back = jax.vjp(crms_norm, mlp_middle, gain_m)
        mlp_grad_up = jnp.einsum(
            "rtc,rtf->cf",
            normed_mlp.astype(jnp.bfloat16),
            up_grad,
            preferred_element_type=jnp.float32,
        )
        mlp_grad_bup = jnp.sum(up_grad.astype(jnp.float32), axis=(0, 1))
        mlp_normed_grad = jnp.einsum(
            "rtf,cf->rtc", up_grad, wup_local, preferred_element_type=jnp.float32
        )
        middle_part, mlp_grad_gm = mlp_norm_back(mlp_normed_grad)
        middle_grad = final_grad + middle_part
        mlp_terms = (mlp_grad_gm, mlp_grad_up, mlp_grad_bup, mlp_grad_down, mlp_grad_bdown)
        mlp_totals = tuple(
            (total_part + new_part for total_part, new_part in zip(mlp_totals, mlp_terms))
        )
        (
            attn_layer_input,
            queries,
            key_heads,
            value_heads,
            visible,
            attended_low,
            middle,
            up_proj,
            attn_doc_lengths,
        ) = kept_state
        middle_low = middle_grad.astype(jnp.bfloat16)
        attn_grad_out = jnp.einsum(
            "rtd,rtc->dc", attended_low, middle_low, preferred_element_type=jnp.float32
        )
        attn_grad_bout = jnp.sum(middle_low.astype(jnp.float32), axis=(0, 1))
        attended_grad = (
            jnp.einsum("rtc,dc->rtd", middle_low, wout_local, preferred_element_type=jnp.float32)
            .astype(jnp.bfloat16)
            .reshape(heads_local)
        )
        attn_probs, row_max, row_total = softmax_parts(queries, key_heads, visible, score_scale)
        probs_grad = jnp.einsum(
            "rqhd,rkhd->rhqk", attended_grad, value_heads, preferred_element_type=jnp.float32
        )
        inner_sum = jnp.sum(attn_probs * probs_grad, axis=-1, keepdims=True)
        scores_grad = (attn_probs * (probs_grad - inner_sum)).astype(jnp.bfloat16)
        query_grad = (
            jnp.einsum(
                "rhqk,rkhd->rqhd", scores_grad, key_heads, preferred_element_type=jnp.float32
            )
            * score_scale
        )
        key_grad_all = (
            jnp.einsum("rhqk,rqhd->rkhd", scores_grad, queries, preferred_element_type=jnp.float32)
            * score_scale
        )
        value_grad_all = jnp.einsum(
            "rhqk,rqhd->rkhd",
            attn_probs.astype(jnp.bfloat16),
            attended_grad,
            preferred_element_type=jnp.float32,
        )
        key_grad = lax.psum_scatter(
            key_grad_all.reshape(row_count, seq_len, model_width).astype(jnp.bfloat16),
            "seq",
            scatter_dimension=1,
            tiled=True,
        ).astype(jnp.float32)
        value_grad = lax.psum_scatter(
            value_grad_all.reshape(row_count, seq_len, model_width).astype(jnp.bfloat16),
            "seq",
            scatter_dimension=1,
            tiled=True,
        ).astype(jnp.float32)
        qkv_grad = jnp.concatenate(
            [query_grad.reshape(row_count, span_len, model_width), key_grad, value_grad], axis=-1
        ).astype(jnp.bfloat16)
        normed, norm_back = jax.vjp(crms_norm, attn_layer_input.astype(jnp.float32), gain_a)
        attn_grad_qkv = jnp.einsum(
            "rtc,rtf->cf", normed.astype(jnp.bfloat16), qkv_grad, preferred_element_type=jnp.float32
        )
        bias_sum = jnp.sum(qkv_grad.astype(jnp.float32), axis=(0, 1))
        attn_grad_bqv = jnp.concatenate([bias_sum[:model_width], bias_sum[2 * model_width :]])
        normed_grad = jnp.einsum(
            "rtf,cf->rtc", qkv_grad, wqkv_local, preferred_element_type=jnp.float32
        )
        input_part, attn_grad_ga = norm_back(normed_grad)
        input_grad_f = middle_grad + input_part
        attn_terms = (attn_grad_qkv, attn_grad_bqv, attn_grad_out, attn_grad_bout, attn_grad_ga)
        attn_totals = tuple(
            (total_part + new_part for total_part, new_part in zip(attn_totals, attn_terms))
        )
        grad_low = input_grad_f.astype(jnp.bfloat16)
        current = lax.dynamic_index_in_dim(input_grads, slot_index, 0, keepdims=False)
        input_grads = lax.dynamic_update_index_in_dim(
            input_grads, jnp.where(is_live, grad_low, current), slot_index, 0
        )
        if turn_index < micro_count:
            back_grad = shifted(grad_low, "section", -1)
    grad_qkv, grad_bqv, grad_out, grad_bout, grad_ga = attn_totals
    grad_gm, grad_up, grad_bup, grad_down, grad_bdown = mlp_totals
    (
        grad_qkv,
        grad_bqv,
        grad_out,
        grad_bout,
        grad_ga,
        grad_gm,
        grad_up,
        grad_bup,
        grad_down,
        grad_bdown,
        square_total,
    ) = lax.psum(
        (
            grad_qkv,
            grad_bqv,
            grad_out,
            grad_bout,
            grad_ga,
            grad_gm,
            grad_up,
            grad_bup,
            grad_down,
            grad_bdown,
            square_sum,
        ),
        ("dp", "seq"),
    )
    rms_log = jnp.sqrt(square_total / (micro_count * row_count * dp_count * seq_len)).reshape(1)
    return (
        outputs[None],
        input_grads[None],
        grad_qkv[None],
        grad_bqv[None],
        grad_out[None],
        grad_bout[None],
        grad_ga[None],
        grad_gm[None],
        grad_up[None],
        grad_bup[None],
        grad_down[None],
        grad_bdown[None],
        rms_log,
    )


def solution(mesh):
    in_specs = (
        P(None, "dp", "seq", None),
        P(None, "dp", "seq", None),
        P(None, "dp", None),
        P("section", None, None),
        P("section", None),
        P("section", None, None),
        P("section", None),
        P("section", None),
        P("section", None),
        P("section", None, None),
        P("section", None),
        P("section", None, None),
        P("section", None),
    )
    out_specs = (
        P("section", None, "dp", "seq", None),
        P("section", None, "dp", "seq", None),
        P("section", None, None),
        P("section", None),
        P("section", None, None),
        P("section", None),
        P("section", None),
        P("section", None),
        P("section", None, None),
        P("section", None),
        P("section", None, None),
        P("section", None),
        P("section"),
    )
    return jax.shard_map(
        on_device, mesh=mesh, in_specs=in_specs, out_specs=out_specs, check_vma=False
    )
```

profile of v0, /device:TPU:0, one launch (start us, length us, event | category | flops | bytes accessed | tf_op | source)
XLA Modules:
  0.0 1396.0 jit_solution(5637286590029553135)
XLA Ops:
  8.1 4.0 fusion.445
  32.3 21.1 %all-gather.9.cloned.1.call-done = bf16[1,1024,768]{2,1,0:T(8,128)(2,1)} async-done(((bf16[1,256,768]{2,1,0:T(8,128)(2,1)}), bf16[1,1024,768]{2,1,0:T(8,128)(2,1)}) %all-gather.9.cloned.1.call-update) | async-done | bytes 1572880 | tf_op jit(solution)/shard_map/all_gather | solution.py:113
  56.0 11.2 fusion.449
  67.2 19.7 %all-gather.7.cloned.1.call-done = bf16[1,1024,768]{2,1,0:T(8,128)(2,1)} async-done(((bf16[1,256,768]{2,1,0:T(8,128)(2,1)}), bf16[1,1024,768]{2,1,0:T(8,128)(2,1)}) %all-gather.7.cloned.1.call-update) | async-done | bytes 1572880 | tf_op jit(solution)/shard_map/all_gather | solution.py:116
  89.4 7.2 fusion.242
  97.4 4.5 fusion.63
  123.9 15.5 %dynamic_update_slice.21 = bf16[2,1,256,767]{2,0,3,1:T(2,128)(2,1)} dynamic-update-slice(bf16[2,1,256,767]{2,0,3,1:T(2,128)(2,1)} %broadcast.1200.clone, bf16[1,1,256,767]{2,0,3,1:T(2,128)(2,1)} %copy.111, s32[]{:T(128)S(6)} %min.19, s32[]{:T(128)} %constant.109.clone.1, s32[]{:T(128)} %constant.109.clone.1, s32[]{:T(128)} %constant.109.clone.1) | dynamic-update-slice | bytes 785412 | tf_op jit(solution)/shard_map/jit(dynamic_update_index_in_dim)/dynamic_update_slice | solution.py:168
  150.8 11.2 fusion.450
  162.0 19.0 %all-gather.11.cloned.1.call-done = bf16[1,1024,768]{2,1,0:T(8,128)(2,1)} async-done(((bf16[1,256,768]{2,1,0:T(8,128)(2,1)}), bf16[1,1024,768]{2,1,0:T(8,128)(2,1)}) %all-gather.11.cloned.1.call-update) | async-done | bytes 1572880 | tf_op jit(solution)/shard_map/all_gather | solution.py:116
  183.9 7.2 fusion.241
  191.9 4.6 fusion.66
  208.6 3.9 fusion.444
  215.6 8.1 convert_reduce_fusion.2
  228.0 11.7 all-gather.17.cloned.1.call-done
  242.3 4.7 broadcast_select_fusion
  247.0 11.3 fusion.451
  258.3 14.1 %all-gather.15.cloned.1.call-done = bf16[1,1024,768]{2,1,0:T(8,128)(2,1)} async-done(((bf16[1,256,768]{2,1,0:T(8,128)(2,1)}), bf16[1,1024,768]{2,1,0:T(8,128)(2,1)}) %all-gather.15.cloned.1.call-update) | async-done | bytes 1572880 | tf_op jit(solution)/shard_map/all_gather | solution.py:116
  275.3 8.3 bitcast_select_fusion.3
  286.3 4.8 fusion.291
  296.1 11.2 fusion.452
  307.3 7.3 fusion.138
  314.7 7.0 multiply_reduce_fusion.2
  321.7 6.0 multiply_convert_fusion.2
  334.8 7.9 fusion.147
  345.1 5.6 fusion.243
  350.7 11.2 fusion.453
  361.8 17.9 %reduce-scatter.7.cloned.1.call-done = bf16[1,256,768]{1,2,0:T(8,128)(2,1)} async-done(((bf16[1,1024,768]{1,2,0:T(8,128)(2,1)}), bf16[1,256,768]{1,2,0:T(8,128)(2,1)}) %reduce-scatter.7.cloned.1.call-update) | async-done | bytes 393232 | tf_op jit(solution)/shard_map/reduce_scatter | solution.py:279
  379.8 3.4 fusion.266
  385.7 3.9 fusion.69
  390.7 6.1 convert_reduce_fusion.1
  404.1 7.3 fusion.141
  411.5 6.6 multiply_reduce_fusion.1
  418.1 6.1 multiply_convert_fusion.1
  427.7 3.3 fusion.335
  431.0 5.8 fusion.302
  436.8 11.2 fusion.454
  448.0 3.3 copy.125
  452.6 15.6 %dynamic_update_slice.24 = bf16[2,1,256,767]{2,0,3,1:T(2,128)(2,1)} dynamic-update-slice(bf16[2,1,256,767]{2,0,3,1:T(2,128)(2,1)} %broadcast.1200, bf16[1,1,256,767]{2,0,3,1:T(2,128)(2,1)} %copy.125, s32[]{:T(128)S(6)} %min.22, s32[]{:T(128)} %constant.109.clone.1, s32[]{:T(128)} %constant.109.clone.1, s32[]{:T(128)} %constant.109.clone.1) | dynamic-update-slice | bytes 785412 | tf_op jit(solution)/shard_map/jit(dynamic_update_index_in_dim)/dynamic_update_slice | solution.py:311
  473.8 5.7 fusion.296
  479.6 5.7 fusion.244
  485.3 5.9 fusion.148
  491.3 3.3 fusion.264
  497.4 5.4 fusion.305
  505.7 6.0 convert_reduce_fusion
  518.8 7.3 fusion.144
  526.1 6.6 multiply_reduce_fusion
  532.8 6.2 multiply_convert_fusion
  542.3 5.7 fusion.295
  555.2 12.2 add_bitcast_fusion.1
  567.5 7.8 add_bitcast_fusion
  575.3 16.7 %reduce-scatter.15.cloned.1.call-done = bf16[1,256,768]{1,2,0:T(8,128)(2,1)} async-done(((bf16[1,1024,768]{1,2,0:T(8,128)(2,1)}), bf16[1,256,768]{1,2,0:T(8,128)(2,1)}) %reduce-scatter.15.cloned.1.call-update) | async-done | bytes 393232 | tf_op jit(solution)/shard_map/reduce_scatter | solution.py:279
  592.0 9.8 add_bitcast_fusion.2
  606.7 15.5 %dynamic_update_slice.22 = bf16[2,1,256,767]{2,0,3,1:T(2,128)(2,1)} dynamic-update-slice(bf16[2,1,256,767]{2,0,3,1:T(2,128)(2,1)} %dynamic_update_slice.21, bf16[1,1,256,767]{2,0,3,1:T(2,128)(2,1)} %copy.117, s32[]{:T(128)S(6)} %min.20, s32[]{:T(128)} %constant.109.clone.1, s32[]{:T(128)} %constant.109.clone.1, s32[]{:T(128)} %constant.109.clone.1) | dynamic-update-slice | bytes 785412 | tf_op jit(solution)/shard_map/jit(dynamic_update_index_in_dim)/dynamic_update_slice | solution.py:168
  630.0 5.7 fusion.427
  640.7 15.6 %dynamic_update_slice.23 = bf16[1,2,1,256,767]{3,1,4,2,0:T(2,128)(2,1)} dynamic-update-slice(bf16[1,2,1,256,767]{3,1,4,2,0:T(2,128)(2,1)} %bitcast.505, bf16[1,1,1,256,767]{3,1,4,2,0:T(2,128)(2,1)} %copy.122, s32[]{:T(128)} %constant.109.clone.1, s32[]{:T(128)S(6)} %min.21, s32[]{:T(128)} %constant.109.clone.1, s32[]{:T(128)} %constant.109.clone.1, s32[]{:T(128)} %constant.109.clone.1) | dynamic-update-slice | bytes 785412 | tf_op jit(solution)/shard_map/jit(dynamic_update_index_in_dim)/dynamic_update_slice | solution.py:168
  661.5 15.5 %dynamic_update_slice.25 = bf16[2,1,256,767]{2,0,3,1:T(2,128)(2,1)} dynamic-update-slice(bf16[2,1,256,767]{2,0,3,1:T(2,128)(2,1)} %dynamic_update_slice.24, bf16[1,1,256,767]{2,0,3,1:T(2,128)(2,1)} %copy.129, s32[]{:T(128)S(6)} %min.23, s32[]{:T(128)} %constant.109.clone.1, s32[]{:T(128)} %constant.109.clone.1, s32[]{:T(128)} %constant.109.clone.1) | dynamic-update-slice | bytes 785412 | tf_op jit(solution)/shard_map/jit(dynamic_update_index_in_dim)/dynamic_update_slice | solution.py:311
  689.8 3.4 fusion.262
  701.0 81.2 %all-reduce = (f32[1,1536]{1,0:T(1,128)}, f32[1,767]{1,0:T(1,128)}, f32[1,767]{1,0:T(1,128)}, f32[1,767]{1,0:T(1,128)}, f32[1,3072]{1,0:T(1,128)}, /*index=5*/f32[1,767]{1,0:T(1,128)}, f32[]{:T(128)}) all-reduce(f32[1,1536]{1,0:T(1,128)} %broadcast_in_dim.243, ...), channel_id=1, replica_groups=mesh['section'=2,'dp'=4,'seq'=4] {'dp','seq'}, use_global_device_ids=true, to_apply=%region_64.65 | all-reduce | flops 7677 | bytes 61416 | tf_op jit(solution)/shard_map/psum | solution.py:330
  782.9 15.6 %dynamic_update_slice.26 = bf16[1,2,1,256,767]{3,1,4,2,0:T(2,128)(2,1)} dynamic-update-slice(bf16[1,2,1,256,767]{3,1,4,2,0:T(2,128)(2,1)} %bitcast.504, bf16[1,1,1,256,767]{3,1,4,2,0:T(2,128)(2,1)} %copy.132, s32[]{:T(128)} %constant.109.clone.1, s32[]{:T(128)S(6)} %min.24, s32[]{:T(128)} %constant.109.clone.1, s32[]{:T(128)} %constant.109.clone.1, s32[]{:T(128)} %constant.109.clone.1) | dynamic-update-slice | bytes 785412 | tf_op jit(solution)/shard_map/jit(dynamic_update_index_in_dim)/dynamic_update_slice | solution.py:311
  798.5 539.0 %all-reduce.4.cloned.1.call-done = (f32[1,767,2304]{2,1,0:T(8,128)}, f32[1,768,767]{2,1,0:T(8,128)}, f32[1,767,3072]{2,1,0:T(8,128)}, f32[1,3072,767]{2,1,0:T(8,128)}) async-done(((f32[1,767,2304]{2,1,0:T(8,128)}, f32[1,768,767]{2,1,0:T(8,128)}, f32[1,767,3072]{2,1,0:T(8,128)}, f32[1,3072,767]{2,1,0:T(8,128)}), (f32[1,767,2304]{2,1,0:T(8,128)}, f32[1,768,767]{2,1,0:T(8,128)}, f32[1,767,3072]{2,1,0:T(8,128)}, ...) | async-done | bytes 28274704 | tf_op jit(solution)/shard_map/psum | solution.py:330
  1337.5 11.3 copy.133
  1348.8 6.7 copy.134
  1355.5 12.2 copy.135
  1367.6 20.4 %copy.136 = f32[1,3072,767]{1,0,2:T(1,128)} copy(f32[1,3072,767]{2,1,0:T(8,128)} %get-tuple-element.109) | data formatting | bytes 18849792
  (440 shorter events, 191.3 us)
Async XLA Ops:
  7.2 9.1 copy-start
  7.2 7.8 copy-start.115
  7.2 46.2 %all-gather.9.cloned.1.call-start = ((), (), s32[]{:S(2)}) async-start(), calls=%async_computation.7 | async-start | bytes 1966080 | tf_op jit(solution)/shard_map/all_gather | solution.py:113
  18.5 8.6 copy-start.117
  19.6 67.2 %all-gather.7.cloned.1.call-start = ((), (), s32[]{:S(2)}) async-start(), calls=%async_computation.6 | async-start | bytes 1966080 | tf_op jit(solution)/shard_map/all_gather | solution.py:116
  20.3 127.9 %all-gather.13.cloned.1.call-start = ((), (), s32[]{:S(2)}) async-start(), calls=%async_computation.9 | async-start | bytes 1966080 | tf_op jit(solution)/shard_map/all_gather | solution.py:113
  27.8 74.1 %copy-start.112 = (f32[767]{0:T(1024)}, f32[767]{0:T(1024)S(1)}, u32[]{:S(2)}) copy-start(f32[767]{0:T(1024)S(1)} %reduce.97) | copy-start | bytes 9208
  89.4 7.2 copy-start.15
  89.4 7.2 copy-start.38
  105.5 5.7 collective-permute-start
  113.9 220.1 %copy-start.93 = (f32[256]{0:T(256)}, f32[256]{0:T(256)S(1)}, u32[]{:S(2)}) copy-start(f32[256]{0:T(256)S(1)} %get-tuple-element.86) | copy-start | bytes 3076
  117.1 63.8 %all-gather.11.cloned.1.call-start = ((), (), s32[]{:S(2)}) async-start(), calls=%async_computation.8 | async-start | bytes 1966080 | tf_op jit(solution)/shard_map/all_gather | solution.py:116
  117.7 122.1 %all-gather.17.cloned.1.call-start = ((), (), s32[]{:S(2)}) async-start(), calls=%async_computation.11 | async-start | bytes 1966080 | tf_op jit(solution)/shard_map/all_gather | solution.py:113
  183.9 7.2 copy-start.16
  183.9 7.2 copy-start.47
  183.9 7.9 copy-start.120
  196.5 6.6 copy-start.50
  199.2 7.1 copy-start.85
  200.0 3.1 collective-permute-start.1
  208.6 63.9 %all-gather.15.cloned.1.call-start = ((), (), s32[]{:S(2)}) async-start(), calls=%async_computation.10 | async-start | bytes 1966080 | tf_op jit(solution)/shard_map/all_gather | solution.py:116
  215.4 146.4 %reduce-scatter.9.cloned.1.call-start = ((), (), s32[]{:S(2)}) async-start(), calls=%async_computation.13 | async-start | bytes 1966080 | tf_op jit(solution)/shard_map/reduce_scatter | solution.py:285
  275.2 8.3 copy-start.17
  275.2 8.3 copy-start.45
  275.3 8.3 copy-start.70
  275.3 8.3 copy-start.72
  314.6 65.1 %reduce-scatter.7.cloned.1.call-start = ((), (), s32[]{:S(2)}) async-start(), calls=%async_computation.12 | async-start | bytes 1966080 | tf_op jit(solution)/shard_map/reduce_scatter | solution.py:279
  314.7 7.0 copy-start.77
  331.0 160.2 %reduce-scatter.13.cloned.1.call-start = ((), (), s32[]{:S(2)}) async-start(), calls=%async_computation.15 | async-start | bytes 1966080 | tf_op jit(solution)/shard_map/reduce_scatter | solution.py:285
  334.7 8.0 copy-start.104
  334.7 8.0 copy-start.106
  334.7 8.0 copy-start.89
  334.7 8.0 copy-start.91
  334.7 8.6 copy-start.108
  334.7 8.6 copy-start.109
  334.7 9.2 copy-start.100
  334.7 9.2 copy-start.102
  334.7 9.7 copy-start.96
  334.7 9.7 copy-start.98
  334.8 10.3 copy-start.37
  384.2 5.5 collective-permute-start.2
  385.7 11.1 slice-start.3
  389.7 7.1 copy-start.11
  390.7 8.4 copy-start.52
  411.4 79.8 %reduce-scatter.11.cloned.1.call-start = ((), (), s32[]{:S(2)}) async-start(), calls=%async_computation.14 | async-start | bytes 1966080 | tf_op jit(solution)/shard_map/reduce_scatter | solution.py:279
  411.4 6.6 copy-start.76
  427.4 147.9 %reduce-scatter.17.cloned.1.call-start = ((), (), s32[]{:S(2)}) async-start(), calls=%async_computation.17 | async-start | bytes 1966080 | tf_op jit(solution)/shard_map/reduce_scatter | solution.py:285
  495.8 7.0 copy-start.74
  495.8 8.9 collective-permute-start.3
  497.4 8.1 copy-start.13
  497.4 14.2 %slice-start.5 = ((s8[4718592]{0:T(1024)(128)(4,1)}), s8[4194304]{0:T(1024)(128)(4,1)S(1)}, s32[]{:S(2)}) async-start(s8[4718592]{0:T(1024)(128)(4,1)} %bitcast.570), calls=%async_computation.24 | async-start | bytes 8388608
  505.4 8.4 copy-start.41
  526.1 65.9 %reduce-scatter.15.cloned.1.call-start = ((), (), s32[]{:S(2)}) async-start(), calls=%async_computation.16 | async-start | bytes 1966080 | tf_op jit(solution)/shard_map/reduce_scatter | solution.py:279
  526.1 6.6 copy-start.75
  542.2 795.3 %all-reduce.4.cloned.1.call-start = ((), (), s32[]{:S(2)}) async-start(), calls=%async_computation.18 | async-start | bytes 56623104 | tf_op jit(solution)/shard_map/psum | solution.py:330
  552.4 15.1 %slice-start = ((s8[9437184]{0:T(1024)(128)(4,1)}), s8[4194304]{0:T(1024)(128)(4,1)S(1)}, s32[]{:S(2)}) async-start(s8[9437184]{0:T(1024)(128)(4,1)} %bitcast.499), calls=%async_computation.19 | async-start | bytes 8388608
  555.2 12.3 slice-start.1
  555.2 12.3 slice-start.2
  555.2 12.3 copy-start.10
  555.2 12.3 copy-start.14
  567.5 24.5 %copy-start.87 = (f32[256]{0:T(256)S(1)}, f32[256]{0:T(256)}, u32[]{:S(2)}) copy-start(f32[256]{0:T(256)} %fusion.426) | copy-start | bytes 3076
  601.8 28.2 %copy-start.114 = (f32[767]{0:T(1024)S(1)}, f32[767]{0:T(1024)}, u32[]{:S(2)}) copy-start(f32[767]{0:T(1024)} %copy-done.112) | copy-start | bytes 9208
  658.6 26.7 %copy-start.81 = (f32[767]{0:T(1024)S(1)}, f32[767]{0:T(1024)}, u32[]{:S(2)}) copy-start(f32[767]{0:T(1024)} %get-tuple-element.116) | copy-start | bytes 9208
  658.6 26.7 %copy-start.83 = (f32[767]{0:T(1024)S(1)}, f32[767]{0:T(1024)}, u32[]{:S(2)}) copy-start(f32[767]{0:T(1024)} %get-tuple-element.114) | copy-start | bytes 9208
  658.6 29.2 %copy-start.82 = (f32[767]{0:T(1024)S(1)}, f32[767]{0:T(1024)}, u32[]{:S(2)}) copy-start(f32[767]{0:T(1024)} %get-tuple-element.110) | copy-start | bytes 9208
  (88 other events, 334.7 us)
Sparse Core Ops, SparseCore 0:
  19.7 33.6 all-gather.8
  55.8 30.9 all-gather.6
  117.2 30.9 all-gather.12
  149.9 30.9 all-gather.10
  208.7 30.9 all-gather.16
  241.4 30.9 all-gather.14
  314.7 30.9 reduce-scatter.8
  348.7 30.9 reduce-scatter.6
  411.5 31.7 reduce-scatter.12
  446.7 30.8 reduce-scatter.10
  526.2 31.9 reduce-scatter.16
  561.0 30.9 reduce-scatter.14
  601.9 735.5 all-reduce.3
where the time goes:
time: 1410 us; the launch traced here: 1400 us
  waiting for transfers between devices  663 us (47%)
  matrix products  303 us (21%)
  local copies, waits for them, and re-layouts  250 us (18%)
  blocking collectives  81.2 us (6%)
  other arithmetic  69.7 us (5%)
  between operations  19.6 us (1%)
    psum x1, waiting for transfers between devices, on_device(): lax.psum((grad_qkv, grad_bqv, grad_out, grad_bout, grad_ga, grad_gm, grad...  539 us
    psum x1, blocking collectives, on_device(): lax.psum((grad_qkv, grad_bqv, grad_out, grad_bout, grad_ga, grad_gm, grad...  81.2 us
    unnamed x278, local copies, waits for them, and re-layouts  69.2 us
    sub x6, matrix products, softmax_parts(): exps = jnp.exp(scores - row_max)  67.1 us
    all_gather x3, waiting for transfers between devices, on_device(): lax.all_gather(qkv[..., 2 * model_width:], 'seq', axis=1, tiled=True)  52.8 us
    dynamic_update_slice x3, local copies, waits for them, and re-layouts, on_device(): lax.dynamic_update_index_in_dim(outputs, jnp.where(is_live, result, curre...  46.7 us
    dynamic_update_slice x3, local copies, waits for them, and re-layouts, on_device(): lax.dynamic_update_index_in_dim(input_grads, jnp.where(is_live, grad_low,...  46.7 us
    reduce_scatter x3, waiting for transfers between devices, on_device(): lax.psum_scatter(key_grad_all.reshape(row_count, seq_len, model_width).as...  34.6 us
  transfers between devices with their start and end apart: 17, of which 10 were waited for; matrix products, arithmetic and copies ran while one was open for 29% of the time, Pallas kernels for 0%

commit v1 on v0

v1 whole, which is shorter than its diff:
```python
import functools

import jax
import jax.numpy as jnp
from jax import lax
from jax.experimental import pallas as pl
from jax.experimental.pallas import tpu as pltpu
from jax.sharding import PartitionSpec as P

HEADS = 12
EPS = 1e-6
NEG = -1e30
F32 = jnp.float32
BF16 = jnp.bfloat16
MIB = 1 << 20
QUAD = 4


def nn(a, b):
    return lax.dot_general(a, b, (((1,), (0,)), ((), ())), preferred_element_type=F32)


def nt(a, b):
    return lax.dot_general(a, b, (((1,), (1,)), ((), ())), preferred_element_type=F32)


def tn(a, b):
    return lax.dot_general(a, b, (((0,), (0,)), ((), ())), preferred_element_type=F32)


def order(core, k):
    if isinstance(k, int):
        return jnp.where(core == 1, k, ((k & 1) << 1) | (k >> 1))
    return jnp.where(core == 1, k, ((k & 1) << 1) | (k >> 1))


def crms_scale(v):
    sq = jnp.sum(v * v, axis=-1, keepdims=True)
    su = jnp.sum(v, axis=-1, keepdims=True)
    full = v.shape[-1] + 1
    return lax.rsqrt((sq + su * su) / full + EPS), su, (sq + su * su) / full


def crms_back(v, gain, grad):
    r, su, _ = crms_scale(v)
    gd = grad * gain
    w = jnp.sum(gd * v, axis=-1, keepdims=True)
    unit = v * r
    dv = gd * r - (w * r * r * r / (v.shape[-1] + 1)) * (v + su)
    return dv, grad * unit, unit * gain


GC = 0.7978845608028654


def gelu_parts(u):
    inner = GC * (u + 0.044715 * (u * u * u))
    th = jnp.tanh(inner)
    return th


def params(mib, **kw):
    return pltpu.CompilerParams(vmem_limit_bytes=mib * MIB, **kw)


def cost(flops, nbytes, trans=0):
    return pl.CostEstimate(flops=int(flops), bytes_accessed=int(nbytes), transcendentals=int(trans))


SMEM = pl.BlockSpec(memory_space=pltpu.SMEM)
VMEM = pl.BlockSpec(memory_space=pltpu.VMEM)
ANY = pl.BlockSpec(memory_space=pl.ANY)


def norm_kernel(x_ref, pv_ref, o_ref):
    x = x_ref[...].astype(F32)
    r, _, _ = crms_scale(x)
    o_ref[...] = (x * r * pv_ref[3:4, : x.shape[-1]]).astype(BF16)


def first_norm(x, pv):
    return pl.pallas_call(
        norm_kernel,
        in_specs=[VMEM, VMEM],
        out_specs=VMEM,
        out_shape=jax.ShapeDtypeStruct(x.shape, BF16),
        compiler_params=params(8),
        cost_estimate=cost(0, x.size * 4),
    )(x, pv)


def visible_bias(ids, n, t, span):
    i = t * span + lax.broadcasted_iota(jnp.int32, (1, span), 1)
    start = jnp.zeros((1, span), jnp.int32)
    for d in range(4):
        end = ids[2 + d]
        start = jnp.maximum(start, jnp.where(i >= end, end, 0))
    j = lax.broadcasted_iota(jnp.int32, (n, span), 0)
    return jnp.where((j >= start) & (j <= i), 0.0, NEG)


def attn_fwd_kernel(
    ids, n0, n1, n2, n3, w_ref, pv_ref, qh, kh, vh, lse, a0, a1, a2, a3, at, bias_scr
):
    c, s = ids[0], ids[1]
    heads, _, hd = qh.shape
    span = n0.shape[0]
    width = heads * hd
    bias = pv_ref[5:6, : 3 * width]
    for p, nb in enumerate((n0, n1, n2, n3)):
        t = jnp.bitwise_xor(order(c, p), s)
        row = pl.multiple_of(t * span, span)
        y = nn(nb[...], w_ref[...]) + bias
        for h in range(heads):
            lo = h * hd
            qh[h, pl.ds(row, span), :] = (y[:, lo : lo + hd] * (hd**-0.5)).astype(BF16)
            kh[h, pl.ds(row, span), :] = y[:, width + lo : width + lo + hd].astype(BF16)
            vh[h, pl.ds(row, span), :] = y[:, 2 * width + lo : 2 * width + lo + hd].astype(BF16)
    for t in range(QUAD):
        n = span * (t + 1)
        bias_scr[:n, :] = visible_bias(ids, n, t, span)

        def head(h, carry, t=t, n=n):
            q = qh[h, t * span : (t + 1) * span, :]
            sc = nt(kh[h, :n, :], q) + bias_scr[:n, :]
            m = jnp.max(sc, axis=0, keepdims=True)
            e = jnp.exp(sc - m)
            tot = jnp.sum(e, axis=0, keepdims=True)
            pr = (e * (1.0 / tot)).astype(BF16)
            o = tn(vh[h, :n, :], pr)
            at[t, pl.ds(pl.multiple_of(h * hd, hd), hd), :] = o.astype(BF16)
            lse[h, t : t + 1, :] = m + jnp.log(tot)
            return carry

        lax.fori_loop(0, heads, head, 0)
    for k, a in enumerate((a0, a1, a2, a3)):
        a[...] = at[jnp.bitwise_xor(s, k)]


def attn_fwd(ids, blocks, w3, pv, heads, hd):
    span, width = blocks[0].shape
    full = span * QUAD
    hh = jax.ShapeDtypeStruct((heads, full, hd), BF16)
    aa = jax.ShapeDtypeStruct((heads * hd, span), BF16)
    return pl.pallas_call(
        attn_fwd_kernel,
        in_specs=[SMEM] + [VMEM] * 6,
        out_specs=[VMEM] * 8,
        out_shape=[hh, hh, hh, jax.ShapeDtypeStruct((heads, QUAD, span), F32), aa, aa, aa, aa],
        scratch_shapes=[
            pltpu.VMEM((QUAD, heads * hd, span), BF16),
            pltpu.VMEM((full, span), F32),
        ],
        compiler_params=params(40),
        cost_estimate=cost(
            2 * full * width * 3 * heads * hd + 3 * 4 * full * full * hd * heads,
            4 * full * width,
            heads * full * full,
        ),
    )(ids, *blocks, w3, pv)


def mlp_fwd_kernel(
    layer, ids, x, a0, a1, a2, a3, wo, pv, pvn, pvb, upo, upr, dno, dnr,
    mid, u, xout, nnext, sq, astk, nm, acc,
):
    j = pl.program_id(0)
    c, s = ids[0], ids[1]
    cc = x.shape[-1]
    own = c == layer

    @pl.when(j == 0)
    def _():
        rows = a0.shape[0]
        m = x[...].astype(F32) + pv[1:2, :cc]
        for k, a in enumerate((a0, a1, a2, a3)):
            row = pl.multiple_of(jnp.bitwise_xor(s, k) * rows, rows)
            m = m + tn(a[...], wo[pl.ds(row, rows), :])
            astk[k] = a[...]
        mid[...] = m
        r, _, _ = crms_scale(m)
        nm[...] = (m * r * pv[4:5, :cc]).astype(BF16)
        acc[...] = m + pv[2:3, :cc]

    wu = lax.select(own, upo[0], upr[0])
    wd = lax.select(own, dno[0], dnr[0])
    ub = nn(nm[...], wu) + pvb[0:1, :]
    u[...] = ub
    act = (0.5 * ub * (1.0 + gelu_parts(ub))).astype(BF16)
    acc[...] += nn(act, wd)

    @pl.when(j == pl.num_programs(0) - 1)
    def _():
        fin = acc[...]
        _, _, ms = crms_scale(fin)
        sq[...] = jnp.broadcast_to(jnp.sum(ms, axis=0, keepdims=True), sq.shape)
        low = fin.astype(BF16)
        xout[...] = low
        lf = low.astype(F32)
        r, _, _ = crms_scale(lf)
        nnext[...] = (lf * r * pvn[3:4, :cc]).astype(BF16)


def mlp_fwd(layer, ids, x, att, wo, pv, pvn, up, dn):
    span, cc = x.shape
    ff = up[0].shape[-1]
    fb = ff // 8
    rows = att[0].shape[0]

    def whole(shape):
        return pl.BlockSpec(shape, lambda j, ids: (0,) * len(shape))

    def pick(mine):
        return lambda j, ids: jnp.where((ids[0] == layer) == mine, j, 0)

    mine, other = pick(True), pick(False)
    grid = pltpu.PrefetchScalarGridSpec(
        num_scalar_prefetch=1,
        grid=(8,),
        in_specs=[whole((span, cc))]
        + [whole((rows, span))] * 4
        + [whole(wo.shape), whole(pv.shape), whole(pvn.shape)]
        + [
            pl.BlockSpec((8, fb), lambda j, ids: (0, j)),
            pl.BlockSpec((1, cc, fb), lambda j, ids: (0, 0, mine(j, ids))),
            pl.BlockSpec((1, cc, fb), lambda j, ids: (0, 0, other(j, ids))),
            pl.BlockSpec((1, fb, cc), lambda j, ids: (0, mine(j, ids), 0)),
            pl.BlockSpec((1, fb, cc), lambda j, ids: (0, other(j, ids), 0)),
        ],
        out_specs=[
            whole((span, cc)),
            pl.BlockSpec((span, fb), lambda j, ids: (0, j)),
            whole((span, cc)),
            whole((span, cc)),
            whole((8, 128)),
            whole((QUAD, rows, span)),
        ],
        scratch_shapes=[pltpu.VMEM((span, cc), BF16), pltpu.VMEM((span, cc), F32)],
    )
    return pl.pallas_call(
        functools.partial(mlp_fwd_kernel, layer),
        grid_spec=grid,
        out_shape=[
            jax.ShapeDtypeStruct((span, cc), F32),
            jax.ShapeDtypeStruct((span, ff), F32),
            jax.ShapeDtypeStruct((span, cc), BF16),
            jax.ShapeDtypeStruct((span, cc), BF16),
            jax.ShapeDtypeStruct((8, 128), F32),
            jax.ShapeDtypeStruct((QUAD, rows, span), BF16),
        ],
        compiler_params=params(40, dimension_semantics=("arbitrary",)),
        cost_estimate=cost(6 * span * cc * ff, 4 * cc * ff + 4 * span * ff, span * ff),
    )(ids, x, *att, wo, pv, pvn, pv, up[0], up[1], dn[0], dn[1])


def mlp_bwd_kernel(
    layer, ids, df, u, mid, wo, pv, upo, upr, dno, dnr,
    lr, rr, dmid, dmlow, g, d0, d1, d2, d3, acc,
):
    j = pl.program_id(0)
    c, s = ids[0], ids[1]
    cc = df.shape[-1]
    fb = u.shape[-1]
    own = c == layer

    @pl.when(j == 0)
    def _():
        acc[...] = jnp.zeros_like(acc)
        g[...] = jnp.zeros_like(g)

    wu = lax.select(own, upo[0], upr[0])
    wd = lax.select(own, dno[0], dnr[0])
    da = nt(df[...], wd)
    ub = u[...]
    th = gelu_parts(ub)
    half = 0.5 * (1.0 + th)
    lr[0] = (ub * half).astype(BF16)
    slope = half + 0.5 * ub * (1.0 - th * th) * (GC * (1.0 + 3 * 0.044715 * (ub * ub)))
    du = (slope * da).astype(BF16)
    lr[1] = du
    g[0:1, pl.ds(pl.multiple_of(j * fb, 128), fb)] = jnp.sum(du.astype(F32), axis=0, keepdims=True)
    acc[...] += nt(du, wu)

    @pl.when(j == pl.num_programs(0) - 1)
    def _():
        dff = df[...].astype(F32)
        dv, gg, nm = crms_back(mid[...], pv[4:5, :cc], acc[...])
        dm = dff + dv
        low = dm.astype(BF16)
        rr[0] = df[...]
        rr[1] = nm.astype(BF16)
        dmid[...] = dm
        dmlow[...] = low
        g[1:2, :cc] = jnp.sum(low.astype(F32), axis=0, keepdims=True)
        g[2:3, :cc] = jnp.sum(dff, axis=0, keepdims=True)
        g[4:5, :cc] = jnp.sum(gg, axis=0, keepdims=True)
        rows = d0.shape[0]
        for k, d in enumerate((d0, d1, d2, d3)):
            row = pl.multiple_of(jnp.bitwise_xor(s, k) * rows, rows)
            d[...] = nt(wo[pl.ds(row, rows), :], low).astype(BF16)


def mlp_bwd(layer, ids, df, u, mid, wo, pv, up, dn):
    span, cc = df.shape
    ff = u.shape[-1]
    fb = ff // 8
    rows = wo.shape[0] // QUAD

    def whole(shape):
        return pl.BlockSpec(shape, lambda j, ids: (0,) * len(shape))

    def pick(mine):
        return lambda j, ids: jnp.where((ids[0] == layer) == mine, j, 0)

    mine, other = pick(True), pick(False)
    grid = pltpu.PrefetchScalarGridSpec(
        num_scalar_prefetch=1,
        grid=(8,),
        in_specs=[
            whole((span, cc)),
            pl.BlockSpec((span, fb), lambda j, ids: (0, j)),
            whole((span, cc)),
            whole(wo.shape),
            whole(pv.shape),
            pl.BlockSpec((1, cc, fb), lambda j, ids: (0, 0, mine(j, ids))),
            pl.BlockSpec((1, cc, fb), lambda j, ids: (0, 0, other(j, ids))),
            pl.BlockSpec((1, fb, cc), lambda j, ids: (0, mine(j, ids), 0)),
            pl.BlockSpec((1, fb, cc), lambda j, ids: (0, other(j, ids), 0)),
        ],
        out_specs=[
            pl.BlockSpec((2, span, fb), lambda j, ids: (0, 0, j)),
            whole((2, span, cc)),
            whole((span, cc)),
            whole((span, cc)),
            whole((8, ff)),
        ]
        + [whole((rows, span))] * 4,
        scratch_shapes=[pltpu.VMEM((span, cc), F32)],
    )
    dd = jax.ShapeDtypeStruct((rows, span), BF16)
    return pl.pallas_call(
        functools.partial(mlp_bwd_kernel, layer),
        grid_spec=grid,
        out_shape=[
            jax.ShapeDtypeStruct((2, span, ff), BF16),
            jax.ShapeDtypeStruct((2, span, cc), BF16),
            jax.ShapeDtypeStruct((span, cc), F32),
            jax.ShapeDtypeStruct((span, cc), BF16),
            jax.ShapeDtypeStruct((8, ff), F32),
            dd, dd, dd, dd,
        ],
        compiler_params=params(40, dimension_semantics=("arbitrary",)),
        cost_estimate=cost(6 * span * cc * ff, 4 * cc * ff + 8 * span * ff, span * ff),
    )(ids, df, u, mid, wo, pv, up[0], up[1], dn[0], dn[1])


def product_kernel(send, ids, lr, rr, att, dmlow, *rest):
    out = rest[-1]
    core = 1 - ids[0] if send else ids[0]
    block = lr.shape[-1]
    part = att.shape[1] // 2
    main = tn(lr[0], rr[0])
    row = pl.multiple_of(core * part, part)
    side = nn(att[0, pl.ds(row, part), :], dmlow[...])
    if send:
        out[:block, :] = main.astype(BF16)
        out[block:, :] = side.astype(BF16)
    else:
        got = rest[0]
        out[:block, :] = (main + got[:block, :].astype(F32)).astype(BF16)
        out[block:, :] = (side + got[block:, :].astype(F32)).astype(BF16)


def product(send, place, ids, lr, rr, att, dmlow, got=None):
    span, cc = dmlow.shape
    block = lr.shape[-1] // QUAD
    rows = att.shape[1]
    total = block + rows // 2

    def core(ids):
        return 1 - ids[0] if send else ids[0]

    def offset(ids):
        return order(core(ids), place)

    in_specs = [
        pl.BlockSpec((1, span, block), lambda i, ids: (core(ids), 0, offset(ids) ^ ids[1])),
        pl.BlockSpec((1, span, cc), lambda i, ids: (core(ids), 0, 0)),
        pl.BlockSpec((1, rows, span), lambda i, ids: (offset(ids), 0, 0)),
        pl.BlockSpec((span, cc), lambda i, ids: (0, 0)),
    ]
    operands = [lr, rr, att, dmlow]
    if not send:
        in_specs.append(pl.BlockSpec((total, cc), lambda i, ids: (0, 0)))
        operands.append(got)
    return pl.pallas_call(
        functools.partial(product_kernel, send),
        grid_spec=pltpu.PrefetchScalarGridSpec(
            num_scalar_prefetch=1,
            grid=(1,),
            in_specs=in_specs,
            out_specs=pl.BlockSpec((total, cc), lambda i, ids: (0, 0)),
        ),
        out_shape=jax.ShapeDtypeStruct((total, cc), BF16),
        compiler_params=params(24, dimension_semantics=("arbitrary",)),
        cost_estimate=cost(2 * span * total * cc, 2 * total * cc * 2),
    )(ids, *operands)


def attn_bwd_kernel(
    ids, n0, n1, n2, n3, w_ref, qh, kh, vh, lse, d0, d1, d2, d3,
    p0, p1, p2, p3, gs, gk, gb, do, dk, dv, dy, acc, bias_scr,
):
    c, s = ids[0], ids[1]
    heads, _, hd = qh.shape
    span = n0.shape[0]
    width = heads * hd
    for k, d in enumerate((d0, d1, d2, d3)):
        do[jnp.bitwise_xor(s, k)] = d[...]
    for t in reversed(range(QUAD)):
        n = span * (t + 1)
        bias_scr[:n, :] = visible_bias(ids, n, t, span)
        for h in range(heads):
            q = qh[h, t * span : (t + 1) * span, :]
            kk = kh[h, :n, :]
            sc = nt(kk, q) + (bias_scr[:n, :] - lse[h, t : t + 1, :])
            pr = jnp.exp(sc)
            dot = do[t, h * hd : (h + 1) * hd, :]
            dp = nn(vh[h, :n, :], dot)
            inner = jnp.sum(pr * dp, axis=0, keepdims=True)
            ds = (pr * (dp - inner)).astype(BF16)
            newk = nn(ds, q)
            newv = nt(pr.astype(BF16), dot)
            if t == QUAD - 1:
                dk[h, :n, :] = newk
                dv[h, :n, :] = newv
            else:
                dk[h, :n, :] += newk
                dv[h, :n, :] += newv
            dq = tn(kk, ds) * (hd**-0.5)
            dy[t * span : (t + 1) * span, h * hd : (h + 1) * hd] = dq.T.astype(BF16)
    for h in range(heads):
        dy[:, width + h * hd : width + (h + 1) * hd] = dk[h].astype(BF16)
        dy[:, 2 * width + h * hd : 2 * width + (h + 1) * hd] = dv[h].astype(BF16)
    total = jnp.zeros((1, 3 * width), F32)
    for p, (nb, out) in enumerate(((n0, p0), (n1, p1), (n2, p2), (n3, p3))):
        row = pl.multiple_of(jnp.bitwise_xor(order(c, p), s) * span, span)
        y = dy[pl.ds(row, span), :]
        out[...] = nt(y, w_ref[...]).astype(BF16)
        total = total + jnp.sum(y.astype(F32), axis=0, keepdims=True)
        g = tn(y, nb[...])
        if p == 0:
            acc[...] = g
        else:
            acc[...] += g
    gb[...] = jnp.broadcast_to(total, gb.shape)
    part = gs.shape[0]

    @pl.when(c == 0)
    def _():
        gk[...] = acc[:part, :].astype(BF16)
        gs[...] = acc[part:, :].astype(BF16)

    @pl.when(c == 1)
    def _():
        gs[...] = acc[:part, :].astype(BF16)
        gk[...] = acc[part:, :].astype(BF16)


def attn_bwd(ids, blocks, w3, qkvl, douts):
    span, cc = blocks[0].shape
    heads, full, hd = qkvl[0].shape
    width = heads * hd
    part = 3 * width // 2
    pp = jax.ShapeDtypeStruct((span, cc), BF16)
    gg = jax.ShapeDtypeStruct((part, cc), BF16)
    return pl.pallas_call(
        attn_bwd_kernel,
        in_specs=[SMEM] + [VMEM] * 13,
        out_specs=[VMEM] * 7,
        out_shape=[pp, pp, pp, pp, gg, gg, jax.ShapeDtypeStruct((8, 3 * width), F32)],
        scratch_shapes=[
            pltpu.VMEM((QUAD, width, span), BF16),
            pltpu.VMEM((heads, full, hd), F32),
            pltpu.VMEM((heads, full, hd), F32),
            pltpu.VMEM((full, 3 * width), BF16),
            pltpu.VMEM((3 * width, cc), F32),
            pltpu.VMEM((full, span), F32),
        ],
        compiler_params=params(48),
        cost_estimate=cost(
            4 * full * cc * 3 * width + 3 * 10 * full * full * hd * heads,
            8 * full * cc,
            heads * full * full,
        ),
    )(ids, *blocks, w3, *qkvl, *douts)


def input_kernel(part, r0, r1, dmid, x, pv, dx, gg):
    cc = x.shape[-1]
    dn = part[...].astype(F32) + r0[...].astype(F32) + r1[...].astype(F32)
    dv, g, _ = crms_back(x[...].astype(F32), pv[3:4, :cc], dn)
    dx[...] = (dmid[...] + dv).astype(BF16)
    gg[...] = jnp.broadcast_to(jnp.sum(g, axis=0, keepdims=True), gg.shape)


def input_grad_of(part, r0, r1, dmid, x, pv):
    return pl.pallas_call(
        input_kernel,
        in_specs=[VMEM] * 6,
        out_specs=[VMEM] * 2,
        out_shape=[
            jax.ShapeDtypeStruct(x.shape, BF16),
            jax.ShapeDtypeStruct((8, x.shape[-1]), F32),
        ],
        compiler_params=params(16),
        cost_estimate=cost(0, x.size * 14),
    )(part, r0, r1, dmid, x, pv)


def place_kernel(place, first, ids, *refs):
    srcs = refs[:4]
    outs = refs[4:7] if first else refs[7:10]
    x0, x1, od, ou, ow, sem = refs[7:] if first else refs[10:]
    c, s = ids[0], ids[1]
    down, up, wout = outs
    f0, r1, r0, f1 = srcs

    @pl.when(c == 0)
    def _():
        a = pltpu.make_async_copy(f0, x0, sem.at[0])
        b = pltpu.make_async_copy(r0, x1, sem.at[1])
        a.start()
        b.start()
        a.wait()
        b.wait()

    @pl.when(c != 0)
    def _():
        a = pltpu.make_async_copy(r1, x0, sem.at[0])
        b = pltpu.make_async_copy(f1, x1, sem.at[1])
        a.start()
        b.start()
        a.wait()
        b.wait()

    block = od.shape[0]
    part = ow.shape[1]
    t0 = jnp.bitwise_xor(((place & 1) << 1) | (place >> 1), s)
    t1 = jnp.bitwise_xor(place, s)
    od[...] = x0[:block, :].astype(F32)
    ow[0] = x0[block:, :].astype(F32)
    ow[1] = x1[block:, :].astype(F32)
    ca = pltpu.make_async_copy(od, down.at[pl.ds(pl.multiple_of(t0 * block, block), block), :], sem.at[0])
    cb = pltpu.make_async_copy(
        ow.at[0], wout.at[pl.ds(pl.multiple_of(t0 * 2 * part, part), part), :], sem.at[1]
    )
    cd = pltpu.make_async_copy(
        ow.at[1], wout.at[pl.ds(pl.multiple_of((t1 * 2 + 1) * part, part), part), :], sem.at[2]
    )
    ca.start()
    cb.start()
    cd.start()
    ou[...] = x1[:block, :].astype(F32).T
    ce = pltpu.make_async_copy(ou, up.at[:, pl.ds(pl.multiple_of(t1 * block, block), block)], sem.at[3])
    ce.start()
    ca.wait()
    cb.wait()
    cd.wait()
    ce.wait()


def place_rows(place, ids, srcs, outs, shapes):
    total, cc = srcs[0].shape
    block = shapes[0][0] // QUAD
    part = total - block
    first = outs is None
    operands = [ids, *srcs] + ([] if first else list(outs))
    return pl.pallas_call(
        functools.partial(place_kernel, place, first),
        in_specs=[SMEM] + [ANY] * (len(operands) - 1),
        out_specs=[ANY] * 3,
        out_shape=[jax.ShapeDtypeStruct(s, F32) for s in shapes],
        input_output_aliases={} if first else {5: 0, 6: 1, 7: 2},
        scratch_shapes=[
            pltpu.VMEM((total, cc), BF16),
            pltpu.VMEM((total, cc), BF16),
            pltpu.VMEM((block, cc), F32),
            pltpu.VMEM((cc, block), F32),
            pltpu.VMEM((2, part, cc), F32),
            pltpu.SemaphoreType.DMA((4,)),
        ],
        compiler_params=params(24),
        cost_estimate=cost(0, 12 * total * cc),
    )(*operands)


def qkv_out_kernel(width, ids, *refs):
    srcs, out, rows, sem = refs[:16], refs[16], refs[17], refs[18]
    c, s = ids[0], ids[1]
    part = 3 * width // 2
    group = QUAD * width

    def copies(place, head, tail):
        t0 = jnp.bitwise_xor(((place & 1) << 1) | (place >> 1), s) * width
        t1 = jnp.bitwise_xor(place, s) * width
        spans = (
            (head, 0, width, t0),
            (head, width, part - width, group + t0),
            (tail, 0, 2 * width - part, group + t1 + (part - width)),
            (tail, 2 * width - part, width, 2 * group + t1),
        )
        return [
            pltpu.make_async_copy(
                src.at[pl.ds(lo, size), :],
                rows.at[pl.ds(pl.multiple_of(dst, width // 2), size), :],
                sem.at[place, i],
            )
            for i, (src, lo, size, dst) in enumerate(spans)
        ]

    def run(pick):
        todo = []
        for p in range(QUAD):
            f0, r1, r0, f1 = srcs[4 * p : 4 * p + 4]
            todo += copies(p, *pick(f0, r1, r0, f1))
        for one in todo:
            one.start()
        for one in todo:
            one.wait()

    @pl.when(c == 0)
    def _():
        run(lambda f0, r1, r0, f1: (f0, r0))

    @pl.when(c != 0)
    def _():
        run(lambda f0, r1, r0, f1: (r1, f1))

    for i in range(3):
        out[:, i * group : (i + 1) * group] = rows[i * group : (i + 1) * group, :].astype(F32).T


def qkv_out(ids, srcs, width, shape):
    cc = srcs[0].shape[-1]
    return pl.pallas_call(
        functools.partial(qkv_out_kernel, width),
        in_specs=[SMEM] + [ANY] * 16,
        out_specs=VMEM,
        out_shape=jax.ShapeDtypeStruct(shape, F32),
        scratch_shapes=[
            pltpu.VMEM((3 * QUAD * width, cc), BF16),
            pltpu.SemaphoreType.DMA((QUAD, 4)),
        ],
        compiler_params=params(32),
        cost_estimate=cost(0, 6 * shape[0] * shape[1]),
    )(ids, *srcs)


def to_first(v):
    pairs = [(i, i ^ 1) for i in range(QUAD)] + [(QUAD + i, QUAD + (i ^ 2)) for i in range(QUAD)]
    return lax.ppermute(v, ("section", "seq"), pairs)


def to_second(v):
    pairs = [(i, i ^ 2) for i in range(QUAD)] + [(QUAD + i, QUAD + (i ^ 1)) for i in range(QUAD)]
    return lax.ppermute(v, ("section", "seq"), pairs)


def to_quad(v, k):
    return lax.ppermute(v, "seq", [(i, i ^ k) for i in range(QUAD)])


def to_core(v):
    return lax.ppermute(v, "section", [(0, 1), (1, 0)])


def dp_partner(v, step):
    n = lax.axis_size("dp")
    return lax.ppermute(v, "dp", [(i, i ^ step) for i in range(n)])


def dp_sum(v):
    n = lax.axis_size("dp")
    z = lax.axis_index("dp")
    rows, cc = v.shape
    piece = rows // n
    steps = []
    cur = v.reshape(n, piece, cc)
    step = 1
    while step < n:
        cur = cur.reshape(cur.shape[0] // 2, 2, piece, cc)
        low = (z & step) == 0
        away = jnp.where(low, cur[:, 1], cur[:, 0])
        keep = jnp.where(low, cur[:, 0], cur[:, 1])
        cur = (keep.astype(F32) + dp_partner(away, step).astype(F32)).astype(BF16)
        steps.append(step)
        step *= 2
    for step in reversed(steps):
        low = (z & step) == 0
        got = dp_partner(cur, step)
        cur = jnp.where(low, jnp.stack([cur, got], 1), jnp.stack([got, cur], 1))
        cur = cur.reshape(-1, piece, cc)
    return cur.reshape(rows, cc)


def add_low(a, b):
    return (a.astype(F32) + b.astype(F32)).astype(BF16)


def quad_gather(own):
    one = to_second(own)
    two = to_first(own)
    three = to_first(one)
    return [own, one, two, three]


def on_device(
    layer_in, cotangent, lengths, w_qkv, bias_qv, w_out, bias_out,
    gain_attn, gain_mlp, w_up, bias_up, w_down, bias_down,
):
    micro, _, span, cc = layer_in.shape
    model = w_out.shape[1]
    ff = w_up.shape[-1]
    hd = model // HEADS
    width = model // QUAD
    heads = width // hd
    c = lax.axis_index("section")
    s = lax.axis_index("seq")
    dp_count = lax.axis_size("dp")
    mine = c == 0

    x0 = lax.dynamic_index_in_dim(layer_in, c, 0, keepdims=False)[0]
    cot = lax.dynamic_index_in_dim(cotangent, c, 0, keepdims=False)[0]
    lens = lax.dynamic_index_in_dim(lengths, c, 0, keepdims=False)[0]
    e0 = lens[0]
    e1 = e0 + lens[1]
    e2 = e1 + lens[2]
    e3 = e2 + lens[3]
    ids = jnp.stack([c, s, e0, e1, e2, e3, c, s]).astype(jnp.int32)

    def row(v, n=ff):
        return jnp.pad(v, ((0, 0), (0, n - v.shape[-1])))

    qb = lax.dynamic_slice_in_dim(bias_qv, s * width, width, 1)
    vb = lax.dynamic_slice_in_dim(bias_qv, model + s * width, width, 1)
    heads_bias = jnp.concatenate([qb, jnp.zeros((1, width), F32), vb], 1)
    pv_own = jnp.concatenate(
        [row(v) for v in (bias_up, bias_out, bias_down, gain_attn, gain_mlp, heads_bias)]
        + [jnp.zeros((2, ff), F32)]
    )
    w3_own = jnp.concatenate(
        [lax.dynamic_slice_in_dim(w_qkv[0], i * model + s * width, width, 1) for i in range(3)], 1
    )
    pv_got = to_core(pv_own)
    w3_got = to_core(w3_own)
    wo_got = to_core(w_out[0])
    up = (w_up, to_core(w_up))
    dn = (w_down, to_core(w_down))
    pv = [jnp.where(mine, pv_own, pv_got), jnp.where(mine, pv_got, pv_own)]
    w3 = [jnp.where(mine, w3_own, w3_got), jnp.where(mine, w3_got, w3_own)]
    wo = [jnp.where(mine, w_out[0], wo_got), jnp.where(mine, wo_got, w_out[0])]

    x = x0
    normed = first_norm(x0, pv[0])
    saved = []
    squares = []
    for l in range(2):
        blocks = quad_gather(normed)
        qh, kh, vh, lse, *att = attn_fwd(ids, blocks, w3[l], pv[l], heads, hd)
        att = [att[0]] + [to_quad(att[k], k) for k in (1, 2, 3)]
        mid, u, xout, normed, sq, astk = mlp_fwd(
            l, ids, x, att, wo[l], pv[l], pv[min(l + 1, 1)], up, dn
        )
        saved.append((x, blocks, (qh, kh, vh, lse), astk, mid, u))
        squares.append(sq[0, 0])
        x = xout
    outs = [saved[1][0], x]

    df = cot
    grads = [None, None]
    smalls = [None, None]
    in_grads = [None, None]
    for l in (1, 0):
        xl, blocks, qkvl, astk, mid, u = saved[l]
        lr, rr, dmid, dmlow, g, *douts = mlp_bwd(l, ids, df, u, mid, wo[l], pv[l], up, dn)
        douts = [douts[0]] + [to_quad(douts[k], k) for k in (1, 2, 3)]
        got = [None] * QUAD
        for p in (3, 1, 2, 0):
            got[p] = to_core(product(True, p, ids, lr, rr, astk, dmlow))
        tot = [None] * QUAD
        for p in (3, 1, 2, 0):
            tot[p] = product(False, p, ids, lr, rr, astk, dmlow, got[p])
        half1 = add_low(tot[1], to_first(tot[3]))
        half0 = add_low(tot[0], to_first(tot[2]))
        quarter = add_low(half0, to_second(half1))

        p0, p1, p2, p3, gs, gk, gb = attn_bwd(ids, blocks, w3[l], qkvl, douts)
        q1 = add_low(p1, to_first(p3))
        dx, gg = input_grad_of(p0, to_first(p2), to_second(q1), dmid, xl, pv[l])
        tq = add_low(gk, to_core(gs))
        grads[l] = (quad_gather(dp_sum(quarter)), quad_gather(dp_sum(tq)))

        spot = jnp.arange(QUAD)[:, None] == s
        qs = jnp.where(spot, gb[0:1, :width], 0.0).reshape(model)
        vs = jnp.where(spot, gb[0:1, 2 * width :], 0.0).reshape(model)
        pad = jnp.zeros((1,), F32)
        smalls[l] = jnp.concatenate(
            [g[0], g[1, :cc], pad, g[2, :cc], pad, gg[0, :cc], pad, g[4, :cc], pad, qs, vs]
            + [jnp.broadcast_to(squares[l], (128,))]
        ).reshape(-1, 128)
        in_grads[l] = dx
        df = dx

    small = jnp.where(mine, smalls[0], smalls[1]) + to_core(jnp.where(mine, smalls[1], smalls[0]))
    for k in (1, 2):
        small = small + to_quad(small, k)
    step = 1
    while step < dp_count:
        small = small + dp_partner(small, step)
        step *= 2
    small = small.reshape(-1)

    def handed(l, i):
        pairs = [(1, 0)] if l == 0 else [(0, 1)]
        return [lax.ppermute(f, "section", pairs) for f in grads[l][i]]

    shapes = [(ff, cc), (cc, ff), (model, cc)]
    outs_w = None
    r1m, r0m = handed(1, 0), handed(0, 0)
    r1q, r0q = handed(1, 1), handed(0, 1)
    srcs = []
    for p in range(QUAD):
        srcs += [grads[0][1][p], r1q[p], r0q[p], grads[1][1][p]]
    grad_qkv = qkv_out(ids, srcs, width, (cc, 3 * model))
    for p in range(QUAD):
        outs_w = place_rows(
            p, ids, [grads[0][0][p], r1m[p], r0m[p], grads[1][0][p]], outs_w, shapes
        )
    grad_down, grad_up, grad_out = outs_w

    def both(pair):
        own = jnp.where(mine, pair[0], pair[1])
        got = to_core(jnp.where(mine, pair[1], pair[0]))
        return jnp.where(mine, jnp.stack([own, got]), jnp.stack([got, own]))[None, :, None]

    layer_out = both(outs)
    input_grad = both(in_grads)

    def take(lo, n):
        return small[lo : lo + n][None]

    d = cc + 1
    at = ff
    total = micro * dp_count * span * QUAD
    base = ff + 4 * d
    rms = jnp.sqrt(small[base + 2 * model] / total).reshape(1)
    return (
        layer_out,
        input_grad,
        grad_qkv[None],
        take(base, 2 * model),
        grad_out[None],
        take(at, cc),
        take(at + 2 * d, cc),
        take(at + 3 * d, cc),
        grad_up[None],
        take(0, ff),
        grad_down[None],
        take(at + d, cc),
        rms,
    )


def solution(mesh):
    two = P("section", None)
    three = P("section", None, None)
    tokens = P(None, "dp", "seq", None)
    stacked = P("section", None, "dp", "seq", None)
    return jax.shard_map(
        on_device,
        mesh=mesh,
        in_specs=(
            tokens, tokens, P(None, "dp", None), three, two, three, two, two, two, three, two, three, two,
        ),
        out_specs=(
            stacked, stacked, three, two, three, two, two, two, three, two, three, two, P("section"),
        ),
        check_vma=False,
    )
```

time: 1410 us -> 639 us (0.45)
  waiting for transfers between devices: 663 us -> 209 us
  matrix products: 303 us -> 0 us
  Pallas kernels: 0 us -> 158 us
  local copies, waits for them, and re-layouts: 250 us -> 123 us
  starting transfers between devices: 8.58 us -> 104 us
  blocking collectives: 81.2 us -> 0 us
  other arithmetic: 69.7 us -> 24.6 us
    psum x1 -> x0, waiting for transfers between devices: 539 us -> none  [on_device(): lax.psum((grad_qkv, grad_bqv, grad_out, grad_bout, grad_ga, grad_gm, grad...]
    dot_general x51 -> x0, matrix products: 236 us -> none  [the longest x3 23.4 us: on_device(): jnp.einsum('rtc,rtf->cf', normed_mlp.astype(jnp.bfloat16), up_grad, prefe...]
    ppermute x4 -> x96, waiting for transfers between devices: 1.32 us -> 209 us  [the longest x18 90.7 us: dp_partner(): return lax.ppermute(v, 'dp', [(i, i ^ step) for i in range(n)])]
    pallas_call x0 -> x32, Pallas kernels: none -> 158 us  [the longest x2 36.7 us: attn_bwd(): pl.pallas_call(attn_bwd_kernel, in_specs=[SMEM] + [VMEM] * 13, out_specs=...]
    ppermute x4 -> x96, starting transfers between devices: 7.49 us -> 104 us  [the longest x16 31.7 us: handed(): return [lax.ppermute(f, 'section', pairs) for f in grads[l][i]]]
    dynamic_update_slice x6 -> x0, local copies, waits for them, and re-layouts: 93.3 us -> none  [the longest x3 46.7 us: on_device(): lax.dynamic_update_index_in_dim(outputs, jnp.where(is_live, result, curre...]
    all_gather x6 -> x0, waiting for transfers between devices: 86.8 us -> none  [the longest x3 52.8 us: on_device(): lax.all_gather(qkv[..., 2 * model_width:], 'seq', axis=1, tiled=True)]
    psum x1 -> x0, blocking collectives: 81.2 us -> none  [on_device(): lax.psum((grad_qkv, grad_bqv, grad_out, grad_bout, grad_ga, grad_gm, grad...]
  transfers between devices with their start and end apart: 17 -> 96, of which waited for: 10 -> 36; matrix products, arithmetic and copies ran while one was open for 29% -> 12% of each run, Pallas kernels for 0% -> 14%
where the time goes in v1:
time: 639 us; the launch traced here: 626 us
  waiting for transfers between devices  209 us (33%)
  Pallas kernels  158 us (25%)
  local copies, waits for them, and re-layouts  123 us (19%)
  starting transfers between devices  104 us (16%)
  other arithmetic  24.6 us (4%)
  between operations  7.33 us (1%)
    unnamed x302, local copies, waits for them, and re-layouts  92.2 us
    ppermute x18, waiting for transfers between devices, dp_partner(): return lax.ppermute(v, 'dp', [(i, i ^ step) for i in range(n)])  90.7 us
    ppermute x10, waiting for transfers between devices, to_second(): return lax.ppermute(v, ('section', 'seq'), pairs)  51.7 us
    ppermute x20, waiting for transfers between devices, to_first(): return lax.ppermute(v, ('section', 'seq'), pairs)  44.1 us
    pallas_call x2, Pallas kernels, attn_bwd(): pl.pallas_call(attn_bwd_kernel, in_specs=[SMEM] + [VMEM] * 13, out_specs=...  36.7 us
    pallas_call x16, Pallas kernels, product(): pl.pallas_call(functools.partial(product_kernel, send), grid_spec=pltpu.P...  35.7 us
    ppermute x16, starting transfers between devices, handed(): return [lax.ppermute(f, 'section', pairs) for f in grads[l][i]]  31.7 us
    pallas_call x2, Pallas kernels, mlp_bwd(): pl.pallas_call(functools.partial(mlp_bwd_kernel, layer), grid_spec=grid,...  24.7 us
  transfers between devices with their start and end apart: 96, of which 36 were waited for; matrix products, arithmetic and copies ran while one was open for 12% of the time, Pallas kernels for 14%

profile of v1, /device:TPU:0, one launch (start us, length us, event | category | flops | bytes accessed | tf_op | source)
XLA Modules:
  0.0 626.4 jit_solution(6607380539351641193)
XLA Ops:
  10.0 5.7 collective-permute-done
  16.0 2.7 collective-permute-start.1
  18.6 5.8 collective-permute-done.1.n1
  30.4 2.2 copy.59
  36.4 10.2 %shard_map.229 = (bf16[3,1024,64]{2,1,0:T(8,128)(2,1)S(1)}, bf16[3,1024,64]{2,1,0:T(8,128)(2,1)S(1)}, bf16[3,1024,64]{2,1,0:T(8,128)(2,1)S(1)}, f32[3,4,256]{2,1...) custom-call(s32[8]{0:T(128)S(1)} %stack.165.ids, ...), custom_call_target="tpu_custom_call" | custom-call | flops 3320709120 | bytes 3141632 | tf_op jit(solution)/shard_map/pallas_call | solution.py:145
  55.8 10.6 %shard_map.230 = (f32[256,767]{1,0:T(8,128)S(1)}, f32[256,3072]{1,0:T(8,128)S(1)}, bf16[256,767]{1,0:T(8,128)(2,1)S(1)}, bf16[256,767]{1,0:T(8,128)(2,1)S(1)}, f...) custom-call(s32[8]{0:T(128)S(1)} %stack.165.ids, bf16[256,767]{1,0:T(8,128)(2,1)S(1)} %bitcast.176, ...), custom_call_target="tpu_custom_call" | custom-call | flops 3619160064 | bytes 12570624 | tf_op jit(solution)/shard_map/pallas_call | solution.py:240
  67.3 9.3 %collective-permute-done.11.n1 = bf16[256,767]{1,0:T(8,128)(2,1)S(1)} collective-permute-done((bf16[256,767]{1,0:T(8,128)(2,1)S(1)}, bf16[256,767]{1,0:T(8,128)(2,1)S(1)}, u32[]{:S(2)}, u32[]{:S(2)}) %collective-permute-start.11) | collective-permute-done | bytes 392736 | tf_op jit(solution)/shard_map/ppermute | solution.py:667
  76.5 2.6 collective-permute-start.13
  79.1 5.7 collective-permute-done.13.n3
  84.9 11.1 %shard_map.231 = (bf16[3,1024,64]{2,1,0:T(8,128)(2,1)S(1)}, bf16[3,1024,64]{2,1,0:T(8,128)(2,1)S(1)}, bf16[3,1024,64]{2,1,0:T(8,128)(2,1)S(1)}, f32[3,4,256]{2,1...) custom-call(s32[8]{0:T(128)S(1)} %stack.165.ids, ...), custom_call_target="tpu_custom_call" | custom-call | flops 3320709120 | bytes 3141632 | tf_op jit(solution)/shard_map/pallas_call | solution.py:145
  107.3 2.3 copy-done.6
  109.6 11.7 %shard_map.232 = (f32[256,767]{1,0:T(8,128)S(1)}, f32[256,3072]{1,0:T(8,128)S(1)}, bf16[256,767]{1,0:T(8,128)(2,1)S(1)}, bf16[256,767]{1,0:T(8,128)(2,1)}, f32[8...) custom-call(s32[8]{0:T(128)S(1)} %stack.165.ids, bf16[256,767]{1,0:T(8,128)(2,1)S(1)} %get-tuple-element.92.x, ...), custom_call_target="tpu_custom_call" | custom-call | flops 3619160064 | bytes 12570624 | tf_op jit(solution)/shard_map/pallas_call | solution.py:240
  123.7 12.4 %shard_map.233 = (bf16[2,256,3072]{2,1,0:T(8,128)(2,1)S(1)}, bf16[2,256,767]{2,1,0:T(8,128)(2,1)S(1)}, f32[256,767]{1,0:T(8,128)S(1)}, bf16[256,767]{1,0:T(8,128...) custom-call(s32[8]{0:T(128)S(1)} %stack.165.ids, ...), custom_call_target="tpu_custom_call" | custom-call | flops 3619160064 | bytes 15716352 | tf_op jit(solution)/shard_map/pallas_call | solution.py:341
  143.6 24.2 %shard_map.234 = (bf16[256,767]{1,0:T(8,128)(2,1)S(1)}, bf16[256,767]{1,0:T(8,128)(2,1)S(1)}, bf16[256,767]{1,0:T(8,128)(2,1)S(1)}, bf16[256,767]{1,0:T(8,128)(2...) custom-call(s32[8]{0:T(128)S(1)} %stack.165.ids, ...), custom_call_target="tpu_custom_call" | custom-call | flops 7849377792 | bytes 6283264 | tf_op jit(solution)/shard_map/pallas_call | solution.py:477
  170.2 2.2 shard_map.248
  180.0 4.0 collective-permute-done.22
  185.7 2.7 collective-permute-start.38
  188.4 5.4 collective-permute-done.38
  195.4 12.4 %shard_map.236 = (bf16[2,256,3072]{2,1,0:T(8,128)(2,1)S(1)}, bf16[2,256,767]{2,1,0:T(8,128)(2,1)S(1)}, f32[256,767]{1,0:T(8,128)S(1)}, bf16[256,767]{1,0:T(8,128...) custom-call(s32[8]{0:T(128)S(1)} %stack.165.ids, ...), custom_call_target="tpu_custom_call" | custom-call | flops 3619160064 | bytes 15716352 | tf_op jit(solution)/shard_map/pallas_call | solution.py:341
  220.4 2.2 shard_map.255
  224.8 12.5 %shard_map.237 = (bf16[256,767]{1,0:T(8,128)(2,1)S(1)}, bf16[256,767]{1,0:T(8,128)(2,1)S(1)}, bf16[256,767]{1,0:T(8,128)(2,1)S(1)}, bf16[256,767]{1,0:T(8,128)(2...) custom-call(s32[8]{0:T(128)S(1)} %stack.165.ids, ...), custom_call_target="tpu_custom_call" | custom-call | flops 7849377792 | bytes 6283264 | tf_op jit(solution)/shard_map/pallas_call | solution.py:477
  239.2 3.5 shard_map.251
  242.8 2.4 shard_map.253
  245.3 3.3 collective-permute-start.40
  250.1 4.6 collective-permute-done.40
  256.2 3.5 shard_map.247
  262.4 2.8 add_convert_fusion.1
  278.9 2.2 maximum_select_fusion.8
  283.2 2.8 shard_map.249
  293.5 2.4 shard_map.243
  296.8 2.4 shard_map.245
  302.0 10.4 %collective-permute-done.75 = bf16[864,767]{1,0:T(8,128)(2,1)} collective-permute-done((bf16[864,767]{1,0:T(8,128)(2,1)}, bf16[864,767]{1,0:T(8,128)(2,1)}, u32[]{:S(2)}, u32[]{:S(2)}) %collective-permute-start.75) | collective-permute-done | bytes 1325408 | tf_op jit(solution)/shard_map/ppermute | solution.py:662
  312.4 2.2 add_convert_fusion
  318.1 11.1 %collective-permute-done.80 = bf16[2,216,767]{2,1,0:T(8,128)(2,1)S(1)} collective-permute-done((bf16[2,216,767]{2,1,0:T(8,128)(2,1)S(1)}, bf16[2,216,767]{2,1,0:T(8,128)(2,1)S(1)}, u32[]{:S(2)}, u32[]{:S(2)}) %collective-permute-start.80) | collective-permute-done | bytes 662720 | tf_op jit(solution)/shard_map/ppermute | solution.py:680
  330.3 10.4 %collective-permute-done.62 = bf16[864,767]{1,0:T(8,128)(2,1)S(1)} collective-permute-done((bf16[864,767]{1,0:T(8,128)(2,1)S(1)}, bf16[864,767]{1,0:T(8,128)(2,1)S(1)}, u32[]{:S(2)}, u32[]{:S(2)}) %collective-permute-start.62) | collective-permute-done | bytes 1325408 | tf_op jit(solution)/shard_map/ppermute | solution.py:662
  344.8 3.8 collective-permute-done.57
  349.4 5.8 collective-permute-done.81
  355.4 12.0 %collective-permute-done.67 = bf16[2,216,767]{2,1,0:T(8,128)(2,1)S(1)} collective-permute-done((bf16[2,216,767]{2,1,0:T(8,128)(2,1)S(1)}, bf16[2,216,767]{2,1,0:T(8,128)(2,1)S(1)}, u32[]{:S(2)}, u32[]{:S(2)}) %collective-permute-start.67) | collective-permute-done | bytes 662720 | tf_op jit(solution)/shard_map/ppermute | solution.py:680
  367.7 3.0 collective-permute-start.68
  373.5 15.3 %collective-permute-done.82 = bf16[1,216,767]{2,1,0:T(8,128)(2,1)S(1)} collective-permute-done((bf16[1,216,767]{2,1,0:T(8,128)(2,1)S(1)}, bf16[1,216,767]{2,1,0:T(8,128)(2,1)S(1)}, u32[]{:S(2)}, u32[]{:S(2)}) %collective-permute-start.82) | collective-permute-done | bytes 331376 | tf_op jit(solution)/shard_map/ppermute | solution.py:680
  390.8 5.0 collective-permute-done.68
  400.0 4.8 collective-permute-done.35
  408.1 14.9 %collective-permute-done.69 = bf16[1,216,767]{2,1,0:T(8,128)(2,1)S(1)} collective-permute-done((bf16[1,216,767]{2,1,0:T(8,128)(2,1)S(1)}, bf16[1,216,767]{2,1,0:T(8,128)(2,1)S(1)}, u32[]{:S(2)}, u32[]{:S(2)}) %collective-permute-start.69) | collective-permute-done | bytes 331376 | tf_op jit(solution)/shard_map/ppermute | solution.py:680
  431.3 9.4 %collective-permute-done.70 = bf16[2,216,767]{2,1,0:T(8,128)(2,1)S(1)} collective-permute-done((bf16[2,216,767]{2,1,0:T(8,128)(2,1)S(1)}, bf16[2,216,767]{2,1,0:T(8,128)(2,1)S(1)}, u32[]{:S(2)}, u32[]{:S(2)}) %collective-permute-start.70) | collective-permute-done | bytes 662720 | tf_op jit(solution)/shard_map/ppermute | solution.py:680
  443.0 3.3 collective-permute-start.94
  453.2 2.4 collective-permute-done.50.refs_10_
  464.4 13.2 %collective-permute-done.84.refs_3_ = bf16[864,767]{1,0:T(8,128)(2,1)S(1)} collective-permute-done((bf16[864,767]{1,0:T(8,128)(2,1)S(1)}, bf16[864,767]{1,0:T(8,128)(2,1)S(1)}, u32[]{:S(2)}, u32[]{:S(2)}) %collective-permute-start.84) | collective-permute-done | bytes 1325408 | tf_op jit(solution)/shard_map/ppermute | solution.py:667
  482.7 23.5 %collective-permute-done.71.refs_0_ = bf16[864,767]{1,0:T(8,128)(2,1)} collective-permute-done((bf16[864,767]{1,0:T(8,128)(2,1)S(1)}, bf16[864,767]{1,0:T(8,128)(2,1)}, u32[]{:S(2)}, u32[]{:S(2)}) %collective-permute-start.71) | collective-permute-done | bytes 1325408 | tf_op jit(solution)/shard_map/ppermute | solution.py:667
  506.2 2.5 collective-permute-start.72
  511.1 5.2 collective-permute-start.90
  519.5 4.7 collective-permute-start.86
  524.3 9.5 %collective-permute-done.72.refs_0_ = bf16[864,767]{1,0:T(8,128)(2,1)} collective-permute-done((bf16[864,767]{1,0:T(8,128)(2,1)}, bf16[864,767]{1,0:T(8,128)(2,1)}, u32[]{:S(2)}, u32[]{:S(2)}) %collective-permute-start.72) | collective-permute-done | bytes 1325408 | tf_op jit(solution)/shard_map/ppermute | solution.py:662
  536.1 3.0 copy.76
  543.9 2.5 maximum_select_fusion.3
  546.4 3.0 copy.77
  557.5 3.8 shard_map.239
  561.3 10.3 %copy.78 = f32[1,767,2304]{2,0,1:T(1,128)} copy(f32[1,767,2304]{2,1,0:T(8,128)S(1)} %bitcast.174) | data formatting | bytes 14137344
  573.7 3.4 shard_map.257
  577.2 3.4 shard_map.258
  580.7 3.4 shard_map.259
  584.1 3.6 copy-done.5
  587.8 12.6 %copy.80 = f32[1,767,3072]{2,0,1:T(1,128)} copy(f32[1,767,3072]{2,1,0:T(8,128)} %bitcast.170) | data formatting | bytes 18849792
  600.3 20.4 %copy.81 = f32[1,3072,767]{1,0,2:T(1,128)} copy(f32[1,3072,767]{2,1,0:T(8,128)} %bitcast.169) | data formatting | bytes 18849792
  620.8 4.3 copy.79
  (563 shorter events, 184.9 us)
Async XLA Ops:
  0.7 55.1 %collective-permute-start.10 = (bf16[1,3072,767]{2,1,0:T(8,128)(2,1)}, bf16[1,3072,767]{2,1,0:T(8,128)(2,1)}, u32[]{:S(2)}, u32[]{:S(2)}) collective-permute-start(bf16[1,3072,767]{2,1,0:T(8,128)(2,1)} %dno.7), channel_id=1, source_target_pairs={{0,16},{16,0},{1,17},{17,1},{2,18},{18,2},{3,19},{19,3},{4,20},{20... | collective-permute-start | bytes 14137352 | tf_op jit(solution)/shard_map/ppermute | solution.py:675
  1.2 54.6 %collective-permute-start.9 = (bf16[1,767,3072]{2,1,0:T(8,128)(2,1)}, bf16[1,767,3072]{2,1,0:T(8,128)(2,1)}, u32[]{:S(2)}, u32[]{:S(2)}) collective-permute-start(bf16[1,767,3072]{2,1,0:T(8,128)(2,1)} %upo.7), channel_id=1, source_target_pairs={{0,16},{16,0},{1,17},{17,1},{2,18},{18,2},{3,19},{19,3},{4,20},{20... | collective-permute-start | bytes 14137352 | tf_op jit(solution)/shard_map/ppermute | solution.py:675
  5.9 20.5 %collective-permute-start.4 = (bf16[767,576]{0,1:T(8,128)(2,1)}, bf16[767,576]{0,1:T(8,128)(2,1)}, u32[]{:S(2)}, u32[]{:S(2)}) collective-permute-start(bf16[767,576]{0,1:T(8,128)(2,1)} %copy.58), channel_id=1, source_target_pairs={{0,16},{16,0},{1,17},{17,1},{2,18},{18,2},{3,19},{19,3},{4,20},{20... | collective-permute-start | bytes 2650760 | tf_op jit(solution)/shard_map/ppermute | solution.py:675
  7.6 42.6 %collective-permute-start.8 = (bf16[768,767]{1,0:T(8,128)(2,1)}, bf16[768,767]{1,0:T(8,128)(2,1)}, u32[]{:S(2)}, u32[]{:S(2)}) collective-permute-start(bf16[768,767]{1,0:T(8,128)(2,1)} %bitcast.10), channel_id=1, source_target_pairs={{0,16},{16,0},{1,17},{17,1},{2,18},{18,2},{3,19},{19,3},{4,20},{20... | collective-permute-start | bytes 3534344 | tf_op jit(solution)/shard_map/ppermute | solution.py:675
  67.1 12.1 %collective-permute-start.12 = (bf16[256,767]{1,0:T(8,128)(2,1)S(1)}, bf16[256,767]{1,0:T(8,128)(2,1)S(1)}, u32[]{:S(2)}, u32[]{:S(2)}) collective-permute-start(bf16[256,767]{1,0:T(8,128)(2,1)S(1)} %get-tuple-element.93.n0), channel_id=1, source_target_pairs={{0,1},{1,0},{2,3},{3,2},{16,18},{17,19},{18,16},{19,17},{4,5},{5,4... | collective-permute-start | bytes 1178120 | tf_op jit(solution)/shard_map/ppermute | solution.py:662
  169.1 68.2 %collective-permute-start.74 = (bf16[864,767]{1,0:T(8,128)(2,1)}, bf16[864,767]{1,0:T(8,128)(2,1)}, u32[]{:S(2)}, u32[]{:S(2)}) collective-permute-start(bf16[864,767]{1,0:T(8,128)(2,1)} %shard_map.250), channel_id=1, source_target_pairs={{0,16},{16,0},{1,17},{17,1},{2,18},{18,2},{3,19},{19,3},{4,20},{20... | collective-permute-start | bytes 3976136 | tf_op jit(solution)/shard_map/ppermute | solution.py:675
  169.6 42.2 %collective-permute-start.77 = (bf16[864,767]{1,0:T(8,128)(2,1)S(1)}, bf16[864,767]{1,0:T(8,128)(2,1)S(1)}, u32[]{:S(2)}, u32[]{:S(2)}) collective-permute-start(bf16[864,767]{1,0:T(8,128)(2,1)S(1)} %shard_map.254), channel_id=1, source_target_pairs={{0,16},{16,0},{1,17},{17,1},{2,18},{18,2},{3,19},{19,3},{4,20},{20... | collective-permute-start | bytes 3976136 | tf_op jit(solution)/shard_map/ppermute | solution.py:675
  178.1 15.8 %collective-permute-start.21 = (bf16[256,767]{1,0:T(8,128)(2,1)S(1)}, bf16[256,767]{1,0:T(8,128)(2,1)S(1)}, u32[]{:S(2)}, u32[]{:S(2)}) collective-permute-start(bf16[256,767]{1,0:T(8,128)(2,1)S(1)} %get-tuple-element.114), channel_id=1, source_target_pairs={{0,1},{1,0},{2,3},{3,2},{16,18},{17,19},{18,16},{19,17},{4,5},{5,4... | collective-permute-start | bytes 1178120 | tf_op jit(solution)/shard_map/ppermute | solution.py:662
  193.8 44.6 %collective-permute-start.76 = (bf16[864,767]{1,0:T(8,128)(2,1)}, bf16[864,767]{1,0:T(8,128)(2,1)}, u32[]{:S(2)}, u32[]{:S(2)}) collective-permute-start(bf16[864,767]{1,0:T(8,128)(2,1)} %shard_map.252), channel_id=1, source_target_pairs={{0,16},{16,0},{1,17},{17,1},{2,18},{18,2},{3,19},{19,3},{4,20},{20... | collective-permute-start | bytes 3976136 | tf_op jit(solution)/shard_map/ppermute | solution.py:675
  193.9 17.4 %collective-permute-start.39 = (bf16[1,72,767]{2,1,0:T(8,128)(2,1)S(1)}, bf16[1,72,767]{2,1,0:T(8,128)(2,1)S(1)}, u32[]{:S(2)}, u32[]{:S(2)}) collective-permute-start(bf16[1,72,767]{2,1,0:T(8,128)(2,1)S(1)} %fusion.10), channel_id=1, source_target_pairs={{0,8},{4,12},{8,0},{12,4},{1,9},{5,13},{9,1},{13,5},{2,10},{6,14},... | collective-permute-start | bytes 331352 | tf_op jit(solution)/shard_map/ppermute | solution.py:680
  207.9 14.7 %collective-permute-start.24 = (bf16[192,256]{1,0:T(8,128)(2,1)S(1)}, bf16[192,256]{1,0:T(8,128)(2,1)S(1)}, u32[]{:S(2)}, u32[]{:S(2)}) collective-permute-start(bf16[192,256]{1,0:T(8,128)(2,1)S(1)} %get-tuple-element.122), channel_id=1, source_target_pairs={{0,1},{1,0},{2,3},{3,2},{4,5},{5,4},{6,7},{7,6},{8,9},{9,8},{10,11... | collective-permute-start | bytes 294920 | tf_op jit(solution)/shard_map/ppermute | solution.py:671
  211.3 11.3 %collective-permute-start.25 = (bf16[192,256]{1,0:T(8,128)(2,1)S(1)}, bf16[192,256]{1,0:T(8,128)(2,1)S(1)}, u32[]{:S(2)}, u32[]{:S(2)}) collective-permute-start(bf16[192,256]{1,0:T(8,128)(2,1)S(1)} %get-tuple-element.123), channel_id=1, source_target_pairs={{0,2},{1,3},{2,0},{3,1},{4,6},{5,7},{6,4},{7,5},{8,10},{9,11},{10,... | collective-permute-start | bytes 294920 | tf_op jit(solution)/shard_map/ppermute | solution.py:671
  211.8 11.3 %collective-permute-start.26 = (bf16[192,256]{1,0:T(8,128)(2,1)S(1)}, bf16[192,256]{1,0:T(8,128)(2,1)S(1)}, u32[]{:S(2)}, u32[]{:S(2)}) collective-permute-start(bf16[192,256]{1,0:T(8,128)(2,1)S(1)} %get-tuple-element.124), channel_id=1, source_target_pairs={{0,3},{1,2},{2,1},{3,0},{4,7},{5,6},{6,5},{7,4},{8,11},{9,10},{10,... | collective-permute-start | bytes 294920 | tf_op jit(solution)/shard_map/ppermute | solution.py:671
  222.6 32.1 %collective-permute-start.73 = (bf16[864,767]{1,0:T(8,128)(2,1)}, bf16[864,767]{1,0:T(8,128)(2,1)}, u32[]{:S(2)}, u32[]{:S(2)}) collective-permute-start(bf16[864,767]{1,0:T(8,128)(2,1)} %shard_map.248), channel_id=1, source_target_pairs={{0,16},{16,0},{1,17},{17,1},{2,18},{18,2},{3,19},{19,3},{4,20},{20... | collective-permute-start | bytes 3976136 | tf_op jit(solution)/shard_map/ppermute | solution.py:675
  222.6 32.7 %collective-permute-start.64 = (bf16[864,767]{1,0:T(8,128)(2,1)}, bf16[864,767]{1,0:T(8,128)(2,1)}, u32[]{:S(2)}, u32[]{:S(2)}) collective-permute-start(bf16[864,767]{1,0:T(8,128)(2,1)} %shard_map.246), channel_id=1, source_target_pairs={{0,16},{16,0},{1,17},{17,1},{2,18},{18,2},{3,19},{19,3},{4,20},{20... | collective-permute-start | bytes 3976136 | tf_op jit(solution)/shard_map/ppermute | solution.py:675
  223.1 38.5 %collective-permute-start.78 = (bf16[864,767]{1,0:T(8,128)(2,1)}, bf16[864,767]{1,0:T(8,128)(2,1)}, u32[]{:S(2)}, u32[]{:S(2)}) collective-permute-start(bf16[864,767]{1,0:T(8,128)(2,1)} %shard_map.255), channel_id=1, source_target_pairs={{0,1},{1,0},{2,3},{3,2},{16,18},{17,19},{18,16},{19,17},{4,5},{5,4... | collective-permute-start | bytes 3976136 | tf_op jit(solution)/shard_map/ppermute | solution.py:662
  248.8 11.0 %collective-permute-start.27 = (bf16[256,767]{1,0:T(8,128)(2,1)S(1)}, bf16[256,767]{1,0:T(8,128)(2,1)S(1)}, u32[]{:S(2)}, u32[]{:S(2)}) collective-permute-start(bf16[256,767]{1,0:T(8,128)(2,1)S(1)} %get-tuple-element.126), channel_id=1, source_target_pairs={{0,1},{1,0},{2,3},{3,2},{16,18},{17,19},{18,16},{19,17},{4,5},{5,4... | collective-permute-start | bytes 1178120 | tf_op jit(solution)/shard_map/ppermute | solution.py:662
  254.7 36.6 %collective-permute-start.61 = (bf16[864,767]{1,0:T(8,128)(2,1)}, bf16[864,767]{1,0:T(8,128)(2,1)}, u32[]{:S(2)}, u32[]{:S(2)}) collective-permute-start(bf16[864,767]{1,0:T(8,128)(2,1)} %shard_map.242), channel_id=1, source_target_pairs={{0,16},{16,0},{1,17},{17,1},{2,18},{18,2},{3,19},{19,3},{4,20},{20... | collective-permute-start | bytes 3976136 | tf_op jit(solution)/shard_map/ppermute | solution.py:675
  254.7 13.3 %collective-permute-start.29 = (bf16[256,767]{1,0:T(8,128)(2,1)S(1)}, bf16[256,767]{1,0:T(8,128)(2,1)S(1)}, u32[]{:S(2)}, u32[]{:S(2)}) collective-permute-start(bf16[256,767]{1,0:T(8,128)(2,1)S(1)} %add_convert_fusion.8), channel_id=1, source_target_pairs={{0,2},{1,3},{2,0},{3,1},{16,17},{17,16},{18,19},{19,18},{4,6},{5,7... | collective-permute-start | bytes 1178120 | tf_op jit(solution)/shard_map/ppermute | solution.py:667
  255.3 40.6 %collective-permute-start.63 = (bf16[864,767]{1,0:T(8,128)(2,1)}, bf16[864,767]{1,0:T(8,128)(2,1)}, u32[]{:S(2)}, u32[]{:S(2)}) collective-permute-start(bf16[864,767]{1,0:T(8,128)(2,1)} %shard_map.244), channel_id=1, source_target_pairs={{0,16},{16,0},{1,17},{17,1},{2,18},{18,2},{3,19},{19,3},{4,20},{20... | collective-permute-start | bytes 3976136 | tf_op jit(solution)/shard_map/ppermute | solution.py:675
  261.6 37.7 %collective-permute-start.65 = (bf16[864,767]{1,0:T(8,128)(2,1)}, bf16[864,767]{1,0:T(8,128)(2,1)}, u32[]{:S(2)}, u32[]{:S(2)}) collective-permute-start(bf16[864,767]{1,0:T(8,128)(2,1)} %shard_map.247), channel_id=1, source_target_pairs={{0,1},{1,0},{2,3},{3,2},{16,18},{17,19},{18,16},{19,17},{4,5},{5,4... | collective-permute-start | bytes 3976136 | tf_op jit(solution)/shard_map/ppermute | solution.py:662
  267.2 45.2 %collective-permute-start.75 = (bf16[864,767]{1,0:T(8,128)(2,1)}, bf16[864,767]{1,0:T(8,128)(2,1)}, u32[]{:S(2)}, u32[]{:S(2)}) collective-permute-start(bf16[864,767]{1,0:T(8,128)(2,1)} %shard_map.251), channel_id=1, source_target_pairs={{0,1},{1,0},{2,3},{3,2},{16,18},{17,19},{18,16},{19,17},{4,5},{5,4... | collective-permute-start | bytes 3976136 | tf_op jit(solution)/shard_map/ppermute | solution.py:662
  268.9 43.6 %collective-permute-start.79 = (bf16[864,767]{1,0:T(8,128)(2,1)}, bf16[864,767]{1,0:T(8,128)(2,1)}, u32[]{:S(2)}, u32[]{:S(2)}) collective-permute-start(bf16[864,767]{1,0:T(8,128)(2,1)} %add_convert_fusion.1), channel_id=1, source_target_pairs={{0,2},{1,3},{2,0},{3,1},{16,17},{17,16},{18,19},{19,18},{4,6},{5,7... | collective-permute-start | bytes 3976136 | tf_op jit(solution)/shard_map/ppermute | solution.py:667
  291.3 25.6 %collective-permute-start.60 = (bf16[864,767]{1,0:T(8,128)(2,1)}, bf16[864,767]{1,0:T(8,128)(2,1)S(1)}, u32[]{:S(2)}, u32[]{:S(2)}) collective-permute-start(bf16[864,767]{1,0:T(8,128)(2,1)} %copy-done.44), channel_id=1, source_target_pairs={{0,16},{16,0},{1,17},{17,1},{2,18},{18,2},{3,19},{19,3},{4,20},{20... | collective-permute-start | bytes 3976136 | tf_op jit(solution)/shard_map/ppermute | solution.py:675
  295.9 44.8 %collective-permute-start.62 = (bf16[864,767]{1,0:T(8,128)(2,1)S(1)}, bf16[864,767]{1,0:T(8,128)(2,1)S(1)}, u32[]{:S(2)}, u32[]{:S(2)}) collective-permute-start(bf16[864,767]{1,0:T(8,128)(2,1)S(1)} %shard_map.243), channel_id=1, source_target_pairs={{0,1},{1,0},{2,3},{3,2},{16,18},{17,19},{18,16},{19,17},{4,5},{5,4... | collective-permute-start | bytes 3976136 | tf_op jit(solution)/shard_map/ppermute | solution.py:662
  301.1 40.2 %collective-permute-start.66 = (bf16[864,767]{1,0:T(8,128)(2,1)S(1)}, bf16[864,767]{1,0:T(8,128)(2,1)S(1)}, u32[]{:S(2)}, u32[]{:S(2)}) collective-permute-start(bf16[864,767]{1,0:T(8,128)(2,1)S(1)} %add_convert_fusion.4), channel_id=1, source_target_pairs={{0,2},{1,3},{2,0},{3,1},{16,17},{17,16},{18,19},{19,18},{4,6},{5,7... | collective-permute-start | bytes 3976136 | tf_op jit(solution)/shard_map/ppermute | solution.py:667
  314.8 14.4 %collective-permute-start.80 = (bf16[2,216,767]{2,1,0:T(8,128)(2,1)S(1)}, bf16[2,216,767]{2,1,0:T(8,128)(2,1)S(1)}, u32[]{:S(2)}, u32[]{:S(2)}) collective-permute-start(bf16[2,216,767]{2,1,0:T(8,128)(2,1)S(1)} %select_bitcast_fusion), channel_id=1, source_target_pairs={{0,4},{4,0},{8,12},{12,8},{1,5},{5,1},{9,13},{13,9},{2,6},{6,2},{1... | collective-permute-start | bytes 1988072 | tf_op jit(solution)/shard_map/ppermute | solution.py:680
  316.7 79.2 %collective-permute-start.17 = (bf16[256,767]{1,0:T(8,128)(2,1)S(1)}, bf16[256,767]{1,0:T(8,128)(2,1)S(1)}, u32[]{:S(2)}, u32[]{:S(2)}) collective-permute-start(bf16[256,767]{1,0:T(8,128)(2,1)S(1)} %copy-done.130), channel_id=1, source_target_pairs={{0,16},{16,0},{1,17},{17,1},{2,18},{18,2},{3,19},{19,3},{4,20},{20... | collective-permute-start | bytes 1178120 | tf_op jit(solution)/shard_map/ppermute | solution.py:675
  316.9 53.9 %collective-permute-start.44 = (bf16[288,767]{1,0:T(8,128)(2,1)S(1)}, bf16[288,767]{1,0:T(8,128)(2,1)S(1)}, u32[]{:S(2)}, u32[]{:S(2)}) collective-permute-start(bf16[288,767]{1,0:T(8,128)(2,1)S(1)} %bitcast.186), channel_id=1, source_target_pairs={{0,2},{1,3},{2,0},{3,1},{16,17},{17,16},{18,19},{19,18},{4,6},{5,7... | collective-permute-start | bytes 1325384 | tf_op jit(solution)/shard_map/ppermute | solution.py:667
  329.2 15.5 %collective-permute-start.33 = (bf16[1,72,767]{2,1,0:T(8,128)(2,1)S(1)}, bf16[1,72,767]{2,1,0:T(8,128)(2,1)S(1)}, u32[]{:S(2)}, u32[]{:S(2)}) collective-permute-start(bf16[1,72,767]{2,1,0:T(8,128)(2,1)S(1)} %select_bitcast_fusion.9), channel_id=1, source_target_pairs={{0,8},{4,12},{8,0},{12,4},{1,9},{5,13},{9,1},{13,5},{2,10},{6,14},... | collective-permute-start | bytes 331352 | tf_op jit(solution)/shard_map/ppermute | solution.py:680
  341.2 14.0 %collective-permute-start.81 = (bf16[1,216,767]{2,1,0:T(8,128)(2,1)S(1)}, bf16[1,216,767]{2,1,0:T(8,128)(2,1)S(1)}, u32[]{:S(2)}, u32[]{:S(2)}) collective-permute-start(bf16[1,216,767]{2,1,0:T(8,128)(2,1)S(1)} %select_bitcast_fusion.4), channel_id=1, source_target_pairs={{0,8},{4,12},{8,0},{12,4},{1,9},{5,13},{9,1},{13,5},{2,10},{6,14},... | collective-permute-start | bytes 994040 | tf_op jit(solution)/shard_map/ppermute | solution.py:680
  344.7 22.8 %collective-permute-start.67 = (bf16[2,216,767]{2,1,0:T(8,128)(2,1)S(1)}, bf16[2,216,767]{2,1,0:T(8,128)(2,1)S(1)}, u32[]{:S(2)}, u32[]{:S(2)}) collective-permute-start(bf16[2,216,767]{2,1,0:T(8,128)(2,1)S(1)} %select_bitcast_fusion.1), channel_id=1, source_target_pairs={{0,4},{4,0},{8,12},{12,8},{1,5},{5,1},{9,13},{13,9},{2,6},{6,2},{1... | collective-permute-start | bytes 1988072 | tf_op jit(solution)/shard_map/ppermute | solution.py:680
  348.7 19.1 %collective-permute-start.34 = (bf16[1,72,767]{2,1,0:T(8,128)(2,1)S(1)}, bf16[1,72,767]{2,1,0:T(8,128)(2,1)S(1)}, u32[]{:S(2)}, u32[]{:S(2)}) collective-permute-start(bf16[1,72,767]{2,1,0:T(8,128)(2,1)S(1)} %fusion.11), channel_id=1, source_target_pairs={{0,8},{4,12},{8,0},{12,4},{1,9},{5,13},{9,1},{13,5},{2,10},{6,14},... | collective-permute-start | bytes 331352 | tf_op jit(solution)/shard_map/ppermute | solution.py:680
  355.3 16.8 %collective-permute-start.58 = (f32[61,128]{1,0:T(8,128)S(1)}, f32[61,128]{1,0:T(8,128)S(1)}, u32[]{:S(2)}, u32[]{:S(2)}) collective-permute-start(f32[61,128]{1,0:T(8,128)S(1)} %add.141), channel_id=1, source_target_pairs={{0,4},{4,0},{8,12},{12,8},{1,5},{5,1},{9,13},{13,9},{2,6},{6,2},{1... | collective-permute-start | bytes 93704 | tf_op jit(solution)/shard_map/ppermute | solution.py:680
  367.4 21.4 %collective-permute-start.82 = (bf16[1,216,767]{2,1,0:T(8,128)(2,1)S(1)}, bf16[1,216,767]{2,1,0:T(8,128)(2,1)S(1)}, u32[]{:S(2)}, u32[]{:S(2)}) collective-permute-start(bf16[1,216,767]{2,1,0:T(8,128)(2,1)S(1)} %fusion.4), channel_id=1, source_target_pairs={{0,8},{4,12},{8,0},{12,4},{1,9},{5,13},{9,1},{13,5},{2,10},{6,14},... | collective-permute-start | bytes 994040 | tf_op jit(solution)/shard_map/ppermute | solution.py:680
  367.7 28.1 %collective-permute-start.68 = (bf16[1,216,767]{2,1,0:T(8,128)(2,1)S(1)}, bf16[1,216,767]{2,1,0:T(8,128)(2,1)S(1)}, u32[]{:S(2)}, u32[]{:S(2)}) collective-permute-start(bf16[1,216,767]{2,1,0:T(8,128)(2,1)S(1)} %select_bitcast_fusion.5), channel_id=1, source_target_pairs={{0,8},{4,12},{8,0},{12,4},{1,9},{5,13},{9,1},{13,5},{2,10},{6,14},... | collective-permute-start | bytes 994040 | tf_op jit(solution)/shard_map/ppermute | solution.py:680
  370.8 27.3 %collective-permute-start.48 = (bf16[288,767]{1,0:T(8,128)(2,1)S(1)}, bf16[288,767]{1,0:T(8,128)(2,1)S(1)}, u32[]{:S(2)}, u32[]{:S(2)}) collective-permute-start(bf16[288,767]{1,0:T(8,128)(2,1)S(1)} %bitcast.187), channel_id=1, source_target_pairs={{0,1},{1,0},{2,3},{3,2},{16,18},{17,19},{18,16},{19,17},{4,5},{5,4... | collective-permute-start | bytes 1325384 | tf_op jit(solution)/shard_map/ppermute | solution.py:662
  372.1 26.3 %collective-permute-start.41 = (bf16[288,767]{1,0:T(8,128)(2,1)S(1)}, bf16[288,767]{1,0:T(8,128)(2,1)S(1)}, u32[]{:S(2)}, u32[]{:S(2)}) collective-permute-start(bf16[288,767]{1,0:T(8,128)(2,1)S(1)} %bitcast.188), channel_id=1, source_target_pairs={{0,16},{1,17},{2,18},{3,19},{4,20},{5,21},{6,22},{7,23},{8,24},{9,... | collective-permute-start | bytes 1325384 | tf_op jit(solution)/shard_map/ppermute | solution.py:826
  388.8 17.5 %collective-permute-start.52 = (bf16[288,767]{1,0:T(8,128)(2,1)S(1)}, bf16[288,767]{1,0:T(8,128)(2,1)S(1)}, u32[]{:S(2)}, u32[]{:S(2)}) collective-permute-start(bf16[288,767]{1,0:T(8,128)(2,1)S(1)} %collective-permute-done.44.refs_7_), channel_id=1, source_target_pairs={{0,1},{1,0},{2,3},{3,2},{16,18},{17,19},{18,16},{19,17},{4,5},{5,4... | collective-permute-start | bytes 1325384 | tf_op jit(solution)/shard_map/ppermute | solution.py:662
  396.0 27.2 %collective-permute-start.45 = (bf16[288,767]{1,0:T(8,128)(2,1)S(1)}, bf16[288,767]{1,0:T(8,128)(2,1)S(1)}, u32[]{:S(2)}, u32[]{:S(2)}) collective-permute-start(bf16[288,767]{1,0:T(8,128)(2,1)S(1)} %collective-permute-done.44.refs_7_), channel_id=1, source_target_pairs={{0,16},{1,17},{2,18},{3,19},{4,20},{5,21},{6,22},{7,23},{8,24},{9,... | collective-permute-start | bytes 1325384 | tf_op jit(solution)/shard_map/ppermute | solution.py:826
  398.4 32.0 %collective-permute-start.83 = (bf16[2,216,767]{2,1,0:T(8,128)(2,1)S(1)}, bf16[2,216,767]{2,1,0:T(8,128)(2,1)S(1)}, u32[]{:S(2)}, u32[]{:S(2)}) collective-permute-start(bf16[2,216,767]{2,1,0:T(8,128)(2,1)S(1)} %maximum_select_fusion.6), channel_id=1, source_target_pairs={{0,4},{4,0},{8,12},{12,8},{1,5},{5,1},{9,13},{13,9},{2,6},{6,2},{1... | collective-permute-start | bytes 1988072 | tf_op jit(solution)/shard_map/ppermute | solution.py:680
  404.8 18.2 %collective-permute-start.69 = (bf16[1,216,767]{2,1,0:T(8,128)(2,1)S(1)}, bf16[1,216,767]{2,1,0:T(8,128)(2,1)S(1)}, u32[]{:S(2)}, u32[]{:S(2)}) collective-permute-start(bf16[1,216,767]{2,1,0:T(8,128)(2,1)S(1)} %fusion.5), channel_id=1, source_target_pairs={{0,8},{4,12},{8,0},{12,4},{1,9},{5,13},{9,1},{13,5},{2,10},{6,14},... | collective-permute-start | bytes 994040 | tf_op jit(solution)/shard_map/ppermute | solution.py:680
  405.0 20.1 %collective-permute-start.49 = (bf16[288,767]{1,0:T(8,128)(2,1)S(1)}, bf16[288,767]{1,0:T(8,128)(2,1)S(1)}, u32[]{:S(2)}, u32[]{:S(2)}) collective-permute-start(bf16[288,767]{1,0:T(8,128)(2,1)S(1)} %collective-permute-done.48.refs_11_), channel_id=1, source_target_pairs={{0,16},{1,17},{2,18},{3,19},{4,20},{5,21},{6,22},{7,23},{8,24},{9,... | collective-permute-start | bytes 1325384 | tf_op jit(solution)/shard_map/ppermute | solution.py:826
  406.3 22.8 %collective-permute-start.43 = (bf16[288,767]{1,0:T(8,128)(2,1)S(1)}, bf16[288,767]{1,0:T(8,128)(2,1)S(1)}, u32[]{:S(2)}, u32[]{:S(2)}) collective-permute-start(bf16[288,767]{1,0:T(8,128)(2,1)S(1)} %bitcast.190), channel_id=1, source_target_pairs={{0,2},{1,3},{2,0},{3,1},{16,17},{17,16},{18,19},{19,18},{4,6},{5,7... | collective-permute-start | bytes 1325384 | tf_op jit(solution)/shard_map/ppermute | solution.py:667
  423.2 17.5 %collective-permute-start.70 = (bf16[2,216,767]{2,1,0:T(8,128)(2,1)S(1)}, bf16[2,216,767]{2,1,0:T(8,128)(2,1)S(1)}, u32[]{:S(2)}, u32[]{:S(2)}) collective-permute-start(bf16[2,216,767]{2,1,0:T(8,128)(2,1)S(1)} %maximum_select_fusion.5), channel_id=1, source_target_pairs={{0,4},{4,0},{8,12},{12,8},{1,5},{5,1},{9,13},{13,9},{2,6},{6,2},{1... | collective-permute-start | bytes 1988072 | tf_op jit(solution)/shard_map/ppermute | solution.py:680
  425.0 17.2 %collective-permute-start.53 = (bf16[288,767]{1,0:T(8,128)(2,1)S(1)}, bf16[288,767]{1,0:T(8,128)(2,1)S(1)}, u32[]{:S(2)}, u32[]{:S(2)}) collective-permute-start(bf16[288,767]{1,0:T(8,128)(2,1)S(1)} %collective-permute-done.52.refs_15_), channel_id=1, source_target_pairs={{0,16},{1,17},{2,18},{3,19},{4,20},{5,21},{6,22},{7,23},{8,24},{9,... | collective-permute-start | bytes 1325384 | tf_op jit(solution)/shard_map/ppermute | solution.py:826
  427.2 19.1 %collective-permute-start.47 = (bf16[288,767]{1,0:T(8,128)(2,1)S(1)}, bf16[288,767]{1,0:T(8,128)(2,1)S(1)}, u32[]{:S(2)}, u32[]{:S(2)}) collective-permute-start(bf16[288,767]{1,0:T(8,128)(2,1)S(1)} %bitcast.191), channel_id=1, source_target_pairs={{0,1},{1,0},{2,3},{3,2},{16,18},{17,19},{18,16},{19,17},{4,5},{5,4... | collective-permute-start | bytes 1325384 | tf_op jit(solution)/shard_map/ppermute | solution.py:662
  429.1 18.2 %collective-permute-start.42 = (bf16[288,767]{1,0:T(8,128)(2,1)S(1)}, bf16[288,767]{1,0:T(8,128)(2,1)S(1)}, u32[]{:S(2)}, u32[]{:S(2)}) collective-permute-start(bf16[288,767]{1,0:T(8,128)(2,1)S(1)} %bitcast.192), channel_id=1, source_target_pairs={{16,0},{17,1},{18,2},{19,3},{20,4},{21,5},{22,6},{23,7},{24,8},{25... | collective-permute-start | bytes 1325384 | tf_op jit(solution)/shard_map/ppermute | solution.py:826
  430.4 19.1 %collective-permute-start.51 = (bf16[288,767]{1,0:T(8,128)(2,1)S(1)}, bf16[288,767]{1,0:T(8,128)(2,1)S(1)}, u32[]{:S(2)}, u32[]{:S(2)}) collective-permute-start(bf16[288,767]{1,0:T(8,128)(2,1)S(1)} %collective-permute-done.43.refs_4_), channel_id=1, source_target_pairs={{0,1},{1,0},{2,3},{3,2},{16,18},{17,19},{18,16},{19,17},{4,5},{5,4... | collective-permute-start | bytes 1325384 | tf_op jit(solution)/shard_map/ppermute | solution.py:662
  440.6 10.5 %collective-permute-start.46 = (bf16[288,767]{1,0:T(8,128)(2,1)S(1)}, bf16[288,767]{1,0:T(8,128)(2,1)S(1)}, u32[]{:S(2)}, u32[]{:S(2)}) collective-permute-start(bf16[288,767]{1,0:T(8,128)(2,1)S(1)} %collective-permute-done.43.refs_4_), channel_id=1, source_target_pairs={{16,0},{17,1},{18,2},{19,3},{20,4},{21,5},{22,6},{23,7},{24,8},{25... | collective-permute-start | bytes 1325384 | tf_op jit(solution)/shard_map/ppermute | solution.py:826
  443.0 19.1 %collective-permute-start.94 = (bf16[864,767]{1,0:T(8,128)(2,1)S(1)}, bf16[864,767]{1,0:T(8,128)(2,1)S(1)}, u32[]{:S(2)}, u32[]{:S(2)}) collective-permute-start(bf16[864,767]{1,0:T(8,128)(2,1)S(1)} %bitcast.178), channel_id=1, source_target_pairs={{0,16},{1,17},{2,18},{3,19},{4,20},{5,21},{6,22},{7,23},{8,24},{9,... | collective-permute-start | bytes 3976136 | tf_op jit(solution)/shard_map/ppermute | solution.py:826
  446.3 31.4 %collective-permute-start.84 = (bf16[864,767]{1,0:T(8,128)(2,1)S(1)}, bf16[864,767]{1,0:T(8,128)(2,1)S(1)}, u32[]{:S(2)}, u32[]{:S(2)}) collective-permute-start(bf16[864,767]{1,0:T(8,128)(2,1)S(1)} %bitcast.179), channel_id=1, source_target_pairs={{0,2},{1,3},{2,0},{3,1},{16,17},{17,16},{18,19},{19,18},{4,6},{5,7... | collective-permute-start | bytes 3976136 | tf_op jit(solution)/shard_map/ppermute | solution.py:667
  448.1 32.2 %collective-permute-start.89 = (bf16[864,767]{1,0:T(8,128)(2,1)S(1)}, bf16[864,767]{1,0:T(8,128)(2,1)}, u32[]{:S(2)}, u32[]{:S(2)}) collective-permute-start(bf16[864,767]{1,0:T(8,128)(2,1)S(1)} %bitcast.180), channel_id=1, source_target_pairs={{0,1},{1,0},{2,3},{3,2},{16,18},{17,19},{18,16},{19,17},{4,5},{5,4... | collective-permute-start | bytes 3976136 | tf_op jit(solution)/shard_map/ppermute | solution.py:662
  449.5 56.7 %collective-permute-start.71 = (bf16[864,767]{1,0:T(8,128)(2,1)S(1)}, bf16[864,767]{1,0:T(8,128)(2,1)}, u32[]{:S(2)}, u32[]{:S(2)}) collective-permute-start(bf16[864,767]{1,0:T(8,128)(2,1)S(1)} %bitcast.182), channel_id=1, source_target_pairs={{0,2},{1,3},{2,0},{3,1},{16,17},{17,16},{18,19},{19,18},{4,6},{5,7... | collective-permute-start | bytes 3976136 | tf_op jit(solution)/shard_map/ppermute | solution.py:667
  460.8 47.9 %collective-permute-start.95 = (bf16[864,767]{1,0:T(8,128)(2,1)S(1)}, bf16[864,767]{1,0:T(8,128)(2,1)S(1)}, u32[]{:S(2)}, u32[]{:S(2)}) collective-permute-start(bf16[864,767]{1,0:T(8,128)(2,1)S(1)} %bitcast.183), channel_id=1, source_target_pairs={{16,0},{17,1},{18,2},{19,3},{20,4},{21,5},{22,6},{23,7},{24,8},{25... | collective-permute-start | bytes 3976136 | tf_op jit(solution)/shard_map/ppermute | solution.py:826
  463.2 47.9 %collective-permute-start.88 = (bf16[864,767]{1,0:T(8,128)(2,1)S(1)}, bf16[864,767]{1,0:T(8,128)(2,1)}, u32[]{:S(2)}, u32[]{:S(2)}) collective-permute-start(bf16[864,767]{1,0:T(8,128)(2,1)S(1)} %bitcast.184), channel_id=1, source_target_pairs={{0,1},{1,0},{2,3},{3,2},{16,18},{17,19},{18,16},{19,17},{4,5},{5,4... | collective-permute-start | bytes 3976136 | tf_op jit(solution)/shard_map/ppermute | solution.py:662
  477.7 38.6 %collective-permute-start.92 = (bf16[864,767]{1,0:T(8,128)(2,1)S(1)}, bf16[864,767]{1,0:T(8,128)(2,1)S(1)}, u32[]{:S(2)}, u32[]{:S(2)}) collective-permute-start(bf16[864,767]{1,0:T(8,128)(2,1)S(1)} %collective-permute-done.84.refs_3_), channel_id=1, source_target_pairs={{0,16},{1,17},{2,18},{3,19},{4,20},{5,21},{6,22},{7,23},{8,24},{9,... | collective-permute-start | bytes 3976136 | tf_op jit(solution)/shard_map/ppermute | solution.py:826
  480.3 39.3 %collective-permute-start.85 = (bf16[864,767]{1,0:T(8,128)(2,1)S(1)}, bf16[864,767]{1,0:T(8,128)(2,1)}, u32[]{:S(2)}, u32[]{:S(2)}) collective-permute-start(bf16[864,767]{1,0:T(8,128)(2,1)S(1)} %collective-permute-done.84.refs_3_), channel_id=1, source_target_pairs={{0,1},{1,0},{2,3},{3,2},{16,18},{17,19},{18,16},{19,17},{4,5},{5,4... | collective-permute-start | bytes 3976136 | tf_op jit(solution)/shard_map/ppermute | solution.py:662
  506.2 27.6 %collective-permute-start.72 = (bf16[864,767]{1,0:T(8,128)(2,1)}, bf16[864,767]{1,0:T(8,128)(2,1)}, u32[]{:S(2)}, u32[]{:S(2)}) collective-permute-start(bf16[864,767]{1,0:T(8,128)(2,1)} %collective-permute-done.71.refs_0_), channel_id=1, source_target_pairs={{0,1},{1,0},{2,3},{3,2},{16,18},{17,19},{18,16},{19,17},{4,5},{5,4... | collective-permute-start | bytes 3976136 | tf_op jit(solution)/shard_map/ppermute | solution.py:662
  509.8 63.9 %collective-permute-start.93 = (bf16[864,767]{1,0:T(8,128)(2,1)}, bf16[864,767]{1,0:T(8,128)(2,1)}, u32[]{:S(2)}, u32[]{:S(2)}) collective-permute-start(bf16[864,767]{1,0:T(8,128)(2,1)} %collective-permute-done.71.refs_0_), channel_id=1, source_target_pairs={{16,0},{17,1},{18,2},{19,3},{20,4},{21,5},{22,6},{23,7},{24,8},{25... | collective-permute-start | bytes 3976136 | tf_op jit(solution)/shard_map/ppermute | solution.py:826
  511.1 66.1 %collective-permute-start.90 = (bf16[864,767]{1,0:T(8,128)(2,1)}, bf16[864,767]{1,0:T(8,128)(2,1)}, u32[]{:S(2)}, u32[]{:S(2)}) collective-permute-start(bf16[864,767]{1,0:T(8,128)(2,1)} %collective-permute-done.89.refs_3_), channel_id=1, source_target_pairs={{0,16},{1,17},{2,18},{3,19},{4,20},{5,21},{6,22},{7,23},{8,24},{9,... | collective-permute-start | bytes 3976136 | tf_op jit(solution)/shard_map/ppermute | solution.py:826
  517.3 59.9 %collective-permute-start.91 = (bf16[864,767]{1,0:T(8,128)(2,1)}, bf16[864,767]{1,0:T(8,128)(2,1)}, u32[]{:S(2)}, u32[]{:S(2)}) collective-permute-start(bf16[864,767]{1,0:T(8,128)(2,1)} %collective-permute-done.88.refs_0_), channel_id=1, source_target_pairs={{16,0},{17,1},{18,2},{19,3},{20,4},{21,5},{22,6},{23,7},{24,8},{25... | collective-permute-start | bytes 3976136 | tf_op jit(solution)/shard_map/ppermute | solution.py:826
  519.5 61.1 %collective-permute-start.86 = (bf16[864,767]{1,0:T(8,128)(2,1)}, bf16[864,767]{1,0:T(8,128)(2,1)}, u32[]{:S(2)}, u32[]{:S(2)}) collective-permute-start(bf16[864,767]{1,0:T(8,128)(2,1)} %collective-permute-done.85.refs_3_), channel_id=1, source_target_pairs={{0,16},{1,17},{2,18},{3,19},{4,20},{5,21},{6,22},{7,23},{8,24},{9,... | collective-permute-start | bytes 3976136 | tf_op jit(solution)/shard_map/ppermute | solution.py:826
  533.8 46.9 %collective-permute-start.87 = (bf16[864,767]{1,0:T(8,128)(2,1)}, bf16[864,767]{1,0:T(8,128)(2,1)}, u32[]{:S(2)}, u32[]{:S(2)}) collective-permute-start(bf16[864,767]{1,0:T(8,128)(2,1)} %collective-permute-done.72.refs_0_), channel_id=1, source_target_pairs={{16,0},{17,1},{18,2},{19,3},{20,4},{21,5},{22,6},{23,7},{24,8},{25... | collective-permute-start | bytes 3976136 | tf_op jit(solution)/shard_map/ppermute | solution.py:826
  (179 other events, 1948.2 us)

commit v2 on v1

--- a/solution.py
+++ b/solution.py
@@ -29,8 +29,6 @@
 
 
 def order(core, k):
-    if isinstance(k, int):
-        return jnp.where(core == 1, k, ((k & 1) << 1) | (k >> 1))
     return jnp.where(core == 1, k, ((k & 1) << 1) | (k >> 1))
 
 
@@ -69,24 +67,54 @@
 
 SMEM = pl.BlockSpec(memory_space=pltpu.SMEM)
 VMEM = pl.BlockSpec(memory_space=pltpu.VMEM)
-ANY = pl.BlockSpec(memory_space=pl.ANY)
-
-
-def norm_kernel(x_ref, pv_ref, o_ref):
-    x = x_ref[...].astype(F32)
-    r, _, _ = crms_scale(x)
-    o_ref[...] = (x * r * pv_ref[3:4, : x.shape[-1]]).astype(BF16)
-
-
-def first_norm(x, pv):
+HBM = pl.BlockSpec(memory_space=pltpu.HBM)
+
+
+def rows_in_kernel(ids, v, o):
+    @pl.when(ids[0] == 0)
+    def _():
+        o[...] = v[:, 0, :].T
+
+    @pl.when(ids[0] != 0)
+    def _():
+        o[...] = v[:, 1, :].T
+
+
+def rows_in(ids, v):
+    micro, _, span, cc = v.shape
     return pl.pallas_call(
-        norm_kernel,
-        in_specs=[VMEM, VMEM],
+        rows_in_kernel,
+        in_specs=[SMEM, VMEM],
         out_specs=VMEM,
-        out_shape=jax.ShapeDtypeStruct(x.shape, BF16),
-        compiler_params=params(8),
-        cost_estimate=cost(0, x.size * 4),
-    )(x, pv)
+        out_shape=jax.ShapeDtypeStruct((span, cc), BF16),
+        compiler_params=params(16),
+        cost_estimate=cost(0, 6 * span * cc),
+    )(ids, jnp.transpose(v[:, 0], (2, 0, 1)))
+
+
+def rows_out_kernel(ids, own, got, o):
+    @pl.when(ids[0] == 0)
+    def _():
+        o[:, 0, :] = own[...].T
+        o[:, 1, :] = got[...].T
+
+    @pl.when(ids[0] != 0)
+    def _():
+        o[:, 0, :] = got[...].T
+        o[:, 1, :] = own[...].T
+
+
+def rows_out(ids, own, got):
+    span, cc = own.shape
+    o = pl.pallas_call(
+        rows_out_kernel,
+        in_specs=[SMEM, VMEM, VMEM],
+        out_specs=VMEM,
+        out_shape=jax.ShapeDtypeStruct((cc, 2, span), BF16),
+        compiler_params=params(16),
+        cost_estimate=cost(0, 8 * span * cc),
+    )(ids, own, got)
+    return jnp.transpose(o, (1, 2, 0))[None, :, None]
 
 
 def visible_bias(ids, n, t, span):
@@ -100,17 +128,23 @@
 
 
 def attn_fwd_kernel(
-    ids, n0, n1, n2, n3, w_ref, pv_ref, qh, kh, vh, lse, a0, a1, a2, a3, at, bias_scr
+    raw, ids, n0, n1, n2, n3, w_ref, pv_ref, qh, kh, vh, lse, a0, a1, a2, a3, *rest
 ):
     c, s = ids[0], ids[1]
     heads, _, hd = qh.shape
-    span = n0.shape[0]
+    span, cc = n0.shape
     width = heads * hd
+    at, bias_scr = rest[-2:]
     bias = pv_ref[5:6, : 3 * width]
     for p, nb in enumerate((n0, n1, n2, n3)):
         t = jnp.bitwise_xor(order(c, p), s)
         row = pl.multiple_of(t * span, span)
-        y = nn(nb[...], w_ref[...]) + bias
+        rows = nb[...]
+        if raw:
+            v = rows.astype(F32)
+            rows = (v * crms_scale(v)[0] * pv_ref[3:4, :cc]).astype(BF16)
+            rest[p][...] = rows
+        y = nn(rows, w_ref[...]) + bias
         for h in range(heads):
             lo = h * hd
             qh[h, pl.ds(row, span), :] = (y[:, lo : lo + hd] * (hd**-0.5)).astype(BF16)
@@ -137,16 +171,17 @@
         a[...] = at[jnp.bitwise_xor(s, k)]
 
 
-def attn_fwd(ids, blocks, w3, pv, heads, hd):
+def attn_fwd(raw, ids, blocks, w3, pv, heads, hd):
     span, width = blocks[0].shape
     full = span * QUAD
     hh = jax.ShapeDtypeStruct((heads, full, hd), BF16)
     aa = jax.ShapeDtypeStruct((heads * hd, span), BF16)
+    normed = [jax.ShapeDtypeStruct((span, width), BF16)] * (QUAD if raw else 0)
     return pl.pallas_call(
-        attn_fwd_kernel,
+        functools.partial(attn_fwd_kernel, raw),
         in_specs=[SMEM] + [VMEM] * 6,
-        out_specs=[VMEM] * 8,
-        out_shape=[hh, hh, hh, jax.ShapeDtypeStruct((heads, QUAD, span), F32), aa, aa, aa, aa],
+        out_specs=[VMEM] * (8 + len(normed)),
+        out_shape=[hh, hh, hh, jax.ShapeDtypeStruct((heads, QUAD, span), F32), aa, aa, aa, aa] + normed,
         scratch_shapes=[
             pltpu.VMEM((QUAD, heads * hd, span), BF16),
             pltpu.VMEM((full, span), F32),
@@ -176,7 +211,7 @@
         for k, a in enumerate((a0, a1, a2, a3)):
             row = pl.multiple_of(jnp.bitwise_xor(s, k) * rows, rows)
             m = m + tn(a[...], wo[pl.ds(row, rows), :])
-            astk[k] = a[...]
+            astk[jnp.bitwise_xor(s, k)] = a[...].T
         mid[...] = m
         r, _, _ = crms_scale(m)
         nm[...] = (m * r * pv[4:5, :cc]).astype(BF16)
@@ -233,7 +268,7 @@
             whole((span, cc)),
             whole((span, cc)),
             whole((8, 128)),
-            whole((QUAD, rows, span)),
+            whole((QUAD, span, rows)),
         ],
         scratch_shapes=[pltpu.VMEM((span, cc), BF16), pltpu.VMEM((span, cc), F32)],
     )
@@ -246,7 +281,7 @@
             jax.ShapeDtypeStruct((span, cc), BF16),
             jax.ShapeDtypeStruct((span, cc), BF16),
             jax.ShapeDtypeStruct((8, 128), F32),
-            jax.ShapeDtypeStruct((QUAD, rows, span), BF16),
+            jax.ShapeDtypeStruct((QUAD, span, rows), BF16),
         ],
         compiler_params=params(40, dimension_semantics=("arbitrary",)),
         cost_estimate=cost(6 * span * cc * ff, 4 * cc * ff + 4 * span * ff, span * ff),
@@ -255,7 +290,7 @@
 
 def mlp_bwd_kernel(
     layer, ids, df, u, mid, wo, pv, upo, upr, dno, dnr,
-    lr, rr, dmid, dmlow, g, d0, d1, d2, d3, acc,
+    lr, rr, dmid, g, d0, d1, d2, d3, acc, wide,
 ):
     j = pl.program_id(0)
     c, s = ids[0], ids[1]
@@ -287,10 +322,13 @@
         dv, gg, nm = crms_back(mid[...], pv[4:5, :cc], acc[...])
         dm = dff + dv
         low = dm.astype(BF16)
-        rr[0] = df[...]
-        rr[1] = nm.astype(BF16)
         dmid[...] = dm
-        dmlow[...] = low
+        quarter = rr.shape[-1]
+        wide[:, cc:] = jnp.zeros((wide.shape[0], wide.shape[1] - cc), BF16)
+        for i, v in enumerate((df[...], nm.astype(BF16), low)):
+            wide[:, :cc] = v
+            for t in range(QUAD):
+                rr[i, t] = wide[:, t * quarter : (t + 1) * quarter]
         g[1:2, :cc] = jnp.sum(low.astype(F32), axis=0, keepdims=True)
         g[2:3, :cc] = jnp.sum(dff, axis=0, keepdims=True)
         g[4:5, :cc] = jnp.sum(gg, axis=0, keepdims=True)
@@ -329,13 +367,12 @@
         ],
         out_specs=[
             pl.BlockSpec((2, span, fb), lambda j, ids: (0, 0, j)),
-            whole((2, span, cc)),
-            whole((span, cc)),
+            whole((3, QUAD, span, (cc + 1) // QUAD)),
             whole((span, cc)),
             whole((8, ff)),
         ]
         + [whole((rows, span))] * 4,
-        scratch_shapes=[pltpu.VMEM((span, cc), F32)],
+        scratch_shapes=[pltpu.VMEM((span, cc), F32), pltpu.VMEM((span, cc + 1), BF16)],
     )
     dd = jax.ShapeDtypeStruct((rows, span), BF16)
     return pl.pallas_call(
@@ -343,9 +380,8 @@
         grid_spec=grid,
         out_shape=[
             jax.ShapeDtypeStruct((2, span, ff), BF16),
-            jax.ShapeDtypeStruct((2, span, cc), BF16),
+            jax.ShapeDtypeStruct((3, QUAD, span, (cc + 1) // QUAD), BF16),
             jax.ShapeDtypeStruct((span, cc), F32),
-            jax.ShapeDtypeStruct((span, cc), BF16),
             jax.ShapeDtypeStruct((8, ff), F32),
             dd, dd, dd, dd,
         ],
@@ -354,57 +390,37 @@
     )(ids, df, u, mid, wo, pv, up[0], up[1], dn[0], dn[1])
 
 
-def product_kernel(send, ids, lr, rr, att, dmlow, *rest):
-    out = rest[-1]
+def product_kernel(send, places, ids, lr, rr, att, *rest):
+    outs = rest[-len(places) :]
     core = 1 - ids[0] if send else ids[0]
-    block = lr.shape[-1]
-    part = att.shape[1] // 2
-    main = tn(lr[0], rr[0])
-    row = pl.multiple_of(core * part, part)
-    side = nn(att[0, pl.ds(row, part), :], dmlow[...])
-    if send:
-        out[:block, :] = main.astype(BF16)
-        out[block:, :] = side.astype(BF16)
-    else:
-        got = rest[0]
-        out[:block, :] = (main + got[:block, :].astype(F32)).astype(BF16)
-        out[block:, :] = (side + got[block:, :].astype(F32)).astype(BF16)
-
-
-def product(send, place, ids, lr, rr, att, dmlow, got=None):
-    span, cc = dmlow.shape
-    block = lr.shape[-1] // QUAD
-    rows = att.shape[1]
-    total = block + rows // 2
-
-    def core(ids):
-        return 1 - ids[0] if send else ids[0]
-
-    def offset(ids):
-        return order(core(ids), place)
-
-    in_specs = [
-        pl.BlockSpec((1, span, block), lambda i, ids: (core(ids), 0, offset(ids) ^ ids[1])),
-        pl.BlockSpec((1, span, cc), lambda i, ids: (core(ids), 0, 0)),
-        pl.BlockSpec((1, rows, span), lambda i, ids: (offset(ids), 0, 0)),
-        pl.BlockSpec((span, cc), lambda i, ids: (0, 0)),
-    ]
-    operands = [lr, rr, att, dmlow]
-    if not send:
-        in_specs.append(pl.BlockSpec((total, cc), lambda i, ids: (0, 0)))
-        operands.append(got)
+    ff = lr.shape[-1]
+    part = att.shape[-1]
+    for i, place in enumerate(places):
+        t = jnp.bitwise_xor(order(core, place), ids[1])
+        out = outs[i]
+        main = tn(rr[core, t], lr[core])
+        low = rr[2, t]
+        sides = [tn(low, att[2 * core + h]) for h in range(2)]
+        if not send:
+            got = rest[i]
+            main = main + got[:, :ff].astype(F32)
+            sides = [v + got[:, ff + h * part : ff + (h + 1) * part].astype(F32) for h, v in enumerate(sides)]
+        out[:, :ff] = main.astype(BF16)
+        for h, v in enumerate(sides):
+            out[:, ff + h * part : ff + (h + 1) * part] = v.astype(BF16)
+
+
+def product(send, places, ids, lr, rr, att, got=()):
+    span, quarter = rr.shape[2:]
+    cols = lr.shape[-1] + 2 * att.shape[-1]
     return pl.pallas_call(
-        functools.partial(product_kernel, send),
-        grid_spec=pltpu.PrefetchScalarGridSpec(
-            num_scalar_prefetch=1,
-            grid=(1,),
-            in_specs=in_specs,
-            out_specs=pl.BlockSpec((total, cc), lambda i, ids: (0, 0)),
-        ),
-        out_shape=jax.ShapeDtypeStruct((total, cc), BF16),
-        compiler_params=params(24, dimension_semantics=("arbitrary",)),
-        cost_estimate=cost(2 * span * total * cc, 2 * total * cc * 2),
-    )(ids, *operands)
+        functools.partial(product_kernel, send, places),
+        in_specs=[SMEM] + [VMEM] * (3 + len(got)),
+        out_specs=[VMEM] * len(places),
+        out_shape=[jax.ShapeDtypeStruct((quarter, cols), BF16)] * len(places),
+        compiler_params=params(32),
+        cost_estimate=cost(2 * span * quarter * cols * len(places), 2 * 4 * quarter * cols * len(places)),
+    )(ids, lr, rr, att, *got)
 
 
 def attn_bwd_kernel(
@@ -413,7 +429,7 @@
 ):
     c, s = ids[0], ids[1]
     heads, _, hd = qh.shape
-    span = n0.shape[0]
+    span, cc = n0.shape
     width = heads * hd
     for k, d in enumerate((d0, d1, d2, d3)):
         do[jnp.bitwise_xor(s, k)] = d[...]
@@ -448,32 +464,24 @@
         y = dy[pl.ds(row, span), :]
         out[...] = nt(y, w_ref[...]).astype(BF16)
         total = total + jnp.sum(y.astype(F32), axis=0, keepdims=True)
-        g = tn(y, nb[...])
+        g = tn(nb[...], y)
         if p == 0:
-            acc[...] = g
+            acc[:cc, :] = g
         else:
-            acc[...] += g
+            acc[:cc, :] += g
     gb[...] = jnp.broadcast_to(total, gb.shape)
     part = gs.shape[0]
-
-    @pl.when(c == 0)
-    def _():
-        gk[...] = acc[:part, :].astype(BF16)
-        gs[...] = acc[part:, :].astype(BF16)
-
-    @pl.when(c == 1)
-    def _():
-        gs[...] = acc[:part, :].astype(BF16)
-        gk[...] = acc[part:, :].astype(BF16)
+    acc[cc:, :] = jnp.zeros((acc.shape[0] - cc, acc.shape[1]), F32)
+    gk[...] = acc[pl.ds(pl.multiple_of(c * part, part), part), :].astype(BF16)
+    gs[...] = acc[pl.ds(pl.multiple_of((1 - c) * part, part), part), :].astype(BF16)
 
 
 def attn_bwd(ids, blocks, w3, qkvl, douts):
     span, cc = blocks[0].shape
     heads, full, hd = qkvl[0].shape
     width = heads * hd
-    part = 3 * width // 2
     pp = jax.ShapeDtypeStruct((span, cc), BF16)
-    gg = jax.ShapeDtypeStruct((part, cc), BF16)
+    gg = jax.ShapeDtypeStruct(((cc + 1) // 2, 3 * width), BF16)
     return pl.pallas_call(
         attn_bwd_kernel,
         in_specs=[SMEM] + [VMEM] * 13,
@@ -484,7 +492,7 @@
             pltpu.VMEM((heads, full, hd), F32),
             pltpu.VMEM((heads, full, hd), F32),
             pltpu.VMEM((full, 3 * width), BF16),
-            pltpu.VMEM((3 * width, cc), F32),
+            pltpu.VMEM((cc + 1, 3 * width), F32),
             pltpu.VMEM((full, span), F32),
         ],
         compiler_params=params(48),
@@ -518,143 +526,144 @@
     )(part, r0, r1, dmid, x, pv)
 
 
+def both_lengths(t, rows, start):
+    @pl.when(t < QUAD - 1)
+    def _():
+        start(rows)
+
+    @pl.when(t == QUAD - 1)
+    def _():
+        start(rows - 1)
+
+
 def place_kernel(place, first, ids, *refs):
     srcs = refs[:4]
     outs = refs[4:7] if first else refs[7:10]
     x0, x1, od, ou, ow, sem = refs[7:] if first else refs[10:]
     c, s = ids[0], ids[1]
     down, up, wout = outs
-    f0, r1, r0, f1 = srcs
+    rows, _, ff = od.shape
+    part = ow.shape[-1]
+
+    def load(a, b):
+        moves = [pltpu.make_async_copy(a, x0, sem.at[0]), pltpu.make_async_copy(b, x1, sem.at[1])]
+        for m in moves:
+            m.start()
+        for m in moves:
+            m.wait()
 
     @pl.when(c == 0)
     def _():
-        a = pltpu.make_async_copy(f0, x0, sem.at[0])
-        b = pltpu.make_async_copy(r0, x1, sem.at[1])
-        a.start()
-        b.start()
-        a.wait()
-        b.wait()
+        load(srcs[0], srcs[1])
 
     @pl.when(c != 0)
     def _():
-        a = pltpu.make_async_copy(r1, x0, sem.at[0])
-        b = pltpu.make_async_copy(f1, x1, sem.at[1])
-        a.start()
-        b.start()
-        a.wait()
-        b.wait()
-
-    block = od.shape[0]
-    part = ow.shape[1]
+        load(srcs[2], srcs[3])
+
     t0 = jnp.bitwise_xor(((place & 1) << 1) | (place >> 1), s)
     t1 = jnp.bitwise_xor(place, s)
-    od[...] = x0[:block, :].astype(F32)
-    ow[0] = x0[block:, :].astype(F32)
-    ow[1] = x1[block:, :].astype(F32)
-    ca = pltpu.make_async_copy(od, down.at[pl.ds(pl.multiple_of(t0 * block, block), block), :], sem.at[0])
-    cb = pltpu.make_async_copy(
-        ow.at[0], wout.at[pl.ds(pl.multiple_of(t0 * 2 * part, part), part), :], sem.at[1]
-    )
-    cd = pltpu.make_async_copy(
-        ow.at[1], wout.at[pl.ds(pl.multiple_of((t1 * 2 + 1) * part, part), part), :], sem.at[2]
-    )
-    ca.start()
-    cb.start()
-    cd.start()
-    ou[...] = x1[:block, :].astype(F32).T
-    ce = pltpu.make_async_copy(ou, up.at[:, pl.ds(pl.multiple_of(t1 * block, block), block)], sem.at[3])
-    ce.start()
-    ca.wait()
-    cb.wait()
-    cd.wait()
-    ce.wait()
-
-
-def place_rows(place, ids, srcs, outs, shapes):
-    total, cc = srcs[0].shape
-    block = shapes[0][0] // QUAD
-    part = total - block
+
+    def moves(n, t, i, src, dst, lo, cols):
+        return [
+            pltpu.make_async_copy(src.at[pl.ds(0, n)], dst.at[pl.ds(t * rows, n)], sem.at[2 * i]),
+            pltpu.make_async_copy(
+                ow.at[i, pl.ds(0, n)], wout.at[pl.ds(t * rows, n), :, pl.ds(lo, cols)], sem.at[2 * i + 1]
+            ),
+        ]
+
+    jobs = ((t0, 0, x0, od, down, 0), (t1, 1, x1, ou, up, part))
+    for t, i, x, o, dst, lo in jobs:
+        o[:, 0, :] = x[:, :ff].astype(F32)
+        ow[i, :, 0, :] = x[:, ff:].astype(F32)
+        both_lengths(t, rows, lambda n: [m.start() for m in moves(n, t, i, o, dst, lo, part)])
+    for t, i, x, o, dst, lo in jobs:
+        both_lengths(t, rows, lambda n: [m.wait() for m in moves(n, t, i, o, dst, lo, part)])
+
+
+def place_rows(place, ids, srcs, outs, cc, ff, model):
+    rows, cols = srcs[0].shape
     first = outs is None
     operands = [ids, *srcs] + ([] if first else list(outs))
     return pl.pallas_call(
         functools.partial(place_kernel, place, first),
-        in_specs=[SMEM] + [ANY] * (len(operands) - 1),
-        out_specs=[ANY] * 3,
-        out_shape=[jax.ShapeDtypeStruct(s, F32) for s in shapes],
+        in_specs=[SMEM] + [HBM] * (len(operands) - 1),
+        out_specs=[HBM] * 3,
+        out_shape=[jax.ShapeDtypeStruct((cc, 1, n), F32) for n in (ff, ff, model)],
         input_output_aliases={} if first else {5: 0, 6: 1, 7: 2},
         scratch_shapes=[
-            pltpu.VMEM((total, cc), BF16),
-            pltpu.VMEM((total, cc), BF16),
-            pltpu.VMEM((block, cc), F32),
-            pltpu.VMEM((cc, block), F32),
-            pltpu.VMEM((2, part, cc), F32),
+            pltpu.VMEM((rows, cols), BF16),
+            pltpu.VMEM((rows, cols), BF16),
+            pltpu.VMEM((rows, 1, ff), F32),
+            pltpu.VMEM((rows, 1, ff), F32),
+            pltpu.VMEM((2, rows, 1, cols - ff), F32),
             pltpu.SemaphoreType.DMA((4,)),
         ],
-        compiler_params=params(24),
-        cost_estimate=cost(0, 12 * total * cc),
+        compiler_params=params(32),
+        cost_estimate=cost(0, 12 * rows * cols),
     )(*operands)
 
 
-def qkv_out_kernel(width, ids, *refs):
-    srcs, out, rows, sem = refs[:16], refs[16], refs[17], refs[18]
+def qkv_out_kernel(ids, *refs):
+    srcs, out, rows, wide, od, sem = refs[:8], *refs[8:]
     c, s = ids[0], ids[1]
-    part = 3 * width // 2
-    group = QUAD * width
-
-    def copies(place, head, tail):
-        t0 = jnp.bitwise_xor(((place & 1) << 1) | (place >> 1), s) * width
-        t1 = jnp.bitwise_xor(place, s) * width
-        spans = (
-            (head, 0, width, t0),
-            (head, width, part - width, group + t0),
-            (tail, 0, 2 * width - part, group + t1 + (part - width)),
-            (tail, 2 * width - part, width, 2 * group + t1),
+    width = rows.shape[-1] // 3
+
+    def load(four):
+        todo = [
+            pltpu.make_async_copy(src, rows.at[jnp.bitwise_xor(s, k)], sem.at[k])
+            for k, src in enumerate(four)
+        ]
+        for m in todo:
+            m.start()
+        for m in todo:
+            m.wait()
+
+    @pl.when(c == 0)
+    def _():
+        load(srcs[:4])
+
+    @pl.when(c != 0)
+    def _():
+        load(srcs[4:])
+
+    step = rows.shape[1] // QUAD
+    moves = []
+    for b in range(QUAD):
+        if b >= 2:
+            moves[b - 2].wait()
+        for t in range(QUAD):
+            v = rows[t, b * step : (b + 1) * step, :].astype(F32)
+            for i in range(3):
+                lo = (i * QUAD + t) * width
+                wide[:, lo : lo + width] = v[:, i * width : (i + 1) * width]
+        od[b % 2, :, 0, :] = wide[...]
+        n = step - (b == QUAD - 1)
+        m = pltpu.make_async_copy(
+            od.at[b % 2, pl.ds(0, n)], out.at[pl.ds(b * step, n)], sem.at[QUAD + b % 2]
         )
-        return [
-            pltpu.make_async_copy(
-                src.at[pl.ds(lo, size), :],
-                rows.at[pl.ds(pl.multiple_of(dst, width // 2), size), :],
-                sem.at[place, i],
-            )
-            for i, (src, lo, size, dst) in enumerate(spans)
-        ]
-
-    def run(pick):
-        todo = []
-        for p in range(QUAD):
-            f0, r1, r0, f1 = srcs[4 * p : 4 * p + 4]
-            todo += copies(p, *pick(f0, r1, r0, f1))
-        for one in todo:
-            one.start()
-        for one in todo:
-            one.wait()
-
-    @pl.when(c == 0)
-    def _():
-        run(lambda f0, r1, r0, f1: (f0, r0))
-
-    @pl.when(c != 0)
-    def _():
-        run(lambda f0, r1, r0, f1: (r1, f1))
-
-    for i in range(3):
-        out[:, i * group : (i + 1) * group] = rows[i * group : (i + 1) * group, :].astype(F32).T
-
-
-def qkv_out(ids, srcs, width, shape):
-    cc = srcs[0].shape[-1]
+        m.start()
+        moves.append(m)
+    for m in moves[-2:]:
+        m.wait()
+
+
+def qkv_out(ids, srcs, cc):
+    _, half, cols = srcs[0].shape
+    full = 2 * half
     return pl.pallas_call(
-        functools.partial(qkv_out_kernel, width),
-        in_specs=[SMEM] + [ANY] * 16,
-        out_specs=VMEM,
-        out_shape=jax.ShapeDtypeStruct(shape, F32),
+        qkv_out_kernel,
+        in_specs=[SMEM] + [HBM] * 8,
+        out_specs=HBM,
+        out_shape=jax.ShapeDtypeStruct((cc, 1, QUAD * cols), F32),
         scratch_shapes=[
-            pltpu.VMEM((3 * QUAD * width, cc), BF16),
-            pltpu.SemaphoreType.DMA((QUAD, 4)),
+            pltpu.VMEM((QUAD, full, cols), BF16),
+            pltpu.VMEM((full // QUAD, QUAD * cols), F32),
+            pltpu.VMEM((2, full // QUAD, 1, QUAD * cols), F32),
+            pltpu.SemaphoreType.DMA((QUAD + 2,)),
         ],
         compiler_params=params(32),
-        cost_estimate=cost(0, 6 * shape[0] * shape[1]),
-    )(ids, *srcs)
+        cost_estimate=cost(0, 6 * cc * QUAD * cols),
+    )(ids, *[v.reshape(full, cols) for v in srcs])
 
 
 def to_first(v):
@@ -680,28 +689,47 @@
     return lax.ppermute(v, "dp", [(i, i ^ step) for i in range(n)])
 
 
-def dp_sum(v):
+def dp_scatter(v):
     n = lax.axis_size("dp")
     z = lax.axis_index("dp")
-    rows, cc = v.shape
+    rows, cols = v.shape
     piece = rows // n
-    steps = []
-    cur = v.reshape(n, piece, cc)
+    cur = v.reshape(n, piece, cols)
     step = 1
     while step < n:
-        cur = cur.reshape(cur.shape[0] // 2, 2, piece, cc)
+        cur = cur.reshape(cur.shape[0] // 2, 2, piece, cols)
         low = (z & step) == 0
         away = jnp.where(low, cur[:, 1], cur[:, 0])
         keep = jnp.where(low, cur[:, 0], cur[:, 1])
-        cur = (keep.astype(F32) + dp_partner(away, step).astype(F32)).astype(BF16)
-        steps.append(step)
+        cur = add_low(keep, dp_partner(away, step))
         step *= 2
-    for step in reversed(steps):
+    return cur[0]
+
+
+def owner_gather(l, v):
+    n = lax.axis_size("dp")
+    z = lax.axis_index("dp")
+    piece, cols = v.shape
+    got = lax.ppermute(v, "section", [(1 - l, l)])
+    cur = jnp.stack([v, got] if l == 0 else [got, v])[:, None]
+    step = n // 2
+    while step:
         low = (z & step) == 0
-        got = dp_partner(cur, step)
-        cur = jnp.where(low, jnp.stack([cur, got], 1), jnp.stack([got, cur], 1))
-        cur = cur.reshape(-1, piece, cc)
-    return cur.reshape(rows, cc)
+        got = lax.ppermute(cur, ("section", "dp"), [(l * n + i, l * n + (i ^ step)) for i in range(n)])
+        pairs = [
+            jnp.where(low, jnp.stack([a, b], 1), jnp.stack([b, a], 1)).reshape(-1, piece, cols)
+            for a, b in ((cur[0], got[0]), (cur[1], got[1]))
+        ]
+        step //= 2
+        if step:
+            cur = jnp.stack(pairs)
+    return [w.reshape(n * piece, cols) for w in pairs]
+
+
+def owner_quad(l, v, k):
+    return lax.ppermute(
+        v, ("section", "seq"), [(l * QUAD + i, l * QUAD + (i ^ k)) for i in range(QUAD)]
+    )
 
 
 def add_low(a, b):
@@ -730,14 +758,13 @@
     dp_count = lax.axis_size("dp")
     mine = c == 0
 
-    x0 = lax.dynamic_index_in_dim(layer_in, c, 0, keepdims=False)[0]
-    cot = lax.dynamic_index_in_dim(cotangent, c, 0, keepdims=False)[0]
     lens = lax.dynamic_index_in_dim(lengths, c, 0, keepdims=False)[0]
     e0 = lens[0]
     e1 = e0 + lens[1]
     e2 = e1 + lens[2]
     e3 = e2 + lens[3]
     ids = jnp.stack([c, s, e0, e1, e2, e3, c, s]).astype(jnp.int32)
+    x = rows_in(ids, layer_in)
 
     def row(v, n=ff):
         return jnp.pad(v, ((0, 0), (0, n - v.shape[-1])))
@@ -761,13 +788,14 @@
     w3 = [jnp.where(mine, w3_own, w3_got), jnp.where(mine, w3_got, w3_own)]
     wo = [jnp.where(mine, w_out[0], wo_got), jnp.where(mine, wo_got, w_out[0])]
 
-    x = x0
-    normed = first_norm(x0, pv[0])
+    normed = x
     saved = []
     squares = []
     for l in range(2):
         blocks = quad_gather(normed)
-        qh, kh, vh, lse, *att = attn_fwd(ids, blocks, w3[l], pv[l], heads, hd)
+        qh, kh, vh, lse, *att = attn_fwd(l == 0, ids, blocks, w3[l], pv[l], heads, hd)
+        if l == 0:
+            att, blocks = att[:QUAD], att[QUAD:]
         att = [att[0]] + [to_quad(att[k], k) for k in (1, 2, 3)]
         mid, u, xout, normed, sq, astk = mlp_fwd(
             l, ids, x, att, wo[l], pv[l], pv[min(l + 1, 1)], up, dn
@@ -777,29 +805,43 @@
         x = xout
     outs = [saved[1][0], x]
 
-    df = cot
-    grads = [None, None]
+    df = rows_in(ids, cotangent)
+    rows_of = [None, None]
+    qkv_of = [None, None]
     smalls = [None, None]
     in_grads = [None, None]
     for l in (1, 0):
         xl, blocks, qkvl, astk, mid, u = saved[l]
-        lr, rr, dmid, dmlow, g, *douts = mlp_bwd(l, ids, df, u, mid, wo[l], pv[l], up, dn)
+        lr, rr, dmid, g, *douts = mlp_bwd(l, ids, df, u, mid, wo[l], pv[l], up, dn)
         douts = [douts[0]] + [to_quad(douts[k], k) for k in (1, 2, 3)]
-        got = [None] * QUAD
-        for p in (3, 1, 2, 0):
-            got[p] = to_core(product(True, p, ids, lr, rr, astk, dmlow))
-        tot = [None] * QUAD
-        for p in (3, 1, 2, 0):
-            tot[p] = product(False, p, ids, lr, rr, astk, dmlow, got[p])
-        half1 = add_low(tot[1], to_first(tot[3]))
-        half0 = add_low(tot[0], to_first(tot[2]))
+        far = [to_core(v) for v in product(True, (3, 2), ids, lr, rr, astk)]
+        near = [to_core(v) for v in product(True, (1, 0), ids, lr, rr, astk)]
+        far = product(False, (3, 2), ids, lr, rr, astk, far)
+        far, douts = lax.optimization_barrier((far, douts))
+        near = product(False, (1, 0), ids, lr, rr, astk, near)
+        half1 = add_low(near[0], to_first(far[0]))
+        half0 = add_low(near[1], to_first(far[1]))
         quarter = add_low(half0, to_second(half1))
 
         p0, p1, p2, p3, gs, gk, gb = attn_bwd(ids, blocks, w3[l], qkvl, douts)
         q1 = add_low(p1, to_first(p3))
         dx, gg = input_grad_of(p0, to_first(p2), to_second(q1), dmid, xl, pv[l])
+
+        f0, g0 = owner_gather(l, dp_scatter(quarter))
+        f1, g1 = owner_quad(l, f0, 2), owner_quad(l, g0, 1)
+        f2, g2 = owner_quad(l, f0, 1), owner_quad(l, g0, 2)
+        f3, g3 = owner_quad(l, f1, 1), owner_quad(l, g1, 2)
+        rows_of[l] = ((f0, g0), (f1, g1), (f2, g2), (f3, g3))
+
         tq = add_low(gk, to_core(gs))
-        grads[l] = (quad_gather(dp_sum(quarter)), quad_gather(dp_sum(tq)))
+        q0 = jnp.stack(owner_gather(l, dp_scatter(tq)))
+        if l == 1:
+            k1, k2 = owner_quad(l, q0, 1), owner_quad(l, q0, 2)
+            k3 = owner_quad(l, k1, 2)
+        else:
+            k1, k2 = owner_quad(l, q0, 1), owner_quad(l, q0, 2)
+            k3 = owner_quad(l, k2, 1)
+        qkv_of[l] = [q0, k1, k2, k3]
 
         spot = jnp.arange(QUAD)[:, None] == s
         qs = jnp.where(spot, gb[0:1, :width], 0.0).reshape(model)
@@ -821,28 +863,16 @@
         step *= 2
     small = small.reshape(-1)
 
-    def handed(l, i):
-        pairs = [(1, 0)] if l == 0 else [(0, 1)]
-        return [lax.ppermute(f, "section", pairs) for f in grads[l][i]]
-
-    shapes = [(ff, cc), (cc, ff), (model, cc)]
+    grad_qkv = qkv_out(ids, [*qkv_of[0], *qkv_of[1]], cc)
     outs_w = None
-    r1m, r0m = handed(1, 0), handed(0, 0)
-    r1q, r0q = handed(1, 1), handed(0, 1)
-    srcs = []
     for p in range(QUAD):
-        srcs += [grads[0][1][p], r1q[p], r0q[p], grads[1][1][p]]
-    grad_qkv = qkv_out(ids, srcs, width, (cc, 3 * model))
-    for p in range(QUAD):
-        outs_w = place_rows(
-            p, ids, [grads[0][0][p], r1m[p], r0m[p], grads[1][0][p]], outs_w, shapes
-        )
+        outs_w = place_rows(p, ids, [*rows_of[0][p], *rows_of[1][p]], outs_w, cc, ff, model)
     grad_down, grad_up, grad_out = outs_w
 
     def both(pair):
         own = jnp.where(mine, pair[0], pair[1])
         got = to_core(jnp.where(mine, pair[1], pair[0]))
-        return jnp.where(mine, jnp.stack([own, got]), jnp.stack([got, own]))[None, :, None]
+        return rows_out(ids, own, got)
 
     layer_out = both(outs)
     input_grad = both(in_grads)
@@ -858,15 +888,15 @@
     return (
         layer_out,
         input_grad,
-        grad_qkv[None],
+        jnp.transpose(grad_qkv, (1, 0, 2)),
         take(base, 2 * model),
-        grad_out[None],
+        jnp.transpose(grad_out, (1, 2, 0)),
         take(at, cc),
         take(at + 2 * d, cc),
         take(at + 3 * d, cc),
-        grad_up[None],
+        jnp.transpose(grad_up, (1, 0, 2)),
         take(0, ff),
-        grad_down[None],
+        jnp.transpose(grad_down, (1, 2, 0)),
         take(at + d, cc),
         rms,
     )

time: 639 us -> 613 us (0.959); the launches traced: 626 us -> 611 us
  local copies, waits for them, and re-layouts: 123 us -> 66.5 us
  starting transfers between devices: 104 us -> 132 us
  Pallas kernels: 158 us -> 165 us
    ppermute x16 -> x30, waiting for transfers between devices: 4.01 us -> 103 us  [the longest x18 52.5 us: owner_quad(): lax.ppermute(v, ('section', 'seq'), [(l * QUAD + i, l * QUAD + (i ^ k)) f...]
    unnamed x302 -> x270, local copies, waits for them, and re-layouts: 92.2 us -> 29.9 us
    ppermute x18 -> x10, waiting for transfers between devices: 90.7 us -> 48.9 us  [dp_partner(): return lax.ppermute(v, 'dp', [(i, i ^ step) for i in range(n)])]
    ppermute x16 -> x30, starting transfers between devices: 31.7 us -> 54.3 us  [the longest x18 37.6 us: owner_quad(): lax.ppermute(v, ('section', 'seq'), [(l * QUAD + i, l * QUAD + (i ^ k)) f...]
    ppermute x20 -> x12, waiting for transfers between devices: 44.1 us -> 22 us  [to_first(): return lax.ppermute(v, ('section', 'seq'), pairs)]
    ppermute x10 -> x6, waiting for transfers between devices: 51.7 us -> 30 us  [to_second(): return lax.ppermute(v, ('section', 'seq'), pairs)]
    ppermute x18, starting transfers between devices: 3.99 us -> 17.9 us  [to_core(): return lax.ppermute(v, 'section', [(0, 1), (1, 0)])]
    ppermute x0 -> x6, local copies, waits for them, and re-layouts: none -> 12.6 us  [owner_quad(): lax.ppermute(v, ('section', 'seq'), [(l * QUAD + i, l * QUAD + (i ^ k)) f...]
  transfers between devices with their start and end apart: 96 -> 90, of which waited for: 36 -> 28; matrix products, arithmetic and copies ran while one was open for 12% -> 11% of each run, Pallas kernels for 14% -> 16%
where the time goes in v2:
time: 613 us; the launch traced here: 611 us
  waiting for transfers between devices  211 us (34%)
  Pallas kernels  165 us (27%)
  starting transfers between devices  132 us (22%)
  local copies, waits for them, and re-layouts  66.5 us (11%)
  other arithmetic  29.2 us (5%)
  between operations  7.56 us (1%)
    ppermute x18, waiting for transfers between devices, owner_quad(): lax.ppermute(v, ('section', 'seq'), [(l * QUAD + i, l * QUAD + (i ^ k)) f...  52.5 us
    ppermute x10, waiting for transfers between devices, dp_partner(): return lax.ppermute(v, 'dp', [(i, i ^ step) for i in range(n)])  48.9 us
    ppermute x8, waiting for transfers between devices, owner_gather(): lax.ppermute(cur, ('section', 'dp'), [(l * n + i, l * n + (i ^ step)) for...  47.6 us
    ppermute x18, starting transfers between devices, owner_quad(): lax.ppermute(v, ('section', 'seq'), [(l * QUAD + i, l * QUAD + (i ^ k)) f...  37.6 us
    ppermute x6, waiting for transfers between devices, to_second(): return lax.ppermute(v, ('section', 'seq'), pairs)  30 us
    unnamed x270, local copies, waits for them, and re-layouts  29.9 us
    pallas_call x2, Pallas kernels, mlp_bwd(): pl.pallas_call(functools.partial(mlp_bwd_kernel, layer), grid_spec=grid,...  26.3 us
    pallas_call x2, Pallas kernels, attn_bwd(): pl.pallas_call(attn_bwd_kernel, in_specs=[SMEM] + [VMEM] * 13, out_specs=...  26.1 us
  transfers between devices with their start and end apart: 90, of which 28 were waited for; matrix products, arithmetic and copies ran while one was open for 11% of the time, Pallas kernels for 16%

profile of v2, /device:TPU:0, one launch (start us, length us, event | category | flops | bytes accessed | tf_op | source)
XLA Modules:
  0.0 610.9 jit_solution(14305712608203225299)
XLA Ops:
  11.9 2.7 collective-permute-start
  17.1 2.7 collective-permute-start.1
  26.5 3.2 collective-permute-done.2.n3
  29.7 10.6 %shard_map.229 = (bf16[3,1024,64]{2,1,0:T(8,128)(2,1)S(1)}, bf16[3,1024,64]{2,1,0:T(8,128)(2,1)S(1)}, bf16[3,1024,64]{2,1,0:T(8,128)(2,1)S(1)}, f32[3,4,256]{2,1...) custom-call(s32[8]{0:T(128)S(1)} %stack.211.ids, ...), custom_call_target="tpu_custom_call" | custom-call | flops 3320709120 | bytes 3141632 | tf_op jit(solution)/shard_map/pallas_call | solution.py:180
  47.3 3.6 collective-permute-done.6.a2
  51.0 10.7 %shard_map.230 = (f32[256,767]{1,0:T(8,128)S(1)}, f32[256,3072]{1,0:T(8,128)S(1)}, bf16[256,767]{1,0:T(8,128)(2,1)S(1)}, bf16[256,767]{1,0:T(8,128)(2,1)S(1)}, f...) custom-call(s32[8]{0:T(128)S(1)} %stack.211.ids, bf16[256,767]{1,0:T(8,128)(2,1)S(1)} %shard_map.228.n0.x, ...), custom_call_target="tpu_custom_call" | custom-call | flops 3619160064 | bytes 12570624 | tf_op jit(solution)/shard_map/pallas_call | solution.py:275
  66.3 10.1 %collective-permute-done.11.n1 = bf16[256,767]{1,0:T(8,128)(2,1)S(1)} collective-permute-done((bf16[256,767]{1,0:T(8,128)(2,1)S(1)}, bf16[256,767]{1,0:T(8,128)(2,1)S(1)}, u32[]{:S(2)}, u32[]{:S(2)}) %collective-permute-start.11) | collective-permute-done | bytes 392736 | tf_op jit(solution)/shard_map/ppermute | solution.py:676
  77.3 6.9 %collective-permute-done.13.n3 = bf16[256,767]{1,0:T(8,128)(2,1)S(1)} collective-permute-done((bf16[256,767]{1,0:T(8,128)(2,1)S(1)}, bf16[256,767]{1,0:T(8,128)(2,1)S(1)}, u32[]{:S(2)}, u32[]{:S(2)}) %collective-permute-start.13) | collective-permute-done | bytes 392736 | tf_op jit(solution)/shard_map/ppermute | solution.py:671
  84.2 10.1 %shard_map.231 = (bf16[3,1024,64]{2,1,0:T(8,128)(2,1)S(1)}, bf16[3,1024,64]{2,1,0:T(8,128)(2,1)S(1)}, bf16[3,1024,64]{2,1,0:T(8,128)(2,1)S(1)}, f32[3,4,256]{2,1...) custom-call(s32[8]{0:T(128)S(1)} %stack.211.ids, ...), custom_call_target="tpu_custom_call" | custom-call | flops 3320709120 | bytes 3141632 | tf_op jit(solution)/shard_map/pallas_call | solution.py:180
  98.0 13.9 %shard_map.234.df = bf16[256,767]{1,0:T(8,128)(2,1)S(1)} custom-call(s32[8]{0:T(128)S(1)} %stack.211.ids, bf16[767,2,256]{2,1,0:T(2,128)(2,1)S(1)} %bitcast.249), custom_call_target="tpu_custom_call" | custom-call | bytes 1178112 | tf_op jit(solution)/shard_map/pallas_call | solution.py:85
  111.9 11.8 %shard_map.232 = (f32[256,767]{1,0:T(8,128)S(1)}, f32[256,3072]{1,0:T(8,128)S(1)}, bf16[256,767]{1,0:T(8,128)(2,1)S(1)}, bf16[256,767]{1,0:T(8,128)(2,1)}, f32[8...) custom-call(s32[8]{0:T(128)S(1)} %stack.211.ids, bf16[256,767]{1,0:T(8,128)(2,1)S(1)} %get-tuple-element.122.x, ...), custom_call_target="tpu_custom_call" | custom-call | flops 3619160064 | bytes 12570624 | tf_op jit(solution)/shard_map/pallas_call | solution.py:275
  123.8 13.2 %shard_map.235 = (bf16[2,256,3072]{2,1,0:T(8,128)(2,1)S(1)}, bf16[3,4,256,192]{3,2,1,0:T(8,128)(2,1)S(1)}, f32[256,767]{1,0:T(8,128)S(1)}, f32[8,3072]{1,0:T(8,1...) custom-call(s32[8]{0:T(128)S(1)} %stack.211.ids, ...), custom_call_target="tpu_custom_call" | custom-call | flops 3619160064 | bytes 15716352 | tf_op jit(solution)/shard_map/pallas_call | solution.py:378
  137.0 2.7 shard_map.236
  147.5 2.9 shard_map.237
  151.6 13.0 %shard_map.238 = (bf16[256,767]{1,0:T(8,128)(2,1)S(1)}, bf16[256,767]{1,0:T(8,128)(2,1)S(1)}, bf16[256,767]{1,0:T(8,128)(2,1)S(1)}, bf16[256,767]{1,0:T(8,128)(2...) custom-call(s32[8]{0:T(128)S(1)} %stack.211.ids, ...), custom_call_target="tpu_custom_call" | custom-call | flops 7849377792 | bytes 6283264 | tf_op jit(solution)/shard_map/pallas_call | solution.py:485
  173.6 3.8 collective-permute-done.24
  179.7 2.8 collective-permute-start.46
  189.7 13.1 %shard_map.240 = (bf16[2,256,3072]{2,1,0:T(8,128)(2,1)S(1)}, bf16[3,4,256,192]{3,2,1,0:T(8,128)(2,1)S(1)}, f32[256,767]{1,0:T(8,128)S(1)}, f32[8,3072]{1,0:T(8,1...) custom-call(s32[8]{0:T(128)S(1)} %stack.211.ids, ...), custom_call_target="tpu_custom_call" | custom-call | flops 3619160064 | bytes 15716352 | tf_op jit(solution)/shard_map/pallas_call | solution.py:378
  202.9 2.7 shard_map.241
  207.6 2.6 shard_map.247
  213.9 2.8 add_convert_fusion.1
  219.5 2.3 copy.117
  221.9 14.5 %collective-permute-start.17 = (bf16[256,767]{1,0:T(8,128)(2,1)}, bf16[256,767]{1,0:T(8,128)(2,1)}, u32[]{:S(2)}, u32[]{:S(2)}) collective-permute-start(bf16[256,767]{1,0:T(8,128)(2,1)} %get-tuple-element.242), channel_id=1, source_target_pairs={{0,16},{16,0},{1,17},{17,1},{2,18},{18,2},{3,19},{19,3},{4,20},{20... | collective-permute-start | bytes 1178120 | tf_op jit(solution)/shard_map/ppermute | solution.py:684
  239.7 4.0 shard_map.242
  246.2 13.2 %shard_map.243 = (bf16[256,767]{1,0:T(8,128)(2,1)S(1)}, bf16[256,767]{1,0:T(8,128)(2,1)S(1)}, bf16[256,767]{1,0:T(8,128)(2,1)S(1)}, bf16[256,767]{1,0:T(8,128)(2...) custom-call(s32[8]{0:T(128)S(1)} %stack.211.ids, ...), custom_call_target="tpu_custom_call" | custom-call | flops 7849377792 | bytes 6283264 | tf_op jit(solution)/shard_map/pallas_call | solution.py:485
  264.8 8.1 %collective-permute-done.32 = bf16[256,767]{1,0:T(8,128)(2,1)} collective-permute-done((bf16[256,767]{1,0:T(8,128)(2,1)}, bf16[256,767]{1,0:T(8,128)(2,1)}, u32[]{:S(2)}, u32[]{:S(2)}) %collective-permute-start.32) | collective-permute-done | bytes 392736 | tf_op jit(solution)/shard_map/ppermute | solution.py:671
  278.4 2.2 add_convert_fusion
  281.6 4.0 collective-permute-done.36
  290.6 3.1 collective-permute-start.37
  293.8 11.0 %collective-permute-done.37 = bf16[1,96,576]{2,1,0:T(8,128)(2,1)S(1)} collective-permute-done((bf16[1,96,576]{2,1,0:T(8,128)(2,1)S(1)}, bf16[1,96,576]{2,1,0:T(8,128)(2,1)S(1)}, u32[]{:S(2)}, u32[]{:S(2)}) %collective-permute-start.37) | collective-permute-done | bytes 110624 | tf_op jit(solution)/shard_map/ppermute | solution.py:689
  314.1 2.9 shard_map.248
  317.1 3.9 collective-permute-start.56
  324.5 3.0 collective-permute-start.78
  329.5 12.4 %collective-permute-done.39 = bf16[2,1,96,576]{3,2,0,1:T(8,128)(2,1)S(1)} collective-permute-done((bf16[2,1,96,576]{3,2,0,1:T(8,128)(2,1)S(1)}, bf16[2,1,96,576]{3,2,0,1:T(8,128)(2,1)S(1)}, u32[]{:S(2)}, u32[]{:S(2)}) %collective-permute-start.39) | collective-permute-done | bytes 221216 | tf_op jit(solution)/shard_map/ppermute | solution.py:718
  343.1 3.4 collective-permute-done.78
  355.0 8.0 %collective-permute-done.40 = bf16[2,2,96,576]{3,2,1,0:T(8,128)(2,1)S(1)} collective-permute-done((bf16[2,2,96,576]{3,2,1,0:T(8,128)(2,1)S(1)}, bf16[2,2,96,576]{3,2,1,0:T(8,128)(2,1)S(1)}, u32[]{:S(2)}, u32[]{:S(2)}) %collective-permute-start.40) | collective-permute-done | bytes 442400 | tf_op jit(solution)/shard_map/ppermute | solution.py:718
  367.7 19.3 %collective-permute-done.62 = bf16[192,3456]{1,0:T(8,128)(2,1)} collective-permute-done((bf16[192,3456]{1,0:T(8,128)(2,1)}, bf16[192,3456]{1,0:T(8,128)(2,1)}, u32[]{:S(2)}, u32[]{:S(2)}) %collective-permute-start.62) | collective-permute-done | bytes 1327136 | tf_op jit(solution)/shard_map/ppermute | solution.py:676
  387.0 2.3 add_convert_fusion.3
  392.5 16.4 %collective-permute-done.63 = bf16[2,48,3456]{2,1,0:T(8,128)(2,1)S(1)} collective-permute-done((bf16[2,48,3456]{2,1,0:T(8,128)(2,1)S(1)}, bf16[2,48,3456]{2,1,0:T(8,128)(2,1)S(1)}, u32[]{:S(2)}, u32[]{:S(2)}) %collective-permute-start.63) | collective-permute-done | bytes 663584 | tf_op jit(solution)/shard_map/ppermute | solution.py:689
  409.5 11.0 %collective-permute-done.64 = bf16[1,48,3456]{2,1,0:T(8,128)(2,1)S(1)} collective-permute-done((bf16[1,48,3456]{2,1,0:T(8,128)(2,1)S(1)}, bf16[1,48,3456]{2,1,0:T(8,128)(2,1)S(1)}, u32[]{:S(2)}, u32[]{:S(2)}) %collective-permute-start.64) | collective-permute-done | bytes 331808 | tf_op jit(solution)/shard_map/ppermute | solution.py:689
  426.4 17.7 %collective-permute-done.66 = bf16[2,1,48,3456]{3,2,0,1:T(8,128)(2,1)S(1)} collective-permute-done((bf16[2,1,48,3456]{3,2,0,1:T(8,128)(2,1)S(1)}, bf16[2,1,48,3456]{3,2,0,1:T(8,128)(2,1)S(1)}, u32[]{:S(2)}, u32[]{:S(2)}) %collective-permute-start.66) | collective-permute-done | bytes 663584 | tf_op jit(solution)/shard_map/ppermute | solution.py:718
  447.5 3.1 collective-permute-start.57
  450.6 2.9 collective-permute-start.42
  455.3 9.4 %collective-permute-done.67 = bf16[2,2,48,3456]{3,2,1,0:T(8,128)(2,1)S(1)} collective-permute-done((bf16[2,2,48,3456]{3,2,1,0:T(8,128)(2,1)S(1)}, bf16[2,2,48,3456]{3,2,1,0:T(8,128)(2,1)S(1)}, u32[]{:S(2)}, u32[]{:S(2)}) %collective-permute-start.67) | collective-permute-done | bytes 1327136 | tf_op jit(solution)/shard_map/ppermute | solution.py:718
  467.3 3.1 collective-permute-start.41
  470.4 3.4 collective-permute-start.43
  476.4 15.0 %collective-permute-done.41 = bf16[2,384,576]{1,2,0:T(8,128)(2,1)S(1)} collective-permute-done((bf16[2,384,576]{1,2,0:T(8,128)(2,1)S(1)}, bf16[2,384,576]{1,2,0:T(8,128)(2,1)S(1)}, u32[]{:S(2)}, u32[]{:S(2)}) %collective-permute-start.41) | collective-permute-done | bytes 884768 | tf_op jit(solution)/shard_map/ppermute | solution.py:730
  492.1 13.8 %collective-permute-done.43 = bf16[2,384,576]{1,2,0:T(8,128)(2,1)S(1)} collective-permute-done((bf16[2,384,576]{1,2,0:T(8,128)(2,1)S(1)}, bf16[2,384,576]{1,2,0:T(8,128)(2,1)S(1)}, u32[]{:S(2)}, u32[]{:S(2)}) %collective-permute-start.43) | collective-permute-done | bytes 884768 | tf_op jit(solution)/shard_map/ppermute | solution.py:730
  505.9 2.6 collective-permute-start.70
  508.6 3.0 collective-permute-start.68
  511.6 2.9 collective-permute-start.87
  515.6 3.2 collective-permute-start.86
  521.6 16.8 %collective-permute-done.70.refs_1_ = bf16[192,3456]{1,0:T(8,128)(2,1)} collective-permute-done((bf16[192,3456]{1,0:T(8,128)(2,1)S(1)}, bf16[192,3456]{1,0:T(8,128)(2,1)}, u32[]{:S(2)}, u32[]{:S(2)}) %collective-permute-start.70) | collective-permute-done | bytes 1327136 | tf_op jit(solution)/shard_map/ppermute | solution.py:730
  540.2 3.1 collective-permute-start.71
  543.3 6.8 %collective-permute-done.87.refs_1_ = bf16[192,3456]{1,0:T(8,128)(2,1)S(1)} collective-permute-done((bf16[192,3456]{1,0:T(8,128)(2,1)S(1)}, bf16[192,3456]{1,0:T(8,128)(2,1)S(1)}, u32[]{:S(2)}, u32[]{:S(2)}) %collective-permute-start.87) | collective-permute-done | bytes 1327136 | tf_op jit(solution)/shard_map/ppermute | solution.py:730
  553.2 2.8 shard_map.233
  565.1 2.3 shard_map.245
  567.4 2.3 copy.121
  573.3 2.3 copy.108
  582.8 6.4 %shard_map.246 = f32[767,1,2304]{2,1,0:T(1,128)} custom-call(s32[8]{0:T(128)S(1)} %stack.211.ids, bf16[768,576]{1,0:T(8,128)(2,1)S(1)} %bitcast.232, bf16[768,576]{1,0:T(8,128)(2,1)S(1)} %bitcast.246, bf16[768,576]{1,0:T(8,128)(2,1)S(1)} %bitcast.245, bf16[768,576]{1,0:T(8,128)(2,1)S(1)} %bitcast.247, bf16[768,576]{1,0:T(8,128)(2,1)S(1)} %bitcast.231, ...), custom_call_target="tpu_custom_call" | custom-call | bytes 10603008 | tf_op jit(solution)/shard_map/pallas_call | solution.py:653
  589.2 4.9 shard_map.251
  594.2 5.4 shard_map.252
  599.6 4.7 shard_map.253
  604.4 5.2 shard_map.254
  (548 shorter events, 169.5 us)
Async XLA Ops:
  0.7 50.3 %collective-permute-start.10 = (bf16[1,3072,767]{2,1,0:T(8,128)(2,1)}, bf16[1,3072,767]{2,1,0:T(8,128)(2,1)}, u32[]{:S(2)}, u32[]{:S(2)}) collective-permute-start(bf16[1,3072,767]{2,1,0:T(8,128)(2,1)} %dno.7), channel_id=1, source_target_pairs={{0,16},{16,0},{1,17},{17,1},{2,18},{18,2},{3,19},{19,3},{4,20},{20... | collective-permute-start | bytes 14137352 | tf_op jit(solution)/shard_map/ppermute | solution.py:684
  1.2 49.8 %collective-permute-start.9 = (bf16[1,767,3072]{2,1,0:T(8,128)(2,1)}, bf16[1,767,3072]{2,1,0:T(8,128)(2,1)}, u32[]{:S(2)}, u32[]{:S(2)}) collective-permute-start(bf16[1,767,3072]{2,1,0:T(8,128)(2,1)} %upo.7), channel_id=1, source_target_pairs={{0,16},{16,0},{1,17},{17,1},{2,18},{18,2},{3,19},{19,3},{4,20},{20... | collective-permute-start | bytes 14137352 | tf_op jit(solution)/shard_map/ppermute | solution.py:684
  5.7 14.6 %collective-permute-start.3 = (bf16[767,576]{0,1:T(8,128)(2,1)}, bf16[767,576]{0,1:T(8,128)(2,1)}, u32[]{:S(2)}, u32[]{:S(2)}) collective-permute-start(bf16[767,576]{0,1:T(8,128)(2,1)} %copy.96), channel_id=1, source_target_pairs={{0,16},{16,0},{1,17},{17,1},{2,18},{18,2},{3,19},{19,3},{4,20},{20... | collective-permute-start | bytes 2650760 | tf_op jit(solution)/shard_map/ppermute | solution.py:684
  20.3 24.6 %collective-permute-start.8 = (bf16[768,767]{1,0:T(8,128)(2,1)}, bf16[768,767]{1,0:T(8,128)(2,1)}, u32[]{:S(2)}, u32[]{:S(2)}) collective-permute-start(bf16[768,767]{1,0:T(8,128)(2,1)} %bitcast.284), channel_id=1, source_target_pairs={{0,16},{16,0},{1,17},{17,1},{2,18},{18,2},{3,19},{19,3},{4,20},{20... | collective-permute-start | bytes 3534344 | tf_op jit(solution)/shard_map/ppermute | solution.py:684
  65.1 11.3 %collective-permute-start.11 = (bf16[256,767]{1,0:T(8,128)(2,1)S(1)}, bf16[256,767]{1,0:T(8,128)(2,1)S(1)}, u32[]{:S(2)}, u32[]{:S(2)}) collective-permute-start(bf16[256,767]{1,0:T(8,128)(2,1)S(1)} %get-tuple-element.123.n0), channel_id=1, source_target_pairs={{0,2},{1,3},{2,0},{3,1},{16,17},{17,16},{18,19},{19,18},{4,6},{5,7... | collective-permute-start | bytes 1178120 | tf_op jit(solution)/shard_map/ppermute | solution.py:676
  65.9 11.4 %collective-permute-start.12 = (bf16[256,767]{1,0:T(8,128)(2,1)S(1)}, bf16[256,767]{1,0:T(8,128)(2,1)S(1)}, u32[]{:S(2)}, u32[]{:S(2)}) collective-permute-start(bf16[256,767]{1,0:T(8,128)(2,1)S(1)} %get-tuple-element.123.n0), channel_id=1, source_target_pairs={{0,1},{1,0},{2,3},{3,2},{16,18},{17,19},{18,16},{19,17},{4,5},{5,4... | collective-permute-start | bytes 1178120 | tf_op jit(solution)/shard_map/ppermute | solution.py:671
  94.4 17.5 %collective-permute-start.14 = (bf16[192,256]{1,0:T(8,128)(2,1)S(1)}, bf16[192,256]{1,0:T(8,128)(2,1)S(1)}, u32[]{:S(2)}, u32[]{:S(2)}) collective-permute-start(bf16[192,256]{1,0:T(8,128)(2,1)S(1)} %get-tuple-element.125), channel_id=1, source_target_pairs={{0,1},{1,0},{2,3},{3,2},{4,5},{5,4},{6,7},{7,6},{8,9},{9,8},{10,11... | collective-permute-start | bytes 294920 | tf_op jit(solution)/shard_map/ppermute | solution.py:680
  95.4 16.5 %collective-permute-start.15 = (bf16[192,256]{1,0:T(8,128)(2,1)S(1)}, bf16[192,256]{1,0:T(8,128)(2,1)S(1)}, u32[]{:S(2)}, u32[]{:S(2)}) collective-permute-start(bf16[192,256]{1,0:T(8,128)(2,1)S(1)} %get-tuple-element.126), channel_id=1, source_target_pairs={{0,2},{1,3},{2,0},{3,1},{4,6},{5,7},{6,4},{7,5},{8,10},{9,11},{10,... | collective-permute-start | bytes 294920 | tf_op jit(solution)/shard_map/ppermute | solution.py:680
  96.2 15.7 %collective-permute-start.16 = (bf16[192,256]{1,0:T(8,128)(2,1)S(1)}, bf16[192,256]{1,0:T(8,128)(2,1)S(1)}, u32[]{:S(2)}, u32[]{:S(2)}) collective-permute-start(bf16[192,256]{1,0:T(8,128)(2,1)S(1)} %get-tuple-element.127), channel_id=1, source_target_pairs={{0,3},{1,2},{2,1},{3,0},{4,7},{5,6},{6,5},{7,4},{8,11},{9,10},{10,... | collective-permute-start | bytes 294920 | tf_op jit(solution)/shard_map/ppermute | solution.py:680
  166.4 16.7 %collective-permute-start.72 = (bf16[192,3456]{1,0:T(8,128)(2,1)S(1)}, bf16[192,3456]{1,0:T(8,128)(2,1)S(1)}, u32[]{:S(2)}, u32[]{:S(2)}) collective-permute-start(bf16[192,3456]{1,0:T(8,128)(2,1)S(1)} %get-tuple-element.205), channel_id=1, source_target_pairs={{0,16},{16,0},{1,17},{17,1},{2,18},{18,2},{3,19},{19,3},{4,20},{20... | collective-permute-start | bytes 3981320 | tf_op jit(solution)/shard_map/ppermute | solution.py:684
  166.8 17.1 %collective-permute-start.73 = (bf16[192,3456]{1,0:T(8,128)(2,1)S(1)}, bf16[192,3456]{1,0:T(8,128)(2,1)S(1)}, u32[]{:S(2)}, u32[]{:S(2)}) collective-permute-start(bf16[192,3456]{1,0:T(8,128)(2,1)S(1)} %get-tuple-element.206), channel_id=1, source_target_pairs={{0,16},{16,0},{1,17},{17,1},{2,18},{18,2},{3,19},{19,3},{4,20},{20... | collective-permute-start | bytes 3981320 | tf_op jit(solution)/shard_map/ppermute | solution.py:684
  170.6 18.4 %collective-permute-start.23 = (bf16[256,767]{1,0:T(8,128)(2,1)S(1)}, bf16[256,767]{1,0:T(8,128)(2,1)S(1)}, u32[]{:S(2)}, u32[]{:S(2)}) collective-permute-start(bf16[256,767]{1,0:T(8,128)(2,1)S(1)} %get-tuple-element.159), channel_id=1, source_target_pairs={{0,1},{1,0},{2,3},{3,2},{16,18},{17,19},{18,16},{19,17},{4,5},{5,4... | collective-permute-start | bytes 1178120 | tf_op jit(solution)/shard_map/ppermute | solution.py:671
  177.5 11.5 %collective-permute-start.25 = (bf16[256,767]{1,0:T(8,128)(2,1)S(1)}, bf16[256,767]{1,0:T(8,128)(2,1)S(1)}, u32[]{:S(2)}, u32[]{:S(2)}) collective-permute-start(bf16[256,767]{1,0:T(8,128)(2,1)S(1)} %add_convert_fusion.9), channel_id=1, source_target_pairs={{0,2},{1,3},{2,0},{3,1},{16,17},{17,16},{18,19},{19,18},{4,6},{5,7... | collective-permute-start | bytes 1178120 | tf_op jit(solution)/shard_map/ppermute | solution.py:676
  183.0 30.2 %collective-permute-start.75 = (bf16[192,3456]{1,0:T(8,128)(2,1)S(1)}, bf16[192,3456]{1,0:T(8,128)(2,1)}, u32[]{:S(2)}, u32[]{:S(2)}) collective-permute-start(bf16[192,3456]{1,0:T(8,128)(2,1)S(1)} %get-tuple-element.210), channel_id=1, source_target_pairs={{0,1},{1,0},{2,3},{3,2},{16,18},{17,19},{18,16},{19,17},{4,5},{5,4... | collective-permute-start | bytes 3981320 | tf_op jit(solution)/shard_map/ppermute | solution.py:671
  187.6 22.6 %collective-permute-start.47 = (bf16[96,576]{1,0:T(8,128)(2,1)S(1)}, bf16[96,576]{1,0:T(8,128)(2,1)S(1)}, u32[]{:S(2)}, u32[]{:S(2)}) collective-permute-start(bf16[96,576]{1,0:T(8,128)(2,1)S(1)} %bitcast.281), channel_id=1, source_target_pairs={{0,16},{1,17},{2,18},{3,19},{4,20},{5,21},{6,22},{7,23},{8,24},{9,... | collective-permute-start | bytes 331784 | tf_op jit(solution)/shard_map/ppermute | solution.py:713
  205.6 16.3 %collective-permute-start.26 = (bf16[192,3456]{1,0:T(8,128)(2,1)}, bf16[192,3456]{1,0:T(8,128)(2,1)}, u32[]{:S(2)}, u32[]{:S(2)}) collective-permute-start(bf16[192,3456]{1,0:T(8,128)(2,1)} %get-tuple-element.169), channel_id=1, source_target_pairs={{0,16},{16,0},{1,17},{17,1},{2,18},{18,2},{3,19},{19,3},{4,20},{20... | collective-permute-start | bytes 3981320 | tf_op jit(solution)/shard_map/ppermute | solution.py:684
  205.6 30.8 %collective-permute-start.27 = (bf16[192,3456]{1,0:T(8,128)(2,1)}, bf16[192,3456]{1,0:T(8,128)(2,1)}, u32[]{:S(2)}, u32[]{:S(2)}) collective-permute-start(bf16[192,3456]{1,0:T(8,128)(2,1)} %get-tuple-element.170), channel_id=1, source_target_pairs={{0,16},{16,0},{1,17},{17,1},{2,18},{18,2},{3,19},{19,3},{4,20},{20... | collective-permute-start | bytes 3981320 | tf_op jit(solution)/shard_map/ppermute | solution.py:684
  206.1 38.7 %collective-permute-start.28 = (bf16[192,256]{1,0:T(8,128)(2,1)}, bf16[192,256]{1,0:T(8,128)(2,1)}, u32[]{:S(2)}, u32[]{:S(2)}) collective-permute-start(bf16[192,256]{1,0:T(8,128)(2,1)} %get-tuple-element.174), channel_id=1, source_target_pairs={{0,1},{1,0},{2,3},{3,2},{4,5},{5,4},{6,7},{7,6},{8,9},{9,8},{10,11... | collective-permute-start | bytes 294920 | tf_op jit(solution)/shard_map/ppermute | solution.py:680
  211.5 34.5 %collective-permute-start.29 = (bf16[192,256]{1,0:T(8,128)(2,1)}, bf16[192,256]{1,0:T(8,128)(2,1)S(1)}, u32[]{:S(2)}, u32[]{:S(2)}) collective-permute-start(bf16[192,256]{1,0:T(8,128)(2,1)} %get-tuple-element.175), channel_id=1, source_target_pairs={{0,2},{1,3},{2,0},{3,1},{4,6},{5,7},{6,4},{7,5},{8,10},{9,11},{10,... | collective-permute-start | bytes 294920 | tf_op jit(solution)/shard_map/ppermute | solution.py:680
  216.7 29.3 %collective-permute-start.30 = (bf16[192,256]{1,0:T(8,128)(2,1)S(1)}, bf16[192,256]{1,0:T(8,128)(2,1)}, u32[]{:S(2)}, u32[]{:S(2)}) collective-permute-start(bf16[192,256]{1,0:T(8,128)(2,1)S(1)} %get-tuple-element.176), channel_id=1, source_target_pairs={{0,3},{1,2},{2,1},{3,0},{4,7},{5,6},{6,5},{7,4},{8,11},{9,10},{10,... | collective-permute-start | bytes 294920 | tf_op jit(solution)/shard_map/ppermute | solution.py:680
  221.9 225.6 %collective-permute-start.17 = (bf16[256,767]{1,0:T(8,128)(2,1)}, bf16[256,767]{1,0:T(8,128)(2,1)}, u32[]{:S(2)}, u32[]{:S(2)}) collective-permute-start(bf16[256,767]{1,0:T(8,128)(2,1)} %get-tuple-element.242), channel_id=1, source_target_pairs={{0,16},{16,0},{1,17},{17,1},{2,18},{18,2},{3,19},{19,3},{4,20},{20... | collective-permute-start | bytes 1178120 | tf_op jit(solution)/shard_map/ppermute | solution.py:684
  236.3 39.9 %collective-permute-start.74 = (bf16[192,3456]{1,0:T(8,128)(2,1)}, bf16[192,3456]{1,0:T(8,128)(2,1)}, u32[]{:S(2)}, u32[]{:S(2)}) collective-permute-start(bf16[192,3456]{1,0:T(8,128)(2,1)} %copy-done.66), channel_id=1, source_target_pairs={{0,1},{1,0},{2,3},{3,2},{16,18},{17,19},{18,16},{19,17},{4,5},{5,4... | collective-permute-start | bytes 3981320 | tf_op jit(solution)/shard_map/ppermute | solution.py:671
  244.8 33.0 %collective-permute-start.76 = (bf16[192,3456]{1,0:T(8,128)(2,1)}, bf16[192,3456]{1,0:T(8,128)(2,1)}, u32[]{:S(2)}, u32[]{:S(2)}) collective-permute-start(bf16[192,3456]{1,0:T(8,128)(2,1)} %add_convert_fusion.1), channel_id=1, source_target_pairs={{0,2},{1,3},{2,0},{3,1},{16,17},{17,16},{18,19},{19,18},{4,6},{5,7... | collective-permute-start | bytes 3981320 | tf_op jit(solution)/shard_map/ppermute | solution.py:676
  262.5 10.4 %collective-permute-start.32 = (bf16[256,767]{1,0:T(8,128)(2,1)}, bf16[256,767]{1,0:T(8,128)(2,1)}, u32[]{:S(2)}, u32[]{:S(2)}) collective-permute-start(bf16[256,767]{1,0:T(8,128)(2,1)} %get-tuple-element.184), channel_id=1, source_target_pairs={{0,1},{1,0},{2,3},{3,2},{16,18},{17,19},{18,16},{19,17},{4,5},{5,4... | collective-permute-start | bytes 1178120 | tf_op jit(solution)/shard_map/ppermute | solution.py:671
  263.6 10.5 %collective-permute-start.35 = (bf16[384,576]{1,0:T(8,128)(2,1)}, bf16[384,576]{1,0:T(8,128)(2,1)}, u32[]{:S(2)}, u32[]{:S(2)}) collective-permute-start(bf16[384,576]{1,0:T(8,128)(2,1)} %get-tuple-element.188), channel_id=1, source_target_pairs={{0,16},{16,0},{1,17},{17,1},{2,18},{18,2},{3,19},{19,3},{4,20},{20... | collective-permute-start | bytes 1327112 | tf_op jit(solution)/shard_map/ppermute | solution.py:684
  272.9 37.1 %collective-permute-start.58 = (bf16[192,3456]{1,0:T(8,128)(2,1)}, bf16[192,3456]{1,0:T(8,128)(2,1)}, u32[]{:S(2)}, u32[]{:S(2)}) collective-permute-start(bf16[192,3456]{1,0:T(8,128)(2,1)} %copy-done.69), channel_id=1, source_target_pairs={{0,16},{16,0},{1,17},{17,1},{2,18},{18,2},{3,19},{19,3},{4,20},{20... | collective-permute-start | bytes 3981320 | tf_op jit(solution)/shard_map/ppermute | solution.py:684
  274.1 12.3 %collective-permute-start.31 = (bf16[256,767]{1,0:T(8,128)(2,1)}, bf16[256,767]{1,0:T(8,128)(2,1)S(1)}, u32[]{:S(2)}, u32[]{:S(2)}) collective-permute-start(bf16[256,767]{1,0:T(8,128)(2,1)} %copy-done.78), channel_id=1, source_target_pairs={{0,1},{1,0},{2,3},{3,2},{16,18},{17,19},{18,16},{19,17},{4,5},{5,4... | collective-permute-start | bytes 1178120 | tf_op jit(solution)/shard_map/ppermute | solution.py:671
  276.3 10.8 %collective-permute-start.33 = (bf16[256,767]{1,0:T(8,128)(2,1)S(1)}, bf16[256,767]{1,0:T(8,128)(2,1)S(1)}, u32[]{:S(2)}, u32[]{:S(2)}) collective-permute-start(bf16[256,767]{1,0:T(8,128)(2,1)S(1)} %add_convert_fusion.8), channel_id=1, source_target_pairs={{0,2},{1,3},{2,0},{3,1},{16,17},{17,16},{18,19},{19,18},{4,6},{5,7... | collective-permute-start | bytes 1178120 | tf_op jit(solution)/shard_map/ppermute | solution.py:676
  285.6 26.0 %collective-permute-start.59 = (bf16[192,3456]{1,0:T(8,128)(2,1)}, bf16[192,3456]{1,0:T(8,128)(2,1)}, u32[]{:S(2)}, u32[]{:S(2)}) collective-permute-start(bf16[192,3456]{1,0:T(8,128)(2,1)} %get-tuple-element.200), channel_id=1, source_target_pairs={{0,16},{16,0},{1,17},{17,1},{2,18},{18,2},{3,19},{19,3},{4,20},{20... | collective-permute-start | bytes 3981320 | tf_op jit(solution)/shard_map/ppermute | solution.py:684
  286.4 36.6 %collective-permute-start.77 = (bf16[2,48,3456]{2,1,0:T(8,128)(2,1)}, bf16[2,48,3456]{2,1,0:T(8,128)(2,1)}, u32[]{:S(2)}, u32[]{:S(2)}) collective-permute-start(bf16[2,48,3456]{2,1,0:T(8,128)(2,1)} %select_bitcast_fusion), channel_id=1, source_target_pairs={{0,4},{4,0},{8,12},{12,8},{1,5},{5,1},{9,13},{13,9},{2,6},{6,2},{1... | collective-permute-start | bytes 1990664 | tf_op jit(solution)/shard_map/ppermute | solution.py:689
  290.6 14.2 %collective-permute-start.37 = (bf16[1,96,576]{2,1,0:T(8,128)(2,1)S(1)}, bf16[1,96,576]{2,1,0:T(8,128)(2,1)S(1)}, u32[]{:S(2)}, u32[]{:S(2)}) collective-permute-start(bf16[1,96,576]{2,1,0:T(8,128)(2,1)S(1)} %select_bitcast_fusion.7), channel_id=1, source_target_pairs={{0,8},{4,12},{8,0},{12,4},{1,9},{5,13},{9,1},{13,5},{2,10},{6,14},... | collective-permute-start | bytes 331784 | tf_op jit(solution)/shard_map/ppermute | solution.py:689
  308.7 12.3 %collective-permute-start.38 = (bf16[96,576]{1,0:T(8,128)(2,1)S(1)}, bf16[96,576]{1,0:T(8,128)(2,1)S(1)}, u32[]{:S(2)}, u32[]{:S(2)}) collective-permute-start(bf16[96,576]{1,0:T(8,128)(2,1)S(1)} %bitcast.278), channel_id=1, source_target_pairs={{16,0},{17,1},{18,2},{19,3},{20,4},{21,5},{22,6},{23,7},{24,8},{25... | collective-permute-start | bytes 331784 | tf_op jit(solution)/shard_map/ppermute | solution.py:713
  310.0 140.5 %collective-permute-start.50 = (bf16[2,384,576]{1,2,0:T(8,128)(2,1)}, bf16[2,384,576]{1,2,0:T(8,128)(2,1)}, u32[]{:S(2)}, u32[]{:S(2)}) collective-permute-start(bf16[2,384,576]{1,2,0:T(8,128)(2,1)} %copy.117), channel_id=1, source_target_pairs={{16,17},{17,16},{18,19},{19,18},{20,21},{21,20},{22,23},{23,22},{2... | collective-permute-start | bytes 2654216 | tf_op jit(solution)/shard_map/ppermute | solution.py:730
  317.1 11.3 %collective-permute-start.56 = (f32[61,128]{1,0:T(8,128)S(1)}, f32[61,128]{1,0:T(8,128)S(1)}, u32[]{:S(2)}, u32[]{:S(2)}) collective-permute-start(f32[61,128]{1,0:T(8,128)S(1)} %add.138), channel_id=1, source_target_pairs={{0,4},{4,0},{8,12},{12,8},{1,5},{5,1},{9,13},{13,9},{2,6},{6,2},{1... | collective-permute-start | bytes 93704 | tf_op jit(solution)/shard_map/ppermute | solution.py:689
  321.0 20.9 %collective-permute-start.39 = (bf16[2,1,96,576]{3,2,0,1:T(8,128)(2,1)S(1)}, bf16[2,1,96,576]{3,2,0,1:T(8,128)(2,1)S(1)}, u32[]{:S(2)}, u32[]{:S(2)}) collective-permute-start(bf16[2,1,96,576]{3,2,0,1:T(8,128)(2,1)S(1)} %maximum_bitcast_fusion.4), channel_id=1, source_target_pairs={{0,8},{4,12},{8,0},{12,4},{1,9},{5,13},{9,1},{13,5},{2,10},{6,14},... | collective-permute-start | bytes 663560 | tf_op jit(solution)/shard_map/ppermute | solution.py:718
  324.5 21.9 %collective-permute-start.78 = (bf16[1,48,3456]{2,1,0:T(8,128)(2,1)S(1)}, bf16[1,48,3456]{2,1,0:T(8,128)(2,1)S(1)}, u32[]{:S(2)}, u32[]{:S(2)}) collective-permute-start(bf16[1,48,3456]{2,1,0:T(8,128)(2,1)S(1)} %select_bitcast_fusion.2), channel_id=1, source_target_pairs={{0,8},{4,12},{8,0},{12,4},{1,9},{5,13},{9,1},{13,5},{2,10},{6,14},... | collective-permute-start | bytes 995336 | tf_op jit(solution)/shard_map/ppermute | solution.py:689
  328.3 23.7 %collective-permute-start.61 = (bf16[192,3456]{1,0:T(8,128)(2,1)S(1)}, bf16[192,3456]{1,0:T(8,128)(2,1)S(1)}, u32[]{:S(2)}, u32[]{:S(2)}) collective-permute-start(bf16[192,3456]{1,0:T(8,128)(2,1)S(1)} %copy-done.68), channel_id=1, source_target_pairs={{0,1},{1,0},{2,3},{3,2},{16,18},{17,19},{18,16},{19,17},{4,5},{5,4... | collective-permute-start | bytes 3981320 | tf_op jit(solution)/shard_map/ppermute | solution.py:671
  341.9 25.8 %collective-permute-start.60 = (bf16[192,3456]{1,0:T(8,128)(2,1)}, bf16[192,3456]{1,0:T(8,128)(2,1)}, u32[]{:S(2)}, u32[]{:S(2)}) collective-permute-start(bf16[192,3456]{1,0:T(8,128)(2,1)} %get-tuple-element.202), channel_id=1, source_target_pairs={{0,1},{1,0},{2,3},{3,2},{16,18},{17,19},{18,16},{19,17},{4,5},{5,4... | collective-permute-start | bytes 3981320 | tf_op jit(solution)/shard_map/ppermute | solution.py:671
  349.2 13.8 %collective-permute-start.40 = (bf16[2,2,96,576]{3,2,1,0:T(8,128)(2,1)S(1)}, bf16[2,2,96,576]{3,2,1,0:T(8,128)(2,1)S(1)}, u32[]{:S(2)}, u32[]{:S(2)}) collective-permute-start(bf16[2,2,96,576]{3,2,1,0:T(8,128)(2,1)S(1)} %copy.101), channel_id=1, source_target_pairs={{0,4},{4,0},{8,12},{12,8},{1,5},{5,1},{9,13},{13,9},{2,6},{6,2},{1... | collective-permute-start | bytes 1327112 | tf_op jit(solution)/shard_map/ppermute | solution.py:718
  352.0 13.9 %collective-permute-start.80 = (bf16[2,1,48,3456]{3,2,0,1:T(8,128)(2,1)}, bf16[2,1,48,3456]{3,2,0,1:T(8,128)(2,1)}, u32[]{:S(2)}, u32[]{:S(2)}) collective-permute-start(bf16[2,1,48,3456]{3,2,0,1:T(8,128)(2,1)} %maximum_bitcast_fusion.1), channel_id=1, source_target_pairs={{16,24},{20,28},{24,16},{28,20},{17,25},{21,29},{25,17},{29,21},{1... | collective-permute-start | bytes 1990664 | tf_op jit(solution)/shard_map/ppermute | solution.py:718
  363.0 24.0 %collective-permute-start.62 = (bf16[192,3456]{1,0:T(8,128)(2,1)}, bf16[192,3456]{1,0:T(8,128)(2,1)}, u32[]{:S(2)}, u32[]{:S(2)}) collective-permute-start(bf16[192,3456]{1,0:T(8,128)(2,1)} %add_convert_fusion.4), channel_id=1, source_target_pairs={{0,2},{1,3},{2,0},{3,1},{16,17},{17,16},{18,19},{19,18},{4,6},{5,7... | collective-permute-start | bytes 3981320 | tf_op jit(solution)/shard_map/ppermute | solution.py:676
  365.9 87.6 %collective-permute-start.51 = (bf16[2,384,576]{1,2,0:T(8,128)(2,1)}, bf16[2,384,576]{1,2,0:T(8,128)(2,1)S(1)}, u32[]{:S(2)}, u32[]{:S(2)}) collective-permute-start(bf16[2,384,576]{1,2,0:T(8,128)(2,1)} %copy.117), channel_id=1, source_target_pairs={{16,18},{17,19},{18,16},{19,17},{20,22},{21,23},{22,20},{23,21},{2... | collective-permute-start | bytes 2654216 | tf_op jit(solution)/shard_map/ppermute | solution.py:730
  389.4 19.5 %collective-permute-start.63 = (bf16[2,48,3456]{2,1,0:T(8,128)(2,1)S(1)}, bf16[2,48,3456]{2,1,0:T(8,128)(2,1)S(1)}, u32[]{:S(2)}, u32[]{:S(2)}) collective-permute-start(bf16[2,48,3456]{2,1,0:T(8,128)(2,1)S(1)} %select_bitcast_fusion.1), channel_id=1, source_target_pairs={{0,4},{4,0},{8,12},{12,8},{1,5},{5,1},{9,13},{13,9},{2,6},{6,2},{1... | collective-permute-start | bytes 1990664 | tf_op jit(solution)/shard_map/ppermute | solution.py:689
  391.8 32.6 %collective-permute-start.81 = (bf16[2,2,48,3456]{3,2,1,0:T(8,128)(2,1)S(1)}, bf16[2,2,48,3456]{3,2,1,0:T(8,128)(2,1)S(1)}, u32[]{:S(2)}, u32[]{:S(2)}) collective-permute-start(bf16[2,2,48,3456]{3,2,1,0:T(8,128)(2,1)S(1)} %copy.129), channel_id=1, source_target_pairs={{16,20},{20,16},{24,28},{28,24},{17,21},{21,17},{25,29},{29,25},{1... | collective-permute-start | bytes 3981320 | tf_op jit(solution)/shard_map/ppermute | solution.py:718
  409.3 11.2 %collective-permute-start.64 = (bf16[1,48,3456]{2,1,0:T(8,128)(2,1)S(1)}, bf16[1,48,3456]{2,1,0:T(8,128)(2,1)S(1)}, u32[]{:S(2)}, u32[]{:S(2)}) collective-permute-start(bf16[1,48,3456]{2,1,0:T(8,128)(2,1)S(1)} %select_bitcast_fusion.3), channel_id=1, source_target_pairs={{0,8},{4,12},{8,0},{12,4},{1,9},{5,13},{9,1},{13,5},{2,10},{6,14},... | collective-permute-start | bytes 995336 | tf_op jit(solution)/shard_map/ppermute | solution.py:689
  424.2 43.1 %collective-permute-start.34 = (bf16[256,767]{1,0:T(8,128)(2,1)S(1)}, bf16[256,767]{1,0:T(8,128)(2,1)S(1)}, u32[]{:S(2)}, u32[]{:S(2)}) collective-permute-start(bf16[256,767]{1,0:T(8,128)(2,1)S(1)} %copy-done.117), channel_id=1, source_target_pairs={{0,16},{16,0},{1,17},{17,1},{2,18},{18,2},{3,19},{19,3},{4,20},{20... | collective-permute-start | bytes 1178120 | tf_op jit(solution)/shard_map/ppermute | solution.py:684
  424.4 19.7 %collective-permute-start.66 = (bf16[2,1,48,3456]{3,2,0,1:T(8,128)(2,1)S(1)}, bf16[2,1,48,3456]{3,2,0,1:T(8,128)(2,1)S(1)}, u32[]{:S(2)}, u32[]{:S(2)}) collective-permute-start(bf16[2,1,48,3456]{3,2,0,1:T(8,128)(2,1)S(1)} %maximum_bitcast_fusion), channel_id=1, source_target_pairs={{0,8},{4,12},{8,0},{12,4},{1,9},{5,13},{9,1},{13,5},{2,10},{6,14},... | collective-permute-start | bytes 1990664 | tf_op jit(solution)/shard_map/ppermute | solution.py:718
  444.7 20.0 %collective-permute-start.67 = (bf16[2,2,48,3456]{3,2,1,0:T(8,128)(2,1)S(1)}, bf16[2,2,48,3456]{3,2,1,0:T(8,128)(2,1)S(1)}, u32[]{:S(2)}, u32[]{:S(2)}) collective-permute-start(bf16[2,2,48,3456]{3,2,1,0:T(8,128)(2,1)S(1)} %copy.124), channel_id=1, source_target_pairs={{0,4},{4,0},{8,12},{12,8},{1,5},{5,1},{9,13},{13,9},{2,6},{6,2},{1... | collective-permute-start | bytes 3981320 | tf_op jit(solution)/shard_map/ppermute | solution.py:718
  447.5 19.1 %collective-permute-start.57 = (f32[61,128]{1,0:T(8,128)S(1)}, f32[61,128]{1,0:T(8,128)S(1)}, u32[]{:S(2)}, u32[]{:S(2)}) collective-permute-start(f32[61,128]{1,0:T(8,128)S(1)} %add.139), channel_id=1, source_target_pairs={{0,8},{4,12},{8,0},{12,4},{1,9},{5,13},{9,1},{13,5},{2,10},{6,14},... | collective-permute-start | bytes 93704 | tf_op jit(solution)/shard_map/ppermute | solution.py:689
  450.6 19.8 %collective-permute-start.42 = (bf16[2,384,576]{1,2,0:T(8,128)(2,1)S(1)}, bf16[2,384,576]{1,2,0:T(8,128)(2,1)S(1)}, u32[]{:S(2)}, u32[]{:S(2)}) collective-permute-start(bf16[2,384,576]{1,2,0:T(8,128)(2,1)S(1)} %copy-done.111), channel_id=1, source_target_pairs={{0,2},{1,3},{2,0},{3,1},{4,6},{5,7},{6,4},{7,5},{8,10},{9,11},{10,... | collective-permute-start | bytes 2654216 | tf_op jit(solution)/shard_map/ppermute | solution.py:730
  453.4 55.1 %collective-permute-start.84 = (bf16[192,3456]{1,0:T(8,128)(2,1)S(1)}, bf16[192,3456]{1,0:T(8,128)(2,1)}, u32[]{:S(2)}, u32[]{:S(2)}) collective-permute-start(bf16[192,3456]{1,0:T(8,128)(2,1)S(1)} %bitcast.236), channel_id=1, source_target_pairs={{16,17},{17,16},{18,19},{19,18},{20,21},{21,20},{22,23},{23,22},{2... | collective-permute-start | bytes 3981320 | tf_op jit(solution)/shard_map/ppermute | solution.py:730
  464.7 46.8 %collective-permute-start.82 = (bf16[192,3456]{1,0:T(8,128)(2,1)S(1)}, bf16[192,3456]{1,0:T(8,128)(2,1)}, u32[]{:S(2)}, u32[]{:S(2)}) collective-permute-start(bf16[192,3456]{1,0:T(8,128)(2,1)S(1)} %bitcast.233), channel_id=1, source_target_pairs={{16,18},{17,19},{18,16},{19,17},{20,22},{21,23},{22,20},{23,21},{2... | collective-permute-start | bytes 3981320 | tf_op jit(solution)/shard_map/ppermute | solution.py:730
  467.3 24.1 %collective-permute-start.41 = (bf16[2,384,576]{1,2,0:T(8,128)(2,1)S(1)}, bf16[2,384,576]{1,2,0:T(8,128)(2,1)S(1)}, u32[]{:S(2)}, u32[]{:S(2)}) collective-permute-start(bf16[2,384,576]{1,2,0:T(8,128)(2,1)S(1)} %copy-done.111), channel_id=1, source_target_pairs={{0,1},{1,0},{2,3},{3,2},{4,5},{5,4},{6,7},{7,6},{8,9},{9,8},{10,11... | collective-permute-start | bytes 2654216 | tf_op jit(solution)/shard_map/ppermute | solution.py:730
  470.4 35.5 %collective-permute-start.43 = (bf16[2,384,576]{1,2,0:T(8,128)(2,1)S(1)}, bf16[2,384,576]{1,2,0:T(8,128)(2,1)S(1)}, u32[]{:S(2)}, u32[]{:S(2)}) collective-permute-start(bf16[2,384,576]{1,2,0:T(8,128)(2,1)S(1)} %collective-permute-done.42), channel_id=1, source_target_pairs={{0,1},{1,0},{2,3},{3,2},{4,5},{5,4},{6,7},{7,6},{8,9},{9,8},{10,11... | collective-permute-start | bytes 2654216 | tf_op jit(solution)/shard_map/ppermute | solution.py:730
  475.6 38.8 %collective-permute-start.89 = (bf16[192,3456]{1,0:T(8,128)(2,1)S(1)}, bf16[192,3456]{1,0:T(8,128)(2,1)S(1)}, u32[]{:S(2)}, u32[]{:S(2)}) collective-permute-start(bf16[192,3456]{1,0:T(8,128)(2,1)S(1)} %bitcast.237), channel_id=1, source_target_pairs={{16,18},{17,19},{18,16},{19,17},{20,22},{21,23},{22,20},{23,21},{2... | collective-permute-start | bytes 3981320 | tf_op jit(solution)/shard_map/ppermute | solution.py:730
  491.4 27.4 %collective-permute-start.88 = (bf16[192,3456]{1,0:T(8,128)(2,1)S(1)}, bf16[192,3456]{1,0:T(8,128)(2,1)S(1)}, u32[]{:S(2)}, u32[]{:S(2)}) collective-permute-start(bf16[192,3456]{1,0:T(8,128)(2,1)S(1)} %bitcast.234), channel_id=1, source_target_pairs={{16,17},{17,16},{18,19},{19,18},{20,21},{21,20},{22,23},{23,22},{2... | collective-permute-start | bytes 3981320 | tf_op jit(solution)/shard_map/ppermute | solution.py:730
  505.9 32.5 %collective-permute-start.70 = (bf16[192,3456]{1,0:T(8,128)(2,1)S(1)}, bf16[192,3456]{1,0:T(8,128)(2,1)}, u32[]{:S(2)}, u32[]{:S(2)}) collective-permute-start(bf16[192,3456]{1,0:T(8,128)(2,1)S(1)} %bitcast.239), channel_id=1, source_target_pairs={{0,1},{1,0},{2,3},{3,2},{4,5},{5,4},{6,7},{7,6},{8,9},{9,8},{10,11... | collective-permute-start | bytes 3981320 | tf_op jit(solution)/shard_map/ppermute | solution.py:730
  508.6 31.6 %collective-permute-start.68 = (bf16[192,3456]{1,0:T(8,128)(2,1)}, bf16[192,3456]{1,0:T(8,128)(2,1)}, u32[]{:S(2)}, u32[]{:S(2)}) collective-permute-start(bf16[192,3456]{1,0:T(8,128)(2,1)} %bitcast.82.refs_0_), channel_id=1, source_target_pairs={{0,2},{1,3},{2,0},{3,1},{4,6},{5,7},{6,4},{7,5},{8,10},{9,11},{10,... | collective-permute-start | bytes 3981320 | tf_op jit(solution)/shard_map/ppermute | solution.py:730
  511.6 38.5 %collective-permute-start.87 = (bf16[192,3456]{1,0:T(8,128)(2,1)S(1)}, bf16[192,3456]{1,0:T(8,128)(2,1)S(1)}, u32[]{:S(2)}, u32[]{:S(2)}) collective-permute-start(bf16[192,3456]{1,0:T(8,128)(2,1)S(1)} %bitcast.240), channel_id=1, source_target_pairs={{0,2},{1,3},{2,0},{3,1},{4,6},{5,7},{6,4},{7,5},{8,10},{9,11},{10,... | collective-permute-start | bytes 3981320 | tf_op jit(solution)/shard_map/ppermute | solution.py:730
  515.6 84.0 %collective-permute-start.86 = (bf16[192,3456]{1,0:T(8,128)(2,1)}, bf16[192,3456]{1,0:T(8,128)(2,1)}, u32[]{:S(2)}, u32[]{:S(2)}) collective-permute-start(bf16[192,3456]{1,0:T(8,128)(2,1)} %bitcast.82.refs_0_), channel_id=1, source_target_pairs={{0,1},{1,0},{2,3},{3,2},{4,5},{5,4},{6,7},{7,6},{8,9},{9,8},{10,11... | collective-permute-start | bytes 3981320 | tf_op jit(solution)/shard_map/ppermute | solution.py:730
  519.9 84.5 %collective-permute-start.85 = (bf16[192,3456]{1,0:T(8,128)(2,1)}, bf16[192,3456]{1,0:T(8,128)(2,1)}, u32[]{:S(2)}, u32[]{:S(2)}) collective-permute-start(bf16[192,3456]{1,0:T(8,128)(2,1)} %collective-permute-done.84.refs_3_), channel_id=1, source_target_pairs={{16,18},{17,19},{18,16},{19,17},{20,22},{21,23},{22,20},{23,21},{2... | collective-permute-start | bytes 3981320 | tf_op jit(solution)/shard_map/ppermute | solution.py:730
  538.4 65.9 %collective-permute-start.83 = (bf16[192,3456]{1,0:T(8,128)(2,1)}, bf16[192,3456]{1,0:T(8,128)(2,1)}, u32[]{:S(2)}, u32[]{:S(2)}) collective-permute-start(bf16[192,3456]{1,0:T(8,128)(2,1)} %collective-permute-done.82.refs_2_), channel_id=1, source_target_pairs={{16,17},{17,16},{18,19},{19,18},{20,21},{21,20},{22,23},{23,22},{2... | collective-permute-start | bytes 3981320 | tf_op jit(solution)/shard_map/ppermute | solution.py:730
  540.2 64.2 %collective-permute-start.71 = (bf16[192,3456]{1,0:T(8,128)(2,1)}, bf16[192,3456]{1,0:T(8,128)(2,1)}, u32[]{:S(2)}, u32[]{:S(2)}) collective-permute-start(bf16[192,3456]{1,0:T(8,128)(2,1)} %collective-permute-done.70.refs_1_), channel_id=1, source_target_pairs={{0,2},{1,3},{2,0},{3,1},{4,6},{5,7},{6,4},{7,5},{8,10},{9,11},{10,... | collective-permute-start | bytes 3981320 | tf_op jit(solution)/shard_map/ppermute | solution.py:730
  551.2 53.2 %collective-permute-start.69 = (bf16[192,3456]{1,0:T(8,128)(2,1)}, bf16[192,3456]{1,0:T(8,128)(2,1)}, u32[]{:S(2)}, u32[]{:S(2)}) collective-permute-start(bf16[192,3456]{1,0:T(8,128)(2,1)} %collective-permute-done.68.refs_0_), channel_id=1, source_target_pairs={{0,1},{1,0},{2,3},{3,2},{4,5},{5,4},{6,7},{7,6},{8,9},{9,8},{10,11... | collective-permute-start | bytes 3981320 | tf_op jit(solution)/shard_map/ppermute | solution.py:730
  (160 other events, 1562.2 us)

commit v3 on v2

--- a/solution.py
+++ b/solution.py
@@ -391,7 +391,7 @@
 
 
 def product_kernel(send, places, ids, lr, rr, att, *rest):
-    outs = rest[-len(places) :]
+    outs = [rest[0].at[i] for i in range(len(places))] if send else rest[1:]
     core = 1 - ids[0] if send else ids[0]
     ff = lr.shape[-1]
     part = att.shape[-1]
@@ -402,7 +402,7 @@
         low = rr[2, t]
         sides = [tn(low, att[2 * core + h]) for h in range(2)]
         if not send:
-            got = rest[i]
+            got = rest[0].at[i]
             main = main + got[:, :ff].astype(F32)
             sides = [v + got[:, ff + h * part : ff + (h + 1) * part].astype(F32) for h, v in enumerate(sides)]
         out[:, :ff] = main.astype(BF16)
@@ -410,14 +410,16 @@
             out[:, ff + h * part : ff + (h + 1) * part] = v.astype(BF16)
 
 
-def product(send, places, ids, lr, rr, att, got=()):
+def product(send, places, ids, lr, rr, att, *got):
     span, quarter = rr.shape[2:]
     cols = lr.shape[-1] + 2 * att.shape[-1]
     return pl.pallas_call(
         functools.partial(product_kernel, send, places),
         in_specs=[SMEM] + [VMEM] * (3 + len(got)),
-        out_specs=[VMEM] * len(places),
-        out_shape=[jax.ShapeDtypeStruct((quarter, cols), BF16)] * len(places),
+        out_specs=VMEM if send else [VMEM] * len(places),
+        out_shape=jax.ShapeDtypeStruct((len(places), quarter, cols), BF16)
+        if send
+        else [jax.ShapeDtypeStruct((quarter, cols), BF16)] * len(places),
         compiler_params=params(32),
         cost_estimate=cost(2 * span * quarter * cols * len(places), 2 * 4 * quarter * cols * len(places)),
     )(ids, lr, rr, att, *got)
@@ -425,7 +427,7 @@
 
 def attn_bwd_kernel(
     ids, n0, n1, n2, n3, w_ref, qh, kh, vh, lse, d0, d1, d2, d3,
-    p0, p1, p2, p3, gs, gk, gb, do, dk, dv, dy, acc, bias_scr,
+    p0, p1, far, gs, gk, gb, do, dk, dv, dy, acc, bias_scr,
 ):
     c, s = ids[0], ids[1]
     heads, _, hd = qh.shape
@@ -459,7 +461,8 @@
         dy[:, width + h * hd : width + (h + 1) * hd] = dk[h].astype(BF16)
         dy[:, 2 * width + h * hd : 2 * width + (h + 1) * hd] = dv[h].astype(BF16)
     total = jnp.zeros((1, 3 * width), F32)
-    for p, (nb, out) in enumerate(((n0, p0), (n1, p1), (n2, p2), (n3, p3))):
+    outs = (p0, p1, far.at[span:], far.at[:span])
+    for p, (nb, out) in enumerate(zip((n0, n1, n2, n3), outs)):
         row = pl.multiple_of(jnp.bitwise_xor(order(c, p), s) * span, span)
         y = dy[pl.ds(row, span), :]
         out[...] = nt(y, w_ref[...]).astype(BF16)
@@ -485,8 +488,8 @@
     return pl.pallas_call(
         attn_bwd_kernel,
         in_specs=[SMEM] + [VMEM] * 13,
-        out_specs=[VMEM] * 7,
-        out_shape=[pp, pp, pp, pp, gg, gg, jax.ShapeDtypeStruct((8, 3 * width), F32)],
+        out_specs=[VMEM] * 6,
+        out_shape=[pp, pp, jax.ShapeDtypeStruct((2 * span, cc), BF16), gg, gg, jax.ShapeDtypeStruct((8, 3 * width), F32)],
         scratch_shapes=[
             pltpu.VMEM((QUAD, width, span), BF16),
             pltpu.VMEM((heads, full, hd), F32),
@@ -506,7 +509,7 @@
 
 def input_kernel(part, r0, r1, dmid, x, pv, dx, gg):
     cc = x.shape[-1]
-    dn = part[...].astype(F32) + r0[...].astype(F32) + r1[...].astype(F32)
+    dn = part[...].astype(F32) + r0[part.shape[0] :, :].astype(F32) + r1[...].astype(F32)
     dv, g, _ = crms_back(x[...].astype(F32), pv[3:4, :cc], dn)
     dx[...] = (dmid[...] + dv).astype(BF16)
     gg[...] = jnp.broadcast_to(jnp.sum(g, axis=0, keepdims=True), gg.shape)
@@ -536,21 +539,25 @@
         start(rows - 1)
 
 
-def place_kernel(place, first, ids, *refs):
+def place_kernel(pair, first, ids, *refs):
     srcs = refs[:4]
     outs = refs[4:7] if first else refs[7:10]
     x0, x1, od, ou, ow, sem = refs[7:] if first else refs[10:]
     c, s = ids[0], ids[1]
     down, up, wout = outs
-    rows, _, ff = od.shape
+    _, rows, _, ff = od.shape
     part = ow.shape[-1]
 
+    def reads(i, a, b):
+        return [
+            pltpu.make_async_copy(a.at[i], x0.at[i], sem.at[0, i]),
+            pltpu.make_async_copy(b.at[i], x1.at[i], sem.at[1, i]),
+        ]
+
     def load(a, b):
-        moves = [pltpu.make_async_copy(a, x0, sem.at[0]), pltpu.make_async_copy(b, x1, sem.at[1])]
-        for m in moves:
-            m.start()
-        for m in moves:
-            m.wait()
+        for i in range(2):
+            for m in reads(i, a, b):
+                m.start()
 
     @pl.when(c == 0)
     def _():
@@ -560,86 +567,101 @@
     def _():
         load(srcs[2], srcs[3])
 
-    t0 = jnp.bitwise_xor(((place & 1) << 1) | (place >> 1), s)
-    t1 = jnp.bitwise_xor(place, s)
-
-    def moves(n, t, i, src, dst, lo, cols):
+    def writes(n, i, side, t):
+        o, dst = ((od, down), (ou, up))[side]
         return [
-            pltpu.make_async_copy(src.at[pl.ds(0, n)], dst.at[pl.ds(t * rows, n)], sem.at[2 * i]),
             pltpu.make_async_copy(
-                ow.at[i, pl.ds(0, n)], wout.at[pl.ds(t * rows, n), :, pl.ds(lo, cols)], sem.at[2 * i + 1]
+                o.at[i, pl.ds(0, n)], dst.at[pl.ds(t * rows, n)], sem.at[2 + side, i]
+            ),
+            pltpu.make_async_copy(
+                ow.at[side, i, pl.ds(0, n)],
+                wout.at[pl.ds(t * rows, n), :, pl.ds(side * part, part)],
+                sem.at[4 + side, i],
             ),
         ]
 
-    jobs = ((t0, 0, x0, od, down, 0), (t1, 1, x1, ou, up, part))
-    for t, i, x, o, dst, lo in jobs:
-        o[:, 0, :] = x[:, :ff].astype(F32)
-        ow[i, :, 0, :] = x[:, ff:].astype(F32)
-        both_lengths(t, rows, lambda n: [m.start() for m in moves(n, t, i, o, dst, lo, part)])
-    for t, i, x, o, dst, lo in jobs:
-        both_lengths(t, rows, lambda n: [m.wait() for m in moves(n, t, i, o, dst, lo, part)])
-
-
-def place_rows(place, ids, srcs, outs, cc, ff, model):
-    rows, cols = srcs[0].shape
+    jobs = []
+    for i in range(2):
+        place = 2 * pair + i
+        for m in reads(i, srcs[0], srcs[1]):
+            m.wait()
+        swapped = ((place & 1) << 1) | (place >> 1)
+        for side, (x, o, k) in enumerate(((x0, od, swapped), (x1, ou, place))):
+            t = jnp.bitwise_xor(k, s)
+            o[i, :, 0, :] = x[i, :, :ff].astype(F32)
+            ow[side, i, :, 0, :] = x[i, :, ff:].astype(F32)
+            both_lengths(t, rows, lambda n: [m.start() for m in writes(n, i, side, t)])
+            jobs.append((i, side, t))
+    for i, side, t in jobs:
+        both_lengths(t, rows, lambda n: [m.wait() for m in writes(n, i, side, t)])
+
+
+def place_rows(pair, ids, srcs, outs, cc, ff, model):
+    _, rows, cols = srcs[0].shape
     first = outs is None
     operands = [ids, *srcs] + ([] if first else list(outs))
     return pl.pallas_call(
-        functools.partial(place_kernel, place, first),
+        functools.partial(place_kernel, pair, first),
         in_specs=[SMEM] + [HBM] * (len(operands) - 1),
         out_specs=[HBM] * 3,
         out_shape=[jax.ShapeDtypeStruct((cc, 1, n), F32) for n in (ff, ff, model)],
         input_output_aliases={} if first else {5: 0, 6: 1, 7: 2},
         scratch_shapes=[
-            pltpu.VMEM((rows, cols), BF16),
-            pltpu.VMEM((rows, cols), BF16),
-            pltpu.VMEM((rows, 1, ff), F32),
-            pltpu.VMEM((rows, 1, ff), F32),
-            pltpu.VMEM((2, rows, 1, cols - ff), F32),
-            pltpu.SemaphoreType.DMA((4,)),
+            pltpu.VMEM((2, rows, cols), BF16),
+            pltpu.VMEM((2, rows, cols), BF16),
+            pltpu.VMEM((2, rows, 1, ff), F32),
+            pltpu.VMEM((2, rows, 1, ff), F32),
+            pltpu.VMEM((2, 2, rows, 1, cols - ff), F32),
+            pltpu.SemaphoreType.DMA((6, 2)),
         ],
-        compiler_params=params(32),
-        cost_estimate=cost(0, 12 * rows * cols),
+        compiler_params=params(40),
+        cost_estimate=cost(0, 24 * rows * cols),
     )(*operands)
 
 
 def qkv_out_kernel(ids, *refs):
-    srcs, out, rows, wide, od, sem = refs[:8], *refs[8:]
+    srcs, out, rows, wide, od, sem = refs[:4], *refs[4:]
     c, s = ids[0], ids[1]
-    width = rows.shape[-1] // 3
-
-    def load(four):
-        todo = [
-            pltpu.make_async_copy(src, rows.at[jnp.bitwise_xor(s, k)], sem.at[k])
-            for k, src in enumerate(four)
+    _, _, half, cols = rows.shape
+    width = cols // 3
+
+    def reads(a, b):
+        return [
+            pltpu.make_async_copy(
+                src.at[p, pl.ds(0, half), :],
+                rows.at[i, jnp.bitwise_xor(p if i else ((p & 1) << 1) | (p >> 1), s)],
+                sem.at[0, i * QUAD + p],
+            )
+            for i, src in enumerate((a, b))
+            for p in range(QUAD)
         ]
-        for m in todo:
+
+    @pl.when(c == 0)
+    def _():
+        for m in reads(srcs[0], srcs[1]):
             m.start()
-        for m in todo:
-            m.wait()
-
-    @pl.when(c == 0)
-    def _():
-        load(srcs[:4])
 
     @pl.when(c != 0)
     def _():
-        load(srcs[4:])
-
-    step = rows.shape[1] // QUAD
+        for m in reads(srcs[2], srcs[3]):
+            m.start()
+
+    for m in reads(srcs[0], srcs[1]):
+        m.wait()
+    step = half // 2
     moves = []
-    for b in range(QUAD):
+    for b in range(4):
         if b >= 2:
             moves[b - 2].wait()
         for t in range(QUAD):
-            v = rows[t, b * step : (b + 1) * step, :].astype(F32)
+            v = rows[b // 2, t, (b % 2) * step : (b % 2 + 1) * step, :].astype(F32)
             for i in range(3):
                 lo = (i * QUAD + t) * width
                 wide[:, lo : lo + width] = v[:, i * width : (i + 1) * width]
         od[b % 2, :, 0, :] = wide[...]
-        n = step - (b == QUAD - 1)
+        n = step - (b == 3)
         m = pltpu.make_async_copy(
-            od.at[b % 2, pl.ds(0, n)], out.at[pl.ds(b * step, n)], sem.at[QUAD + b % 2]
+            od.at[b % 2, pl.ds(0, n)], out.at[pl.ds(b * step, n)], sem.at[1, b % 2]
         )
         m.start()
         moves.append(m)
@@ -648,22 +670,22 @@
 
 
 def qkv_out(ids, srcs, cc):
-    _, half, cols = srcs[0].shape
-    full = 2 * half
+    cols = srcs[0].shape[-1]
+    half = (cc + 1) // 2
     return pl.pallas_call(
         qkv_out_kernel,
-        in_specs=[SMEM] + [HBM] * 8,
+        in_specs=[SMEM] + [HBM] * 4,
         out_specs=HBM,
         out_shape=jax.ShapeDtypeStruct((cc, 1, QUAD * cols), F32),
         scratch_shapes=[
-            pltpu.VMEM((QUAD, full, cols), BF16),
-            pltpu.VMEM((full // QUAD, QUAD * cols), F32),
-            pltpu.VMEM((2, full // QUAD, 1, QUAD * cols), F32),
-            pltpu.SemaphoreType.DMA((QUAD + 2,)),
+            pltpu.VMEM((2, QUAD, half, cols), BF16),
+            pltpu.VMEM((half // 2, QUAD * cols), F32),
+            pltpu.VMEM((2, half // 2, 1, QUAD * cols), F32),
+            pltpu.SemaphoreType.DMA((2, 2 * QUAD)),
         ],
         compiler_params=params(32),
         cost_estimate=cost(0, 6 * cc * QUAD * cols),
-    )(ids, *[v.reshape(full, cols) for v in srcs])
+    )(ids, *srcs)
 
 
 def to_first(v):
@@ -689,47 +711,72 @@
     return lax.ppermute(v, "dp", [(i, i ^ step) for i in range(n)])
 
 
-def dp_scatter(v):
-    n = lax.axis_size("dp")
-    z = lax.axis_index("dp")
-    rows, cols = v.shape
-    piece = rows // n
-    cur = v.reshape(n, piece, cols)
-    step = 1
-    while step < n:
-        cur = cur.reshape(cur.shape[0] // 2, 2, piece, cols)
-        low = (z & step) == 0
-        away = jnp.where(low, cur[:, 1], cur[:, 0])
-        keep = jnp.where(low, cur[:, 0], cur[:, 1])
-        cur = add_low(keep, dp_partner(away, step))
-        step *= 2
-    return cur[0]
-
-
-def owner_gather(l, v):
-    n = lax.axis_size("dp")
-    z = lax.axis_index("dp")
-    piece, cols = v.shape
-    got = lax.ppermute(v, "section", [(1 - l, l)])
-    cur = jnp.stack([v, got] if l == 0 else [got, v])[:, None]
-    step = n // 2
-    while step:
-        low = (z & step) == 0
-        got = lax.ppermute(cur, ("section", "dp"), [(l * n + i, l * n + (i ^ step)) for i in range(n)])
-        pairs = [
-            jnp.where(low, jnp.stack([a, b], 1), jnp.stack([b, a], 1)).reshape(-1, piece, cols)
-            for a, b in ((cur[0], got[0]), (cur[1], got[1]))
-        ]
-        step //= 2
-        if step:
-            cur = jnp.stack(pairs)
-    return [w.reshape(n * piece, cols) for w in pairs]
-
-
-def owner_quad(l, v, k):
-    return lax.ppermute(
-        v, ("section", "seq"), [(l * QUAD + i, l * QUAD + (i ^ k)) for i in range(QUAD)]
-    )
+def to_owner(l, v):
+    return lax.ppermute(v, "section", [(1 - l, l)])
+
+
+def tied(*v):
+    return lax.optimization_barrier(v)
+
+
+class Order:
+    def __init__(self, token):
+        self.token = token
+
+    def wait(self, *v):
+        *v, self.token = lax.optimization_barrier((*v, self.token))
+        return v
+
+    def run(self, step, *operands):
+        out = step(*self.wait(*operands))
+        out, self.token = lax.optimization_barrier((out, self.token))
+        return out
+
+
+class DpSum:
+    def __init__(self, order_of, make, *operands):
+        self.value = None
+        self.steps = self.work(order_of, make, operands)
+
+    def go(self):
+        next(self.steps, None)
+
+    def finish(self):
+        for _ in self.steps:
+            pass
+        return self.value
+
+    def work(self, order_of, make, operands):
+        n = lax.axis_size("dp")
+        z = lax.axis_index("dp")
+
+        def split(v, step):
+            left = v.shape[0] // n * step if v.ndim == 2 else v.shape[1]
+            v = v.reshape(n // (2 * step), 2, left, v.shape[-1])
+            low = (z & step) == 0
+            return jnp.where(low, v[:, 1], v[:, 0]), jnp.where(low, v[:, 0], v[:, 1])
+
+        def join(v, got, step):
+            low = (z & step) == 0
+            both = jnp.where(low, jnp.stack([v, got], 1), jnp.stack([got, v], 1))
+            return both.reshape(-1, *v.shape[1:])
+
+        away, keep = order_of.run(lambda *v: split(make(*v), 1), *operands)
+        step = 1
+        while step < n:
+            got = dp_partner(away, step)
+            yield
+            step *= 2
+            if step < n:
+                away, keep = order_of.run(lambda a, b, s=step: split(add_low(a, b), s), keep, got)
+            else:
+                v = order_of.run(add_low, keep, got)
+        while step > 1:
+            step //= 2
+            got = dp_partner(v, step)
+            yield
+            v = order_of.run(functools.partial(join, step=step), v, got)
+        self.value = v.reshape(-1, v.shape[-1])
 
 
 def add_low(a, b):
@@ -765,6 +812,7 @@
     e3 = e2 + lens[3]
     ids = jnp.stack([c, s, e0, e1, e2, e3, c, s]).astype(jnp.int32)
     x = rows_in(ids, layer_in)
+    x, w_qkv = tied(x, w_qkv)
 
     def row(v, n=ff):
         return jnp.pad(v, ((0, 0), (0, n - v.shape[-1])))
@@ -805,77 +853,168 @@
         x = xout
     outs = [saved[1][0], x]
 
+    order_of = Order(ids)
+    run = order_of.run
+
+    def first_part(l, df):
+        lr, rr, dmid, g, *douts = run(
+            lambda v: mlp_bwd(l, ids, v, saved[l][5], saved[l][4], wo[l], pv[l], up, dn), df
+        )
+        return lr, rr, dmid, g, [douts[0]] + [to_quad(douts[k], k) for k in (1, 2, 3)]
+
+    def send(l, places, lr, rr):
+        return run(lambda a, b: product(True, places, ids, a, b, saved[l][3]), lr, rr)
+
+    def keep(l, places, lr, rr, got):
+        return run(lambda a, b, v: product(False, places, ids, a, b, saved[l][3], v), lr, rr, got)
+
+    def attention(l, douts):
+        outs = run(lambda *v: attn_bwd(ids, saved[l][1], w3[l], saved[l][2], v), *douts)
+        return (*outs, to_first(outs[2]), to_core(outs[3]))
+
+    def input_part(l, p0, pr, q, dmid):
+        return run(lambda *v: input_grad_of(*v, saved[l][0], pv[l]), p0, pr, q, dmid)
+
+    def projection(l, gk, gs_got, g, gb, gg):
+        pad = jnp.zeros((1,), F32)
+        heads_sum = jnp.concatenate([gb[0, :width], gb[0, 2 * width :]])
+        v = jnp.concatenate(
+            [g[0], g[1, :cc], pad, g[2, :cc], pad, gg[0, :cc], pad, g[4, :cc], pad]
+            + [jnp.broadcast_to(squares[l], (128,)), heads_sum]
+        )
+        v = jnp.pad(v, (0, 32 * 3 * width - v.shape[0])).reshape(32, 3 * width).astype(BF16)
+        return jnp.concatenate([add_low(gk, gs_got), v])
+
+    def wait(*v):
+        out = order_of.wait(*v)
+        return out[0] if len(out) == 1 else out
+
+    def pair_up(a, b):
+        return jnp.stack([a, b])
+
+    def add_first(a, b):
+        return add_low(a, b[:span])
+
     df = rows_in(ids, cotangent)
-    rows_of = [None, None]
-    qkv_of = [None, None]
-    smalls = [None, None]
-    in_grads = [None, None]
-    for l in (1, 0):
-        xl, blocks, qkvl, astk, mid, u = saved[l]
-        lr, rr, dmid, g, *douts = mlp_bwd(l, ids, df, u, mid, wo[l], pv[l], up, dn)
-        douts = [douts[0]] + [to_quad(douts[k], k) for k in (1, 2, 3)]
-        far = [to_core(v) for v in product(True, (3, 2), ids, lr, rr, astk)]
-        near = [to_core(v) for v in product(True, (1, 0), ids, lr, rr, astk)]
-        far = product(False, (3, 2), ids, lr, rr, astk, far)
-        far, douts = lax.optimization_barrier((far, douts))
-        near = product(False, (1, 0), ids, lr, rr, astk, near)
-        half1 = add_low(near[0], to_first(far[0]))
-        half0 = add_low(near[1], to_first(far[1]))
-        quarter = add_low(half0, to_second(half1))
-
-        p0, p1, p2, p3, gs, gk, gb = attn_bwd(ids, blocks, w3[l], qkvl, douts)
-        q1 = add_low(p1, to_first(p3))
-        dx, gg = input_grad_of(p0, to_first(p2), to_second(q1), dmid, xl, pv[l])
-
-        f0, g0 = owner_gather(l, dp_scatter(quarter))
-        f1, g1 = owner_quad(l, f0, 2), owner_quad(l, g0, 1)
-        f2, g2 = owner_quad(l, f0, 1), owner_quad(l, g0, 2)
-        f3, g3 = owner_quad(l, f1, 1), owner_quad(l, g1, 2)
-        rows_of[l] = ((f0, g0), (f1, g1), (f2, g2), (f3, g3))
-
-        tq = add_low(gk, to_core(gs))
-        q0 = jnp.stack(owner_gather(l, dp_scatter(tq)))
-        if l == 1:
-            k1, k2 = owner_quad(l, q0, 1), owner_quad(l, q0, 2)
-            k3 = owner_quad(l, k1, 2)
-        else:
-            k1, k2 = owner_quad(l, q0, 1), owner_quad(l, q0, 2)
-            k3 = owner_quad(l, k2, 1)
-        qkv_of[l] = [q0, k1, k2, k3]
-
-        spot = jnp.arange(QUAD)[:, None] == s
-        qs = jnp.where(spot, gb[0:1, :width], 0.0).reshape(model)
-        vs = jnp.where(spot, gb[0:1, 2 * width :], 0.0).reshape(model)
-        pad = jnp.zeros((1,), F32)
-        smalls[l] = jnp.concatenate(
-            [g[0], g[1, :cc], pad, g[2, :cc], pad, gg[0, :cc], pad, g[4, :cc], pad, qs, vs]
-            + [jnp.broadcast_to(squares[l], (128,))]
-        ).reshape(-1, 128)
-        in_grads[l] = dx
-        df = dx
-
-    small = jnp.where(mine, smalls[0], smalls[1]) + to_core(jnp.where(mine, smalls[1], smalls[0]))
-    for k in (1, 2):
-        small = small + to_quad(small, k)
-    step = 1
-    while step < dp_count:
-        small = small + dp_partner(small, step)
-        step *= 2
-    small = small.reshape(-1)
-
-    grad_qkv = qkv_out(ids, [*qkv_of[0], *qkv_of[1]], cc)
-    outs_w = None
-    for p in range(QUAD):
-        outs_w = place_rows(p, ids, [*rows_of[0][p], *rows_of[1][p]], outs_w, cc, ff, model)
-    grad_down, grad_up, grad_out = outs_w
-
-    def both(pair):
-        own = jnp.where(mine, pair[0], pair[1])
-        got = to_core(jnp.where(mine, pair[1], pair[0]))
-        return rows_out(ids, own, got)
-
-    layer_out = both(outs)
-    input_grad = both(in_grads)
+    out_got = to_core(jnp.where(mine, outs[1], outs[0]))
+    lr1, rr1, dmid1, g1, douts1 = first_part(1, df)
+    out_got = wait(out_got)
+
+    far1 = to_core(send(1, (3, 2), lr1, rr1))
+    near1 = send(1, (1, 0), lr1, rr1)
+    far1, *douts1 = wait(far1, *douts1)
+
+    far1 = keep(1, (3, 2), lr1, rr1, far1)
+    x1a, near1 = to_first(far1[0]), to_core(near1)
+    p0, p1, _, _, gk1, gb1, pr, gs_got = attention(1, douts1)
+    x1a, near1 = wait(x1a, near1)
+
+    near1 = keep(1, (1, 0), lr1, rr1, near1)
+    half1 = run(add_low, near1[0], x1a)
+    pr, gs_got = wait(pr, gs_got)
+
+    q = to_second(run(add_first, p1, pr))
+    q = wait(q)
+
+    x1b, half1 = wait(far1[1], half1)
+    x1b, x2 = to_first(x1b), to_second(half1)
+    dx1, gg1 = input_part(1, p0, pr, q, dmid1)
+    qkv_sum1 = DpSum(order_of, functools.partial(projection, 1), gk1, gs_got, g1, gb1, gg1)
+    lr0, rr0, dmid0, g0, douts0 = first_part(0, dx1)
+    x1b, x2 = wait(x1b, x2)
+
+    far0 = to_core(send(0, (3, 2), lr0, rr0))
+    near0 = send(0, (1, 0), lr0, rr0)
+    far0, *douts0 = wait(far0, *douts0)
+
+    far0 = keep(0, (3, 2), lr0, rr0, far0)
+    x1a, near0 = to_first(far0[0]), to_core(near0)
+    sum1 = DpSum(order_of, lambda a, b, d: add_low(add_low(a, b), d), near1[1], x1b, x2)
+    sum1.go()
+    p0, p1, _, _, gk0, gb0, pr, gs_got = attention(0, douts0)
+    x1a, near0 = wait(x1a, near0)
+    sum1.go()
+
+    near0 = keep(0, (1, 0), lr0, rr0, near0)
+    half1 = run(add_low, near0[0], x1a)
+    qkv_sum1.go()
+    pr, gs_got = wait(pr, gs_got)
+
+    q = to_second(run(add_first, p1, pr))
+    q = wait(q)
+
+    x1b, half1 = wait(far0[1], half1)
+    x1b, x2 = to_first(x1b), to_second(half1)
+    dx0, gg0 = input_part(0, p0, pr, q, dmid0)
+    qkv_sum1.go()
+    sum1.go()
+    qkv_sum0 = DpSum(order_of, functools.partial(projection, 0), gk0, gs_got, g0, gb0, gg0)
+    qkv_sum0.go()
+    qkv_sum1.go()
+    sum1.go()
+    qkv_sum0.go()
+    qkv_sum1.go()
+    x1b, x2 = wait(x1b, x2)
+
+    own1 = sum1.finish()
+    sum0 = DpSum(order_of, lambda a, b, d: add_low(add_low(a, b), d), near0[1], x1b, x2)
+    next1 = to_second(own1)
+    sum0.go()
+    qkv_own1 = qkv_sum1.finish()
+    qkv_next1 = to_second(qkv_own1)
+    in_got = to_core(run(lambda a, b: jnp.where(mine, a, b), dx1, dx0))
+    qkv_sum0.go()
+    next1, qkv_next1, in_got = wait(next1, qkv_next1, in_got)
+
+    pair1 = run(pair_up, own1, next1)
+    rest1 = to_first(pair1)
+    sum0.go()
+    qkv_pair1 = run(pair_up, qkv_own1, qkv_next1)
+    qkv_rest1 = to_first(qkv_pair1)
+    qkv_sum0.go()
+
+    sum0.go()
+    qkv_own0 = qkv_sum0.finish()
+    qkv_next0 = to_second(qkv_own0)
+    rest1, qkv_rest1 = wait(rest1, qkv_rest1)
+    pair1_got = to_owner(1, pair1)
+    qkv1 = run(lambda a, b: jnp.concatenate([a, b]), qkv_pair1, qkv_rest1)
+    qkv_next0, pair1_got = wait(qkv_next0, pair1_got)
+
+    qkv_pair0 = run(pair_up, qkv_own0, qkv_next0)
+    qkv_rest0 = to_first(qkv_pair0)
+    rest1_got = to_owner(1, rest1)
+    sum0.go()
+    rest1_got, qkv_rest0 = wait(rest1_got, qkv_rest0)
+
+    own0 = sum0.finish()
+    next0, qkv1_got = to_second(own0), to_owner(1, qkv1)
+    qkv0 = run(lambda a, b: jnp.concatenate([a, b]), qkv_pair0, qkv_rest0)
+    next0, qkv1_got = wait(next0, qkv1_got)
+
+    pair0 = run(pair_up, own0, next0)
+    rest0, pair0_got = to_first(pair0), to_owner(0, pair0)
+    qkv0_got = to_owner(0, qkv0)
+    layer_out = run(
+        lambda a, b, d: rows_out(ids, jnp.where(mine, a, b), d), outs[0], outs[1], out_got
+    )
+    input_grad = run(lambda a, b, d: rows_out(ids, jnp.where(mine, a, b), d), dx0, dx1, in_got)
+    pair0_got = wait(pair0_got)
+    outs_w = run(
+        lambda *v: place_rows(0, ids, v, None, cc, ff, model), pair0, pair0_got, pair1_got, pair1
+    )
+    qkv0_got = wait(qkv0_got)
+    grad_qkv = run(lambda *v: qkv_out(ids, v, cc), qkv0, qkv0_got, qkv1_got, qkv1)
+    rest0 = wait(rest0)
+    rest0_got = wait(to_owner(0, rest0))
+    grad_down, grad_up, grad_out = place_rows(
+        1, order_of.token, [rest0, rest0_got, rest1_got, rest1], outs_w, cc, ff, model
+    )
+
+    half = (cc + 1) // 2
+    tails = [v[:, half:].astype(F32).reshape(QUAD, -1) for v in (qkv0, qkv0_got, qkv1_got, qkv1)]
+    tails = [jnp.where(mine, tails[0], tails[2]), jnp.where(mine, tails[1], tails[3])]
+    small = jnp.sum(tails[0] + tails[1], 0)
 
     def take(lo, n):
         return small[lo : lo + n][None]
@@ -884,12 +1023,22 @@
     at = ff
     total = micro * dp_count * span * QUAD
     base = ff + 4 * d
-    rms = jnp.sqrt(small[base + 2 * model] / total).reshape(1)
+    rms = jnp.sqrt(small[base] / total).reshape(1)
+    seq_of = jnp.arange(QUAD)
+    heads_of = jnp.zeros((QUAD, 2 * width), F32)
+    for chain in range(2):
+        for p in range(QUAD):
+            here = seq_of == jnp.bitwise_xor(order(chain, p), s)
+            row_of = tails[chain][p, base + 128 : base + 128 + 2 * width]
+            heads_of = heads_of + jnp.where(here[:, None], row_of, 0.0)
+    grad_bqv = jnp.concatenate(
+        [heads_of[:, i * width : (i + 1) * width].reshape(model) for i in range(2)]
+    )
     return (
         layer_out,
         input_grad,
         jnp.transpose(grad_qkv, (1, 0, 2)),
-        take(base, 2 * model),
+        grad_bqv[None],
         jnp.transpose(grad_out, (1, 2, 0)),
         take(at, cc),
         take(at + 2 * d, cc),

time: 613 us -> 517 us (0.84)
  starting transfers between devices: 132 us -> 79.7 us
  local copies, waits for them, and re-layouts: 66.5 us -> 39.3 us
  Pallas kernels: 165 us -> 144 us
  waiting for transfers between devices: 211 us -> 219 us
  other arithmetic: 29.2 us -> 21.8 us
    ppermute x30 -> x6, waiting for transfers between devices: 103 us -> 0.02 us  [to_owner(): return lax.ppermute(v, 'section', [(1 - l, l)])]
    ppermute x12 -> x14, waiting for transfers between devices: 22 us -> 68.7 us  [to_first(): return lax.ppermute(v, ('section', 'seq'), pairs)]
    ppermute x30 -> x6, starting transfers between devices: 54.3 us -> 9.24 us  [to_owner(): return lax.ppermute(v, 'section', [(1 - l, l)])]
    ppermute x10 -> x16, waiting for transfers between devices: 48.9 us -> 82.4 us  [dp_partner(): return lax.ppermute(v, 'dp', [(i, i ^ step) for i in range(n)])]
    ppermute x6 -> x10, waiting for transfers between devices: 30 us -> 53.7 us  [to_second(): return lax.ppermute(v, ('section', 'seq'), pairs)]
    ppermute x18 -> x13, starting transfers between devices: 17.9 us -> 2.27 us  [to_core(): return lax.ppermute(v, 'section', [(0, 1), (1, 0)])]
    pallas_call x2, Pallas kernels: 15.7 us -> 2.9 us  [rows_in(): pl.pallas_call(rows_in_kernel, in_specs=[SMEM, VMEM], out_specs=VMEM, out...]
    ppermute x6 -> x0, local copies, waits for them, and re-layouts: 12.6 us -> none  [owner_quad(): lax.ppermute(v, ('section', 'seq'), [(l * QUAD + i, l * QUAD + (i ^ k)) f...]
  transfers between devices with their start and end apart: 90 -> 71, of which waited for: 28 -> 37; matrix products, arithmetic and copies ran while one was open for 11% -> 7% of each run, Pallas kernels for 16% -> 20%
where the time goes in v3:
time: 517 us; the launch traced here: 511 us
  waiting for transfers between devices  219 us (42%)
  Pallas kernels  144 us (28%)
  starting transfers between devices  79.7 us (15%)
  local copies, waits for them, and re-layouts  39.3 us (8%)
  other arithmetic  21.8 us (4%)
  between operations  7.07 us (1%)
    ppermute x16, waiting for transfers between devices, dp_partner(): return lax.ppermute(v, 'dp', [(i, i ^ step) for i in range(n)])  82.4 us
    ppermute x14, waiting for transfers between devices, to_first(): return lax.ppermute(v, ('section', 'seq'), pairs)  68.7 us
    ppermute x10, waiting for transfers between devices, to_second(): return lax.ppermute(v, ('section', 'seq'), pairs)  53.7 us
    pallas_call x2, Pallas kernels, attn_bwd(): pl.pallas_call(attn_bwd_kernel, in_specs=[SMEM] + [VMEM] * 13, out_specs=...  26.9 us
    pallas_call x2, Pallas kernels, mlp_bwd(): pl.pallas_call(functools.partial(mlp_bwd_kernel, layer), grid_spec=grid,...  25.6 us
    unnamed x222, local copies, waits for them, and re-layouts  22.8 us
    pallas_call x2, Pallas kernels, mlp_fwd(): pl.pallas_call(functools.partial(mlp_fwd_kernel, layer), grid_spec=grid,...  22.8 us
    ppermute x14, starting transfers between devices, to_first(): return lax.ppermute(v, ('section', 'seq'), pairs)  22.2 us
  transfers between devices with their start and end apart: 71, of which 37 were waited for; matrix products, arithmetic and copies ran while one was open for 7% of the time, Pallas kernels for 20%

profile of v3, /device:TPU:0, one launch (start us, length us, event | category | flops | bytes accessed | tf_op | source)
XLA Modules:
  0.0 510.8 jit_solution(4520268267158338067)
XLA Ops:
  7.9 2.1 dynamic-slice_bitcast_fusion.2
  12.3 2.5 collective-permute-start
  17.3 2.4 collective-permute-start.1
  20.6 2.1 collective-permute-start.2
  26.0 3.7 collective-permute-done.2.n3
  29.7 10.7 %shard_map.229 = (bf16[3,1024,64]{2,1,0:T(8,128)(2,1)S(1)}, bf16[3,1024,64]{2,1,0:T(8,128)(2,1)S(1)}, bf16[3,1024,64]{2,1,0:T(8,128)(2,1)S(1)}, f32[3,4,256]{2,1...) custom-call(s32[8]{0:T(128)S(1)} %stack.157.ids, ...), custom_call_target="tpu_custom_call" | custom-call | flops 3320709120 | bytes 3141632 | tf_op jit(solution)/shard_map/pallas_call | solution.py:180
  42.2 2.1 collective-permute-start.5
  47.4 2.6 collective-permute-done.6.a2
  51.1 10.7 %shard_map.230 = (f32[256,767]{1,0:T(8,128)S(1)}, f32[256,3072]{1,0:T(8,128)S(1)}, bf16[256,767]{1,0:T(8,128)(2,1)S(1)}, bf16[256,767]{1,0:T(8,128)(2,1)S(1)}, f...) custom-call(s32[8]{0:T(128)S(1)} %stack.157.ids, bf16[256,767]{1,0:T(8,128)(2,1)S(1)} %shard_map.228.n0.x, ...), custom_call_target="tpu_custom_call" | custom-call | flops 3619160064 | bytes 12570624 | tf_op jit(solution)/shard_map/pallas_call | solution.py:275
  64.9 10.4 %collective-permute-done.11.n1 = bf16[256,767]{1,0:T(8,128)(2,1)S(1)} collective-permute-done((bf16[256,767]{1,0:T(8,128)(2,1)S(1)}, bf16[256,767]{1,0:T(8,128)(2,1)S(1)}, u32[]{:S(2)}, u32[]{:S(2)}) %collective-permute-start.11) | collective-permute-done | bytes 392736 | tf_op jit(solution)/shard_map/ppermute | solution.py:698
  75.4 7.6 %collective-permute-done.13.n3 = bf16[256,767]{1,0:T(8,128)(2,1)S(1)} collective-permute-done((bf16[256,767]{1,0:T(8,128)(2,1)S(1)}, bf16[256,767]{1,0:T(8,128)(2,1)S(1)}, u32[]{:S(2)}, u32[]{:S(2)}) %collective-permute-start.13) | collective-permute-done | bytes 392736 | tf_op jit(solution)/shard_map/ppermute | solution.py:693
  83.0 10.2 %shard_map.231 = (bf16[3,1024,64]{2,1,0:T(8,128)(2,1)S(1)}, bf16[3,1024,64]{2,1,0:T(8,128)(2,1)S(1)}, bf16[3,1024,64]{2,1,0:T(8,128)(2,1)S(1)}, f32[3,4,256]{2,1...) custom-call(s32[8]{0:T(128)S(1)} %stack.157.ids, ...), custom_call_target="tpu_custom_call" | custom-call | flops 3320709120 | bytes 3141632 | tf_op jit(solution)/shard_map/pallas_call | solution.py:180
  95.5 3.1 collective-permute-start.16
  101.1 12.2 %shard_map.232 = (f32[256,767]{1,0:T(8,128)S(1)}, f32[256,3072]{1,0:T(8,128)S(1)}, bf16[256,767]{1,0:T(8,128)(2,1)S(1)}, bf16[256,767]{1,0:T(8,128)(2,1)}, f32[8...) custom-call(s32[8]{0:T(128)S(1)} %stack.157.ids, bf16[256,767]{1,0:T(8,128)(2,1)S(1)} %get-tuple-element.873.x, ...), custom_call_target="tpu_custom_call" | custom-call | flops 3619160064 | bytes 12570624 | tf_op jit(solution)/shard_map/pallas_call | solution.py:275
  116.0 12.5 %shard_map.234 = (bf16[2,256,3072]{2,1,0:T(8,128)(2,1)S(1)}, bf16[3,4,256,192]{3,2,1,0:T(8,128)(2,1)S(1)}, f32[256,767]{1,0:T(8,128)S(1)}, f32[8,3072]{1,0:T(8,1...) custom-call(s32[8]{0:T(128)S(1)} %stack.157.ids, ...), custom_call_target="tpu_custom_call" | custom-call | flops 3619160064 | bytes 15716352 | tf_op jit(solution)/shard_map/pallas_call | solution.py:378
  131.6 3.0 shard_map.236
  136.8 1.8 collective-permute-start.20
  139.9 2.8 collective-permute-done.20.d2
  144.1 2.2 shard_map.237
  153.5 13.3 %shard_map.238 = (bf16[256,767]{1,0:T(8,128)(2,1)S(1)}, bf16[256,767]{1,0:T(8,128)(2,1)S(1)}, bf16[512,767]{1,0:T(8,128)(2,1)}, bf16[384,576]{1,0:T(8,128)(2,1)}...) custom-call(s32[8]{0:T(128)S(1)} %stack.157.ids, bf16[256,767]{1,0:T(8,128)(2,1)S(1)} %get-tuple-element.474.n0, ...), custom_call_target="tpu_custom_call" | custom-call | flops 7849377792 | bytes 6283264 | tf_op jit(solution)/shard_map/pallas_call | solution.py:488
  169.7 2.2 add_convert_fusion.5
  172.0 7.1 %collective-permute-done.22.r0 = bf16[512,767]{1,0:T(8,128)(2,1)S(1)} collective-permute-done((bf16[512,767]{1,0:T(8,128)(2,1)}, bf16[512,767]{1,0:T(8,128)(2,1)S(1)}, u32[]{:S(2)}, u32[]{:S(2)}) %collective-permute-start.22) | collective-permute-done | bytes 785440 | tf_op jit(solution)/shard_map/ppermute | solution.py:693
  179.9 7.2 %collective-permute-done.26.r1 = bf16[256,767]{1,0:T(8,128)(2,1)S(1)} collective-permute-done((bf16[256,767]{1,0:T(8,128)(2,1)S(1)}, bf16[256,767]{1,0:T(8,128)(2,1)S(1)}, u32[]{:S(2)}, u32[]{:S(2)}) %collective-permute-start.26) | collective-permute-done | bytes 392736 | tf_op jit(solution)/shard_map/ppermute | solution.py:698
  190.1 13.2 %shard_map.241 = (bf16[2,256,3072]{2,1,0:T(8,128)(2,1)S(1)}, bf16[3,4,256,192]{3,2,1,0:T(8,128)(2,1)S(1)}, f32[256,767]{1,0:T(8,128)S(1)}, f32[8,3072]{1,0:T(8,1...) custom-call(s32[8]{0:T(128)S(1)} %stack.157.ids, ...), custom_call_target="tpu_custom_call" | custom-call | flops 3619160064 | bytes 15716352 | tf_op jit(solution)/shard_map/pallas_call | solution.py:378
  203.3 13.8 %collective-permute-done.27 = bf16[192,3456]{1,0:T(8,128)(2,1)S(1)} collective-permute-done((bf16[192,3456]{1,0:T(8,128)(2,1)S(1)}, bf16[192,3456]{1,0:T(8,128)(2,1)S(1)}, u32[]{:S(2)}, u32[]{:S(2)}) %collective-permute-start.27) | collective-permute-done | bytes 1327136 | tf_op jit(solution)/shard_map/ppermute | solution.py:693
  217.1 3.0 shard_map.242
  220.3 1.8 collective-permute-start.30
  229.4 3.6 shard_map.244
  235.5 1.9 collective-permute-start.35
  237.4 13.6 %shard_map.245 = (bf16[256,767]{1,0:T(8,128)(2,1)S(1)}, bf16[256,767]{1,0:T(8,128)(2,1)S(1)}, bf16[512,767]{1,0:T(8,128)(2,1)}, bf16[384,576]{1,0:T(8,128)(2,1)}...) custom-call(s32[8]{0:T(128)S(1)} %stack.157.ids, bf16[256,767]{1,0:T(8,128)(2,1)S(1)} %copy-done.82, ...), custom_call_target="tpu_custom_call" | custom-call | flops 7849377792 | bytes 6283264 | tf_op jit(solution)/shard_map/pallas_call | solution.py:488
  256.4 3.3 add_convert_fusion.2
  266.9 2.6 collective-permute-start.43
  269.5 3.0 collective-permute-done.38.r1
  272.5 1.8 shard_map.247
  274.3 5.0 collective-permute-done.41
  279.5 4.6 collective-permute-done.43
  287.4 3.0 collective-permute-start.46
  291.3 7.3 %collective-permute-start.39 = (bf16[192,3456]{1,0:T(8,128)(2,1)S(1)}, bf16[192,3456]{1,0:T(8,128)(2,1)S(1)}, u32[]{:S(2)}, u32[]{:S(2)}) collective-permute-start(bf16[192,3456]{1,0:T(8,128)(2,1)S(1)} %copy-done.60), channel_id=1, source_target_pairs={{0,1},{1,0},{2,3},{3,2},{16,18},{17,19},{18,16},{19,17},{4,5},{5,4... | collective-permute-start | bytes 3981320 | tf_op jit(solution)/shard_map/ppermute | solution.py:693
  299.7 2.0 collective-permute-done.42
  301.7 4.5 collective-permute-done.46
  306.4 1.9 collective-permute-start.44
  308.4 13.6 %collective-permute-done.44 = bf16[1,104,576]{2,1,0:T(8,128)(2,1)S(1)} collective-permute-done((bf16[1,104,576]{2,1,0:T(8,128)(2,1)S(1)}, bf16[1,104,576]{2,1,0:T(8,128)(2,1)S(1)}, u32[]{:S(2)}, u32[]{:S(2)}) %collective-permute-start.44) | collective-permute-done | bytes 119840 | tf_op jit(solution)/shard_map/ppermute | solution.py:711
  322.1 4.2 collective-permute-start.50
  328.5 2.1 collective-permute-start.49
  333.2 9.6 %collective-permute-done.53 = bf16[1,104,576]{2,1,0:T(8,128)(2,1)S(1)} collective-permute-done((bf16[1,104,576]{2,1,0:T(8,128)(2,1)S(1)}, bf16[1,104,576]{2,1,0:T(8,128)(2,1)S(1)}, u32[]{:S(2)}, u32[]{:S(2)}) %collective-permute-start.53) | collective-permute-done | bytes 119840 | tf_op jit(solution)/shard_map/ppermute | solution.py:711
  342.9 9.2 %collective-permute-done.51 = bf16[416,576]{1,0:T(8,128)(2,1)S(1)} collective-permute-done((bf16[416,576]{1,0:T(8,128)(2,1)S(1)}, bf16[416,576]{1,0:T(8,128)(2,1)S(1)}, u32[]{:S(2)}, u32[]{:S(2)}) %collective-permute-start.51) | collective-permute-done | bytes 479264 | tf_op jit(solution)/shard_map/ppermute | solution.py:698
  352.4 6.9 %collective-permute-done.48 = bf16[2,48,3456]{2,1,0:T(8,128)(2,1)S(1)} collective-permute-done((bf16[2,48,3456]{2,1,0:T(8,128)(2,1)S(1)}, bf16[2,48,3456]{2,1,0:T(8,128)(2,1)S(1)}, u32[]{:S(2)}, u32[]{:S(2)}) %collective-permute-start.48) | collective-permute-done | bytes 663584 | tf_op jit(solution)/shard_map/ppermute | solution.py:711
  361.6 2.5 collective-permute-start.55
  365.7 17.4 %collective-permute-done.55 = bf16[1,104,576]{2,1,0:T(8,128)(2,1)S(1)} collective-permute-done((bf16[1,104,576]{2,1,0:T(8,128)(2,1)S(1)}, bf16[1,104,576]{2,1,0:T(8,128)(2,1)S(1)}, u32[]{:S(2)}, u32[]{:S(2)}) %collective-permute-start.55) | collective-permute-done | bytes 119840 | tf_op jit(solution)/shard_map/ppermute | solution.py:711
  384.1 7.4 %collective-permute-done.57 = bf16[2,104,576]{2,1,0:T(8,128)(2,1)S(1)} collective-permute-done((bf16[2,104,576]{2,1,0:T(8,128)(2,1)S(1)}, bf16[2,104,576]{2,1,0:T(8,128)(2,1)S(1)}, u32[]{:S(2)}, u32[]{:S(2)}) %collective-permute-start.57) | collective-permute-done | bytes 239648 | tf_op jit(solution)/shard_map/ppermute | solution.py:711
  391.7 11.0 %collective-permute-done.61 = bf16[2,416,576]{2,1,0:T(8,128)(2,1)S(1)} collective-permute-done((bf16[2,416,576]{2,1,0:T(8,128)(2,1)S(1)}, bf16[2,416,576]{2,1,0:T(8,128)(2,1)S(1)}, u32[]{:S(2)}, u32[]{:S(2)}) %collective-permute-start.61) | collective-permute-done | bytes 958496 | tf_op jit(solution)/shard_map/ppermute | solution.py:693
  406.7 7.0 %collective-permute-done.58 = bf16[416,576]{1,0:T(8,128)(2,1)S(1)} collective-permute-done((bf16[416,576]{1,0:T(8,128)(2,1)S(1)}, bf16[416,576]{1,0:T(8,128)(2,1)S(1)}, u32[]{:S(2)}, u32[]{:S(2)}) %collective-permute-start.58) | collective-permute-done | bytes 479264 | tf_op jit(solution)/shard_map/ppermute | solution.py:698
  413.8 7.3 %collective-permute-done.56 = bf16[1,48,3456]{2,1,0:T(8,128)(2,1)S(1)} collective-permute-done((bf16[1,48,3456]{2,1,0:T(8,128)(2,1)S(1)}, bf16[1,48,3456]{2,1,0:T(8,128)(2,1)S(1)}, u32[]{:S(2)}, u32[]{:S(2)}) %collective-permute-start.56) | collective-permute-done | bytes 331808 | tf_op jit(solution)/shard_map/ppermute | solution.py:711
  421.8 2.0 collective-permute-start.66
  423.8 12.3 %collective-permute-done.64 = bf16[2,416,576]{2,1,0:T(8,128)(2,1)S(1)} collective-permute-done((bf16[2,416,576]{2,1,0:T(8,128)(2,1)S(1)}, bf16[2,416,576]{2,1,0:T(8,128)(2,1)S(1)}, u32[]{:S(2)}, u32[]{:S(2)}) %collective-permute-start.64) | collective-permute-done | bytes 958496 | tf_op jit(solution)/shard_map/ppermute | solution.py:693
  436.2 2.4 collective-permute-done.62
  440.7 16.1 %collective-permute-done.65 = bf16[192,3456]{1,0:T(8,128)(2,1)S(1)} collective-permute-done((bf16[192,3456]{1,0:T(8,128)(2,1)S(1)}, bf16[192,3456]{1,0:T(8,128)(2,1)S(1)}, u32[]{:S(2)}, u32[]{:S(2)}) %collective-permute-start.65) | collective-permute-done | bytes 1327136 | tf_op jit(solution)/shard_map/ppermute | solution.py:698
  461.3 2.3 shard_map.248
  463.6 2.3 shard_map.249
  465.9 5.5 %shard_map.250 = (f32[767,1,3072]{2,1,0:T(1,128)}, f32[767,1,3072]{2,1,0:T(1,128)}, f32[767,1,768]{2,1,0:T(1,128)}) custom-call(s32[8]{0:T(128)S(1)} %stack.157.ids, bf16[2,192,3456]{2,1,0:T(8,128)(2,1)S(1)} %pad_maximum_fusion.1.refs_0_, bf16[2,192,3456]{2,1,0:T(8,128)(2,1)S(1)} %collective-permute-done.68.refs_1_, ...), custom_call_target="tpu_custom_call" | custom-call | bytes 15925248 | tf_op jit(solution)/shard_map/pallas_call | solution.py:603
  471.5 7.8 %shard_map.251 = f32[767,1,2304]{2,1,0:T(1,128)} custom-call(s32[8]{0:T(128)S(1)} %stack.157.ids, bf16[4,416,576]{2,1,0:T(8,128)(2,1)S(1)} %pad_maximum_fusion.3.refs_0_, bf16[4,416,576]{2,1,0:T(8,128)(2,1)S(1)} %collective-permute-done.67.refs_1_, bf16[4,416,576]{2,1,0:T(8,128)(2,1)S(1)} %collective-permute-done.66.refs_2_, ...), custom_call_target="tpu_custom_call" | custom-call | bytes 10603008 | tf_op jit(solution)/shard_map/pallas_call | solution.py:675
  479.3 11.4 %collective-permute-done.69.refs_0_ = bf16[2,192,3456]{2,1,0:T(8,128)(2,1)} collective-permute-done((bf16[2,192,3456]{2,1,0:T(8,128)(2,1)S(1)}, bf16[2,192,3456]{2,1,0:T(8,128)(2,1)}, u32[]{:S(2)}, u32[]{:S(2)}) %collective-permute-start.69) | collective-permute-done | bytes 2654240 | tf_op jit(solution)/shard_map/ppermute | solution.py:693
  499.1 1.7 copy-done.16
  502.6 6.8 %shard_map.252 = (f32[767,1,3072]{2,1,0:T(1,128)}, f32[767,1,3072]{2,1,0:T(1,128)}, f32[767,1,768]{2,1,0:T(1,128)}) custom-call(s32[8]{0:T(128)S(1)} %stack.157.ids, bf16[2,192,3456]{2,1,0:T(8,128)(2,1)} %collective-permute-done.69.refs_0_, ...), custom_call_target="tpu_custom_call", output_to_operand_aliasing={{0}: (5, {}), {1}: (6, {}), {2}: (7, {})} | custom-call | bytes 15925248 | tf_op jit(solution)/shard_map/pallas_call | solution.py:603
  (439 shorter events, 110.5 us)
Async XLA Ops:
  0.7 50.4 %collective-permute-start.9 = (bf16[1,767,3072]{2,1,0:T(8,128)(2,1)}, bf16[1,767,3072]{2,1,0:T(8,128)(2,1)}, u32[]{:S(2)}, u32[]{:S(2)}) collective-permute-start(bf16[1,767,3072]{2,1,0:T(8,128)(2,1)} %upo.7), channel_id=1, source_target_pairs={{0,16},{16,0},{1,17},{17,1},{2,18},{18,2},{3,19},{19,3},{4,20},{20... | collective-permute-start | bytes 14137352 | tf_op jit(solution)/shard_map/ppermute | solution.py:706
  1.2 49.9 %collective-permute-start.10 = (bf16[1,3072,767]{2,1,0:T(8,128)(2,1)}, bf16[1,3072,767]{2,1,0:T(8,128)(2,1)}, u32[]{:S(2)}, u32[]{:S(2)}) collective-permute-start(bf16[1,3072,767]{2,1,0:T(8,128)(2,1)} %dno.7), channel_id=1, source_target_pairs={{0,16},{16,0},{1,17},{17,1},{2,18},{18,2},{3,19},{19,3},{4,20},{20... | collective-permute-start | bytes 14137352 | tf_op jit(solution)/shard_map/ppermute | solution.py:706
  11.9 8.7 %collective-permute-start.3 = (bf16[767,576]{0,1:T(8,128)(2,1)}, bf16[767,576]{0,1:T(8,128)(2,1)}, u32[]{:S(2)}, u32[]{:S(2)}) collective-permute-start(bf16[767,576]{0,1:T(8,128)(2,1)} %copy.45), channel_id=1, source_target_pairs={{0,16},{16,0},{1,17},{17,1},{2,18},{18,2},{3,19},{19,3},{4,20},{20... | collective-permute-start | bytes 2650760 | tf_op jit(solution)/shard_map/ppermute | solution.py:706
  12.3 8.3 %collective-permute-start = (bf16[256,767]{1,0:T(8,128)(2,1)S(1)}, bf16[256,767]{1,0:T(8,128)(2,1)S(1)}, u32[]{:S(2)}, u32[]{:S(2)}) collective-permute-start(bf16[256,767]{1,0:T(8,128)(2,1)S(1)} %shard_map.228.n0.x), channel_id=1, source_target_pairs={{0,2},{1,3},{2,0},{3,1},{16,17},{17,16},{18,19},{19,18},{4,6},{5,7... | collective-permute-start | bytes 1178120 | tf_op jit(solution)/shard_map/ppermute | solution.py:698
  17.3 8.7 %collective-permute-start.1 = (bf16[256,767]{1,0:T(8,128)(2,1)S(1)}, bf16[256,767]{1,0:T(8,128)(2,1)S(1)}, u32[]{:S(2)}, u32[]{:S(2)}) collective-permute-start(bf16[256,767]{1,0:T(8,128)(2,1)S(1)} %shard_map.228.n0.x), channel_id=1, source_target_pairs={{0,1},{1,0},{2,3},{3,2},{16,18},{17,19},{18,16},{19,17},{4,5},{5,4... | collective-permute-start | bytes 1178120 | tf_op jit(solution)/shard_map/ppermute | solution.py:693
  20.6 24.9 %collective-permute-start.8 = (bf16[768,767]{1,0:T(8,128)(2,1)}, bf16[768,767]{1,0:T(8,128)(2,1)}, u32[]{:S(2)}, u32[]{:S(2)}) collective-permute-start(bf16[768,767]{1,0:T(8,128)(2,1)} %bitcast.176), channel_id=1, source_target_pairs={{0,16},{16,0},{1,17},{17,1},{2,18},{18,2},{3,19},{19,3},{4,20},{20... | collective-permute-start | bytes 3534344 | tf_op jit(solution)/shard_map/ppermute | solution.py:706
  20.6 9.1 %collective-permute-start.2 = (bf16[256,767]{1,0:T(8,128)(2,1)S(1)}, bf16[256,767]{1,0:T(8,128)(2,1)S(1)}, u32[]{:S(2)}, u32[]{:S(2)}) collective-permute-start(bf16[256,767]{1,0:T(8,128)(2,1)S(1)} %collective-permute-done.n1), channel_id=1, source_target_pairs={{0,1},{1,0},{2,3},{3,2},{16,18},{17,19},{18,16},{19,17},{4,5},{5,4... | collective-permute-start | bytes 1178120 | tf_op jit(solution)/shard_map/ppermute | solution.py:693
  44.3 5.7 %collective-permute-start.6 = (bf16[192,256]{1,0:T(8,128)(2,1)S(1)}, bf16[192,256]{1,0:T(8,128)(2,1)S(1)}, u32[]{:S(2)}, u32[]{:S(2)}) collective-permute-start(bf16[192,256]{1,0:T(8,128)(2,1)S(1)} %get-tuple-element.471), channel_id=1, source_target_pairs={{0,2},{1,3},{2,0},{3,1},{4,6},{5,7},{6,4},{7,5},{8,10},{9,11},{10,... | collective-permute-start | bytes 294920 | tf_op jit(solution)/shard_map/ppermute | solution.py:702
  45.5 5.5 %collective-permute-start.7 = (bf16[192,256]{1,0:T(8,128)(2,1)S(1)}, bf16[192,256]{1,0:T(8,128)(2,1)S(1)}, u32[]{:S(2)}, u32[]{:S(2)}) collective-permute-start(bf16[192,256]{1,0:T(8,128)(2,1)S(1)} %get-tuple-element.472), channel_id=1, source_target_pairs={{0,3},{1,2},{2,1},{3,0},{4,7},{5,6},{6,5},{7,4},{8,11},{9,10},{10,... | collective-permute-start | bytes 294920 | tf_op jit(solution)/shard_map/ppermute | solution.py:702
  63.4 11.8 %collective-permute-start.11 = (bf16[256,767]{1,0:T(8,128)(2,1)S(1)}, bf16[256,767]{1,0:T(8,128)(2,1)S(1)}, u32[]{:S(2)}, u32[]{:S(2)}) collective-permute-start(bf16[256,767]{1,0:T(8,128)(2,1)S(1)} %get-tuple-element.474.n0), channel_id=1, source_target_pairs={{0,2},{1,3},{2,0},{3,1},{16,17},{17,16},{18,19},{19,18},{4,6},{5,7... | collective-permute-start | bytes 1178120 | tf_op jit(solution)/shard_map/ppermute | solution.py:698
  64.2 11.1 %collective-permute-start.12 = (bf16[256,767]{1,0:T(8,128)(2,1)S(1)}, bf16[256,767]{1,0:T(8,128)(2,1)S(1)}, u32[]{:S(2)}, u32[]{:S(2)}) collective-permute-start(bf16[256,767]{1,0:T(8,128)(2,1)S(1)} %get-tuple-element.474.n0), channel_id=1, source_target_pairs={{0,1},{1,0},{2,3},{3,2},{16,18},{17,19},{18,16},{19,17},{4,5},{5,4... | collective-permute-start | bytes 1178120 | tf_op jit(solution)/shard_map/ppermute | solution.py:693
  75.3 7.8 %collective-permute-start.13 = (bf16[256,767]{1,0:T(8,128)(2,1)S(1)}, bf16[256,767]{1,0:T(8,128)(2,1)S(1)}, u32[]{:S(2)}, u32[]{:S(2)}) collective-permute-start(bf16[256,767]{1,0:T(8,128)(2,1)S(1)} %collective-permute-done.11.n1), channel_id=1, source_target_pairs={{0,1},{1,0},{2,3},{3,2},{16,18},{17,19},{18,16},{19,17},{4,5},{5,4... | collective-permute-start | bytes 1178120 | tf_op jit(solution)/shard_map/ppermute | solution.py:693
  95.5 5.7 %collective-permute-start.16 = (bf16[192,256]{1,0:T(8,128)(2,1)S(1)}, bf16[192,256]{1,0:T(8,128)(2,1)S(1)}, u32[]{:S(2)}, u32[]{:S(2)}) collective-permute-start(bf16[192,256]{1,0:T(8,128)(2,1)S(1)} %get-tuple-element.478), channel_id=1, source_target_pairs={{0,3},{1,2},{2,1},{3,0},{4,7},{5,6},{6,5},{7,4},{8,11},{9,10},{10,... | collective-permute-start | bytes 294920 | tf_op jit(solution)/shard_map/ppermute | solution.py:702
  114.1 15.0 %collective-permute-start.17 = (bf16[256,767]{1,0:T(8,128)(2,1)S(1)}, bf16[256,767]{1,0:T(8,128)(2,1)S(1)}, u32[]{:S(2)}, u32[]{:S(2)}) collective-permute-start(bf16[256,767]{1,0:T(8,128)(2,1)S(1)} %broadcast_select_fusion.7), channel_id=1, source_target_pairs={{0,16},{16,0},{1,17},{17,1},{2,18},{18,2},{3,19},{19,3},{4,20},{20... | collective-permute-start | bytes 1178120 | tf_op jit(solution)/shard_map/ppermute | solution.py:706
  131.5 12.6 %collective-permute-start.18 = (bf16[2,192,3456]{2,1,0:T(8,128)(2,1)S(1)}, bf16[2,192,3456]{2,1,0:T(8,128)(2,1)S(1)}, u32[]{:S(2)}, u32[]{:S(2)}) collective-permute-start(bf16[2,192,3456]{2,1,0:T(8,128)(2,1)S(1)} %shard_map.235), channel_id=1, source_target_pairs={{0,16},{16,0},{1,17},{17,1},{2,18},{18,2},{3,19},{19,3},{4,20},{20... | collective-permute-start | bytes 7962632 | tf_op jit(solution)/shard_map/ppermute | solution.py:706
  134.7 33.4 %collective-permute-start.25 = (bf16[2,192,3456]{2,1,0:T(8,128)(2,1)}, bf16[2,192,3456]{2,1,0:T(8,128)(2,1)S(1)}, u32[]{:S(2)}, u32[]{:S(2)}) collective-permute-start(bf16[2,192,3456]{2,1,0:T(8,128)(2,1)} %shard_map.236), channel_id=1, source_target_pairs={{0,16},{16,0},{1,17},{17,1},{2,18},{18,2},{3,19},{19,3},{4,20},{20... | collective-permute-start | bytes 7962632 | tf_op jit(solution)/shard_map/ppermute | solution.py:706
  136.8 5.9 %collective-permute-start.20 = (bf16[192,256]{1,0:T(8,128)(2,1)S(1)}, bf16[192,256]{1,0:T(8,128)(2,1)S(1)}, u32[]{:S(2)}, u32[]{:S(2)}) collective-permute-start(bf16[192,256]{1,0:T(8,128)(2,1)S(1)} %get-tuple-element.508), channel_id=1, source_target_pairs={{0,2},{1,3},{2,0},{3,1},{4,6},{5,7},{6,4},{7,5},{8,10},{9,11},{10,... | collective-permute-start | bytes 294920 | tf_op jit(solution)/shard_map/ppermute | solution.py:702
  147.4 20.7 %collective-permute-start.24 = (bf16[192,3456]{1,0:T(8,128)(2,1)}, bf16[192,3456]{1,0:T(8,128)(2,1)}, u32[]{:S(2)}, u32[]{:S(2)}) collective-permute-start(bf16[192,3456]{1,0:T(8,128)(2,1)} %get-tuple-element.542), channel_id=1, source_target_pairs={{0,1},{1,0},{2,3},{3,2},{16,18},{17,19},{18,16},{19,17},{4,5},{5,4... | collective-permute-start | bytes 3981320 | tf_op jit(solution)/shard_map/ppermute | solution.py:693
  166.8 12.3 %collective-permute-start.22 = (bf16[512,767]{1,0:T(8,128)(2,1)}, bf16[512,767]{1,0:T(8,128)(2,1)S(1)}, u32[]{:S(2)}, u32[]{:S(2)}) collective-permute-start(bf16[512,767]{1,0:T(8,128)(2,1)} %get-tuple-element.540), channel_id=1, source_target_pairs={{0,1},{1,0},{2,3},{3,2},{16,18},{17,19},{18,16},{19,17},{4,5},{5,4... | collective-permute-start | bytes 2356232 | tf_op jit(solution)/shard_map/ppermute | solution.py:693
  179.2 7.8 %collective-permute-start.26 = (bf16[256,767]{1,0:T(8,128)(2,1)S(1)}, bf16[256,767]{1,0:T(8,128)(2,1)S(1)}, u32[]{:S(2)}, u32[]{:S(2)}) collective-permute-start(bf16[256,767]{1,0:T(8,128)(2,1)S(1)} %add_convert_fusion.11), channel_id=1, source_target_pairs={{0,2},{1,3},{2,0},{3,1},{16,17},{17,16},{18,19},{19,18},{4,6},{5,7... | collective-permute-start | bytes 1178120 | tf_op jit(solution)/shard_map/ppermute | solution.py:698
  187.1 30.1 %collective-permute-start.27 = (bf16[192,3456]{1,0:T(8,128)(2,1)S(1)}, bf16[192,3456]{1,0:T(8,128)(2,1)S(1)}, u32[]{:S(2)}, u32[]{:S(2)}) collective-permute-start(bf16[192,3456]{1,0:T(8,128)(2,1)S(1)} %copy-done.62), channel_id=1, source_target_pairs={{0,1},{1,0},{2,3},{3,2},{16,18},{17,19},{18,16},{19,17},{4,5},{5,4... | collective-permute-start | bytes 3981320 | tf_op jit(solution)/shard_map/ppermute | solution.py:693
  188.3 28.9 %collective-permute-start.28 = (bf16[192,3456]{1,0:T(8,128)(2,1)S(1)}, bf16[192,3456]{1,0:T(8,128)(2,1)S(1)}, u32[]{:S(2)}, u32[]{:S(2)}) collective-permute-start(bf16[192,3456]{1,0:T(8,128)(2,1)S(1)} %add_convert_fusion.5), channel_id=1, source_target_pairs={{0,2},{1,3},{2,0},{3,1},{16,17},{17,16},{18,19},{19,18},{4,6},{5,7... | collective-permute-start | bytes 3981320 | tf_op jit(solution)/shard_map/ppermute | solution.py:698
  220.2 9.2 %collective-permute-start.29 = (bf16[2,192,3456]{2,1,0:T(8,128)(2,1)}, bf16[2,192,3456]{2,1,0:T(8,128)(2,1)}, u32[]{:S(2)}, u32[]{:S(2)}) collective-permute-start(bf16[2,192,3456]{2,1,0:T(8,128)(2,1)} %shard_map.242), channel_id=1, source_target_pairs={{0,16},{16,0},{1,17},{17,1},{2,18},{18,2},{3,19},{19,3},{4,20},{20... | collective-permute-start | bytes 7962632 | tf_op jit(solution)/shard_map/ppermute | solution.py:706
  220.3 8.2 %collective-permute-start.30 = (bf16[192,256]{1,0:T(8,128)(2,1)}, bf16[192,256]{1,0:T(8,128)(2,1)}, u32[]{:S(2)}, u32[]{:S(2)}) collective-permute-start(bf16[192,256]{1,0:T(8,128)(2,1)} %get-tuple-element.607), channel_id=1, source_target_pairs={{0,1},{1,0},{2,3},{3,2},{4,5},{5,4},{6,7},{7,6},{8,9},{9,8},{10,11... | collective-permute-start | bytes 294920 | tf_op jit(solution)/shard_map/ppermute | solution.py:702
  222.1 7.3 %collective-permute-start.31 = (bf16[192,256]{1,0:T(8,128)(2,1)}, bf16[192,256]{1,0:T(8,128)(2,1)}, u32[]{:S(2)}, u32[]{:S(2)}) collective-permute-start(bf16[192,256]{1,0:T(8,128)(2,1)} %get-tuple-element.608), channel_id=1, source_target_pairs={{0,2},{1,3},{2,0},{3,1},{4,6},{5,7},{6,4},{7,5},{8,10},{9,11},{10,... | collective-permute-start | bytes 294920 | tf_op jit(solution)/shard_map/ppermute | solution.py:702
  223.0 6.4 %collective-permute-start.32 = (bf16[192,256]{1,0:T(8,128)(2,1)}, bf16[192,256]{1,0:T(8,128)(2,1)}, u32[]{:S(2)}, u32[]{:S(2)}) collective-permute-start(bf16[192,256]{1,0:T(8,128)(2,1)} %get-tuple-element.609), channel_id=1, source_target_pairs={{0,3},{1,2},{2,1},{3,0},{4,7},{5,6},{6,5},{7,4},{8,11},{9,10},{10,... | collective-permute-start | bytes 294920 | tf_op jit(solution)/shard_map/ppermute | solution.py:702
  228.4 24.0 %collective-permute-start.34 = (bf16[2,192,3456]{2,1,0:T(8,128)(2,1)S(1)}, bf16[2,192,3456]{2,1,0:T(8,128)(2,1)S(1)}, u32[]{:S(2)}, u32[]{:S(2)}) collective-permute-start(bf16[2,192,3456]{2,1,0:T(8,128)(2,1)S(1)} %shard_map.243), channel_id=1, source_target_pairs={{0,16},{16,0},{1,17},{17,1},{2,18},{18,2},{3,19},{19,3},{4,20},{20... | collective-permute-start | bytes 7962632 | tf_op jit(solution)/shard_map/ppermute | solution.py:706
  233.1 19.4 %collective-permute-start.33 = (bf16[192,3456]{1,0:T(8,128)(2,1)}, bf16[192,3456]{1,0:T(8,128)(2,1)}, u32[]{:S(2)}, u32[]{:S(2)}) collective-permute-start(bf16[192,3456]{1,0:T(8,128)(2,1)} %get-tuple-element.623), channel_id=1, source_target_pairs={{0,1},{1,0},{2,3},{3,2},{16,18},{17,19},{18,16},{19,17},{4,5},{5,4... | collective-permute-start | bytes 3981320 | tf_op jit(solution)/shard_map/ppermute | solution.py:693
  235.5 17.0 %collective-permute-start.35 = (bf16[2,48,3456]{2,1,0:T(8,128)(2,1)S(1)}, bf16[2,48,3456]{2,1,0:T(8,128)(2,1)}, u32[]{:S(2)}, u32[]{:S(2)}) collective-permute-start(bf16[2,48,3456]{2,1,0:T(8,128)(2,1)S(1)} %get-tuple-element.660), channel_id=1, source_target_pairs={{0,4},{4,0},{8,12},{12,8},{1,5},{5,1},{9,13},{13,9},{2,6},{6,2},{1... | collective-permute-start | bytes 1990664 | tf_op jit(solution)/shard_map/ppermute | solution.py:711
  251.1 10.8 %collective-permute-start.37 = (bf16[384,576]{1,0:T(8,128)(2,1)}, bf16[384,576]{1,0:T(8,128)(2,1)}, u32[]{:S(2)}, u32[]{:S(2)}) collective-permute-start(bf16[384,576]{1,0:T(8,128)(2,1)} %get-tuple-element.683), channel_id=1, source_target_pairs={{0,16},{16,0},{1,17},{17,1},{2,18},{18,2},{3,19},{19,3},{4,20},{20... | collective-permute-start | bytes 1327112 | tf_op jit(solution)/shard_map/ppermute | solution.py:706
  251.2 12.4 %collective-permute-start.36 = (bf16[512,767]{1,0:T(8,128)(2,1)}, bf16[512,767]{1,0:T(8,128)(2,1)}, u32[]{:S(2)}, u32[]{:S(2)}) collective-permute-start(bf16[512,767]{1,0:T(8,128)(2,1)} %get-tuple-element.682), channel_id=1, source_target_pairs={{0,1},{1,0},{2,3},{3,2},{16,18},{17,19},{18,16},{19,17},{4,5},{5,4... | collective-permute-start | bytes 2356232 | tf_op jit(solution)/shard_map/ppermute | solution.py:693
  264.7 7.8 %collective-permute-start.38 = (bf16[256,767]{1,0:T(8,128)(2,1)S(1)}, bf16[256,767]{1,0:T(8,128)(2,1)S(1)}, u32[]{:S(2)}, u32[]{:S(2)}) collective-permute-start(bf16[256,767]{1,0:T(8,128)(2,1)S(1)} %add_convert_fusion.10), channel_id=1, source_target_pairs={{0,2},{1,3},{2,0},{3,1},{16,17},{17,16},{18,19},{19,18},{4,6},{5,7... | collective-permute-start | bytes 1178120 | tf_op jit(solution)/shard_map/ppermute | solution.py:698
  265.6 13.8 %collective-permute-start.41 = (bf16[2,104,576]{2,1,0:T(8,128)(2,1)S(1)}, bf16[2,104,576]{2,1,0:T(8,128)(2,1)S(1)}, u32[]{:S(2)}, u32[]{:S(2)}) collective-permute-start(bf16[2,104,576]{2,1,0:T(8,128)(2,1)S(1)} %get-tuple-element.709), channel_id=1, source_target_pairs={{0,4},{4,0},{8,12},{12,8},{1,5},{5,1},{9,13},{13,9},{2,6},{6,2},{1... | collective-permute-start | bytes 718856 | tf_op jit(solution)/shard_map/ppermute | solution.py:711
  266.9 17.2 %collective-permute-start.43 = (bf16[1,48,3456]{2,1,0:T(8,128)(2,1)S(1)}, bf16[1,48,3456]{2,1,0:T(8,128)(2,1)S(1)}, u32[]{:S(2)}, u32[]{:S(2)}) collective-permute-start(bf16[1,48,3456]{2,1,0:T(8,128)(2,1)S(1)} %copy-done.103), channel_id=1, source_target_pairs={{0,8},{4,12},{8,0},{12,4},{1,9},{5,13},{9,1},{13,5},{2,10},{6,14},... | collective-permute-start | bytes 995336 | tf_op jit(solution)/shard_map/ppermute | solution.py:711
  286.0 15.7 %collective-permute-start.42 = (bf16[1,104,576]{2,1,0:T(8,128)(2,1)S(1)}, bf16[1,104,576]{2,1,0:T(8,128)(2,1)S(1)}, u32[]{:S(2)}, u32[]{:S(2)}) collective-permute-start(bf16[1,104,576]{2,1,0:T(8,128)(2,1)S(1)} %get-tuple-element.726), channel_id=1, source_target_pairs={{0,8},{4,12},{8,0},{12,4},{1,9},{5,13},{9,1},{13,5},{2,10},{6,14},... | collective-permute-start | bytes 359432 | tf_op jit(solution)/shard_map/ppermute | solution.py:711
  287.4 18.8 %collective-permute-start.46 = (bf16[1,48,3456]{2,1,0:T(8,128)(2,1)S(1)}, bf16[1,48,3456]{2,1,0:T(8,128)(2,1)S(1)}, u32[]{:S(2)}, u32[]{:S(2)}) collective-permute-start(bf16[1,48,3456]{2,1,0:T(8,128)(2,1)S(1)} %copy-done.99), channel_id=1, source_target_pairs={{0,8},{4,12},{8,0},{12,4},{1,9},{5,13},{9,1},{13,5},{2,10},{6,14},... | collective-permute-start | bytes 995336 | tf_op jit(solution)/shard_map/ppermute | solution.py:711
  290.4 17.9 %collective-permute-start.45 = (bf16[2,104,576]{2,1,0:T(8,128)(2,1)S(1)}, bf16[2,104,576]{2,1,0:T(8,128)(2,1)S(1)}, u32[]{:S(2)}, u32[]{:S(2)}) collective-permute-start(bf16[2,104,576]{2,1,0:T(8,128)(2,1)S(1)} %fusion.7), channel_id=1, source_target_pairs={{0,4},{4,0},{8,12},{12,8},{1,5},{5,1},{9,13},{13,9},{2,6},{6,2},{1... | collective-permute-start | bytes 718856 | tf_op jit(solution)/shard_map/ppermute | solution.py:711
  291.3 35.0 %collective-permute-start.39 = (bf16[192,3456]{1,0:T(8,128)(2,1)S(1)}, bf16[192,3456]{1,0:T(8,128)(2,1)S(1)}, u32[]{:S(2)}, u32[]{:S(2)}) collective-permute-start(bf16[192,3456]{1,0:T(8,128)(2,1)S(1)} %copy-done.60), channel_id=1, source_target_pairs={{0,1},{1,0},{2,3},{3,2},{16,18},{17,19},{18,16},{19,17},{4,5},{5,4... | collective-permute-start | bytes 3981320 | tf_op jit(solution)/shard_map/ppermute | solution.py:693
  298.6 27.7 %collective-permute-start.40 = (bf16[192,3456]{1,0:T(8,128)(2,1)S(1)}, bf16[192,3456]{1,0:T(8,128)(2,1)S(1)}, u32[]{:S(2)}, u32[]{:S(2)}) collective-permute-start(bf16[192,3456]{1,0:T(8,128)(2,1)S(1)} %copy-done.93), channel_id=1, source_target_pairs={{0,2},{1,3},{2,0},{3,1},{16,17},{17,16},{18,19},{19,18},{4,6},{5,7... | collective-permute-start | bytes 3981320 | tf_op jit(solution)/shard_map/ppermute | solution.py:698
  306.3 20.0 %collective-permute-start.47 = (bf16[2,48,3456]{2,1,0:T(8,128)(2,1)S(1)}, bf16[2,48,3456]{2,1,0:T(8,128)(2,1)S(1)}, u32[]{:S(2)}, u32[]{:S(2)}) collective-permute-start(bf16[2,48,3456]{2,1,0:T(8,128)(2,1)S(1)} %maximum_select_fusion.2), channel_id=1, source_target_pairs={{0,4},{4,0},{8,12},{12,8},{1,5},{5,1},{9,13},{13,9},{2,6},{6,2},{1... | collective-permute-start | bytes 1990664 | tf_op jit(solution)/shard_map/ppermute | solution.py:711
  306.4 15.7 %collective-permute-start.44 = (bf16[1,104,576]{2,1,0:T(8,128)(2,1)S(1)}, bf16[1,104,576]{2,1,0:T(8,128)(2,1)S(1)}, u32[]{:S(2)}, u32[]{:S(2)}) collective-permute-start(bf16[1,104,576]{2,1,0:T(8,128)(2,1)S(1)} %add_convert_fusion.17), channel_id=1, source_target_pairs={{0,8},{4,12},{8,0},{12,4},{1,9},{5,13},{9,1},{13,5},{2,10},{6,14},... | collective-permute-start | bytes 359432 | tf_op jit(solution)/shard_map/ppermute | solution.py:711
  322.1 10.2 %collective-permute-start.50 = (bf16[2,104,576]{2,1,0:T(8,128)(2,1)S(1)}, bf16[2,104,576]{2,1,0:T(8,128)(2,1)S(1)}, u32[]{:S(2)}, u32[]{:S(2)}) collective-permute-start(bf16[2,104,576]{2,1,0:T(8,128)(2,1)S(1)} %maximum_select_fusion.6), channel_id=1, source_target_pairs={{0,4},{4,0},{8,12},{12,8},{1,5},{5,1},{9,13},{13,9},{2,6},{6,2},{1... | collective-permute-start | bytes 718856 | tf_op jit(solution)/shard_map/ppermute | solution.py:711
  328.5 23.6 %collective-permute-start.49 = (bf16[192,3456]{1,0:T(8,128)(2,1)S(1)}, bf16[192,3456]{1,0:T(8,128)(2,1)S(1)}, u32[]{:S(2)}, u32[]{:S(2)}) collective-permute-start(bf16[192,3456]{1,0:T(8,128)(2,1)S(1)} %bitcast.159), channel_id=1, source_target_pairs={{0,2},{1,3},{2,0},{3,1},{16,17},{17,16},{18,19},{19,18},{4,6},{5,7... | collective-permute-start | bytes 3981320 | tf_op jit(solution)/shard_map/ppermute | solution.py:698
  332.5 19.6 %collective-permute-start.51 = (bf16[416,576]{1,0:T(8,128)(2,1)S(1)}, bf16[416,576]{1,0:T(8,128)(2,1)S(1)}, u32[]{:S(2)}, u32[]{:S(2)}) collective-permute-start(bf16[416,576]{1,0:T(8,128)(2,1)S(1)} %bitcast.169), channel_id=1, source_target_pairs={{0,2},{1,3},{2,0},{3,1},{16,17},{17,16},{18,19},{19,18},{4,6},{5,7... | collective-permute-start | bytes 1437704 | tf_op jit(solution)/shard_map/ppermute | solution.py:698
  333.0 9.8 %collective-permute-start.52 = (bf16[256,767]{1,0:T(8,128)(2,1)S(1)}, bf16[256,767]{1,0:T(8,128)(2,1)S(1)}, u32[]{:S(2)}, u32[]{:S(2)}) collective-permute-start(bf16[256,767]{1,0:T(8,128)(2,1)S(1)} %broadcast_select_fusion.6), channel_id=1, source_target_pairs={{0,16},{16,0},{1,17},{17,1},{2,18},{18,2},{3,19},{19,3},{4,20},{20... | collective-permute-start | bytes 1178120 | tf_op jit(solution)/shard_map/ppermute | solution.py:706
  333.1 9.7 %collective-permute-start.53 = (bf16[1,104,576]{2,1,0:T(8,128)(2,1)S(1)}, bf16[1,104,576]{2,1,0:T(8,128)(2,1)S(1)}, u32[]{:S(2)}, u32[]{:S(2)}) collective-permute-start(bf16[1,104,576]{2,1,0:T(8,128)(2,1)S(1)} %get-tuple-element.795), channel_id=1, source_target_pairs={{0,8},{4,12},{8,0},{12,4},{1,9},{5,13},{9,1},{13,5},{2,10},{6,14},... | collective-permute-start | bytes 359432 | tf_op jit(solution)/shard_map/ppermute | solution.py:711
  342.8 16.5 %collective-permute-start.48 = (bf16[2,48,3456]{2,1,0:T(8,128)(2,1)S(1)}, bf16[2,48,3456]{2,1,0:T(8,128)(2,1)S(1)}, u32[]{:S(2)}, u32[]{:S(2)}) collective-permute-start(bf16[2,48,3456]{2,1,0:T(8,128)(2,1)S(1)} %fusion.3), channel_id=1, source_target_pairs={{0,4},{4,0},{8,12},{12,8},{1,5},{5,1},{9,13},{13,9},{2,6},{6,2},{1... | collective-permute-start | bytes 1990664 | tf_op jit(solution)/shard_map/ppermute | solution.py:711
  359.3 43.4 %collective-permute-start.60 = (bf16[2,192,3456]{2,1,0:T(8,128)(2,1)S(1)}, bf16[2,192,3456]{2,1,0:T(8,128)(2,1)S(1)}, u32[]{:S(2)}, u32[]{:S(2)}) collective-permute-start(bf16[2,192,3456]{2,1,0:T(8,128)(2,1)S(1)} %pad_maximum_fusion.refs_3_), channel_id=1, source_target_pairs={{0,1},{1,0},{2,3},{3,2},{16,18},{17,19},{18,16},{19,17},{4,5},{5,4... | collective-permute-start | bytes 7962632 | tf_op jit(solution)/shard_map/ppermute | solution.py:693
  361.1 22.9 %collective-permute-start.54 = (bf16[1,48,3456]{2,1,0:T(8,128)(2,1)S(1)}, bf16[1,48,3456]{2,1,0:T(8,128)(2,1)S(1)}, u32[]{:S(2)}, u32[]{:S(2)}) collective-permute-start(bf16[1,48,3456]{2,1,0:T(8,128)(2,1)S(1)} %get-tuple-element.811), channel_id=1, source_target_pairs={{0,8},{4,12},{8,0},{12,4},{1,9},{5,13},{9,1},{13,5},{2,10},{6,14},... | collective-permute-start | bytes 995336 | tf_op jit(solution)/shard_map/ppermute | solution.py:711
  361.6 21.5 %collective-permute-start.55 = (bf16[1,104,576]{2,1,0:T(8,128)(2,1)S(1)}, bf16[1,104,576]{2,1,0:T(8,128)(2,1)S(1)}, u32[]{:S(2)}, u32[]{:S(2)}) collective-permute-start(bf16[1,104,576]{2,1,0:T(8,128)(2,1)S(1)} %add_convert_fusion.16), channel_id=1, source_target_pairs={{0,8},{4,12},{8,0},{12,4},{1,9},{5,13},{9,1},{13,5},{2,10},{6,14},... | collective-permute-start | bytes 359432 | tf_op jit(solution)/shard_map/ppermute | solution.py:711
  364.1 49.6 %collective-permute-start.59 = (bf16[2,192,3456]{2,1,0:T(8,128)(2,1)S(1)}, bf16[2,192,3456]{2,1,0:T(8,128)(2,1)S(1)}, u32[]{:S(2)}, u32[]{:S(2)}) collective-permute-start(bf16[2,192,3456]{2,1,0:T(8,128)(2,1)S(1)} %pad_maximum_fusion.refs_3_), channel_id=1, source_target_pairs={{0,16},{1,17},{2,18},{3,19},{4,20},{5,21},{6,22},{7,23},{8,24},{9,... | collective-permute-start | bytes 7962632 | tf_op jit(solution)/shard_map/ppermute | solution.py:715
  383.2 8.3 %collective-permute-start.57 = (bf16[2,104,576]{2,1,0:T(8,128)(2,1)S(1)}, bf16[2,104,576]{2,1,0:T(8,128)(2,1)S(1)}, u32[]{:S(2)}, u32[]{:S(2)}) collective-permute-start(bf16[2,104,576]{2,1,0:T(8,128)(2,1)S(1)} %maximum_select_fusion.7), channel_id=1, source_target_pairs={{0,4},{4,0},{8,12},{12,8},{1,5},{5,1},{9,13},{13,9},{2,6},{6,2},{1... | collective-permute-start | bytes 718856 | tf_op jit(solution)/shard_map/ppermute | solution.py:711
  383.3 19.4 %collective-permute-start.61 = (bf16[2,416,576]{2,1,0:T(8,128)(2,1)S(1)}, bf16[2,416,576]{2,1,0:T(8,128)(2,1)S(1)}, u32[]{:S(2)}, u32[]{:S(2)}) collective-permute-start(bf16[2,416,576]{2,1,0:T(8,128)(2,1)S(1)} %pad_maximum_fusion.4), channel_id=1, source_target_pairs={{0,1},{1,0},{2,3},{3,2},{16,18},{17,19},{18,16},{19,17},{4,5},{5,4... | collective-permute-start | bytes 2875400 | tf_op jit(solution)/shard_map/ppermute | solution.py:693
  402.7 33.4 %collective-permute-start.63 = (bf16[2,192,3456]{2,1,0:T(8,128)(2,1)S(1)}, bf16[2,192,3456]{2,1,0:T(8,128)(2,1)S(1)}, u32[]{:S(2)}, u32[]{:S(2)}) collective-permute-start(bf16[2,192,3456]{2,1,0:T(8,128)(2,1)S(1)} %collective-permute-done.60.refs_3_), channel_id=1, source_target_pairs={{0,16},{1,17},{2,18},{3,19},{4,20},{5,21},{6,22},{7,23},{8,24},{9,... | collective-permute-start | bytes 7962632 | tf_op jit(solution)/shard_map/ppermute | solution.py:715
  404.3 9.3 %collective-permute-start.58 = (bf16[416,576]{1,0:T(8,128)(2,1)S(1)}, bf16[416,576]{1,0:T(8,128)(2,1)S(1)}, u32[]{:S(2)}, u32[]{:S(2)}) collective-permute-start(bf16[416,576]{1,0:T(8,128)(2,1)S(1)} %bitcast.171), channel_id=1, source_target_pairs={{0,2},{1,3},{2,0},{3,1},{16,17},{17,16},{18,19},{19,18},{4,6},{5,7... | collective-permute-start | bytes 1437704 | tf_op jit(solution)/shard_map/ppermute | solution.py:698
  406.0 15.2 %collective-permute-start.56 = (bf16[1,48,3456]{2,1,0:T(8,128)(2,1)S(1)}, bf16[1,48,3456]{2,1,0:T(8,128)(2,1)S(1)}, u32[]{:S(2)}, u32[]{:S(2)}) collective-permute-start(bf16[1,48,3456]{2,1,0:T(8,128)(2,1)S(1)} %add_convert_fusion.12), channel_id=1, source_target_pairs={{0,8},{4,12},{8,0},{12,4},{1,9},{5,13},{9,1},{13,5},{2,10},{6,14},... | collective-permute-start | bytes 995336 | tf_op jit(solution)/shard_map/ppermute | solution.py:711
  421.2 15.0 %collective-permute-start.64 = (bf16[2,416,576]{2,1,0:T(8,128)(2,1)S(1)}, bf16[2,416,576]{2,1,0:T(8,128)(2,1)S(1)}, u32[]{:S(2)}, u32[]{:S(2)}) collective-permute-start(bf16[2,416,576]{2,1,0:T(8,128)(2,1)S(1)} %pad_maximum_fusion.5), channel_id=1, source_target_pairs={{0,1},{1,0},{2,3},{3,2},{16,18},{17,19},{18,16},{19,17},{4,5},{5,4... | collective-permute-start | bytes 2875400 | tf_op jit(solution)/shard_map/ppermute | solution.py:693
  421.7 16.8 %collective-permute-start.62 = (bf16[2,48,3456]{2,1,0:T(8,128)(2,1)S(1)}, bf16[2,48,3456]{2,1,0:T(8,128)(2,1)S(1)}, u32[]{:S(2)}, u32[]{:S(2)}) collective-permute-start(bf16[2,48,3456]{2,1,0:T(8,128)(2,1)S(1)} %maximum_select_fusion.3), channel_id=1, source_target_pairs={{0,4},{4,0},{8,12},{12,8},{1,5},{5,1},{9,13},{13,9},{2,6},{6,2},{1... | collective-permute-start | bytes 1990664 | tf_op jit(solution)/shard_map/ppermute | solution.py:711
  421.8 18.8 %collective-permute-start.66 = (bf16[4,416,576]{2,1,0:T(8,128)(2,1)S(1)}, bf16[4,416,576]{2,1,0:T(8,128)(2,1)S(1)}, u32[]{:S(2)}, u32[]{:S(2)}) collective-permute-start(bf16[4,416,576]{2,1,0:T(8,128)(2,1)S(1)} %pad_maximum_fusion.2.refs_3_), channel_id=1, source_target_pairs={{0,16},{1,17},{2,18},{3,19},{4,20},{5,21},{6,22},{7,23},{8,24},{9,... | collective-permute-start | bytes 5750792 | tf_op jit(solution)/shard_map/ppermute | solution.py:715
  438.9 17.8 %collective-permute-start.65 = (bf16[192,3456]{1,0:T(8,128)(2,1)S(1)}, bf16[192,3456]{1,0:T(8,128)(2,1)S(1)}, u32[]{:S(2)}, u32[]{:S(2)}) collective-permute-start(bf16[192,3456]{1,0:T(8,128)(2,1)S(1)} %bitcast.161), channel_id=1, source_target_pairs={{0,2},{1,3},{2,0},{3,1},{16,17},{17,16},{18,19},{19,18},{4,6},{5,7... | collective-permute-start | bytes 3981320 | tf_op jit(solution)/shard_map/ppermute | solution.py:698
  457.1 8.9 %collective-permute-start.68 = (bf16[2,192,3456]{2,1,0:T(8,128)(2,1)S(1)}, bf16[2,192,3456]{2,1,0:T(8,128)(2,1)S(1)}, u32[]{:S(2)}, u32[]{:S(2)}) collective-permute-start(bf16[2,192,3456]{2,1,0:T(8,128)(2,1)S(1)} %pad_maximum_fusion.1.refs_0_), channel_id=1, source_target_pairs={{16,0},{17,1},{18,2},{19,3},{20,4},{21,5},{22,6},{23,7},{24,8},{25... | collective-permute-start | bytes 7962632 | tf_op jit(solution)/shard_map/ppermute | solution.py:715
  458.5 32.2 %collective-permute-start.69 = (bf16[2,192,3456]{2,1,0:T(8,128)(2,1)S(1)}, bf16[2,192,3456]{2,1,0:T(8,128)(2,1)}, u32[]{:S(2)}, u32[]{:S(2)}) collective-permute-start(bf16[2,192,3456]{2,1,0:T(8,128)(2,1)S(1)} %pad_maximum_fusion.1.refs_0_), channel_id=1, source_target_pairs={{0,1},{1,0},{2,3},{3,2},{16,18},{17,19},{18,16},{19,17},{4,5},{5,4... | collective-permute-start | bytes 7962632 | tf_op jit(solution)/shard_map/ppermute | solution.py:693
  459.9 11.5 %collective-permute-start.67 = (bf16[4,416,576]{2,1,0:T(8,128)(2,1)S(1)}, bf16[4,416,576]{2,1,0:T(8,128)(2,1)S(1)}, u32[]{:S(2)}, u32[]{:S(2)}) collective-permute-start(bf16[4,416,576]{2,1,0:T(8,128)(2,1)S(1)} %pad_maximum_fusion.3.refs_0_), channel_id=1, source_target_pairs={{16,0},{17,1},{18,2},{19,3},{20,4},{21,5},{22,6},{23,7},{24,8},{25... | collective-permute-start | bytes 5750792 | tf_op jit(solution)/shard_map/ppermute | solution.py:715
  490.7 8.4 %collective-permute-start.70 = (bf16[2,192,3456]{2,1,0:T(8,128)(2,1)}, bf16[2,192,3456]{2,1,0:T(8,128)(2,1)}, u32[]{:S(2)}, u32[]{:S(2)}) collective-permute-start(bf16[2,192,3456]{2,1,0:T(8,128)(2,1)} %collective-permute-done.69.refs_0_), channel_id=1, source_target_pairs={{16,0},{17,1},{18,2},{19,3},{20,4},{21,5},{22,6},{23,7},{24,8},{25... | collective-permute-start | bytes 7962632 | tf_op jit(solution)/shard_map/ppermute | solution.py:715
  (118 other events, 1070.3 us)

commit v4 on v3

--- a/solution.py
+++ b/solution.py
@@ -426,15 +426,27 @@
 
 
 def attn_bwd_kernel(
-    ids, n0, n1, n2, n3, w_ref, qh, kh, vh, lse, d0, d1, d2, d3,
+    ids, n0, n1, n2, n3, w_hbm, q_hbm, k_hbm, v_hbm, l_hbm, d0, d1, d2, d3,
     p0, p1, far, gs, gk, gb, do, dk, dv, dy, acc, bias_scr,
+    nb, w_ref, qh, kh, vh, lse, sem,
 ):
     c, s = ids[0], ids[1]
     heads, _, hd = qh.shape
     span, cc = n0.shape
     width = heads * hd
+    moves = [
+        pltpu.make_async_copy(src, dst, sem.at[i])
+        for i, (src, dst) in enumerate(
+            [(q_hbm, qh), (k_hbm, kh), (v_hbm, vh), (l_hbm, lse), (w_hbm, w_ref)]
+            + [(n, nb.at[i]) for i, n in enumerate((n0, n1, n2, n3))]
+        )
+    ]
+    for m in moves:
+        m.start()
     for k, d in enumerate((d0, d1, d2, d3)):
         do[jnp.bitwise_xor(s, k)] = d[...]
+    for m in moves[:4]:
+        m.wait()
     for t in reversed(range(QUAD)):
         n = span * (t + 1)
         bias_scr[:n, :] = visible_bias(ids, n, t, span)
@@ -460,14 +472,15 @@
     for h in range(heads):
         dy[:, width + h * hd : width + (h + 1) * hd] = dk[h].astype(BF16)
         dy[:, 2 * width + h * hd : 2 * width + (h + 1) * hd] = dv[h].astype(BF16)
+    for m in moves[4:]:
+        m.wait()
     total = jnp.zeros((1, 3 * width), F32)
-    outs = (p0, p1, far.at[span:], far.at[:span])
-    for p, (nb, out) in enumerate(zip((n0, n1, n2, n3), outs)):
+    for p, out in enumerate((p0, p1, far.at[span:], far.at[:span])):
         row = pl.multiple_of(jnp.bitwise_xor(order(c, p), s) * span, span)
         y = dy[pl.ds(row, span), :]
         out[...] = nt(y, w_ref[...]).astype(BF16)
         total = total + jnp.sum(y.astype(F32), axis=0, keepdims=True)
-        g = tn(nb[...], y)
+        g = tn(nb[p], y)
         if p == 0:
             acc[:cc, :] = g
         else:
@@ -487,7 +500,7 @@
     gg = jax.ShapeDtypeStruct(((cc + 1) // 2, 3 * width), BF16)
     return pl.pallas_call(
         attn_bwd_kernel,
-        in_specs=[SMEM] + [VMEM] * 13,
+        in_specs=[SMEM] + [HBM] * 9 + [VMEM] * 4,
         out_specs=[VMEM] * 6,
         out_shape=[pp, pp, jax.ShapeDtypeStruct((2 * span, cc), BF16), gg, gg, jax.ShapeDtypeStruct((8, 3 * width), F32)],
         scratch_shapes=[
@@ -497,6 +510,13 @@
             pltpu.VMEM((full, 3 * width), BF16),
             pltpu.VMEM((cc + 1, 3 * width), F32),
             pltpu.VMEM((full, span), F32),
+            pltpu.VMEM((QUAD, span, cc), BF16),
+            pltpu.VMEM(w3.shape, BF16),
+            pltpu.VMEM((heads, full, hd), BF16),
+            pltpu.VMEM((heads, full, hd), BF16),
+            pltpu.VMEM((heads, full, hd), BF16),
+            pltpu.VMEM((heads, QUAD, span), F32),
+            pltpu.SemaphoreType.DMA((9,)),
         ],
         compiler_params=params(48),
         cost_estimate=cost(
@@ -539,83 +559,80 @@
         start(rows - 1)
 
 
-def place_kernel(pair, first, ids, *refs):
-    srcs = refs[:4]
-    outs = refs[4:7] if first else refs[7:10]
-    x0, x1, od, ou, ow, sem = refs[7:] if first else refs[10:]
+def place_kernel(places, first, ids, *refs):
+    n = len(places)
+    srcs = refs[: 4 * n]
+    refs = refs[4 * n :]
+    outs = refs[:3] if first else refs[3:6]
+    x0, x1, od, ou, ow, sem = refs[3:] if first else refs[6:]
     c, s = ids[0], ids[1]
     down, up, wout = outs
     _, rows, _, ff = od.shape
     part = ow.shape[-1]
 
-    def reads(i, a, b):
+    def reads(i, j):
         return [
-            pltpu.make_async_copy(a.at[i], x0.at[i], sem.at[0, i]),
-            pltpu.make_async_copy(b.at[i], x1.at[i], sem.at[1, i]),
+            pltpu.make_async_copy(srcs[4 * i + j], x0.at[i], sem.at[0, i]),
+            pltpu.make_async_copy(srcs[4 * i + j + 1], x1.at[i], sem.at[1, i]),
         ]
 
-    def load(a, b):
-        for i in range(2):
-            for m in reads(i, a, b):
-                m.start()
-
-    @pl.when(c == 0)
-    def _():
-        load(srcs[0], srcs[1])
-
-    @pl.when(c != 0)
-    def _():
-        load(srcs[2], srcs[3])
-
-    def writes(n, i, side, t):
+    for core in range(2):
+
+        @pl.when(c == core)
+        def _():
+            for i in range(n):
+                for m in reads(i, 2 * core):
+                    m.start()
+
+    def writes(length, i, side, t):
         o, dst = ((od, down), (ou, up))[side]
         return [
             pltpu.make_async_copy(
-                o.at[i, pl.ds(0, n)], dst.at[pl.ds(t * rows, n)], sem.at[2 + side, i]
+                o.at[i, pl.ds(0, length)], dst.at[pl.ds(t * rows, length)], sem.at[2 + side, i]
             ),
             pltpu.make_async_copy(
-                ow.at[side, i, pl.ds(0, n)],
-                wout.at[pl.ds(t * rows, n), :, pl.ds(side * part, part)],
+                ow.at[side, i, pl.ds(0, length)],
+                wout.at[pl.ds(t * rows, length), :, pl.ds(side * part, part)],
                 sem.at[4 + side, i],
             ),
         ]
 
     jobs = []
-    for i in range(2):
-        place = 2 * pair + i
-        for m in reads(i, srcs[0], srcs[1]):
+    for i, place in enumerate(places):
+        for m in reads(i, 0):
             m.wait()
         swapped = ((place & 1) << 1) | (place >> 1)
         for side, (x, o, k) in enumerate(((x0, od, swapped), (x1, ou, place))):
             t = jnp.bitwise_xor(k, s)
             o[i, :, 0, :] = x[i, :, :ff].astype(F32)
             ow[side, i, :, 0, :] = x[i, :, ff:].astype(F32)
-            both_lengths(t, rows, lambda n: [m.start() for m in writes(n, i, side, t)])
+            both_lengths(t, rows, lambda length: [m.start() for m in writes(length, i, side, t)])
             jobs.append((i, side, t))
     for i, side, t in jobs:
-        both_lengths(t, rows, lambda n: [m.wait() for m in writes(n, i, side, t)])
-
-
-def place_rows(pair, ids, srcs, outs, cc, ff, model):
-    _, rows, cols = srcs[0].shape
+        both_lengths(t, rows, lambda length: [m.wait() for m in writes(length, i, side, t)])
+
+
+def place_rows(places, ids, srcs, outs, cc, ff, model):
+    rows, cols = srcs[0].shape
+    n = len(places)
     first = outs is None
     operands = [ids, *srcs] + ([] if first else list(outs))
     return pl.pallas_call(
-        functools.partial(place_kernel, pair, first),
+        functools.partial(place_kernel, places, first),
         in_specs=[SMEM] + [HBM] * (len(operands) - 1),
         out_specs=[HBM] * 3,
-        out_shape=[jax.ShapeDtypeStruct((cc, 1, n), F32) for n in (ff, ff, model)],
-        input_output_aliases={} if first else {5: 0, 6: 1, 7: 2},
+        out_shape=[jax.ShapeDtypeStruct((cc, 1, m), F32) for m in (ff, ff, model)],
+        input_output_aliases={} if first else {4 * n + 1 + i: i for i in range(3)},
         scratch_shapes=[
-            pltpu.VMEM((2, rows, cols), BF16),
-            pltpu.VMEM((2, rows, cols), BF16),
-            pltpu.VMEM((2, rows, 1, ff), F32),
-            pltpu.VMEM((2, rows, 1, ff), F32),
-            pltpu.VMEM((2, 2, rows, 1, cols - ff), F32),
-            pltpu.SemaphoreType.DMA((6, 2)),
+            pltpu.VMEM((n, rows, cols), BF16),
+            pltpu.VMEM((n, rows, cols), BF16),
+            pltpu.VMEM((n, rows, 1, ff), F32),
+            pltpu.VMEM((n, rows, 1, ff), F32),
+            pltpu.VMEM((2, n, rows, 1, cols - ff), F32),
+            pltpu.SemaphoreType.DMA((6, n)),
         ],
         compiler_params=params(40),
-        cost_estimate=cost(0, 24 * rows * cols),
+        cost_estimate=cost(0, 12 * n * rows * cols),
     )(*operands)
 
 
@@ -901,8 +918,9 @@
     out_got = wait(out_got)
 
     far1 = to_core(send(1, (3, 2), lr1, rr1))
+    douts1 = wait(*douts1)
     near1 = send(1, (1, 0), lr1, rr1)
-    far1, *douts1 = wait(far1, *douts1)
+    far1 = wait(far1)
 
     far1 = keep(1, (3, 2), lr1, rr1, far1)
     x1a, near1 = to_first(far1[0]), to_core(near1)
@@ -921,20 +939,20 @@
     dx1, gg1 = input_part(1, p0, pr, q, dmid1)
     qkv_sum1 = DpSum(order_of, functools.partial(projection, 1), gk1, gs_got, g1, gb1, gg1)
     lr0, rr0, dmid0, g0, douts0 = first_part(0, dx1)
-    x1b, x2 = wait(x1b, x2)
-
     far0 = to_core(send(0, (3, 2), lr0, rr0))
     near0 = send(0, (1, 0), lr0, rr0)
+    x1b, x2 = wait(x1b, x2)
+
+    sum1 = DpSum(order_of, lambda a, b, d: add_low(add_low(a, b), d), near1[1], x1b, x2)
+    sum1.go()
     far0, *douts0 = wait(far0, *douts0)
 
     far0 = keep(0, (3, 2), lr0, rr0, far0)
     x1a, near0 = to_first(far0[0]), to_core(near0)
-    sum1 = DpSum(order_of, lambda a, b, d: add_low(add_low(a, b), d), near1[1], x1b, x2)
-    sum1.go()
     p0, p1, _, _, gk0, gb0, pr, gs_got = attention(0, douts0)
     x1a, near0 = wait(x1a, near0)
+
     sum1.go()
-
     near0 = keep(0, (1, 0), lr0, rr0, near0)
     half1 = run(add_low, near0[0], x1a)
     qkv_sum1.go()
@@ -943,72 +961,89 @@
     q = to_second(run(add_first, p1, pr))
     q = wait(q)
 
-    x1b, half1 = wait(far0[1], half1)
-    x1b, x2 = to_first(x1b), to_second(half1)
+    x1b = to_first(wait(far0[1]))
     dx0, gg0 = input_part(0, p0, pr, q, dmid0)
     qkv_sum1.go()
     sum1.go()
+    x1b, half1 = wait(x1b, half1)
+
+    x2 = to_second(half1)
+    sum1.go()
+    half0 = run(add_low, near0[1], x1b)
     qkv_sum0 = DpSum(order_of, functools.partial(projection, 0), gk0, gs_got, g0, gb0, gg0)
     qkv_sum0.go()
     qkv_sum1.go()
-    sum1.go()
+    x2 = wait(x2)
+    own1 = sum1.finish()
+
+    have1 = [own1, to_second(own1), to_first(own1)]
+    sum0 = DpSum(order_of, add_low, half0, x2)
+    sum0.go()
+    qkv_sum1.go()
     qkv_sum0.go()
-    qkv_sum1.go()
-    x1b, x2 = wait(x1b, x2)
-
-    own1 = sum1.finish()
-    sum0 = DpSum(order_of, lambda a, b, d: add_low(add_low(a, b), d), near0[1], x1b, x2)
-    next1 = to_second(own1)
     sum0.go()
+    have1[1], have1[2] = wait(have1[1], have1[2])
+
+    have1.append(to_first(have1[1]))
     qkv_own1 = qkv_sum1.finish()
+    qkv_sum0.go()
+    got1 = [to_owner(1, own1)]
+    sum0.go()
+    have1[3], got1[0] = wait(have1[3], got1[0])
+
     qkv_next1 = to_second(qkv_own1)
-    in_got = to_core(run(lambda a, b: jnp.where(mine, a, b), dx1, dx0))
+    got1.append(to_owner(1, have1[1]))
     qkv_sum0.go()
-    next1, qkv_next1, in_got = wait(next1, qkv_next1, in_got)
-
-    pair1 = run(pair_up, own1, next1)
-    rest1 = to_first(pair1)
+    qkv_next1, got1[1] = wait(qkv_next1, got1[1])
+    qkv_pair1 = run(pair_up, qkv_own1, qkv_next1)
     sum0.go()
-    qkv_pair1 = run(pair_up, qkv_own1, qkv_next1)
+
     qkv_rest1 = to_first(qkv_pair1)
-    qkv_sum0.go()
-
-    sum0.go()
+    got1.append(to_owner(1, have1[2]))
     qkv_own0 = qkv_sum0.finish()
     qkv_next0 = to_second(qkv_own0)
-    rest1, qkv_rest1 = wait(rest1, qkv_rest1)
-    pair1_got = to_owner(1, pair1)
-    qkv1 = run(lambda a, b: jnp.concatenate([a, b]), qkv_pair1, qkv_rest1)
-    qkv_next0, pair1_got = wait(qkv_next0, pair1_got)
-
+    qkv_rest1, got1[2], qkv_next0 = wait(qkv_rest1, got1[2], qkv_next0)
+
+    own0 = sum0.finish()
+    have0 = [own0, to_second(own0), to_first(own0)]
+    got1.append(to_owner(1, have1[3]))
     qkv_pair0 = run(pair_up, qkv_own0, qkv_next0)
     qkv_rest0 = to_first(qkv_pair0)
-    rest1_got = to_owner(1, rest1)
-    sum0.go()
-    rest1_got, qkv_rest0 = wait(rest1_got, qkv_rest0)
-
-    own0 = sum0.finish()
-    next0, qkv1_got = to_second(own0), to_owner(1, qkv1)
-    qkv0 = run(lambda a, b: jnp.concatenate([a, b]), qkv_pair0, qkv_rest0)
-    next0, qkv1_got = wait(next0, qkv1_got)
-
-    pair0 = run(pair_up, own0, next0)
-    rest0, pair0_got = to_first(pair0), to_owner(0, pair0)
-    qkv0_got = to_owner(0, qkv0)
+    got1[3] = wait(got1[3])
+    got0 = [to_owner(0, own0)]
+    in_got = to_core(run(lambda a, b: jnp.where(mine, a, b), dx1, dx0))
+    qkv1 = run(lambda a, b: jnp.concatenate([a, b]), qkv_pair1, qkv_rest1)
     layer_out = run(
         lambda a, b, d: rows_out(ids, jnp.where(mine, a, b), d), outs[0], outs[1], out_got
     )
+    got0[0], in_got = wait(got0[0], in_got)
+
+    def place(places, outs_w):
+        srcs = [v[p] for p in places for v in (have0, got0, got1, have1)]
+        n = len(srcs)
+        return run(
+            lambda *v: place_rows(places, ids, v[:n], v[n:] or None, cc, ff, model), *srcs, *outs_w
+        )
+
+    outs_w = place((0,), ())
     input_grad = run(lambda a, b, d: rows_out(ids, jnp.where(mine, a, b), d), dx0, dx1, in_got)
-    pair0_got = wait(pair0_got)
-    outs_w = run(
-        lambda *v: place_rows(0, ids, v, None, cc, ff, model), pair0, pair0_got, pair1_got, pair1
-    )
-    qkv0_got = wait(qkv0_got)
+    have0[1], have0[2], qkv_rest0 = wait(have0[1], have0[2], qkv_rest0)
+
+    have0.append(to_first(have0[1]))
+    got0 += [to_owner(0, have0[1]), to_owner(0, have0[2])]
+    qkv0 = run(lambda a, b: jnp.concatenate([a, b]), qkv_pair0, qkv_rest0)
+    got0[1], got0[2] = wait(got0[1], got0[2])
+    qkv0_got, qkv1_got = to_owner(0, qkv0), to_owner(1, qkv1)
+    outs_w = place((1,), outs_w)
+    qkv0_got, qkv1_got = wait(qkv0_got, qkv1_got)
+    outs_w = place((2,), outs_w)
+    have0[3] = wait(have0[3])
+
+    got0.append(to_owner(0, have0[3]))
     grad_qkv = run(lambda *v: qkv_out(ids, v, cc), qkv0, qkv0_got, qkv1_got, qkv1)
-    rest0 = wait(rest0)
-    rest0_got = wait(to_owner(0, rest0))
+    got0[3] = wait(got0[3])
     grad_down, grad_up, grad_out = place_rows(
-        1, order_of.token, [rest0, rest0_got, rest1_got, rest1], outs_w, cc, ff, model
+        (3,), order_of.token, [v[3] for v in (have0, got0, got1, have1)], outs_w, cc, ff, model
     )
 
     half = (cc + 1) // 2

time: 517 us -> 511 us (0.988)
  waiting for transfers between devices: 219 us -> 164 us
  starting transfers between devices: 79.7 us -> 99.4 us
  other arithmetic: 21.8 us -> 31.7 us
  local copies, waits for them, and re-layouts: 39.3 us -> 48.7 us
  Pallas kernels: 144 us -> 153 us
    ppermute x16, waiting for transfers between devices: 82.4 us -> 34.8 us  [dp_partner(): return lax.ppermute(v, 'dp', [(i, i ^ step) for i in range(n)])]
    ppermute x16, starting transfers between devices: 19.1 us -> 35.1 us  [dp_partner(): return lax.ppermute(v, 'dp', [(i, i ^ step) for i in range(n)])]
    unnamed x222 -> x246, local copies, waits for them, and re-layouts: 22.8 us -> 30.1 us
    ppermute x14 -> x16, waiting for transfers between devices: 68.7 us -> 62 us  [to_first(): return lax.ppermute(v, ('section', 'seq'), pairs)]
    ppermute x6 -> x10, starting transfers between devices: 9.24 us -> 15.6 us  [to_owner(): return lax.ppermute(v, 'section', [(1 - l, l)])]
    pallas_call x4 -> x6, Pallas kernels: 39.3 us -> 45.3 us  [the longest x2 26.2 us: attn_bwd(): pl.pallas_call(attn_bwd_kernel, in_specs=[SMEM] + [HBM] * 9 + [VMEM] * 4,...]
    ppermute x14 -> x16, starting transfers between devices: 22.2 us -> 17.7 us  [to_first(): return lax.ppermute(v, ('section', 'seq'), pairs)]
    convert_element_type x12 -> x13, other arithmetic: 9.99 us -> 14.3 us  [add_low(): return (a.astype(F32) + b.astype(F32)).astype(BF16)]
  transfers between devices with their start and end apart: 71 -> 77, of which waited for: 37 -> 32; matrix products, arithmetic and copies ran while one was open for 7% -> 10% of each run, Pallas kernels for 20% -> 22%
where the time goes in v4:
time: 511 us; the launch traced here: 504 us
  waiting for transfers between devices  164 us (32%)
  Pallas kernels  153 us (30%)
  starting transfers between devices  99.4 us (19%)
  local copies, waits for them, and re-layouts  48.7 us (10%)
  other arithmetic  31.7 us (6%)
  between operations  7.12 us (1%)
    ppermute x16, waiting for transfers between devices, to_first(): return lax.ppermute(v, ('section', 'seq'), pairs)  62 us
    ppermute x10, waiting for transfers between devices, to_second(): return lax.ppermute(v, ('section', 'seq'), pairs)  49.2 us
    ppermute x16, starting transfers between devices, dp_partner(): return lax.ppermute(v, 'dp', [(i, i ^ step) for i in range(n)])  35.1 us
    ppermute x16, waiting for transfers between devices, dp_partner(): return lax.ppermute(v, 'dp', [(i, i ^ step) for i in range(n)])  34.8 us
    unnamed x246, local copies, waits for them, and re-layouts  30.1 us
    pallas_call x2, Pallas kernels, attn_bwd(): pl.pallas_call(attn_bwd_kernel, in_specs=[SMEM] + [HBM] * 9 + [VMEM] * 4,...  26.2 us
    pallas_call x2, Pallas kernels, mlp_bwd(): pl.pallas_call(functools.partial(mlp_bwd_kernel, layer), grid_spec=grid,...  25 us
    pallas_call x2, Pallas kernels, mlp_fwd(): pl.pallas_call(functools.partial(mlp_fwd_kernel, layer), grid_spec=grid,...  22.9 us
  transfers between devices with their start and end apart: 77, of which 32 were waited for; matrix products, arithmetic and copies ran while one was open for 10% of the time, Pallas kernels for 22%

profile of v4, /device:TPU:0, one launch (start us, length us, event | category | flops | bytes accessed | tf_op | source)
XLA Modules:
  0.0 504.3 jit_solution(10432790934313873400)
XLA Ops:
  7.9 2.1 dynamic-slice_bitcast_fusion.2
  12.4 2.5 collective-permute-start
  17.4 2.3 collective-permute-start.1
  20.7 2.2 collective-permute-start.2
  27.1 2.6 collective-permute-done.2.n3
  29.7 10.7 %shard_map.229 = (bf16[3,1024,64]{2,1,0:T(8,128)(2,1)S(1)}, bf16[3,1024,64]{2,1,0:T(8,128)(2,1)S(1)}, bf16[3,1024,64]{2,1,0:T(8,128)(2,1)S(1)}, f32[3,4,256]{2,1...) custom-call(s32[8]{0:T(128)S(1)} %stack.139.ids, ...), custom_call_target="tpu_custom_call" | custom-call | flops 3320709120 | bytes 3141632 | tf_op jit(solution)/shard_map/pallas_call | solution.py:180
  42.8 2.1 collective-permute-start.5
  47.9 2.6 collective-permute-done.6.a2
  52.0 10.7 %shard_map.230 = (f32[256,767]{1,0:T(8,128)S(1)}, f32[256,3072]{1,0:T(8,128)S(1)}, bf16[256,767]{1,0:T(8,128)(2,1)S(1)}, bf16[256,767]{1,0:T(8,128)(2,1)S(1)}, f...) custom-call(s32[8]{0:T(128)S(1)} %stack.139.ids, bf16[256,767]{1,0:T(8,128)(2,1)S(1)} %shard_map.228.n0.x, ...), custom_call_target="tpu_custom_call" | custom-call | flops 3619160064 | bytes 12570624 | tf_op jit(solution)/shard_map/pallas_call | solution.py:275
  64.0 10.7 %collective-permute-done.11.n1 = bf16[256,767]{1,0:T(8,128)(2,1)S(1)} collective-permute-done((bf16[256,767]{1,0:T(8,128)(2,1)S(1)}, bf16[256,767]{1,0:T(8,128)(2,1)S(1)}, u32[]{:S(2)}, u32[]{:S(2)}) %collective-permute-start.11) | collective-permute-done | bytes 392736 | tf_op jit(solution)/shard_map/ppermute | solution.py:715
  74.7 7.8 %collective-permute-done.13.n3 = bf16[256,767]{1,0:T(8,128)(2,1)S(1)} collective-permute-done((bf16[256,767]{1,0:T(8,128)(2,1)S(1)}, bf16[256,767]{1,0:T(8,128)(2,1)S(1)}, u32[]{:S(2)}, u32[]{:S(2)}) %collective-permute-start.13) | collective-permute-done | bytes 392736 | tf_op jit(solution)/shard_map/ppermute | solution.py:710
  82.5 10.2 %shard_map.231 = (bf16[3,1024,64]{2,1,0:T(8,128)(2,1)S(1)}, bf16[3,1024,64]{2,1,0:T(8,128)(2,1)S(1)}, bf16[3,1024,64]{2,1,0:T(8,128)(2,1)S(1)}, f32[3,4,256]{2,1...) custom-call(s32[8]{0:T(128)S(1)} %stack.139.ids, ...), custom_call_target="tpu_custom_call" | custom-call | flops 3320709120 | bytes 3141632 | tf_op jit(solution)/shard_map/pallas_call | solution.py:180
  96.2 2.8 collective-permute-start.16
  101.7 12.3 %shard_map.232 = (f32[256,767]{1,0:T(8,128)S(1)}, f32[256,3072]{1,0:T(8,128)S(1)}, bf16[256,767]{1,0:T(8,128)(2,1)S(1)}, bf16[256,767]{1,0:T(8,128)(2,1)}, f32[8...) custom-call(s32[8]{0:T(128)S(1)} %stack.139.ids, bf16[256,767]{1,0:T(8,128)(2,1)S(1)} %get-tuple-element.895.x, ...), custom_call_target="tpu_custom_call" | custom-call | flops 3619160064 | bytes 12570624 | tf_op jit(solution)/shard_map/pallas_call | solution.py:275
  116.7 12.5 %shard_map.234 = (bf16[2,256,3072]{2,1,0:T(8,128)(2,1)S(1)}, bf16[3,4,256,192]{3,2,1,0:T(8,128)(2,1)S(1)}, f32[256,767]{1,0:T(8,128)S(1)}, f32[8,3072]{1,0:T(8,1...) custom-call(s32[8]{0:T(128)S(1)} %stack.139.ids, ...), custom_call_target="tpu_custom_call" | custom-call | flops 3619160064 | bytes 15716352 | tf_op jit(solution)/shard_map/pallas_call | solution.py:378
  132.4 2.1 collective-permute-start.18
  137.8 3.6 collective-permute-done.19.d2
  141.4 3.0 shard_map.236
  144.6 3.0 shard_map.237
  148.6 12.7 %shard_map.238 = (bf16[256,767]{1,0:T(8,128)(2,1)S(1)}, bf16[256,767]{1,0:T(8,128)(2,1)S(1)}, bf16[512,767]{1,0:T(8,128)(2,1)S(1)}, bf16[384,576]{1,0:T(8,128)(2...) custom-call(s32[8]{0:T(128)S(1)} %stack.139.ids, bf16[256,767]{1,0:T(8,128)(2,1)S(1)} %get-tuple-element.508.n0, ...), custom_call_target="tpu_custom_call" | custom-call | flops 7849377792 | bytes 6283264 | tf_op jit(solution)/shard_map/pallas_call | solution.py:501
  162.4 3.3 collective-permute-done.24
  167.3 3.2 add_convert_fusion.5
  170.5 3.4 collective-permute-done.22.r0
  175.5 6.4 %collective-permute-done.26.r1 = bf16[256,767]{1,0:T(8,128)(2,1)S(1)} collective-permute-done((bf16[256,767]{1,0:T(8,128)(2,1)S(1)}, bf16[256,767]{1,0:T(8,128)(2,1)S(1)}, u32[]{:S(2)}, u32[]{:S(2)}) %collective-permute-start.26) | collective-permute-done | bytes 392736 | tf_op jit(solution)/shard_map/ppermute | solution.py:715
  185.3 12.5 %shard_map.241 = (bf16[2,256,3072]{2,1,0:T(8,128)(2,1)S(1)}, bf16[3,4,256,192]{3,2,1,0:T(8,128)(2,1)S(1)}, f32[256,767]{1,0:T(8,128)S(1)}, f32[8,3072]{1,0:T(8,1...) custom-call(s32[8]{0:T(128)S(1)} %stack.139.ids, ...), custom_call_target="tpu_custom_call" | custom-call | flops 3619160064 | bytes 15716352 | tf_op jit(solution)/shard_map/pallas_call | solution.py:378
  197.9 3.0 shard_map.242
  203.5 3.0 shard_map.243
  208.9 5.3 %collective-permute-done.31 = bf16[192,3456]{1,0:T(8,128)(2,1)} collective-permute-done((bf16[192,3456]{1,0:T(8,128)(2,1)}, bf16[192,3456]{1,0:T(8,128)(2,1)}, u32[]{:S(2)}, u32[]{:S(2)}) %collective-permute-start.31) | collective-permute-done | bytes 1327136 | tf_op jit(solution)/shard_map/ppermute | solution.py:710
  215.4 2.2 add_convert_fusion.3
  220.8 3.5 shard_map.244
  239.7 13.5 %shard_map.245 = (bf16[256,767]{1,0:T(8,128)(2,1)S(1)}, bf16[256,767]{1,0:T(8,128)(2,1)S(1)}, bf16[512,767]{1,0:T(8,128)(2,1)}, bf16[384,576]{1,0:T(8,128)(2,1)}...) custom-call(s32[8]{0:T(128)S(1)} %stack.139.ids, bf16[256,767]{1,0:T(8,128)(2,1)S(1)} %copy-done.99, ...), custom_call_target="tpu_custom_call" | custom-call | flops 7849377792 | bytes 6283264 | tf_op jit(solution)/shard_map/pallas_call | solution.py:501
  255.4 2.8 shard_map.246
  258.3 3.3 add_convert_fusion.2
  267.8 2.7 collective-permute-start.42
  270.6 4.0 collective-permute-done.39.r1
  276.3 5.2 %collective-permute-done.36 = bf16[2,104,576]{2,1,0:T(8,128)(2,1)S(1)} collective-permute-done((bf16[2,104,576]{2,1,0:T(8,128)(2,1)S(1)}, bf16[2,104,576]{2,1,0:T(8,128)(2,1)S(1)}, u32[]{:S(2)}, u32[]{:S(2)}) %collective-permute-start.36) | collective-permute-done | bytes 239648 | tf_op jit(solution)/shard_map/ppermute | solution.py:728
  285.0 2.9 collective-permute-start.40
  287.9 11.4 %collective-permute-done.41 = bf16[192,3456]{1,0:T(8,128)(2,1)S(1)} collective-permute-done((bf16[192,3456]{1,0:T(8,128)(2,1)S(1)}, bf16[192,3456]{1,0:T(8,128)(2,1)S(1)}, u32[]{:S(2)}, u32[]{:S(2)}) %collective-permute-start.41) | collective-permute-done | bytes 1327136 | tf_op jit(solution)/shard_map/ppermute | solution.py:710
  303.4 5.8 %collective-permute-start.46 = (bf16[2,48,3456]{2,1,0:T(8,128)(2,1)}, bf16[2,48,3456]{2,1,0:T(8,128)(2,1)S(1)}, u32[]{:S(2)}, u32[]{:S(2)}) collective-permute-start(bf16[2,48,3456]{2,1,0:T(8,128)(2,1)} %maximum_select_fusion.2), channel_id=1, source_target_pairs={{0,4},{4,0},{8,12},{12,8},{1,5},{5,1},{9,13},{13,9},{2,6},{6,2},{1... | collective-permute-start | bytes 1990664 | tf_op jit(solution)/shard_map/ppermute | solution.py:728
  311.4 3.0 collective-permute-start.44
  314.5 5.0 collective-permute-done.45
  319.4 5.0 collective-permute-done.46
  334.7 10.4 %collective-permute-done.50 = bf16[2,48,3456]{2,1,0:T(8,128)(2,1)S(1)} collective-permute-done((bf16[2,48,3456]{2,1,0:T(8,128)(2,1)S(1)}, bf16[2,48,3456]{2,1,0:T(8,128)(2,1)S(1)}, u32[]{:S(2)}, u32[]{:S(2)}) %collective-permute-start.50) | collective-permute-done | bytes 663584 | tf_op jit(solution)/shard_map/ppermute | solution.py:728
  345.0 4.8 collective-permute-start.54
  350.1 7.7 %collective-permute-done.48.refs_3_ = bf16[192,3456]{1,0:T(8,128)(2,1)S(1)} collective-permute-done((bf16[192,3456]{1,0:T(8,128)(2,1)S(1)}, bf16[192,3456]{1,0:T(8,128)(2,1)S(1)}, u32[]{:S(2)}, u32[]{:S(2)}) %collective-permute-start.48) | collective-permute-done | bytes 1327136 | tf_op jit(solution)/shard_map/ppermute | solution.py:715
  357.8 5.7 %collective-permute-start.58 = (bf16[1,48,3456]{2,1,0:T(8,128)(2,1)S(1)}, bf16[1,48,3456]{2,1,0:T(8,128)(2,1)S(1)}, u32[]{:S(2)}, u32[]{:S(2)}) collective-permute-start(bf16[1,48,3456]{2,1,0:T(8,128)(2,1)S(1)} %get-tuple-element.842), channel_id=1, source_target_pairs={{0,8},{4,12},{8,0},{12,4},{1,9},{5,13},{9,1},{13,5},{2,10},{6,14},... | collective-permute-start | bytes 995336 | tf_op jit(solution)/shard_map/ppermute | solution.py:728
  365.1 10.4 %collective-permute-done.58 = bf16[1,48,3456]{2,1,0:T(8,128)(2,1)S(1)} collective-permute-done((bf16[1,48,3456]{2,1,0:T(8,128)(2,1)S(1)}, bf16[1,48,3456]{2,1,0:T(8,128)(2,1)S(1)}, u32[]{:S(2)}, u32[]{:S(2)}) %collective-permute-start.58) | collective-permute-done | bytes 331808 | tf_op jit(solution)/shard_map/ppermute | solution.py:728
  375.5 2.7 collective-permute-start.52
  378.4 3.0 collective-permute-start.62
  382.8 8.3 %collective-permute-done.52 = bf16[416,576]{1,0:T(8,128)(2,1)S(1)} collective-permute-done((bf16[416,576]{1,0:T(8,128)(2,1)S(1)}, bf16[416,576]{1,0:T(8,128)(2,1)S(1)}, u32[]{:S(2)}, u32[]{:S(2)}) %collective-permute-start.52) | collective-permute-done | bytes 479264 | tf_op jit(solution)/shard_map/ppermute | solution.py:715
  391.3 2.5 collective-permute-start.61
  395.6 2.6 collective-permute-done.61
  401.6 6.2 %collective-permute-done.63 = bf16[416,576]{1,0:T(8,128)(2,1)S(1)} collective-permute-done((bf16[416,576]{1,0:T(8,128)(2,1)S(1)}, bf16[416,576]{1,0:T(8,128)(2,1)S(1)}, u32[]{:S(2)}, u32[]{:S(2)}) %collective-permute-start.63) | collective-permute-done | bytes 479264 | tf_op jit(solution)/shard_map/ppermute | solution.py:715
  417.0 2.3 shard_map.248
  419.3 3.5 collective-permute-start.72
  422.8 3.7 shard_map.249
  426.5 2.5 shard_map.250
  429.0 25.3 %collective-permute-done.70 = bf16[2,416,576]{2,1,0:T(8,128)(2,1)S(1)} collective-permute-done((bf16[2,416,576]{2,1,0:T(8,128)(2,1)S(1)}, bf16[2,416,576]{2,1,0:T(8,128)(2,1)S(1)}, u32[]{:S(2)}, u32[]{:S(2)}) %collective-permute-start.70) | collective-permute-done | bytes 958496 | tf_op jit(solution)/shard_map/ppermute | solution.py:710
  461.4 2.9 collective-permute-done.73.refs_1_
  467.7 5.1 %shard_map.251 = (f32[767,1,3072]{2,1,0:T(1,128)}, f32[767,1,3072]{2,1,0:T(1,128)}, f32[767,1,768]{2,1,0:T(1,128)}) custom-call(s32[8]{0:T(128)S(1)} %stack.139.ids, bf16[192,3456]{1,0:T(8,128)(2,1)} %collective-permute-done.68.refs_0_, ...), custom_call_target="tpu_custom_call", output_to_operand_aliasing={{0}: (5, {}), {1}: (6, {}), {2}: (7, {})} | custom-call | bytes 7962624 | tf_op jit(solution)/shard_map/pallas_call | solution.py:620
  472.8 5.1 %shard_map.252 = (f32[767,1,3072]{2,1,0:T(1,128)}, f32[767,1,3072]{2,1,0:T(1,128)}, f32[767,1,768]{2,1,0:T(1,128)}) custom-call(s32[8]{0:T(128)S(1)} %stack.139.ids, bf16[192,3456]{1,0:T(8,128)(2,1)} %collective-permute-done.69.refs_0_, ...), custom_call_target="tpu_custom_call", output_to_operand_aliasing={{0}: (5, {}), {1}: (6, {}), {2}: (7, {})} | custom-call | bytes 7962624 | tf_op jit(solution)/shard_map/pallas_call | solution.py:620
  479.8 2.0 add_reduce_fusion
  483.2 7.3 %shard_map.253 = f32[767,1,2304]{2,1,0:T(1,128)} custom-call(s32[8]{0:T(128)S(1)} %stack.139.ids, bf16[4,416,576]{2,1,0:T(8,128)(2,1)} %pad_maximum_fusion.1.refs_0_, bf16[4,416,576]{2,1,0:T(8,128)(2,1)} %collective-permute-done.71.refs_1_, bf16[4,416,576]{2,1,0:T(8,128)(2,1)} %collective-permute-done.72.refs_2_, ...), custom_call_target="tpu_custom_call" | custom-call | bytes 10603008 | tf_op jit(solution)/shard_map/pallas_call | solution.py:692
  497.7 5.2 %shard_map.254 = (f32[767,1,3072]{2,1,0:T(1,128)}, f32[767,1,3072]{2,1,0:T(1,128)}, f32[767,1,768]{2,1,0:T(1,128)}) custom-call(s32[8]{0:T(128)S(1)} %stack.139.ids, bf16[192,3456]{1,0:T(8,128)(2,1)} %collective-permute-done.75.refs_0_, ...), custom_call_target="tpu_custom_call", output_to_operand_aliasing={{0}: (5, {}), {1}: (6, {}), {2}: (7, {})} | custom-call | bytes 7962624 | tf_op jit(solution)/shard_map/pallas_call | solution.py:620
  (476 shorter events, 139.1 us)
Async XLA Ops:
  0.7 51.2 %collective-permute-start.10 = (bf16[1,3072,767]{2,1,0:T(8,128)(2,1)}, bf16[1,3072,767]{2,1,0:T(8,128)(2,1)}, u32[]{:S(2)}, u32[]{:S(2)}) collective-permute-start(bf16[1,3072,767]{2,1,0:T(8,128)(2,1)} %dno.7), channel_id=1, source_target_pairs={{0,16},{16,0},{1,17},{17,1},{2,18},{18,2},{3,19},{19,3},{4,20},{20... | collective-permute-start | bytes 14137352 | tf_op jit(solution)/shard_map/ppermute | solution.py:723
  1.2 50.7 %collective-permute-start.9 = (bf16[1,767,3072]{2,1,0:T(8,128)(2,1)}, bf16[1,767,3072]{2,1,0:T(8,128)(2,1)}, u32[]{:S(2)}, u32[]{:S(2)}) collective-permute-start(bf16[1,767,3072]{2,1,0:T(8,128)(2,1)} %upo.7), channel_id=1, source_target_pairs={{0,16},{16,0},{1,17},{17,1},{2,18},{18,2},{3,19},{19,3},{4,20},{20... | collective-permute-start | bytes 14137352 | tf_op jit(solution)/shard_map/ppermute | solution.py:723
  12.0 8.7 %collective-permute-start.3 = (bf16[767,576]{0,1:T(8,128)(2,1)}, bf16[767,576]{0,1:T(8,128)(2,1)S(1)}, u32[]{:S(2)}, u32[]{:S(2)}) collective-permute-start(bf16[767,576]{0,1:T(8,128)(2,1)} %copy.51), channel_id=1, source_target_pairs={{0,16},{16,0},{1,17},{17,1},{2,18},{18,2},{3,19},{19,3},{4,20},{20... | collective-permute-start | bytes 2650760 | tf_op jit(solution)/shard_map/ppermute | solution.py:723
  12.4 8.3 %collective-permute-start = (bf16[256,767]{1,0:T(8,128)(2,1)S(1)}, bf16[256,767]{1,0:T(8,128)(2,1)S(1)}, u32[]{:S(2)}, u32[]{:S(2)}) collective-permute-start(bf16[256,767]{1,0:T(8,128)(2,1)S(1)} %shard_map.228.n0.x), channel_id=1, source_target_pairs={{0,2},{1,3},{2,0},{3,1},{16,17},{17,16},{18,19},{19,18},{4,6},{5,7... | collective-permute-start | bytes 1178120 | tf_op jit(solution)/shard_map/ppermute | solution.py:715
  17.4 9.6 %collective-permute-start.1 = (bf16[256,767]{1,0:T(8,128)(2,1)S(1)}, bf16[256,767]{1,0:T(8,128)(2,1)S(1)}, u32[]{:S(2)}, u32[]{:S(2)}) collective-permute-start(bf16[256,767]{1,0:T(8,128)(2,1)S(1)} %shard_map.228.n0.x), channel_id=1, source_target_pairs={{0,1},{1,0},{2,3},{3,2},{16,18},{17,19},{18,16},{19,17},{4,5},{5,4... | collective-permute-start | bytes 1178120 | tf_op jit(solution)/shard_map/ppermute | solution.py:710
  20.7 25.7 %collective-permute-start.8 = (bf16[768,767]{1,0:T(8,128)(2,1)}, bf16[768,767]{1,0:T(8,128)(2,1)}, u32[]{:S(2)}, u32[]{:S(2)}) collective-permute-start(bf16[768,767]{1,0:T(8,128)(2,1)} %bitcast.173), channel_id=1, source_target_pairs={{0,16},{16,0},{1,17},{17,1},{2,18},{18,2},{3,19},{19,3},{4,20},{20... | collective-permute-start | bytes 3534344 | tf_op jit(solution)/shard_map/ppermute | solution.py:723
  20.7 9.0 %collective-permute-start.2 = (bf16[256,767]{1,0:T(8,128)(2,1)S(1)}, bf16[256,767]{1,0:T(8,128)(2,1)S(1)}, u32[]{:S(2)}, u32[]{:S(2)}) collective-permute-start(bf16[256,767]{1,0:T(8,128)(2,1)S(1)} %collective-permute-done.n1), channel_id=1, source_target_pairs={{0,1},{1,0},{2,3},{3,2},{16,18},{17,19},{18,16},{19,17},{4,5},{5,4... | collective-permute-start | bytes 1178120 | tf_op jit(solution)/shard_map/ppermute | solution.py:710
  62.6 12.1 %collective-permute-start.11 = (bf16[256,767]{1,0:T(8,128)(2,1)S(1)}, bf16[256,767]{1,0:T(8,128)(2,1)S(1)}, u32[]{:S(2)}, u32[]{:S(2)}) collective-permute-start(bf16[256,767]{1,0:T(8,128)(2,1)S(1)} %get-tuple-element.508.n0), channel_id=1, source_target_pairs={{0,2},{1,3},{2,0},{3,1},{16,17},{17,16},{18,19},{19,18},{4,6},{5,7... | collective-permute-start | bytes 1178120 | tf_op jit(solution)/shard_map/ppermute | solution.py:715
  63.3 11.4 %collective-permute-start.12 = (bf16[256,767]{1,0:T(8,128)(2,1)S(1)}, bf16[256,767]{1,0:T(8,128)(2,1)S(1)}, u32[]{:S(2)}, u32[]{:S(2)}) collective-permute-start(bf16[256,767]{1,0:T(8,128)(2,1)S(1)} %get-tuple-element.508.n0), channel_id=1, source_target_pairs={{0,1},{1,0},{2,3},{3,2},{16,18},{17,19},{18,16},{19,17},{4,5},{5,4... | collective-permute-start | bytes 1178120 | tf_op jit(solution)/shard_map/ppermute | solution.py:710
  74.7 7.8 %collective-permute-start.13 = (bf16[256,767]{1,0:T(8,128)(2,1)S(1)}, bf16[256,767]{1,0:T(8,128)(2,1)S(1)}, u32[]{:S(2)}, u32[]{:S(2)}) collective-permute-start(bf16[256,767]{1,0:T(8,128)(2,1)S(1)} %collective-permute-done.11.n1), channel_id=1, source_target_pairs={{0,1},{1,0},{2,3},{3,2},{16,18},{17,19},{18,16},{19,17},{4,5},{5,4... | collective-permute-start | bytes 1178120 | tf_op jit(solution)/shard_map/ppermute | solution.py:710
  114.0 16.7 %collective-permute-start.17 = (bf16[256,767]{1,0:T(8,128)(2,1)S(1)}, bf16[256,767]{1,0:T(8,128)(2,1)S(1)}, u32[]{:S(2)}, u32[]{:S(2)}) collective-permute-start(bf16[256,767]{1,0:T(8,128)(2,1)S(1)} %broadcast_select_fusion.7), channel_id=1, source_target_pairs={{0,16},{16,0},{1,17},{17,1},{2,18},{18,2},{3,19},{19,3},{4,20},{20... | collective-permute-start | bytes 1178120 | tf_op jit(solution)/shard_map/ppermute | solution.py:723
  132.3 12.3 %collective-permute-start.21 = (bf16[2,192,3456]{2,1,0:T(8,128)(2,1)S(1)}, bf16[2,192,3456]{2,1,0:T(8,128)(2,1)S(1)}, u32[]{:S(2)}, u32[]{:S(2)}) collective-permute-start(bf16[2,192,3456]{2,1,0:T(8,128)(2,1)S(1)} %shard_map.235), channel_id=1, source_target_pairs={{0,16},{16,0},{1,17},{17,1},{2,18},{18,2},{3,19},{19,3},{4,20},{20... | collective-permute-start | bytes 7962632 | tf_op jit(solution)/shard_map/ppermute | solution.py:723
  144.5 17.9 %collective-permute-start.25 = (bf16[2,192,3456]{2,1,0:T(8,128)(2,1)}, bf16[2,192,3456]{2,1,0:T(8,128)(2,1)S(1)}, u32[]{:S(2)}, u32[]{:S(2)}) collective-permute-start(bf16[2,192,3456]{2,1,0:T(8,128)(2,1)} %shard_map.236), channel_id=1, source_target_pairs={{0,16},{16,0},{1,17},{17,1},{2,18},{18,2},{3,19},{19,3},{4,20},{20... | collective-permute-start | bytes 7962632 | tf_op jit(solution)/shard_map/ppermute | solution.py:723
  147.5 18.1 %collective-permute-start.24 = (bf16[192,3456]{1,0:T(8,128)(2,1)}, bf16[192,3456]{1,0:T(8,128)(2,1)}, u32[]{:S(2)}, u32[]{:S(2)}) collective-permute-start(bf16[192,3456]{1,0:T(8,128)(2,1)} %get-tuple-element.577), channel_id=1, source_target_pairs={{0,1},{1,0},{2,3},{3,2},{16,18},{17,19},{18,16},{19,17},{4,5},{5,4... | collective-permute-start | bytes 3981320 | tf_op jit(solution)/shard_map/ppermute | solution.py:710
  161.3 12.6 %collective-permute-start.22 = (bf16[512,767]{1,0:T(8,128)(2,1)S(1)}, bf16[512,767]{1,0:T(8,128)(2,1)S(1)}, u32[]{:S(2)}, u32[]{:S(2)}) collective-permute-start(bf16[512,767]{1,0:T(8,128)(2,1)S(1)} %get-tuple-element.575), channel_id=1, source_target_pairs={{0,1},{1,0},{2,3},{3,2},{16,18},{17,19},{18,16},{19,17},{4,5},{5,4... | collective-permute-start | bytes 2356232 | tf_op jit(solution)/shard_map/ppermute | solution.py:710
  162.4 8.1 %collective-permute-start.23 = (bf16[384,576]{1,0:T(8,128)(2,1)S(1)}, bf16[384,576]{1,0:T(8,128)(2,1)S(1)}, u32[]{:S(2)}, u32[]{:S(2)}) collective-permute-start(bf16[384,576]{1,0:T(8,128)(2,1)S(1)} %get-tuple-element.576), channel_id=1, source_target_pairs={{0,16},{16,0},{1,17},{17,1},{2,18},{18,2},{3,19},{19,3},{4,20},{20... | collective-permute-start | bytes 1327112 | tf_op jit(solution)/shard_map/ppermute | solution.py:723
  174.1 7.8 %collective-permute-start.26 = (bf16[256,767]{1,0:T(8,128)(2,1)S(1)}, bf16[256,767]{1,0:T(8,128)(2,1)S(1)}, u32[]{:S(2)}, u32[]{:S(2)}) collective-permute-start(bf16[256,767]{1,0:T(8,128)(2,1)S(1)} %add_convert_fusion.11), channel_id=1, source_target_pairs={{0,2},{1,3},{2,0},{3,1},{16,17},{17,16},{18,19},{19,18},{4,6},{5,7... | collective-permute-start | bytes 1178120 | tf_op jit(solution)/shard_map/ppermute | solution.py:715
  181.9 32.3 %collective-permute-start.31 = (bf16[192,3456]{1,0:T(8,128)(2,1)}, bf16[192,3456]{1,0:T(8,128)(2,1)}, u32[]{:S(2)}, u32[]{:S(2)}) collective-permute-start(bf16[192,3456]{1,0:T(8,128)(2,1)} %get-tuple-element.648), channel_id=1, source_target_pairs={{0,1},{1,0},{2,3},{3,2},{16,18},{17,19},{18,16},{19,17},{4,5},{5,4... | collective-permute-start | bytes 3981320 | tf_op jit(solution)/shard_map/ppermute | solution.py:710
  183.0 32.5 %collective-permute-start.32 = (bf16[192,3456]{1,0:T(8,128)(2,1)}, bf16[192,3456]{1,0:T(8,128)(2,1)}, u32[]{:S(2)}, u32[]{:S(2)}) collective-permute-start(bf16[192,3456]{1,0:T(8,128)(2,1)} %add_convert_fusion.5), channel_id=1, source_target_pairs={{0,2},{1,3},{2,0},{3,1},{16,17},{17,16},{18,19},{19,18},{4,6},{5,7... | collective-permute-start | bytes 3981320 | tf_op jit(solution)/shard_map/ppermute | solution.py:715
  201.0 19.8 %collective-permute-start.27 = (bf16[2,192,3456]{2,1,0:T(8,128)(2,1)}, bf16[2,192,3456]{2,1,0:T(8,128)(2,1)}, u32[]{:S(2)}, u32[]{:S(2)}) collective-permute-start(bf16[2,192,3456]{2,1,0:T(8,128)(2,1)} %shard_map.242), channel_id=1, source_target_pairs={{0,16},{16,0},{1,17},{17,1},{2,18},{18,2},{3,19},{19,3},{4,20},{20... | collective-permute-start | bytes 7962632 | tf_op jit(solution)/shard_map/ppermute | solution.py:723
  206.6 12.3 %collective-permute-start.28 = (bf16[192,256]{1,0:T(8,128)(2,1)S(1)}, bf16[192,256]{1,0:T(8,128)(2,1)S(1)}, u32[]{:S(2)}, u32[]{:S(2)}) collective-permute-start(bf16[192,256]{1,0:T(8,128)(2,1)S(1)} %copy-done.87), channel_id=1, source_target_pairs={{0,1},{1,0},{2,3},{3,2},{4,5},{5,4},{6,7},{7,6},{8,9},{9,8},{10,11... | collective-permute-start | bytes 294920 | tf_op jit(solution)/shard_map/ppermute | solution.py:719
  208.2 11.3 %collective-permute-start.29 = (bf16[192,256]{1,0:T(8,128)(2,1)S(1)}, bf16[192,256]{1,0:T(8,128)(2,1)S(1)}, u32[]{:S(2)}, u32[]{:S(2)}) collective-permute-start(bf16[192,256]{1,0:T(8,128)(2,1)S(1)} %copy-done.85), channel_id=1, source_target_pairs={{0,2},{1,3},{2,0},{3,1},{4,6},{5,7},{6,4},{7,5},{8,10},{9,11},{10,... | collective-permute-start | bytes 294920 | tf_op jit(solution)/shard_map/ppermute | solution.py:719
  215.4 38.3 %collective-permute-start.34 = (bf16[2,192,3456]{2,1,0:T(8,128)(2,1)}, bf16[2,192,3456]{2,1,0:T(8,128)(2,1)}, u32[]{:S(2)}, u32[]{:S(2)}) collective-permute-start(bf16[2,192,3456]{2,1,0:T(8,128)(2,1)} %shard_map.243), channel_id=1, source_target_pairs={{0,16},{16,0},{1,17},{17,1},{2,18},{18,2},{3,19},{19,3},{4,20},{20... | collective-permute-start | bytes 7962632 | tf_op jit(solution)/shard_map/ppermute | solution.py:723
  225.4 28.4 %collective-permute-start.33 = (bf16[192,3456]{1,0:T(8,128)(2,1)}, bf16[192,3456]{1,0:T(8,128)(2,1)}, u32[]{:S(2)}, u32[]{:S(2)}) collective-permute-start(bf16[192,3456]{1,0:T(8,128)(2,1)} %get-tuple-element.671), channel_id=1, source_target_pairs={{0,1},{1,0},{2,3},{3,2},{16,18},{17,19},{18,16},{19,17},{4,5},{5,4... | collective-permute-start | bytes 3981320 | tf_op jit(solution)/shard_map/ppermute | solution.py:710
  227.6 26.2 %collective-permute-start.35 = (bf16[2,48,3456]{2,1,0:T(8,128)(2,1)}, bf16[2,48,3456]{2,1,0:T(8,128)(2,1)S(1)}, u32[]{:S(2)}, u32[]{:S(2)}) collective-permute-start(bf16[2,48,3456]{2,1,0:T(8,128)(2,1)} %get-tuple-element.700), channel_id=1, source_target_pairs={{0,4},{4,0},{8,12},{12,8},{1,5},{5,1},{9,13},{13,9},{2,6},{6,2},{1... | collective-permute-start | bytes 1990664 | tf_op jit(solution)/shard_map/ppermute | solution.py:728
  253.2 12.4 %collective-permute-start.37 = (bf16[512,767]{1,0:T(8,128)(2,1)}, bf16[512,767]{1,0:T(8,128)(2,1)}, u32[]{:S(2)}, u32[]{:S(2)}) collective-permute-start(bf16[512,767]{1,0:T(8,128)(2,1)} %get-tuple-element.729), channel_id=1, source_target_pairs={{0,1},{1,0},{2,3},{3,2},{16,18},{17,19},{18,16},{19,17},{4,5},{5,4... | collective-permute-start | bytes 2356232 | tf_op jit(solution)/shard_map/ppermute | solution.py:710
  253.8 10.0 %collective-permute-start.38 = (bf16[384,576]{1,0:T(8,128)(2,1)}, bf16[384,576]{1,0:T(8,128)(2,1)}, u32[]{:S(2)}, u32[]{:S(2)}) collective-permute-start(bf16[384,576]{1,0:T(8,128)(2,1)} %get-tuple-element.730), channel_id=1, source_target_pairs={{0,16},{16,0},{1,17},{17,1},{2,18},{18,2},{3,19},{19,3},{4,20},{20... | collective-permute-start | bytes 1327112 | tf_op jit(solution)/shard_map/ppermute | solution.py:723
  266.7 7.8 %collective-permute-start.39 = (bf16[256,767]{1,0:T(8,128)(2,1)S(1)}, bf16[256,767]{1,0:T(8,128)(2,1)S(1)}, u32[]{:S(2)}, u32[]{:S(2)}) collective-permute-start(bf16[256,767]{1,0:T(8,128)(2,1)S(1)} %add_convert_fusion.10), channel_id=1, source_target_pairs={{0,2},{1,3},{2,0},{3,1},{16,17},{17,16},{18,19},{19,18},{4,6},{5,7... | collective-permute-start | bytes 1178120 | tf_op jit(solution)/shard_map/ppermute | solution.py:715
  267.5 14.0 %collective-permute-start.36 = (bf16[2,104,576]{2,1,0:T(8,128)(2,1)S(1)}, bf16[2,104,576]{2,1,0:T(8,128)(2,1)S(1)}, u32[]{:S(2)}, u32[]{:S(2)}) collective-permute-start(bf16[2,104,576]{2,1,0:T(8,128)(2,1)S(1)} %get-tuple-element.727), channel_id=1, source_target_pairs={{0,4},{4,0},{8,12},{12,8},{1,5},{5,1},{9,13},{13,9},{2,6},{6,2},{1... | collective-permute-start | bytes 718856 | tf_op jit(solution)/shard_map/ppermute | solution.py:728
  267.8 16.5 %collective-permute-start.42 = (bf16[1,48,3456]{2,1,0:T(8,128)(2,1)S(1)}, bf16[1,48,3456]{2,1,0:T(8,128)(2,1)S(1)}, u32[]{:S(2)}, u32[]{:S(2)}) collective-permute-start(bf16[1,48,3456]{2,1,0:T(8,128)(2,1)S(1)} %copy-done.114), channel_id=1, source_target_pairs={{0,8},{4,12},{8,0},{12,4},{1,9},{5,13},{9,1},{13,5},{2,10},{6,14},... | collective-permute-start | bytes 995336 | tf_op jit(solution)/shard_map/ppermute | solution.py:728
  281.5 17.8 %collective-permute-start.41 = (bf16[192,3456]{1,0:T(8,128)(2,1)S(1)}, bf16[192,3456]{1,0:T(8,128)(2,1)S(1)}, u32[]{:S(2)}, u32[]{:S(2)}) collective-permute-start(bf16[192,3456]{1,0:T(8,128)(2,1)S(1)} %copy-done.67), channel_id=1, source_target_pairs={{0,1},{1,0},{2,3},{3,2},{16,18},{17,19},{18,16},{19,17},{4,5},{5,4... | collective-permute-start | bytes 3981320 | tf_op jit(solution)/shard_map/ppermute | solution.py:710
  284.4 14.9 %collective-permute-start.43 = (bf16[1,48,3456]{2,1,0:T(8,128)(2,1)S(1)}, bf16[1,48,3456]{2,1,0:T(8,128)(2,1)S(1)}, u32[]{:S(2)}, u32[]{:S(2)}) collective-permute-start(bf16[1,48,3456]{2,1,0:T(8,128)(2,1)S(1)} %add_convert_fusion.13), channel_id=1, source_target_pairs={{0,8},{4,12},{8,0},{12,4},{1,9},{5,13},{9,1},{13,5},{2,10},{6,14},... | collective-permute-start | bytes 995336 | tf_op jit(solution)/shard_map/ppermute | solution.py:728
  285.0 25.5 %collective-permute-start.40 = (bf16[1,104,576]{2,1,0:T(8,128)(2,1)}, bf16[1,104,576]{2,1,0:T(8,128)(2,1)}, u32[]{:S(2)}, u32[]{:S(2)}) collective-permute-start(bf16[1,104,576]{2,1,0:T(8,128)(2,1)} %get-tuple-element.757), channel_id=1, source_target_pairs={{0,8},{4,12},{8,0},{12,4},{1,9},{5,13},{9,1},{13,5},{2,10},{6,14},... | collective-permute-start | bytes 359432 | tf_op jit(solution)/shard_map/ppermute | solution.py:728
  301.3 18.2 %collective-permute-start.45 = (bf16[192,3456]{1,0:T(8,128)(2,1)}, bf16[192,3456]{1,0:T(8,128)(2,1)}, u32[]{:S(2)}, u32[]{:S(2)}) collective-permute-start(bf16[192,3456]{1,0:T(8,128)(2,1)} %add_convert_fusion.2), channel_id=1, source_target_pairs={{0,2},{1,3},{2,0},{3,1},{16,17},{17,16},{18,19},{19,18},{4,6},{5,7... | collective-permute-start | bytes 3981320 | tf_op jit(solution)/shard_map/ppermute | solution.py:715
  303.4 21.0 %collective-permute-start.46 = (bf16[2,48,3456]{2,1,0:T(8,128)(2,1)}, bf16[2,48,3456]{2,1,0:T(8,128)(2,1)S(1)}, u32[]{:S(2)}, u32[]{:S(2)}) collective-permute-start(bf16[2,48,3456]{2,1,0:T(8,128)(2,1)} %maximum_select_fusion.2), channel_id=1, source_target_pairs={{0,4},{4,0},{8,12},{12,8},{1,5},{5,1},{9,13},{13,9},{2,6},{6,2},{1... | collective-permute-start | bytes 1990664 | tf_op jit(solution)/shard_map/ppermute | solution.py:728
  311.4 19.6 %collective-permute-start.44 = (bf16[1,104,576]{2,1,0:T(8,128)(2,1)S(1)}, bf16[1,104,576]{2,1,0:T(8,128)(2,1)S(1)}, u32[]{:S(2)}, u32[]{:S(2)}) collective-permute-start(bf16[1,104,576]{2,1,0:T(8,128)(2,1)S(1)} %add_convert_fusion.17), channel_id=1, source_target_pairs={{0,8},{4,12},{8,0},{12,4},{1,9},{5,13},{9,1},{13,5},{2,10},{6,14},... | collective-permute-start | bytes 359432 | tf_op jit(solution)/shard_map/ppermute | solution.py:728
  314.4 18.1 %collective-permute-start.51 = (bf16[2,104,576]{2,1,0:T(8,128)(2,1)S(1)}, bf16[2,104,576]{2,1,0:T(8,128)(2,1)S(1)}, u32[]{:S(2)}, u32[]{:S(2)}) collective-permute-start(bf16[2,104,576]{2,1,0:T(8,128)(2,1)S(1)} %fusion.7), channel_id=1, source_target_pairs={{0,4},{4,0},{8,12},{12,8},{1,5},{5,1},{9,13},{13,9},{2,6},{6,2},{1... | collective-permute-start | bytes 718856 | tf_op jit(solution)/shard_map/ppermute | solution.py:728
  328.0 17.0 %collective-permute-start.50 = (bf16[2,48,3456]{2,1,0:T(8,128)(2,1)S(1)}, bf16[2,48,3456]{2,1,0:T(8,128)(2,1)S(1)}, u32[]{:S(2)}, u32[]{:S(2)}) collective-permute-start(bf16[2,48,3456]{2,1,0:T(8,128)(2,1)S(1)} %fusion.3), channel_id=1, source_target_pairs={{0,4},{4,0},{8,12},{12,8},{1,5},{5,1},{9,13},{13,9},{2,6},{6,2},{1... | collective-permute-start | bytes 1990664 | tf_op jit(solution)/shard_map/ppermute | solution.py:728
  328.5 29.3 %collective-permute-start.48 = (bf16[192,3456]{1,0:T(8,128)(2,1)S(1)}, bf16[192,3456]{1,0:T(8,128)(2,1)S(1)}, u32[]{:S(2)}, u32[]{:S(2)}) collective-permute-start(bf16[192,3456]{1,0:T(8,128)(2,1)S(1)} %bitcast.148), channel_id=1, source_target_pairs={{0,2},{1,3},{2,0},{3,1},{16,17},{17,16},{18,19},{19,18},{4,6},{5,7... | collective-permute-start | bytes 3981320 | tf_op jit(solution)/shard_map/ppermute | solution.py:715
  330.0 33.5 %collective-permute-start.49 = (bf16[192,3456]{1,0:T(8,128)(2,1)S(1)}, bf16[192,3456]{1,0:T(8,128)(2,1)S(1)}, u32[]{:S(2)}, u32[]{:S(2)}) collective-permute-start(bf16[192,3456]{1,0:T(8,128)(2,1)S(1)} %bitcast.149), channel_id=1, source_target_pairs={{0,1},{1,0},{2,3},{3,2},{16,18},{17,19},{18,16},{19,17},{4,5},{5,4... | collective-permute-start | bytes 3981320 | tf_op jit(solution)/shard_map/ppermute | solution.py:710
  331.1 47.3 %collective-permute-start.57 = (bf16[192,3456]{1,0:T(8,128)(2,1)S(1)}, bf16[192,3456]{1,0:T(8,128)(2,1)S(1)}, u32[]{:S(2)}, u32[]{:S(2)}) collective-permute-start(bf16[192,3456]{1,0:T(8,128)(2,1)S(1)} %bitcast.150), channel_id=1, source_target_pairs={{0,16},{1,17},{2,18},{3,19},{4,20},{5,21},{6,22},{7,23},{8,24},{9,... | collective-permute-start | bytes 3981320 | tf_op jit(solution)/shard_map/ppermute | solution.py:732
  332.6 30.8 %collective-permute-start.47 = (bf16[2,104,576]{2,1,0:T(8,128)(2,1)S(1)}, bf16[2,104,576]{2,1,0:T(8,128)(2,1)S(1)}, u32[]{:S(2)}, u32[]{:S(2)}) collective-permute-start(bf16[2,104,576]{2,1,0:T(8,128)(2,1)S(1)} %maximum_select_fusion.6), channel_id=1, source_target_pairs={{0,4},{4,0},{8,12},{12,8},{1,5},{5,1},{9,13},{13,9},{2,6},{6,2},{1... | collective-permute-start | bytes 718856 | tf_op jit(solution)/shard_map/ppermute | solution.py:728
  345.0 20.1 %collective-permute-start.54 = (bf16[1,104,576]{2,1,0:T(8,128)(2,1)S(1)}, bf16[1,104,576]{2,1,0:T(8,128)(2,1)S(1)}, u32[]{:S(2)}, u32[]{:S(2)}) collective-permute-start(bf16[1,104,576]{2,1,0:T(8,128)(2,1)S(1)} %get-tuple-element.835), channel_id=1, source_target_pairs={{0,8},{4,12},{8,0},{12,4},{1,9},{5,13},{9,1},{13,5},{2,10},{6,14},... | collective-permute-start | bytes 359432 | tf_op jit(solution)/shard_map/ppermute | solution.py:728
  357.8 17.7 %collective-permute-start.58 = (bf16[1,48,3456]{2,1,0:T(8,128)(2,1)S(1)}, bf16[1,48,3456]{2,1,0:T(8,128)(2,1)S(1)}, u32[]{:S(2)}, u32[]{:S(2)}) collective-permute-start(bf16[1,48,3456]{2,1,0:T(8,128)(2,1)S(1)} %get-tuple-element.842), channel_id=1, source_target_pairs={{0,8},{4,12},{8,0},{12,4},{1,9},{5,13},{9,1},{13,5},{2,10},{6,14},... | collective-permute-start | bytes 995336 | tf_op jit(solution)/shard_map/ppermute | solution.py:728
  363.5 17.9 %collective-permute-start.56 = (bf16[192,3456]{1,0:T(8,128)(2,1)S(1)}, bf16[192,3456]{1,0:T(8,128)(2,1)S(1)}, u32[]{:S(2)}, u32[]{:S(2)}) collective-permute-start(bf16[192,3456]{1,0:T(8,128)(2,1)S(1)} %collective-permute-done.48.refs_3_), channel_id=1, source_target_pairs={{0,1},{1,0},{2,3},{3,2},{16,18},{17,19},{18,16},{19,17},{4,5},{5,4... | collective-permute-start | bytes 3981320 | tf_op jit(solution)/shard_map/ppermute | solution.py:710
  363.5 27.7 %collective-permute-start.53 = (bf16[192,3456]{1,0:T(8,128)(2,1)S(1)}, bf16[192,3456]{1,0:T(8,128)(2,1)S(1)}, u32[]{:S(2)}, u32[]{:S(2)}) collective-permute-start(bf16[192,3456]{1,0:T(8,128)(2,1)S(1)} %collective-permute-done.48.refs_3_), channel_id=1, source_target_pairs={{0,16},{1,17},{2,18},{3,19},{4,20},{5,21},{6,22},{7,23},{8,24},{9,... | collective-permute-start | bytes 3981320 | tf_op jit(solution)/shard_map/ppermute | solution.py:732
  375.5 7.2 %collective-permute-start.55 = (bf16[1,104,576]{2,1,0:T(8,128)(2,1)S(1)}, bf16[1,104,576]{2,1,0:T(8,128)(2,1)S(1)}, u32[]{:S(2)}, u32[]{:S(2)}) collective-permute-start(bf16[1,104,576]{2,1,0:T(8,128)(2,1)S(1)} %add_convert_fusion.16), channel_id=1, source_target_pairs={{0,8},{4,12},{8,0},{12,4},{1,9},{5,13},{9,1},{13,5},{2,10},{6,14},... | collective-permute-start | bytes 359432 | tf_op jit(solution)/shard_map/ppermute | solution.py:728
  375.5 15.6 %collective-permute-start.52 = (bf16[416,576]{1,0:T(8,128)(2,1)S(1)}, bf16[416,576]{1,0:T(8,128)(2,1)S(1)}, u32[]{:S(2)}, u32[]{:S(2)}) collective-permute-start(bf16[416,576]{1,0:T(8,128)(2,1)S(1)} %bitcast.168), channel_id=1, source_target_pairs={{0,2},{1,3},{2,0},{3,1},{16,17},{17,16},{18,19},{19,18},{4,6},{5,7... | collective-permute-start | bytes 1437704 | tf_op jit(solution)/shard_map/ppermute | solution.py:715
  378.4 13.0 %collective-permute-start.62 = (bf16[1,48,3456]{2,1,0:T(8,128)(2,1)S(1)}, bf16[1,48,3456]{2,1,0:T(8,128)(2,1)S(1)}, u32[]{:S(2)}, u32[]{:S(2)}) collective-permute-start(bf16[1,48,3456]{2,1,0:T(8,128)(2,1)S(1)} %add_convert_fusion.12), channel_id=1, source_target_pairs={{0,8},{4,12},{8,0},{12,4},{1,9},{5,13},{9,1},{13,5},{2,10},{6,14},... | collective-permute-start | bytes 995336 | tf_op jit(solution)/shard_map/ppermute | solution.py:728
  381.4 20.2 %collective-permute-start.60 = (bf16[192,3456]{1,0:T(8,128)(2,1)S(1)}, bf16[192,3456]{1,0:T(8,128)(2,1)S(1)}, u32[]{:S(2)}, u32[]{:S(2)}) collective-permute-start(bf16[192,3456]{1,0:T(8,128)(2,1)S(1)} %collective-permute-done.49.refs_3_), channel_id=1, source_target_pairs={{0,16},{1,17},{2,18},{3,19},{4,20},{5,21},{6,22},{7,23},{8,24},{9,... | collective-permute-start | bytes 3981320 | tf_op jit(solution)/shard_map/ppermute | solution.py:732
  393.8 15.0 %collective-permute-start.59 = (bf16[2,416,576]{2,1,0:T(8,128)(2,1)S(1)}, bf16[2,416,576]{2,1,0:T(8,128)(2,1)S(1)}, u32[]{:S(2)}, u32[]{:S(2)}) collective-permute-start(bf16[2,416,576]{2,1,0:T(8,128)(2,1)S(1)} %pad_maximum_fusion.2), channel_id=1, source_target_pairs={{0,1},{1,0},{2,3},{3,2},{16,18},{17,19},{18,16},{19,17},{4,5},{5,4... | collective-permute-start | bytes 2875400 | tf_op jit(solution)/shard_map/ppermute | solution.py:710
  395.4 13.4 %collective-permute-start.65 = (bf16[2,48,3456]{2,1,0:T(8,128)(2,1)S(1)}, bf16[2,48,3456]{2,1,0:T(8,128)(2,1)S(1)}, u32[]{:S(2)}, u32[]{:S(2)}) collective-permute-start(bf16[2,48,3456]{2,1,0:T(8,128)(2,1)S(1)} %maximum_select_fusion.3), channel_id=1, source_target_pairs={{0,4},{4,0},{8,12},{12,8},{1,5},{5,1},{9,13},{13,9},{2,6},{6,2},{1... | collective-permute-start | bytes 1990664 | tf_op jit(solution)/shard_map/ppermute | solution.py:728
  398.4 9.3 %collective-permute-start.63 = (bf16[416,576]{1,0:T(8,128)(2,1)S(1)}, bf16[416,576]{1,0:T(8,128)(2,1)S(1)}, u32[]{:S(2)}, u32[]{:S(2)}) collective-permute-start(bf16[416,576]{1,0:T(8,128)(2,1)S(1)} %bitcast.170), channel_id=1, source_target_pairs={{0,2},{1,3},{2,0},{3,1},{16,17},{17,16},{18,19},{19,18},{4,6},{5,7... | collective-permute-start | bytes 1437704 | tf_op jit(solution)/shard_map/ppermute | solution.py:715
  400.2 14.4 %collective-permute-start.64 = (bf16[192,3456]{1,0:T(8,128)(2,1)S(1)}, bf16[192,3456]{1,0:T(8,128)(2,1)S(1)}, u32[]{:S(2)}, u32[]{:S(2)}) collective-permute-start(bf16[192,3456]{1,0:T(8,128)(2,1)S(1)} %collective-permute-done.56.refs_3_), channel_id=1, source_target_pairs={{0,16},{1,17},{2,18},{3,19},{4,20},{5,21},{6,22},{7,23},{8,24},{9,... | collective-permute-start | bytes 3981320 | tf_op jit(solution)/shard_map/ppermute | solution.py:732
  409.2 13.6 %collective-permute-start.66 = (bf16[192,3456]{1,0:T(8,128)(2,1)S(1)}, bf16[192,3456]{1,0:T(8,128)(2,1)S(1)}, u32[]{:S(2)}, u32[]{:S(2)}) collective-permute-start(bf16[192,3456]{1,0:T(8,128)(2,1)S(1)} %bitcast.152), channel_id=1, source_target_pairs={{16,0},{17,1},{18,2},{19,3},{20,4},{21,5},{22,6},{23,7},{24,8},{25... | collective-permute-start | bytes 3981320 | tf_op jit(solution)/shard_map/ppermute | solution.py:732
  410.6 43.7 %collective-permute-start.68 = (bf16[192,3456]{1,0:T(8,128)(2,1)S(1)}, bf16[192,3456]{1,0:T(8,128)(2,1)}, u32[]{:S(2)}, u32[]{:S(2)}) collective-permute-start(bf16[192,3456]{1,0:T(8,128)(2,1)S(1)} %bitcast.153), channel_id=1, source_target_pairs={{0,2},{1,3},{2,0},{3,1},{16,17},{17,16},{18,19},{19,18},{4,6},{5,7... | collective-permute-start | bytes 3981320 | tf_op jit(solution)/shard_map/ppermute | solution.py:715
  412.3 42.0 %collective-permute-start.69 = (bf16[192,3456]{1,0:T(8,128)(2,1)S(1)}, bf16[192,3456]{1,0:T(8,128)(2,1)}, u32[]{:S(2)}, u32[]{:S(2)}) collective-permute-start(bf16[192,3456]{1,0:T(8,128)(2,1)S(1)} %bitcast.154), channel_id=1, source_target_pairs={{0,1},{1,0},{2,3},{3,2},{16,18},{17,19},{18,16},{19,17},{4,5},{5,4... | collective-permute-start | bytes 3981320 | tf_op jit(solution)/shard_map/ppermute | solution.py:710
  412.9 41.4 %collective-permute-start.70 = (bf16[2,416,576]{2,1,0:T(8,128)(2,1)S(1)}, bf16[2,416,576]{2,1,0:T(8,128)(2,1)S(1)}, u32[]{:S(2)}, u32[]{:S(2)}) collective-permute-start(bf16[2,416,576]{2,1,0:T(8,128)(2,1)S(1)} %pad_maximum_fusion.3), channel_id=1, source_target_pairs={{0,1},{1,0},{2,3},{3,2},{16,18},{17,19},{18,16},{19,17},{4,5},{5,4... | collective-permute-start | bytes 2875400 | tf_op jit(solution)/shard_map/ppermute | solution.py:710
  419.3 53.5 %collective-permute-start.72 = (bf16[4,416,576]{2,1,0:T(8,128)(2,1)S(1)}, bf16[4,416,576]{2,1,0:T(8,128)(2,1)}, u32[]{:S(2)}, u32[]{:S(2)}) collective-permute-start(bf16[4,416,576]{2,1,0:T(8,128)(2,1)S(1)} %pad_maximum_fusion.refs_3_), channel_id=1, source_target_pairs={{0,16},{1,17},{2,18},{3,19},{4,20},{5,21},{6,22},{7,23},{8,24},{9,... | collective-permute-start | bytes 5750792 | tf_op jit(solution)/shard_map/ppermute | solution.py:732
  456.0 16.8 %collective-permute-start.71 = (bf16[4,416,576]{2,1,0:T(8,128)(2,1)}, bf16[4,416,576]{2,1,0:T(8,128)(2,1)}, u32[]{:S(2)}, u32[]{:S(2)}) collective-permute-start(bf16[4,416,576]{2,1,0:T(8,128)(2,1)} %pad_maximum_fusion.1.refs_0_), channel_id=1, source_target_pairs={{16,0},{17,1},{18,2},{19,3},{20,4},{21,5},{22,6},{23,7},{24,8},{25... | collective-permute-start | bytes 5750792 | tf_op jit(solution)/shard_map/ppermute | solution.py:732
  457.3 7.0 %collective-permute-start.73 = (bf16[192,3456]{1,0:T(8,128)(2,1)}, bf16[192,3456]{1,0:T(8,128)(2,1)}, u32[]{:S(2)}, u32[]{:S(2)}) collective-permute-start(bf16[192,3456]{1,0:T(8,128)(2,1)} %collective-permute-done.68.refs_0_), channel_id=1, source_target_pairs={{16,0},{17,1},{18,2},{19,3},{20,4},{21,5},{22,6},{23,7},{24,8},{25... | collective-permute-start | bytes 3981320 | tf_op jit(solution)/shard_map/ppermute | solution.py:732
  458.6 7.8 %collective-permute-start.74 = (bf16[192,3456]{1,0:T(8,128)(2,1)}, bf16[192,3456]{1,0:T(8,128)(2,1)}, u32[]{:S(2)}, u32[]{:S(2)}) collective-permute-start(bf16[192,3456]{1,0:T(8,128)(2,1)} %collective-permute-done.69.refs_0_), channel_id=1, source_target_pairs={{16,0},{17,1},{18,2},{19,3},{20,4},{21,5},{22,6},{23,7},{24,8},{25... | collective-permute-start | bytes 3981320 | tf_op jit(solution)/shard_map/ppermute | solution.py:732
  459.9 18.2 %collective-permute-start.75 = (bf16[192,3456]{1,0:T(8,128)(2,1)}, bf16[192,3456]{1,0:T(8,128)(2,1)}, u32[]{:S(2)}, u32[]{:S(2)}) collective-permute-start(bf16[192,3456]{1,0:T(8,128)(2,1)} %collective-permute-done.68.refs_0_), channel_id=1, source_target_pairs={{0,1},{1,0},{2,3},{3,2},{16,18},{17,19},{18,16},{19,17},{4,5},{5,4... | collective-permute-start | bytes 3981320 | tf_op jit(solution)/shard_map/ppermute | solution.py:710
  478.0 19.7 %collective-permute-start.76 = (bf16[192,3456]{1,0:T(8,128)(2,1)}, bf16[192,3456]{1,0:T(8,128)(2,1)}, u32[]{:S(2)}, u32[]{:S(2)}) collective-permute-start(bf16[192,3456]{1,0:T(8,128)(2,1)} %collective-permute-done.75.refs_0_), channel_id=1, source_target_pairs={{16,0},{17,1},{18,2},{19,3},{20,4},{21,5},{22,6},{23,7},{24,8},{25... | collective-permute-start | bytes 3981320 | tf_op jit(solution)/shard_map/ppermute | solution.py:732
  (136 other events, 1232.9 us)

commit v5 on v4

--- a/solution.py
+++ b/solution.py
@@ -186,7 +186,7 @@
             pltpu.VMEM((QUAD, heads * hd, span), BF16),
             pltpu.VMEM((full, span), F32),
         ],
-        compiler_params=params(40),
+        compiler_params=params(22),
         cost_estimate=cost(
             2 * full * width * 3 * heads * hd + 3 * 4 * full * full * hd * heads,
             4 * full * width,
@@ -283,7 +283,7 @@
             jax.ShapeDtypeStruct((8, 128), F32),
             jax.ShapeDtypeStruct((QUAD, span, rows), BF16),
         ],
-        compiler_params=params(40, dimension_semantics=("arbitrary",)),
+        compiler_params=params(22, dimension_semantics=("arbitrary",)),
         cost_estimate=cost(6 * span * cc * ff, 4 * cc * ff + 4 * span * ff, span * ff),
     )(ids, x, *att, wo, pv, pvn, pv, up[0], up[1], dn[0], dn[1])
 
@@ -385,7 +385,7 @@
             jax.ShapeDtypeStruct((8, ff), F32),
             dd, dd, dd, dd,
         ],
-        compiler_params=params(40, dimension_semantics=("arbitrary",)),
+        compiler_params=params(24, dimension_semantics=("arbitrary",)),
         cost_estimate=cost(6 * span * cc * ff, 4 * cc * ff + 8 * span * ff, span * ff),
     )(ids, df, u, mid, wo, pv, up[0], up[1], dn[0], dn[1])
 
@@ -420,7 +420,7 @@
         out_shape=jax.ShapeDtypeStruct((len(places), quarter, cols), BF16)
         if send
         else [jax.ShapeDtypeStruct((quarter, cols), BF16)] * len(places),
-        compiler_params=params(32),
+        compiler_params=params(22),
         cost_estimate=cost(2 * span * quarter * cols * len(places), 2 * 4 * quarter * cols * len(places)),
     )(ids, lr, rr, att, *got)
 
@@ -518,7 +518,7 @@
             pltpu.VMEM((heads, QUAD, span), F32),
             pltpu.SemaphoreType.DMA((9,)),
         ],
-        compiler_params=params(48),
+        compiler_params=params(30),
         cost_estimate=cost(
             4 * full * cc * 3 * width + 3 * 10 * full * full * hd * heads,
             8 * full * cc,
@@ -631,7 +631,7 @@
             pltpu.VMEM((2, n, rows, 1, cols - ff), F32),
             pltpu.SemaphoreType.DMA((6, n)),
         ],
-        compiler_params=params(40),
+        compiler_params=params(16),
         cost_estimate=cost(0, 12 * n * rows * cols),
     )(*operands)
 
@@ -700,8 +700,72 @@
             pltpu.VMEM((2, half // 2, 1, QUAD * cols), F32),
             pltpu.SemaphoreType.DMA((2, 2 * QUAD)),
         ],
-        compiler_params=params(32),
+        compiler_params=params(18),
         cost_estimate=cost(0, 6 * cc * QUAD * cols),
+    )(ids, *srcs)
+
+
+def vectors_kernel(count, ids, *refs):
+    srcs, outs, (rows, heads, sem) = refs[:4], refs[4:-3], refs[-3:]
+    c, s = ids[0], ids[1]
+    _, _, tall, row_len = rows.shape
+    top = srcs[0].shape[1] - tall
+
+    def reads(pair):
+        return [
+            pltpu.make_async_copy(v.at[p, pl.ds(top, tall), :], rows.at[i, p], sem.at[i * QUAD + p])
+            for i, v in enumerate(pair)
+            for p in range(QUAD)
+        ]
+
+    for core in range(2):
+
+        @pl.when(c == core)
+        def _():
+            for m in reads(srcs[2 * core : 2 * core + 2]):
+                m.start()
+
+    for m in reads(srcs[:2]):
+        m.wait()
+    total = jnp.zeros((tall, row_len), F32)
+    for i in range(2):
+        for p in range(QUAD):
+            total = total + rows[i, p].astype(F32)
+    at = 0
+    for o in outs[:5]:
+        n = o.shape[1]
+        for lo in range(0, n, row_len):
+            size = min(row_len, n - lo)
+            o[0:1, lo : lo + size] = total[at : at + 1, :size]
+            at += 1
+    heads[...] = jnp.zeros_like(heads)
+    for i in range(2):
+        for p in range(QUAD):
+            k = p if i else ((p & 1) << 1) | (p >> 1)
+            heads[jnp.bitwise_xor(k, s)] += rows[i, p, at : at + 8, :].astype(F32)
+    width = row_len // 3
+    for part in range(2):
+        for t in range(QUAD):
+            lo = (part * QUAD + t) * width
+            outs[5][0:1, lo : lo + width] = heads[t, 0:1, part * width : (part + 1) * width]
+    outs[6][0:1, :] = jnp.sqrt(total[at + 1 : at + 2, : outs[6].shape[1]] / count)
+
+
+def vectors_out(ids, srcs, count, cc, ff, model):
+    row_len = srcs[0].shape[-1]
+    shapes = [ff, cc, cc, cc, cc, 2 * model, 128]
+    return pl.pallas_call(
+        functools.partial(vectors_kernel, count),
+        in_specs=[SMEM] + [HBM] * 4,
+        out_specs=[VMEM] * 7,
+        out_shape=[jax.ShapeDtypeStruct((1, n), F32) for n in shapes],
+        scratch_shapes=[
+            pltpu.VMEM((2, QUAD, 32, row_len), BF16),
+            pltpu.VMEM((QUAD, 8, row_len), F32),
+            pltpu.SemaphoreType.DMA((2 * QUAD,)),
+        ],
+        compiler_params=params(8),
+        cost_estimate=cost(0, 1 << 19),
     )(ids, *srcs)
 
 
@@ -893,13 +957,15 @@
         return run(lambda *v: input_grad_of(*v, saved[l][0], pv[l]), p0, pr, q, dmid)
 
     def projection(l, gk, gs_got, g, gb, gg):
-        pad = jnp.zeros((1,), F32)
         heads_sum = jnp.concatenate([gb[0, :width], gb[0, 2 * width :]])
-        v = jnp.concatenate(
-            [g[0], g[1, :cc], pad, g[2, :cc], pad, gg[0, :cc], pad, g[4, :cc], pad]
-            + [jnp.broadcast_to(squares[l], (128,)), heads_sum]
-        )
-        v = jnp.pad(v, (0, 32 * 3 * width - v.shape[0])).reshape(32, 3 * width).astype(BF16)
+        row_len = 3 * width
+        vectors = [
+            g[0], g[1, :cc], g[2, :cc], gg[0, :cc], g[4, :cc], heads_sum,
+            jnp.broadcast_to(squares[l], (row_len,)),
+        ]
+        v = [jnp.pad(x, (0, -x.shape[0] % row_len)) for x in vectors]
+        v = jnp.concatenate(v).reshape(-1, row_len)
+        v = jnp.pad(v, ((0, 32 - v.shape[0]), (0, 0))).astype(BF16)
         return jnp.concatenate([add_low(gk, gs_got), v])
 
     def wait(*v):
@@ -1037,6 +1103,10 @@
     outs_w = place((1,), outs_w)
     qkv0_got, qkv1_got = wait(qkv0_got, qkv1_got)
     outs_w = place((2,), outs_w)
+    count = micro * dp_count * span * QUAD
+    vectors = run(
+        lambda *v: vectors_out(ids, v, count, cc, ff, model), qkv0, qkv0_got, qkv1_got, qkv1
+    )
     have0[3] = wait(have0[3])
 
     got0.append(to_owner(0, have0[3]))
@@ -1046,43 +1116,21 @@
         (3,), order_of.token, [v[3] for v in (have0, got0, got1, have1)], outs_w, cc, ff, model
     )
 
-    half = (cc + 1) // 2
-    tails = [v[:, half:].astype(F32).reshape(QUAD, -1) for v in (qkv0, qkv0_got, qkv1_got, qkv1)]
-    tails = [jnp.where(mine, tails[0], tails[2]), jnp.where(mine, tails[1], tails[3])]
-    small = jnp.sum(tails[0] + tails[1], 0)
-
-    def take(lo, n):
-        return small[lo : lo + n][None]
-
-    d = cc + 1
-    at = ff
-    total = micro * dp_count * span * QUAD
-    base = ff + 4 * d
-    rms = jnp.sqrt(small[base] / total).reshape(1)
-    seq_of = jnp.arange(QUAD)
-    heads_of = jnp.zeros((QUAD, 2 * width), F32)
-    for chain in range(2):
-        for p in range(QUAD):
-            here = seq_of == jnp.bitwise_xor(order(chain, p), s)
-            row_of = tails[chain][p, base + 128 : base + 128 + 2 * width]
-            heads_of = heads_of + jnp.where(here[:, None], row_of, 0.0)
-    grad_bqv = jnp.concatenate(
-        [heads_of[:, i * width : (i + 1) * width].reshape(model) for i in range(2)]
-    )
+    grad_bup, grad_bout, grad_bdown, grad_ga, grad_gm, grad_bqv, rms = vectors
     return (
         layer_out,
         input_grad,
         jnp.transpose(grad_qkv, (1, 0, 2)),
-        grad_bqv[None],
+        grad_bqv,
         jnp.transpose(grad_out, (1, 2, 0)),
-        take(at, cc),
-        take(at + 2 * d, cc),
-        take(at + 3 * d, cc),
+        grad_bout,
+        grad_ga,
+        grad_gm,
         jnp.transpose(grad_up, (1, 0, 2)),
-        take(0, ff),
+        grad_bup,
         jnp.transpose(grad_down, (1, 2, 0)),
-        take(at + d, cc),
-        rms,
+        grad_bdown,
+        rms[0, :1],
     )
 
 

time: 511 us -> 495 us (0.969)
  local copies, waits for them, and re-layouts: 48.7 us -> 38.9 us
  other arithmetic: 31.7 us -> 24 us
  waiting for transfers between devices: 164 us -> 170 us
    ppermute x10, waiting for transfers between devices: 49.2 us -> 41.4 us  [to_second(): return lax.ppermute(v, ('section', 'seq'), pairs)]
    ppermute x16, waiting for transfers between devices: 62 us -> 69.4 us  [to_first(): return lax.ppermute(v, ('section', 'seq'), pairs)]
    ppermute x16, waiting for transfers between devices: 34.8 us -> 40.8 us  [dp_partner(): return lax.ppermute(v, 'dp', [(i, i ^ step) for i in range(n)])]
    ppermute x16, starting transfers between devices: 35.1 us -> 40.4 us  [dp_partner(): return lax.ppermute(v, 'dp', [(i, i ^ step) for i in range(n)])]
    unnamed x246 -> x232, local copies, waits for them, and re-layouts: 30.1 us -> 27.7 us
  transfers between devices with their start and end apart: 77 -> 77, of which waited for: 32 -> 37; matrix products, arithmetic and copies ran while one was open for 10% -> 7% of each run, Pallas kernels for 22% -> 23%
where the time goes in v5:
time: 495 us; the launch traced here: 490 us
  waiting for transfers between devices  170 us (34%)
  Pallas kernels  148 us (30%)
  starting transfers between devices  103 us (21%)
  local copies, waits for them, and re-layouts  38.9 us (8%)
  other arithmetic  24 us (5%)
  between operations  5.71 us (1%)
    ppermute x16, waiting for transfers between devices, to_first(): return lax.ppermute(v, ('section', 'seq'), pairs)  69.4 us
    ppermute x10, waiting for transfers between devices, to_second(): return lax.ppermute(v, ('section', 'seq'), pairs)  41.4 us
    ppermute x16, waiting for transfers between devices, dp_partner(): return lax.ppermute(v, 'dp', [(i, i ^ step) for i in range(n)])  40.8 us
    ppermute x16, starting transfers between devices, dp_partner(): return lax.ppermute(v, 'dp', [(i, i ^ step) for i in range(n)])  40.4 us
    unnamed x232, local copies, waits for them, and re-layouts  27.7 us
    pallas_call x2, Pallas kernels, attn_bwd(): pl.pallas_call(attn_bwd_kernel, in_specs=[SMEM] + [HBM] * 9 + [VMEM] * 4,...  26.6 us
    pallas_call x2, Pallas kernels, mlp_bwd(): pl.pallas_call(functools.partial(mlp_bwd_kernel, layer), grid_spec=grid,...  23.9 us
    pallas_call x2, Pallas kernels, mlp_fwd(): pl.pallas_call(functools.partial(mlp_fwd_kernel, layer), grid_spec=grid,...  21.8 us
  transfers between devices with their start and end apart: 77, of which 37 were waited for; matrix products, arithmetic and copies ran while one was open for 7% of the time, Pallas kernels for 23%

profile of v5, /device:TPU:0, one launch (start us, length us, event | category | flops | bytes accessed | tf_op | source)
XLA Modules:
  0.0 489.9 jit_solution(721762881173035101)
XLA Ops:
  7.9 3.1 dynamic-slice_bitcast_fusion.2
  14.0 2.6 collective-permute-start
  20.6 2.4 collective-permute-done.n1
  22.9 2.4 collective-permute-start.2
  28.8 2.4 collective-permute-done.2.n3
  33.0 10.7 %shard_map.229 = (bf16[3,1024,64]{2,1,0:T(8,128)(2,1)S(1)}, bf16[3,1024,64]{2,1,0:T(8,128)(2,1)S(1)}, bf16[3,1024,64]{2,1,0:T(8,128)(2,1)S(1)}, f32[3,4,256]{2,1...) custom-call(s32[8]{0:T(128)S(1)} %stack.139.ids, ...), custom_call_target="tpu_custom_call" | custom-call | flops 3320709120 | bytes 3141632 | tf_op jit(solution)/shard_map/pallas_call | solution.py:180
  43.8 2.1 collective-permute-start.5
  45.9 2.3 collective-permute-start.6
  53.7 9.7 %shard_map.230 = (f32[256,767]{1,0:T(8,128)S(1)}, f32[256,3072]{1,0:T(8,128)S(1)}, bf16[256,767]{1,0:T(8,128)(2,1)S(1)}, bf16[256,767]{1,0:T(8,128)(2,1)S(1)}, f...) custom-call(s32[8]{0:T(128)S(1)} %stack.139.ids, bf16[256,767]{1,0:T(8,128)(2,1)S(1)} %shard_map.228.n0.x, ...), custom_call_target="tpu_custom_call" | custom-call | flops 3619160064 | bytes 12570624 | tf_op jit(solution)/shard_map/pallas_call | solution.py:275
  64.7 10.8 %collective-permute-done.11.n1 = bf16[256,767]{1,0:T(8,128)(2,1)S(1)} collective-permute-done((bf16[256,767]{1,0:T(8,128)(2,1)S(1)}, bf16[256,767]{1,0:T(8,128)(2,1)S(1)}, u32[]{:S(2)}, u32[]{:S(2)}) %collective-permute-start.11) | collective-permute-done | bytes 392736 | tf_op jit(solution)/shard_map/ppermute | solution.py:779
  75.5 7.8 %collective-permute-done.13.n3 = bf16[256,767]{1,0:T(8,128)(2,1)S(1)} collective-permute-done((bf16[256,767]{1,0:T(8,128)(2,1)S(1)}, bf16[256,767]{1,0:T(8,128)(2,1)S(1)}, u32[]{:S(2)}, u32[]{:S(2)}) %collective-permute-start.13) | collective-permute-done | bytes 392736 | tf_op jit(solution)/shard_map/ppermute | solution.py:774
  83.3 10.2 %shard_map.231 = (bf16[3,1024,64]{2,1,0:T(8,128)(2,1)S(1)}, bf16[3,1024,64]{2,1,0:T(8,128)(2,1)S(1)}, bf16[3,1024,64]{2,1,0:T(8,128)(2,1)S(1)}, f32[3,4,256]{2,1...) custom-call(s32[8]{0:T(128)S(1)} %stack.139.ids, ...), custom_call_target="tpu_custom_call" | custom-call | flops 3320709120 | bytes 3141632 | tf_op jit(solution)/shard_map/pallas_call | solution.py:180
  94.1 3.0 collective-permute-start.16
  99.7 12.1 %shard_map.232 = (f32[256,767]{1,0:T(8,128)S(1)}, f32[256,3072]{1,0:T(8,128)S(1)}, bf16[256,767]{1,0:T(8,128)(2,1)S(1)}, bf16[256,767]{1,0:T(8,128)(2,1)}, f32[8...) custom-call(s32[8]{0:T(128)S(1)} %stack.139.ids, bf16[256,767]{1,0:T(8,128)(2,1)S(1)} %get-tuple-element.915.x, ...), custom_call_target="tpu_custom_call" | custom-call | flops 3619160064 | bytes 12570624 | tf_op jit(solution)/shard_map/pallas_call | solution.py:275
  118.1 12.2 %shard_map.234 = (bf16[2,256,3072]{2,1,0:T(8,128)(2,1)S(1)}, bf16[3,4,256,192]{3,2,1,0:T(8,128)(2,1)S(1)}, f32[256,767]{1,0:T(8,128)S(1)}, f32[8,3072]{1,0:T(8,1...) custom-call(s32[8]{0:T(128)S(1)} %stack.139.ids, ...), custom_call_target="tpu_custom_call" | custom-call | flops 3619160064 | bytes 15716352 | tf_op jit(solution)/shard_map/pallas_call | solution.py:378
  132.0 1.9 collective-permute-start.18
  137.3 2.7 collective-permute-done.19.d2
  142.8 2.7 shard_map.237
  146.7 13.0 %shard_map.238 = (bf16[256,767]{1,0:T(8,128)(2,1)S(1)}, bf16[256,767]{1,0:T(8,128)(2,1)S(1)}, bf16[512,767]{1,0:T(8,128)(2,1)S(1)}, bf16[384,576]{1,0:T(8,128)(2...) custom-call(s32[8]{0:T(128)S(1)} %stack.139.ids, bf16[256,767]{1,0:T(8,128)(2,1)S(1)} %copy-done.56, ...), custom_call_target="tpu_custom_call" | custom-call | flops 7849377792 | bytes 6283264 | tf_op jit(solution)/shard_map/pallas_call | solution.py:501
  160.6 2.6 collective-permute-done.24
  166.3 5.4 %collective-permute-done.22.r0 = bf16[512,767]{1,0:T(8,128)(2,1)S(1)} collective-permute-done((bf16[512,767]{1,0:T(8,128)(2,1)S(1)}, bf16[512,767]{1,0:T(8,128)(2,1)S(1)}, u32[]{:S(2)}, u32[]{:S(2)}) %collective-permute-start.22) | collective-permute-done | bytes 785440 | tf_op jit(solution)/shard_map/ppermute | solution.py:774
  173.3 6.4 %collective-permute-done.26.r1 = bf16[256,767]{1,0:T(8,128)(2,1)S(1)} collective-permute-done((bf16[256,767]{1,0:T(8,128)(2,1)S(1)}, bf16[256,767]{1,0:T(8,128)(2,1)S(1)}, u32[]{:S(2)}, u32[]{:S(2)}) %collective-permute-start.26) | collective-permute-done | bytes 392736 | tf_op jit(solution)/shard_map/ppermute | solution.py:779
  183.1 11.8 %shard_map.241 = (bf16[2,256,3072]{2,1,0:T(8,128)(2,1)S(1)}, bf16[3,4,256,192]{3,2,1,0:T(8,128)(2,1)S(1)}, f32[256,767]{1,0:T(8,128)S(1)}, f32[8,3072]{1,0:T(8,1...) custom-call(s32[8]{0:T(128)S(1)} %stack.139.ids, ...), custom_call_target="tpu_custom_call" | custom-call | flops 3619160064 | bytes 15716352 | tf_op jit(solution)/shard_map/pallas_call | solution.py:378
  195.0 3.3 shard_map.242
  200.3 3.0 shard_map.243
  205.1 6.9 %collective-permute-done.31 = bf16[192,3456]{1,0:T(8,128)(2,1)} collective-permute-done((bf16[192,3456]{1,0:T(8,128)(2,1)}, bf16[192,3456]{1,0:T(8,128)(2,1)}, u32[]{:S(2)}, u32[]{:S(2)}) %collective-permute-start.31) | collective-permute-done | bytes 1327136 | tf_op jit(solution)/shard_map/ppermute | solution.py:774
  213.9 2.4 add_convert_fusion.3
  219.4 3.5 shard_map.244
  239.3 13.6 %shard_map.245 = (bf16[256,767]{1,0:T(8,128)(2,1)S(1)}, bf16[256,767]{1,0:T(8,128)(2,1)S(1)}, bf16[512,767]{1,0:T(8,128)(2,1)}, bf16[384,576]{1,0:T(8,128)(2,1)}...) custom-call(s32[8]{0:T(128)S(1)} %stack.139.ids, bf16[256,767]{1,0:T(8,128)(2,1)S(1)} %copy-done.92, ...), custom_call_target="tpu_custom_call" | custom-call | flops 7849377792 | bytes 6283264 | tf_op jit(solution)/shard_map/pallas_call | solution.py:501
  255.1 2.8 shard_map.246
  257.9 3.2 add_convert_fusion.2
  262.8 2.5 collective-permute-done.37.r0
  267.6 2.6 collective-permute-start.42
  270.2 4.1 collective-permute-done.39.r1
  276.0 4.9 collective-permute-done.36
  284.5 2.9 collective-permute-start.40
  287.4 11.3 %collective-permute-done.41 = bf16[192,3456]{1,0:T(8,128)(2,1)S(1)} collective-permute-done((bf16[192,3456]{1,0:T(8,128)(2,1)S(1)}, bf16[192,3456]{1,0:T(8,128)(2,1)S(1)}, u32[]{:S(2)}, u32[]{:S(2)}) %collective-permute-start.41) | collective-permute-done | bytes 1327136 | tf_op jit(solution)/shard_map/ppermute | solution.py:774
  301.8 6.1 %collective-permute-start.46 = (bf16[2,48,3456]{2,1,0:T(8,128)(2,1)S(1)}, bf16[2,48,3456]{2,1,0:T(8,128)(2,1)S(1)}, u32[]{:S(2)}, u32[]{:S(2)}) collective-permute-start(bf16[2,48,3456]{2,1,0:T(8,128)(2,1)S(1)} %maximum_select_fusion.2), channel_id=1, source_target_pairs={{0,4},{4,0},{8,12},{12,8},{1,5},{5,1},{9,13},{13,9},{2,6},{6,2},{1... | collective-permute-start | bytes 1990664 | tf_op jit(solution)/shard_map/ppermute | solution.py:792
  310.9 3.0 collective-permute-start.44
  314.0 3.6 collective-permute-done.45
  317.7 7.5 %collective-permute-done.46 = bf16[2,48,3456]{2,1,0:T(8,128)(2,1)S(1)} collective-permute-done((bf16[2,48,3456]{2,1,0:T(8,128)(2,1)S(1)}, bf16[2,48,3456]{2,1,0:T(8,128)(2,1)S(1)}, u32[]{:S(2)}, u32[]{:S(2)}) %collective-permute-start.46) | collective-permute-done | bytes 663584 | tf_op jit(solution)/shard_map/ppermute | solution.py:792
  332.4 11.3 %collective-permute-done.50 = bf16[2,48,3456]{2,1,0:T(8,128)(2,1)S(1)} collective-permute-done((bf16[2,48,3456]{2,1,0:T(8,128)(2,1)S(1)}, bf16[2,48,3456]{2,1,0:T(8,128)(2,1)S(1)}, u32[]{:S(2)}, u32[]{:S(2)}) %collective-permute-start.50) | collective-permute-done | bytes 663584 | tf_op jit(solution)/shard_map/ppermute | solution.py:792
  343.7 5.7 %collective-permute-start.54 = (bf16[1,104,576]{2,1,0:T(8,128)(2,1)S(1)}, bf16[1,104,576]{2,1,0:T(8,128)(2,1)S(1)}, u32[]{:S(2)}, u32[]{:S(2)}) collective-permute-start(bf16[1,104,576]{2,1,0:T(8,128)(2,1)S(1)} %get-tuple-element.855), channel_id=1, source_target_pairs={{0,8},{4,12},{8,0},{12,4},{1,9},{5,13},{9,1},{13,5},{2,10},{6,14},... | collective-permute-start | bytes 359432 | tf_op jit(solution)/shard_map/ppermute | solution.py:792
  350.0 10.0 %collective-permute-start.58 = (bf16[1,48,3456]{2,1,0:T(8,128)(2,1)S(1)}, bf16[1,48,3456]{2,1,0:T(8,128)(2,1)S(1)}, u32[]{:S(2)}, u32[]{:S(2)}) collective-permute-start(bf16[1,48,3456]{2,1,0:T(8,128)(2,1)S(1)} %get-tuple-element.862), channel_id=1, source_target_pairs={{0,8},{4,12},{8,0},{12,4},{1,9},{5,13},{9,1},{13,5},{2,10},{6,14},... | collective-permute-start | bytes 995336 | tf_op jit(solution)/shard_map/ppermute | solution.py:792
  362.7 11.6 %collective-permute-done.58 = bf16[1,48,3456]{2,1,0:T(8,128)(2,1)S(1)} collective-permute-done((bf16[1,48,3456]{2,1,0:T(8,128)(2,1)S(1)}, bf16[1,48,3456]{2,1,0:T(8,128)(2,1)S(1)}, u32[]{:S(2)}, u32[]{:S(2)}) %collective-permute-start.58) | collective-permute-done | bytes 331808 | tf_op jit(solution)/shard_map/ppermute | solution.py:792
  374.4 4.0 collective-permute-start.52
  378.5 3.0 collective-permute-start.62
  382.9 7.8 %collective-permute-done.52 = bf16[416,576]{1,0:T(8,128)(2,1)S(1)} collective-permute-done((bf16[416,576]{1,0:T(8,128)(2,1)S(1)}, bf16[416,576]{1,0:T(8,128)(2,1)S(1)}, u32[]{:S(2)}, u32[]{:S(2)}) %collective-permute-start.52) | collective-permute-done | bytes 479264 | tf_op jit(solution)/shard_map/ppermute | solution.py:779
  390.9 3.3 collective-permute-start.61
  395.0 3.7 collective-permute-done.61
  398.9 2.1 collective-permute-start.63
  402.4 5.9 %collective-permute-done.63 = bf16[416,576]{1,0:T(8,128)(2,1)S(1)} collective-permute-done((bf16[416,576]{1,0:T(8,128)(2,1)S(1)}, bf16[416,576]{1,0:T(8,128)(2,1)S(1)}, u32[]{:S(2)}, u32[]{:S(2)}) %collective-permute-start.63) | collective-permute-done | bytes 479264 | tf_op jit(solution)/shard_map/ppermute | solution.py:779
  411.1 2.1 collective-permute-start.68
  417.6 2.3 shard_map.248
  421.8 3.9 shard_map.249
  425.7 2.3 shard_map.250
  428.0 26.8 %collective-permute-done.70 = bf16[2,416,576]{2,1,0:T(8,128)(2,1)S(1)} collective-permute-done((bf16[2,416,576]{2,1,0:T(8,128)(2,1)S(1)}, bf16[2,416,576]{2,1,0:T(8,128)(2,1)S(1)}, u32[]{:S(2)}, u32[]{:S(2)}) %collective-permute-start.70) | collective-permute-done | bytes 958496 | tf_op jit(solution)/shard_map/ppermute | solution.py:774
  459.5 3.6 collective-permute-done.73.refs_1_
  463.1 1.9 collective-permute-done.74.refs_1_
  465.0 3.7 shard_map.251
  468.7 3.7 shard_map.252
  474.1 2.7 collective-permute-done.75.refs_0_
  478.1 7.8 %shard_map.254 = f32[767,1,2304]{2,1,0:T(1,128)} custom-call(s32[8]{0:T(128)S(1)} %stack.139.ids, bf16[4,416,576]{2,1,0:T(8,128)(2,1)S(1)} %pad_maximum_fusion.1.refs_0_, bf16[4,416,576]{2,1,0:T(8,128)(2,1)S(1)} %collective-permute-done.71.refs_1_, bf16[4,416,576]{2,1,0:T(8,128)(2,1)S(1)} %collective-permute-done.72.refs_2_, ...), custom_call_target="tpu_custom_call" | custom-call | bytes 10603008 | tf_op jit(solution)/shard_map/pallas_call | solution.py:692
  485.9 3.7 shard_map.255
  (454 shorter events, 123.8 us)
Async XLA Ops:
  0.7 53.0 %collective-permute-start.10 = (bf16[1,3072,767]{2,1,0:T(8,128)(2,1)}, bf16[1,3072,767]{2,1,0:T(8,128)(2,1)}, u32[]{:S(2)}, u32[]{:S(2)}) collective-permute-start(bf16[1,3072,767]{2,1,0:T(8,128)(2,1)} %dno.7), channel_id=1, source_target_pairs={{0,16},{16,0},{1,17},{17,1},{2,18},{18,2},{3,19},{19,3},{4,20},{20... | collective-permute-start | bytes 14137352 | tf_op jit(solution)/shard_map/ppermute | solution.py:787
  1.2 52.5 %collective-permute-start.9 = (bf16[1,767,3072]{2,1,0:T(8,128)(2,1)}, bf16[1,767,3072]{2,1,0:T(8,128)(2,1)}, u32[]{:S(2)}, u32[]{:S(2)}) collective-permute-start(bf16[1,767,3072]{2,1,0:T(8,128)(2,1)} %upo.7), channel_id=1, source_target_pairs={{0,16},{16,0},{1,17},{17,1},{2,18},{18,2},{3,19},{19,3},{4,20},{20... | collective-permute-start | bytes 14137352 | tf_op jit(solution)/shard_map/ppermute | solution.py:787
  13.5 9.4 %collective-permute-start.3 = (bf16[767,576]{0,1:T(8,128)(2,1)S(1)}, bf16[767,576]{0,1:T(8,128)(2,1)}, u32[]{:S(2)}, u32[]{:S(2)}) collective-permute-start(bf16[767,576]{0,1:T(8,128)(2,1)S(1)} %copy.51), channel_id=1, source_target_pairs={{0,16},{16,0},{1,17},{17,1},{2,18},{18,2},{3,19},{19,3},{4,20},{20... | collective-permute-start | bytes 2650760 | tf_op jit(solution)/shard_map/ppermute | solution.py:787
  14.0 8.9 %collective-permute-start = (bf16[256,767]{1,0:T(8,128)(2,1)S(1)}, bf16[256,767]{1,0:T(8,128)(2,1)S(1)}, u32[]{:S(2)}, u32[]{:S(2)}) collective-permute-start(bf16[256,767]{1,0:T(8,128)(2,1)S(1)} %shard_map.228.n0.x), channel_id=1, source_target_pairs={{0,2},{1,3},{2,0},{3,1},{16,17},{17,16},{18,19},{19,18},{4,6},{5,7... | collective-permute-start | bytes 1178120 | tf_op jit(solution)/shard_map/ppermute | solution.py:779
  19.1 9.6 %collective-permute-start.1 = (bf16[256,767]{1,0:T(8,128)(2,1)S(1)}, bf16[256,767]{1,0:T(8,128)(2,1)S(1)}, u32[]{:S(2)}, u32[]{:S(2)}) collective-permute-start(bf16[256,767]{1,0:T(8,128)(2,1)S(1)} %shard_map.228.n0.x), channel_id=1, source_target_pairs={{0,1},{1,0},{2,3},{3,2},{16,18},{17,19},{18,16},{19,17},{4,5},{5,4... | collective-permute-start | bytes 1178120 | tf_op jit(solution)/shard_map/ppermute | solution.py:774
  22.9 25.2 %collective-permute-start.8 = (bf16[768,767]{1,0:T(8,128)(2,1)}, bf16[768,767]{1,0:T(8,128)(2,1)}, u32[]{:S(2)}, u32[]{:S(2)}) collective-permute-start(bf16[768,767]{1,0:T(8,128)(2,1)} %bitcast.11), channel_id=1, source_target_pairs={{0,16},{16,0},{1,17},{17,1},{2,18},{18,2},{3,19},{19,3},{4,20},{20... | collective-permute-start | bytes 3534344 | tf_op jit(solution)/shard_map/ppermute | solution.py:787
  22.9 8.2 %collective-permute-start.2 = (bf16[256,767]{1,0:T(8,128)(2,1)S(1)}, bf16[256,767]{1,0:T(8,128)(2,1)S(1)}, u32[]{:S(2)}, u32[]{:S(2)}) collective-permute-start(bf16[256,767]{1,0:T(8,128)(2,1)S(1)} %collective-permute-done.n1), channel_id=1, source_target_pairs={{0,1},{1,0},{2,3},{3,2},{16,18},{17,19},{18,16},{19,17},{4,5},{5,4... | collective-permute-start | bytes 1178120 | tf_op jit(solution)/shard_map/ppermute | solution.py:774
  63.5 12.0 %collective-permute-start.11 = (bf16[256,767]{1,0:T(8,128)(2,1)S(1)}, bf16[256,767]{1,0:T(8,128)(2,1)S(1)}, u32[]{:S(2)}, u32[]{:S(2)}) collective-permute-start(bf16[256,767]{1,0:T(8,128)(2,1)S(1)} %get-tuple-element.528.n0), channel_id=1, source_target_pairs={{0,2},{1,3},{2,0},{3,1},{16,17},{17,16},{18,19},{19,18},{4,6},{5,7... | collective-permute-start | bytes 1178120 | tf_op jit(solution)/shard_map/ppermute | solution.py:779
  64.2 11.3 %collective-permute-start.12 = (bf16[256,767]{1,0:T(8,128)(2,1)S(1)}, bf16[256,767]{1,0:T(8,128)(2,1)S(1)}, u32[]{:S(2)}, u32[]{:S(2)}) collective-permute-start(bf16[256,767]{1,0:T(8,128)(2,1)S(1)} %get-tuple-element.528.n0), channel_id=1, source_target_pairs={{0,1},{1,0},{2,3},{3,2},{16,18},{17,19},{18,16},{19,17},{4,5},{5,4... | collective-permute-start | bytes 1178120 | tf_op jit(solution)/shard_map/ppermute | solution.py:774
  75.5 7.8 %collective-permute-start.13 = (bf16[256,767]{1,0:T(8,128)(2,1)S(1)}, bf16[256,767]{1,0:T(8,128)(2,1)S(1)}, u32[]{:S(2)}, u32[]{:S(2)}) collective-permute-start(bf16[256,767]{1,0:T(8,128)(2,1)S(1)} %collective-permute-done.11.n1), channel_id=1, source_target_pairs={{0,1},{1,0},{2,3},{3,2},{16,18},{17,19},{18,16},{19,17},{4,5},{5,4... | collective-permute-start | bytes 1178120 | tf_op jit(solution)/shard_map/ppermute | solution.py:774
  113.5 16.8 %collective-permute-start.17 = (bf16[256,767]{1,0:T(8,128)(2,1)S(1)}, bf16[256,767]{1,0:T(8,128)(2,1)S(1)}, u32[]{:S(2)}, u32[]{:S(2)}) collective-permute-start(bf16[256,767]{1,0:T(8,128)(2,1)S(1)} %broadcast_select_fusion.7), channel_id=1, source_target_pairs={{0,16},{16,0},{1,17},{17,1},{2,18},{18,2},{3,19},{19,3},{4,20},{20... | collective-permute-start | bytes 1178120 | tf_op jit(solution)/shard_map/ppermute | solution.py:787
  131.9 10.9 %collective-permute-start.21 = (bf16[2,192,3456]{2,1,0:T(8,128)(2,1)S(1)}, bf16[2,192,3456]{2,1,0:T(8,128)(2,1)S(1)}, u32[]{:S(2)}, u32[]{:S(2)}) collective-permute-start(bf16[2,192,3456]{2,1,0:T(8,128)(2,1)S(1)} %shard_map.235), channel_id=1, source_target_pairs={{0,16},{16,0},{1,17},{17,1},{2,18},{18,2},{3,19},{19,3},{4,20},{20... | collective-permute-start | bytes 7962632 | tf_op jit(solution)/shard_map/ppermute | solution.py:787
  142.7 17.9 %collective-permute-start.25 = (bf16[2,192,3456]{2,1,0:T(8,128)(2,1)S(1)}, bf16[2,192,3456]{2,1,0:T(8,128)(2,1)S(1)}, u32[]{:S(2)}, u32[]{:S(2)}) collective-permute-start(bf16[2,192,3456]{2,1,0:T(8,128)(2,1)S(1)} %shard_map.236), channel_id=1, source_target_pairs={{0,16},{16,0},{1,17},{17,1},{2,18},{18,2},{3,19},{19,3},{4,20},{20... | collective-permute-start | bytes 7962632 | tf_op jit(solution)/shard_map/ppermute | solution.py:787
  145.4 17.8 %collective-permute-start.24 = (bf16[192,3456]{1,0:T(8,128)(2,1)S(1)}, bf16[192,3456]{1,0:T(8,128)(2,1)S(1)}, u32[]{:S(2)}, u32[]{:S(2)}) collective-permute-start(bf16[192,3456]{1,0:T(8,128)(2,1)S(1)} %get-tuple-element.597), channel_id=1, source_target_pairs={{0,1},{1,0},{2,3},{3,2},{16,18},{17,19},{18,16},{19,17},{4,5},{5,4... | collective-permute-start | bytes 3981320 | tf_op jit(solution)/shard_map/ppermute | solution.py:774
  159.7 12.1 %collective-permute-start.22 = (bf16[512,767]{1,0:T(8,128)(2,1)S(1)}, bf16[512,767]{1,0:T(8,128)(2,1)S(1)}, u32[]{:S(2)}, u32[]{:S(2)}) collective-permute-start(bf16[512,767]{1,0:T(8,128)(2,1)S(1)} %get-tuple-element.595), channel_id=1, source_target_pairs={{0,1},{1,0},{2,3},{3,2},{16,18},{17,19},{18,16},{19,17},{4,5},{5,4... | collective-permute-start | bytes 2356232 | tf_op jit(solution)/shard_map/ppermute | solution.py:774
  171.9 7.8 %collective-permute-start.26 = (bf16[256,767]{1,0:T(8,128)(2,1)S(1)}, bf16[256,767]{1,0:T(8,128)(2,1)S(1)}, u32[]{:S(2)}, u32[]{:S(2)}) collective-permute-start(bf16[256,767]{1,0:T(8,128)(2,1)S(1)} %add_convert_fusion.11), channel_id=1, source_target_pairs={{0,2},{1,3},{2,0},{3,1},{16,17},{17,16},{18,19},{19,18},{4,6},{5,7... | collective-permute-start | bytes 1178120 | tf_op jit(solution)/shard_map/ppermute | solution.py:779
  179.7 32.3 %collective-permute-start.31 = (bf16[192,3456]{1,0:T(8,128)(2,1)}, bf16[192,3456]{1,0:T(8,128)(2,1)}, u32[]{:S(2)}, u32[]{:S(2)}) collective-permute-start(bf16[192,3456]{1,0:T(8,128)(2,1)} %get-tuple-element.668), channel_id=1, source_target_pairs={{0,1},{1,0},{2,3},{3,2},{16,18},{17,19},{18,16},{19,17},{4,5},{5,4... | collective-permute-start | bytes 3981320 | tf_op jit(solution)/shard_map/ppermute | solution.py:774
  180.8 33.0 %collective-permute-start.32 = (bf16[192,3456]{1,0:T(8,128)(2,1)}, bf16[192,3456]{1,0:T(8,128)(2,1)}, u32[]{:S(2)}, u32[]{:S(2)}) collective-permute-start(bf16[192,3456]{1,0:T(8,128)(2,1)} %add_convert_fusion.5), channel_id=1, source_target_pairs={{0,2},{1,3},{2,0},{3,1},{16,17},{17,16},{18,19},{19,18},{4,6},{5,7... | collective-permute-start | bytes 3981320 | tf_op jit(solution)/shard_map/ppermute | solution.py:779
  198.3 21.1 %collective-permute-start.27 = (bf16[2,192,3456]{2,1,0:T(8,128)(2,1)}, bf16[2,192,3456]{2,1,0:T(8,128)(2,1)}, u32[]{:S(2)}, u32[]{:S(2)}) collective-permute-start(bf16[2,192,3456]{2,1,0:T(8,128)(2,1)} %shard_map.242), channel_id=1, source_target_pairs={{0,16},{16,0},{1,17},{17,1},{2,18},{18,2},{3,19},{19,3},{4,20},{20... | collective-permute-start | bytes 7962632 | tf_op jit(solution)/shard_map/ppermute | solution.py:787
  203.4 14.1 %collective-permute-start.28 = (bf16[192,256]{1,0:T(8,128)(2,1)S(1)}, bf16[192,256]{1,0:T(8,128)(2,1)S(1)}, u32[]{:S(2)}, u32[]{:S(2)}) collective-permute-start(bf16[192,256]{1,0:T(8,128)(2,1)S(1)} %copy-done.78), channel_id=1, source_target_pairs={{0,1},{1,0},{2,3},{3,2},{4,5},{5,4},{6,7},{7,6},{8,9},{9,8},{10,11... | collective-permute-start | bytes 294920 | tf_op jit(solution)/shard_map/ppermute | solution.py:783
  204.5 13.6 %collective-permute-start.29 = (bf16[192,256]{1,0:T(8,128)(2,1)S(1)}, bf16[192,256]{1,0:T(8,128)(2,1)S(1)}, u32[]{:S(2)}, u32[]{:S(2)}) collective-permute-start(bf16[192,256]{1,0:T(8,128)(2,1)S(1)} %copy-done.76), channel_id=1, source_target_pairs={{0,2},{1,3},{2,0},{3,1},{4,6},{5,7},{6,4},{7,5},{8,10},{9,11},{10,... | collective-permute-start | bytes 294920 | tf_op jit(solution)/shard_map/ppermute | solution.py:783
  212.0 6.7 %collective-permute-start.30 = (bf16[192,256]{1,0:T(8,128)(2,1)S(1)}, bf16[192,256]{1,0:T(8,128)(2,1)S(1)}, u32[]{:S(2)}, u32[]{:S(2)}) collective-permute-start(bf16[192,256]{1,0:T(8,128)(2,1)S(1)} %copy-done.74), channel_id=1, source_target_pairs={{0,3},{1,2},{2,1},{3,0},{4,7},{5,6},{6,5},{7,4},{8,11},{9,10},{10,... | collective-permute-start | bytes 294920 | tf_op jit(solution)/shard_map/ppermute | solution.py:783
  213.8 40.1 %collective-permute-start.34 = (bf16[2,192,3456]{2,1,0:T(8,128)(2,1)}, bf16[2,192,3456]{2,1,0:T(8,128)(2,1)}, u32[]{:S(2)}, u32[]{:S(2)}) collective-permute-start(bf16[2,192,3456]{2,1,0:T(8,128)(2,1)} %shard_map.243), channel_id=1, source_target_pairs={{0,16},{16,0},{1,17},{17,1},{2,18},{18,2},{3,19},{19,3},{4,20},{20... | collective-permute-start | bytes 7962632 | tf_op jit(solution)/shard_map/ppermute | solution.py:787
  224.0 30.0 %collective-permute-start.33 = (bf16[192,3456]{1,0:T(8,128)(2,1)}, bf16[192,3456]{1,0:T(8,128)(2,1)}, u32[]{:S(2)}, u32[]{:S(2)}) collective-permute-start(bf16[192,3456]{1,0:T(8,128)(2,1)} %get-tuple-element.691), channel_id=1, source_target_pairs={{0,1},{1,0},{2,3},{3,2},{16,18},{17,19},{18,16},{19,17},{4,5},{5,4... | collective-permute-start | bytes 3981320 | tf_op jit(solution)/shard_map/ppermute | solution.py:774
  225.6 28.4 %collective-permute-start.35 = (bf16[2,48,3456]{2,1,0:T(8,128)(2,1)}, bf16[2,48,3456]{2,1,0:T(8,128)(2,1)S(1)}, u32[]{:S(2)}, u32[]{:S(2)}) collective-permute-start(bf16[2,48,3456]{2,1,0:T(8,128)(2,1)} %get-tuple-element.720), channel_id=1, source_target_pairs={{0,4},{4,0},{8,12},{12,8},{1,5},{5,1},{9,13},{13,9},{2,6},{6,2},{1... | collective-permute-start | bytes 1990664 | tf_op jit(solution)/shard_map/ppermute | solution.py:792
  253.0 12.4 %collective-permute-start.37 = (bf16[512,767]{1,0:T(8,128)(2,1)}, bf16[512,767]{1,0:T(8,128)(2,1)}, u32[]{:S(2)}, u32[]{:S(2)}) collective-permute-start(bf16[512,767]{1,0:T(8,128)(2,1)} %get-tuple-element.749), channel_id=1, source_target_pairs={{0,1},{1,0},{2,3},{3,2},{16,18},{17,19},{18,16},{19,17},{4,5},{5,4... | collective-permute-start | bytes 2356232 | tf_op jit(solution)/shard_map/ppermute | solution.py:774
  254.0 8.8 %collective-permute-start.38 = (bf16[384,576]{1,0:T(8,128)(2,1)}, bf16[384,576]{1,0:T(8,128)(2,1)}, u32[]{:S(2)}, u32[]{:S(2)}) collective-permute-start(bf16[384,576]{1,0:T(8,128)(2,1)} %get-tuple-element.750), channel_id=1, source_target_pairs={{0,16},{16,0},{1,17},{17,1},{2,18},{18,2},{3,19},{19,3},{4,20},{20... | collective-permute-start | bytes 1327112 | tf_op jit(solution)/shard_map/ppermute | solution.py:787
  266.4 7.8 %collective-permute-start.39 = (bf16[256,767]{1,0:T(8,128)(2,1)S(1)}, bf16[256,767]{1,0:T(8,128)(2,1)S(1)}, u32[]{:S(2)}, u32[]{:S(2)}) collective-permute-start(bf16[256,767]{1,0:T(8,128)(2,1)S(1)} %add_convert_fusion.10), channel_id=1, source_target_pairs={{0,2},{1,3},{2,0},{3,1},{16,17},{17,16},{18,19},{19,18},{4,6},{5,7... | collective-permute-start | bytes 1178120 | tf_op jit(solution)/shard_map/ppermute | solution.py:779
  267.1 13.8 %collective-permute-start.36 = (bf16[2,104,576]{2,1,0:T(8,128)(2,1)S(1)}, bf16[2,104,576]{2,1,0:T(8,128)(2,1)S(1)}, u32[]{:S(2)}, u32[]{:S(2)}) collective-permute-start(bf16[2,104,576]{2,1,0:T(8,128)(2,1)S(1)} %get-tuple-element.747), channel_id=1, source_target_pairs={{0,4},{4,0},{8,12},{12,8},{1,5},{5,1},{9,13},{13,9},{2,6},{6,2},{1... | collective-permute-start | bytes 718856 | tf_op jit(solution)/shard_map/ppermute | solution.py:792
  267.6 16.3 %collective-permute-start.42 = (bf16[1,48,3456]{2,1,0:T(8,128)(2,1)S(1)}, bf16[1,48,3456]{2,1,0:T(8,128)(2,1)S(1)}, u32[]{:S(2)}, u32[]{:S(2)}) collective-permute-start(bf16[1,48,3456]{2,1,0:T(8,128)(2,1)S(1)} %copy-done.106), channel_id=1, source_target_pairs={{0,8},{4,12},{8,0},{12,4},{1,9},{5,13},{9,1},{13,5},{2,10},{6,14},... | collective-permute-start | bytes 995336 | tf_op jit(solution)/shard_map/ppermute | solution.py:792
  280.9 17.8 %collective-permute-start.41 = (bf16[192,3456]{1,0:T(8,128)(2,1)S(1)}, bf16[192,3456]{1,0:T(8,128)(2,1)S(1)}, u32[]{:S(2)}, u32[]{:S(2)}) collective-permute-start(bf16[192,3456]{1,0:T(8,128)(2,1)S(1)} %copy-done.54), channel_id=1, source_target_pairs={{0,1},{1,0},{2,3},{3,2},{16,18},{17,19},{18,16},{19,17},{4,5},{5,4... | collective-permute-start | bytes 3981320 | tf_op jit(solution)/shard_map/ppermute | solution.py:774
  283.9 15.0 %collective-permute-start.43 = (bf16[1,48,3456]{2,1,0:T(8,128)(2,1)S(1)}, bf16[1,48,3456]{2,1,0:T(8,128)(2,1)S(1)}, u32[]{:S(2)}, u32[]{:S(2)}) collective-permute-start(bf16[1,48,3456]{2,1,0:T(8,128)(2,1)S(1)} %add_convert_fusion.13), channel_id=1, source_target_pairs={{0,8},{4,12},{8,0},{12,4},{1,9},{5,13},{9,1},{13,5},{2,10},{6,14},... | collective-permute-start | bytes 995336 | tf_op jit(solution)/shard_map/ppermute | solution.py:792
  284.5 24.7 %collective-permute-start.40 = (bf16[1,104,576]{2,1,0:T(8,128)(2,1)}, bf16[1,104,576]{2,1,0:T(8,128)(2,1)}, u32[]{:S(2)}, u32[]{:S(2)}) collective-permute-start(bf16[1,104,576]{2,1,0:T(8,128)(2,1)} %get-tuple-element.777), channel_id=1, source_target_pairs={{0,8},{4,12},{8,0},{12,4},{1,9},{5,13},{9,1},{13,5},{2,10},{6,14},... | collective-permute-start | bytes 359432 | tf_op jit(solution)/shard_map/ppermute | solution.py:792
  299.5 18.2 %collective-permute-start.45 = (bf16[192,3456]{1,0:T(8,128)(2,1)}, bf16[192,3456]{1,0:T(8,128)(2,1)}, u32[]{:S(2)}, u32[]{:S(2)}) collective-permute-start(bf16[192,3456]{1,0:T(8,128)(2,1)} %add_convert_fusion.2), channel_id=1, source_target_pairs={{0,2},{1,3},{2,0},{3,1},{16,17},{17,16},{18,19},{19,18},{4,6},{5,7... | collective-permute-start | bytes 3981320 | tf_op jit(solution)/shard_map/ppermute | solution.py:779
  301.8 23.4 %collective-permute-start.46 = (bf16[2,48,3456]{2,1,0:T(8,128)(2,1)S(1)}, bf16[2,48,3456]{2,1,0:T(8,128)(2,1)S(1)}, u32[]{:S(2)}, u32[]{:S(2)}) collective-permute-start(bf16[2,48,3456]{2,1,0:T(8,128)(2,1)S(1)} %maximum_select_fusion.2), channel_id=1, source_target_pairs={{0,4},{4,0},{8,12},{12,8},{1,5},{5,1},{9,13},{13,9},{2,6},{6,2},{1... | collective-permute-start | bytes 1990664 | tf_op jit(solution)/shard_map/ppermute | solution.py:792
  310.9 17.9 %collective-permute-start.44 = (bf16[1,104,576]{2,1,0:T(8,128)(2,1)S(1)}, bf16[1,104,576]{2,1,0:T(8,128)(2,1)S(1)}, u32[]{:S(2)}, u32[]{:S(2)}) collective-permute-start(bf16[1,104,576]{2,1,0:T(8,128)(2,1)S(1)} %add_convert_fusion.17), channel_id=1, source_target_pairs={{0,8},{4,12},{8,0},{12,4},{1,9},{5,13},{9,1},{13,5},{2,10},{6,14},... | collective-permute-start | bytes 359432 | tf_op jit(solution)/shard_map/ppermute | solution.py:792
  314.0 16.9 %collective-permute-start.51 = (bf16[2,104,576]{2,1,0:T(8,128)(2,1)S(1)}, bf16[2,104,576]{2,1,0:T(8,128)(2,1)S(1)}, u32[]{:S(2)}, u32[]{:S(2)}) collective-permute-start(bf16[2,104,576]{2,1,0:T(8,128)(2,1)S(1)} %fusion.11), channel_id=1, source_target_pairs={{0,4},{4,0},{8,12},{12,8},{1,5},{5,1},{9,13},{13,9},{2,6},{6,2},{1... | collective-permute-start | bytes 718856 | tf_op jit(solution)/shard_map/ppermute | solution.py:792
  327.4 16.4 %collective-permute-start.50 = (bf16[2,48,3456]{2,1,0:T(8,128)(2,1)S(1)}, bf16[2,48,3456]{2,1,0:T(8,128)(2,1)S(1)}, u32[]{:S(2)}, u32[]{:S(2)}) collective-permute-start(bf16[2,48,3456]{2,1,0:T(8,128)(2,1)S(1)} %fusion.5), channel_id=1, source_target_pairs={{0,4},{4,0},{8,12},{12,8},{1,5},{5,1},{9,13},{13,9},{2,6},{6,2},{1... | collective-permute-start | bytes 1990664 | tf_op jit(solution)/shard_map/ppermute | solution.py:792
  327.4 22.6 %collective-permute-start.48 = (bf16[192,3456]{1,0:T(8,128)(2,1)S(1)}, bf16[192,3456]{1,0:T(8,128)(2,1)S(1)}, u32[]{:S(2)}, u32[]{:S(2)}) collective-permute-start(bf16[192,3456]{1,0:T(8,128)(2,1)S(1)} %bitcast.151), channel_id=1, source_target_pairs={{0,2},{1,3},{2,0},{3,1},{16,17},{17,16},{18,19},{19,18},{4,6},{5,7... | collective-permute-start | bytes 3981320 | tf_op jit(solution)/shard_map/ppermute | solution.py:779
  328.7 31.3 %collective-permute-start.49 = (bf16[192,3456]{1,0:T(8,128)(2,1)S(1)}, bf16[192,3456]{1,0:T(8,128)(2,1)S(1)}, u32[]{:S(2)}, u32[]{:S(2)}) collective-permute-start(bf16[192,3456]{1,0:T(8,128)(2,1)S(1)} %bitcast.152), channel_id=1, source_target_pairs={{0,1},{1,0},{2,3},{3,2},{16,18},{17,19},{18,16},{19,17},{4,5},{5,4... | collective-permute-start | bytes 3981320 | tf_op jit(solution)/shard_map/ppermute | solution.py:774
  328.8 49.6 %collective-permute-start.57 = (bf16[192,3456]{1,0:T(8,128)(2,1)S(1)}, bf16[192,3456]{1,0:T(8,128)(2,1)S(1)}, u32[]{:S(2)}, u32[]{:S(2)}) collective-permute-start(bf16[192,3456]{1,0:T(8,128)(2,1)S(1)} %bitcast.153), channel_id=1, source_target_pairs={{0,16},{1,17},{2,18},{3,19},{4,20},{5,21},{6,22},{7,23},{8,24},{9,... | collective-permute-start | bytes 3981320 | tf_op jit(solution)/shard_map/ppermute | solution.py:796
  331.0 30.1 %collective-permute-start.47 = (bf16[2,104,576]{2,1,0:T(8,128)(2,1)S(1)}, bf16[2,104,576]{2,1,0:T(8,128)(2,1)S(1)}, u32[]{:S(2)}, u32[]{:S(2)}) collective-permute-start(bf16[2,104,576]{2,1,0:T(8,128)(2,1)S(1)} %maximum_select_fusion.6), channel_id=1, source_target_pairs={{0,4},{4,0},{8,12},{12,8},{1,5},{5,1},{9,13},{13,9},{2,6},{6,2},{1... | collective-permute-start | bytes 718856 | tf_op jit(solution)/shard_map/ppermute | solution.py:792
  343.7 19.0 %collective-permute-start.54 = (bf16[1,104,576]{2,1,0:T(8,128)(2,1)S(1)}, bf16[1,104,576]{2,1,0:T(8,128)(2,1)S(1)}, u32[]{:S(2)}, u32[]{:S(2)}) collective-permute-start(bf16[1,104,576]{2,1,0:T(8,128)(2,1)S(1)} %get-tuple-element.855), channel_id=1, source_target_pairs={{0,8},{4,12},{8,0},{12,4},{1,9},{5,13},{9,1},{13,5},{2,10},{6,14},... | collective-permute-start | bytes 359432 | tf_op jit(solution)/shard_map/ppermute | solution.py:792
  350.0 24.4 %collective-permute-start.58 = (bf16[1,48,3456]{2,1,0:T(8,128)(2,1)S(1)}, bf16[1,48,3456]{2,1,0:T(8,128)(2,1)S(1)}, u32[]{:S(2)}, u32[]{:S(2)}) collective-permute-start(bf16[1,48,3456]{2,1,0:T(8,128)(2,1)S(1)} %get-tuple-element.862), channel_id=1, source_target_pairs={{0,8},{4,12},{8,0},{12,4},{1,9},{5,13},{9,1},{13,5},{2,10},{6,14},... | collective-permute-start | bytes 995336 | tf_op jit(solution)/shard_map/ppermute | solution.py:792
  360.0 21.5 %collective-permute-start.56 = (bf16[192,3456]{1,0:T(8,128)(2,1)S(1)}, bf16[192,3456]{1,0:T(8,128)(2,1)S(1)}, u32[]{:S(2)}, u32[]{:S(2)}) collective-permute-start(bf16[192,3456]{1,0:T(8,128)(2,1)S(1)} %collective-permute-done.48.refs_3_), channel_id=1, source_target_pairs={{0,1},{1,0},{2,3},{3,2},{16,18},{17,19},{18,16},{19,17},{4,5},{5,4... | collective-permute-start | bytes 3981320 | tf_op jit(solution)/shard_map/ppermute | solution.py:774
  361.1 29.6 %collective-permute-start.53 = (bf16[192,3456]{1,0:T(8,128)(2,1)S(1)}, bf16[192,3456]{1,0:T(8,128)(2,1)S(1)}, u32[]{:S(2)}, u32[]{:S(2)}) collective-permute-start(bf16[192,3456]{1,0:T(8,128)(2,1)S(1)} %collective-permute-done.48.refs_3_), channel_id=1, source_target_pairs={{0,16},{1,17},{2,18},{3,19},{4,20},{5,21},{6,22},{7,23},{8,24},{9,... | collective-permute-start | bytes 3981320 | tf_op jit(solution)/shard_map/ppermute | solution.py:796
  374.3 8.5 %collective-permute-start.55 = (bf16[1,104,576]{2,1,0:T(8,128)(2,1)S(1)}, bf16[1,104,576]{2,1,0:T(8,128)(2,1)S(1)}, u32[]{:S(2)}, u32[]{:S(2)}) collective-permute-start(bf16[1,104,576]{2,1,0:T(8,128)(2,1)S(1)} %add_convert_fusion.16), channel_id=1, source_target_pairs={{0,8},{4,12},{8,0},{12,4},{1,9},{5,13},{9,1},{13,5},{2,10},{6,14},... | collective-permute-start | bytes 359432 | tf_op jit(solution)/shard_map/ppermute | solution.py:792
  374.4 16.4 %collective-permute-start.52 = (bf16[416,576]{1,0:T(8,128)(2,1)S(1)}, bf16[416,576]{1,0:T(8,128)(2,1)S(1)}, u32[]{:S(2)}, u32[]{:S(2)}) collective-permute-start(bf16[416,576]{1,0:T(8,128)(2,1)S(1)} %bitcast.172), channel_id=1, source_target_pairs={{0,2},{1,3},{2,0},{3,1},{16,17},{17,16},{18,19},{19,18},{4,6},{5,7... | collective-permute-start | bytes 1437704 | tf_op jit(solution)/shard_map/ppermute | solution.py:779
  378.5 12.5 %collective-permute-start.62 = (bf16[1,48,3456]{2,1,0:T(8,128)(2,1)S(1)}, bf16[1,48,3456]{2,1,0:T(8,128)(2,1)S(1)}, u32[]{:S(2)}, u32[]{:S(2)}) collective-permute-start(bf16[1,48,3456]{2,1,0:T(8,128)(2,1)S(1)} %add_convert_fusion.12), channel_id=1, source_target_pairs={{0,8},{4,12},{8,0},{12,4},{1,9},{5,13},{9,1},{13,5},{2,10},{6,14},... | collective-permute-start | bytes 995336 | tf_op jit(solution)/shard_map/ppermute | solution.py:792
  381.5 20.9 %collective-permute-start.60 = (bf16[192,3456]{1,0:T(8,128)(2,1)S(1)}, bf16[192,3456]{1,0:T(8,128)(2,1)S(1)}, u32[]{:S(2)}, u32[]{:S(2)}) collective-permute-start(bf16[192,3456]{1,0:T(8,128)(2,1)S(1)} %collective-permute-done.49.refs_3_), channel_id=1, source_target_pairs={{0,16},{1,17},{2,18},{3,19},{4,20},{5,21},{6,22},{7,23},{8,24},{9,... | collective-permute-start | bytes 3981320 | tf_op jit(solution)/shard_map/ppermute | solution.py:796
  390.9 7.7 %collective-permute-start.61 = (bf16[2,104,576]{2,1,0:T(8,128)(2,1)S(1)}, bf16[2,104,576]{2,1,0:T(8,128)(2,1)S(1)}, u32[]{:S(2)}, u32[]{:S(2)}) collective-permute-start(bf16[2,104,576]{2,1,0:T(8,128)(2,1)S(1)} %maximum_select_fusion.7), channel_id=1, source_target_pairs={{0,4},{4,0},{8,12},{12,8},{1,5},{5,1},{9,13},{13,9},{2,6},{6,2},{1... | collective-permute-start | bytes 718856 | tf_op jit(solution)/shard_map/ppermute | solution.py:792
  394.3 15.0 %collective-permute-start.59 = (bf16[2,416,576]{2,1,0:T(8,128)(2,1)S(1)}, bf16[2,416,576]{2,1,0:T(8,128)(2,1)S(1)}, u32[]{:S(2)}, u32[]{:S(2)}) collective-permute-start(bf16[2,416,576]{2,1,0:T(8,128)(2,1)S(1)} %pad_maximum_fusion.2), channel_id=1, source_target_pairs={{0,1},{1,0},{2,3},{3,2},{16,18},{17,19},{18,16},{19,17},{4,5},{5,4... | collective-permute-start | bytes 2875400 | tf_op jit(solution)/shard_map/ppermute | solution.py:774
  394.8 14.4 %collective-permute-start.65 = (bf16[2,48,3456]{2,1,0:T(8,128)(2,1)S(1)}, bf16[2,48,3456]{2,1,0:T(8,128)(2,1)S(1)}, u32[]{:S(2)}, u32[]{:S(2)}) collective-permute-start(bf16[2,48,3456]{2,1,0:T(8,128)(2,1)S(1)} %maximum_select_fusion.3), channel_id=1, source_target_pairs={{0,4},{4,0},{8,12},{12,8},{1,5},{5,1},{9,13},{13,9},{2,6},{6,2},{1... | collective-permute-start | bytes 1990664 | tf_op jit(solution)/shard_map/ppermute | solution.py:792
  398.9 9.4 %collective-permute-start.63 = (bf16[416,576]{1,0:T(8,128)(2,1)S(1)}, bf16[416,576]{1,0:T(8,128)(2,1)S(1)}, u32[]{:S(2)}, u32[]{:S(2)}) collective-permute-start(bf16[416,576]{1,0:T(8,128)(2,1)S(1)} %bitcast.174), channel_id=1, source_target_pairs={{0,2},{1,3},{2,0},{3,1},{16,17},{17,16},{18,19},{19,18},{4,6},{5,7... | collective-permute-start | bytes 1437704 | tf_op jit(solution)/shard_map/ppermute | solution.py:779
  401.0 14.4 %collective-permute-start.64 = (bf16[192,3456]{1,0:T(8,128)(2,1)S(1)}, bf16[192,3456]{1,0:T(8,128)(2,1)S(1)}, u32[]{:S(2)}, u32[]{:S(2)}) collective-permute-start(bf16[192,3456]{1,0:T(8,128)(2,1)S(1)} %collective-permute-done.56.refs_3_), channel_id=1, source_target_pairs={{0,16},{1,17},{2,18},{3,19},{4,20},{5,21},{6,22},{7,23},{8,24},{9,... | collective-permute-start | bytes 3981320 | tf_op jit(solution)/shard_map/ppermute | solution.py:796
  409.6 12.1 %collective-permute-start.66 = (bf16[192,3456]{1,0:T(8,128)(2,1)S(1)}, bf16[192,3456]{1,0:T(8,128)(2,1)S(1)}, u32[]{:S(2)}, u32[]{:S(2)}) collective-permute-start(bf16[192,3456]{1,0:T(8,128)(2,1)S(1)} %bitcast.155), channel_id=1, source_target_pairs={{16,0},{17,1},{18,2},{19,3},{20,4},{21,5},{22,6},{23,7},{24,8},{25... | collective-permute-start | bytes 3981320 | tf_op jit(solution)/shard_map/ppermute | solution.py:796
  411.1 43.7 %collective-permute-start.68 = (bf16[192,3456]{1,0:T(8,128)(2,1)S(1)}, bf16[192,3456]{1,0:T(8,128)(2,1)S(1)}, u32[]{:S(2)}, u32[]{:S(2)}) collective-permute-start(bf16[192,3456]{1,0:T(8,128)(2,1)S(1)} %bitcast.156), channel_id=1, source_target_pairs={{0,2},{1,3},{2,0},{3,1},{16,17},{17,16},{18,19},{19,18},{4,6},{5,7... | collective-permute-start | bytes 3981320 | tf_op jit(solution)/shard_map/ppermute | solution.py:779
  413.2 41.6 %collective-permute-start.69 = (bf16[192,3456]{1,0:T(8,128)(2,1)S(1)}, bf16[192,3456]{1,0:T(8,128)(2,1)S(1)}, u32[]{:S(2)}, u32[]{:S(2)}) collective-permute-start(bf16[192,3456]{1,0:T(8,128)(2,1)S(1)} %bitcast.157), channel_id=1, source_target_pairs={{0,1},{1,0},{2,3},{3,2},{16,18},{17,19},{18,16},{19,17},{4,5},{5,4... | collective-permute-start | bytes 3981320 | tf_op jit(solution)/shard_map/ppermute | solution.py:774
  413.8 40.9 %collective-permute-start.70 = (bf16[2,416,576]{2,1,0:T(8,128)(2,1)S(1)}, bf16[2,416,576]{2,1,0:T(8,128)(2,1)S(1)}, u32[]{:S(2)}, u32[]{:S(2)}) collective-permute-start(bf16[2,416,576]{2,1,0:T(8,128)(2,1)S(1)} %pad_maximum_fusion.3), channel_id=1, source_target_pairs={{0,1},{1,0},{2,3},{3,2},{16,18},{17,19},{18,16},{19,17},{4,5},{5,4... | collective-permute-start | bytes 2875400 | tf_op jit(solution)/shard_map/ppermute | solution.py:774
  419.9 48.7 %collective-permute-start.72 = (bf16[4,416,576]{2,1,0:T(8,128)(2,1)S(1)}, bf16[4,416,576]{2,1,0:T(8,128)(2,1)S(1)}, u32[]{:S(2)}, u32[]{:S(2)}) collective-permute-start(bf16[4,416,576]{2,1,0:T(8,128)(2,1)S(1)} %pad_maximum_fusion.refs_3_), channel_id=1, source_target_pairs={{0,16},{1,17},{2,18},{3,19},{4,20},{5,21},{6,22},{7,23},{8,24},{9,... | collective-permute-start | bytes 5750792 | tf_op jit(solution)/shard_map/ppermute | solution.py:796
  455.1 13.6 %collective-permute-start.71 = (bf16[4,416,576]{2,1,0:T(8,128)(2,1)S(1)}, bf16[4,416,576]{2,1,0:T(8,128)(2,1)S(1)}, u32[]{:S(2)}, u32[]{:S(2)}) collective-permute-start(bf16[4,416,576]{2,1,0:T(8,128)(2,1)S(1)} %pad_maximum_fusion.1.refs_0_), channel_id=1, source_target_pairs={{16,0},{17,1},{18,2},{19,3},{20,4},{21,5},{22,6},{23,7},{24,8},{25... | collective-permute-start | bytes 5750792 | tf_op jit(solution)/shard_map/ppermute | solution.py:796
  457.7 7.3 %collective-permute-start.74 = (bf16[192,3456]{1,0:T(8,128)(2,1)S(1)}, bf16[192,3456]{1,0:T(8,128)(2,1)S(1)}, u32[]{:S(2)}, u32[]{:S(2)}) collective-permute-start(bf16[192,3456]{1,0:T(8,128)(2,1)S(1)} %collective-permute-done.69.refs_0_), channel_id=1, source_target_pairs={{16,0},{17,1},{18,2},{19,3},{20,4},{21,5},{22,6},{23,7},{24,8},{25... | collective-permute-start | bytes 3981320 | tf_op jit(solution)/shard_map/ppermute | solution.py:796
  459.0 17.8 %collective-permute-start.75 = (bf16[192,3456]{1,0:T(8,128)(2,1)S(1)}, bf16[192,3456]{1,0:T(8,128)(2,1)S(1)}, u32[]{:S(2)}, u32[]{:S(2)}) collective-permute-start(bf16[192,3456]{1,0:T(8,128)(2,1)S(1)} %collective-permute-done.68.refs_0_), channel_id=1, source_target_pairs={{0,1},{1,0},{2,3},{3,2},{16,18},{17,19},{18,16},{19,17},{4,5},{5,4... | collective-permute-start | bytes 3981320 | tf_op jit(solution)/shard_map/ppermute | solution.py:774
  476.8 9.1 %collective-permute-start.76 = (bf16[192,3456]{1,0:T(8,128)(2,1)S(1)}, bf16[192,3456]{1,0:T(8,128)(2,1)S(1)}, u32[]{:S(2)}, u32[]{:S(2)}) collective-permute-start(bf16[192,3456]{1,0:T(8,128)(2,1)S(1)} %collective-permute-done.75.refs_0_), channel_id=1, source_target_pairs={{16,0},{17,1},{18,2},{19,3},{20,4},{21,5},{22,6},{23,7},{24,8},{25... | collective-permute-start | bytes 3981320 | tf_op jit(solution)/shard_map/ppermute | solution.py:796
  (129 other events, 1087.8 us)

commit v6 on v5

--- a/solution.py
+++ b/solution.py
@@ -128,13 +128,13 @@
 
 
 def attn_fwd_kernel(
-    raw, ids, n0, n1, n2, n3, w_ref, pv_ref, qh, kh, vh, lse, a0, a1, a2, a3, *rest
+    raw, ids, n0, n1, n2, n3, w_ref, pv_ref, q_hbm, k_hbm, v_hbm, l_hbm, n_hbm,
+    a0, a1, a2, a3, qh, kh, vh, lse, nb_scr, at, bias_scr, sem,
 ):
     c, s = ids[0], ids[1]
     heads, _, hd = qh.shape
     span, cc = n0.shape
     width = heads * hd
-    at, bias_scr = rest[-2:]
     bias = pv_ref[5:6, : 3 * width]
     for p, nb in enumerate((n0, n1, n2, n3)):
         t = jnp.bitwise_xor(order(c, p), s)
@@ -143,13 +143,23 @@
         if raw:
             v = rows.astype(F32)
             rows = (v * crms_scale(v)[0] * pv_ref[3:4, :cc]).astype(BF16)
-            rest[p][...] = rows
+            nb_scr[p] = rows
         y = nn(rows, w_ref[...]) + bias
         for h in range(heads):
             lo = h * hd
             qh[h, pl.ds(row, span), :] = (y[:, lo : lo + hd] * (hd**-0.5)).astype(BF16)
             kh[h, pl.ds(row, span), :] = y[:, width + lo : width + lo + hd].astype(BF16)
             vh[h, pl.ds(row, span), :] = y[:, 2 * width + lo : 2 * width + lo + hd].astype(BF16)
+    moves = [
+        pltpu.make_async_copy(src, dst, sem.at[i])
+        for i, (src, dst) in enumerate(
+            [(qh, q_hbm), (kh, k_hbm), (vh, v_hbm), (lse, l_hbm)]
+            + [(nb_scr.at[p] if raw else nb, n_hbm.at[p]) for p, nb in enumerate((n0, n1, n2, n3))]
+        )
+    ]
+    for i, m in enumerate(moves):
+        if i != 3:
+            m.start()
     for t in range(QUAD):
         n = span * (t + 1)
         bias_scr[:n, :] = visible_bias(ids, n, t, span)
@@ -167,8 +177,11 @@
             return carry
 
         lax.fori_loop(0, heads, head, 0)
+    moves[3].start()
     for k, a in enumerate((a0, a1, a2, a3)):
         a[...] = at[jnp.bitwise_xor(s, k)]
+    for m in moves:
+        m.wait()
 
 
 def attn_fwd(raw, ids, blocks, w3, pv, heads, hd):
@@ -176,15 +189,19 @@
     full = span * QUAD
     hh = jax.ShapeDtypeStruct((heads, full, hd), BF16)
     aa = jax.ShapeDtypeStruct((heads * hd, span), BF16)
-    normed = [jax.ShapeDtypeStruct((span, width), BF16)] * (QUAD if raw else 0)
+    saved = [hh, hh, hh, jax.ShapeDtypeStruct((heads, QUAD, span), F32)]
+    nb = jax.ShapeDtypeStruct((QUAD, span, width), BF16)
     return pl.pallas_call(
         functools.partial(attn_fwd_kernel, raw),
         in_specs=[SMEM] + [VMEM] * 6,
-        out_specs=[VMEM] * (8 + len(normed)),
-        out_shape=[hh, hh, hh, jax.ShapeDtypeStruct((heads, QUAD, span), F32), aa, aa, aa, aa] + normed,
-        scratch_shapes=[
+        out_specs=[HBM] * 5 + [VMEM] * 4,
+        out_shape=[*saved, nb, aa, aa, aa, aa],
+        scratch_shapes=[pltpu.VMEM(v.shape, v.dtype) for v in saved]
+        + [
+            pltpu.VMEM(nb.shape if raw else (1, 8, 128), BF16),
             pltpu.VMEM((QUAD, heads * hd, span), BF16),
             pltpu.VMEM((full, span), F32),
+            pltpu.SemaphoreType.DMA((8,)),
         ],
         compiler_params=params(22),
         cost_estimate=cost(
@@ -239,7 +256,7 @@
 def mlp_fwd(layer, ids, x, att, wo, pv, pvn, up, dn):
     span, cc = x.shape
     ff = up[0].shape[-1]
-    fb = ff // 8
+    fb = ff // 4
     rows = att[0].shape[0]
 
     def whole(shape):
@@ -251,7 +268,7 @@
     mine, other = pick(True), pick(False)
     grid = pltpu.PrefetchScalarGridSpec(
         num_scalar_prefetch=1,
-        grid=(8,),
+        grid=(4,),
         in_specs=[whole((span, cc))]
         + [whole((rows, span))] * 4
         + [whole(wo.shape), whole(pv.shape), whole(pvn.shape)]
@@ -283,7 +300,7 @@
             jax.ShapeDtypeStruct((8, 128), F32),
             jax.ShapeDtypeStruct((QUAD, span, rows), BF16),
         ],
-        compiler_params=params(22, dimension_semantics=("arbitrary",)),
+        compiler_params=params(32, dimension_semantics=("arbitrary",)),
         cost_estimate=cost(6 * span * cc * ff, 4 * cc * ff + 4 * span * ff, span * ff),
     )(ids, x, *att, wo, pv, pvn, pv, up[0], up[1], dn[0], dn[1])
 
@@ -341,7 +358,7 @@
 def mlp_bwd(layer, ids, df, u, mid, wo, pv, up, dn):
     span, cc = df.shape
     ff = u.shape[-1]
-    fb = ff // 8
+    fb = ff // 4
     rows = wo.shape[0] // QUAD
 
     def whole(shape):
@@ -353,7 +370,7 @@
     mine, other = pick(True), pick(False)
     grid = pltpu.PrefetchScalarGridSpec(
         num_scalar_prefetch=1,
-        grid=(8,),
+        grid=(4,),
         in_specs=[
             whole((span, cc)),
             pl.BlockSpec((span, fb), lambda j, ids: (0, j)),
@@ -385,7 +402,7 @@
             jax.ShapeDtypeStruct((8, ff), F32),
             dd, dd, dd, dd,
         ],
-        compiler_params=params(24, dimension_semantics=("arbitrary",)),
+        compiler_params=params(32, dimension_semantics=("arbitrary",)),
         cost_estimate=cost(6 * span * cc * ff, 4 * cc * ff + 8 * span * ff, span * ff),
     )(ids, df, u, mid, wo, pv, up[0], up[1], dn[0], dn[1])
 
@@ -426,19 +443,18 @@
 
 
 def attn_bwd_kernel(
-    ids, n0, n1, n2, n3, w_hbm, q_hbm, k_hbm, v_hbm, l_hbm, d0, d1, d2, d3,
+    ids, n_hbm, w_hbm, q_hbm, k_hbm, v_hbm, l_hbm, d0, d1, d2, d3,
     p0, p1, far, gs, gk, gb, do, dk, dv, dy, acc, bias_scr,
     nb, w_ref, qh, kh, vh, lse, sem,
 ):
     c, s = ids[0], ids[1]
     heads, _, hd = qh.shape
-    span, cc = n0.shape
+    _, span, cc = nb.shape
     width = heads * hd
     moves = [
         pltpu.make_async_copy(src, dst, sem.at[i])
         for i, (src, dst) in enumerate(
-            [(q_hbm, qh), (k_hbm, kh), (v_hbm, vh), (l_hbm, lse), (w_hbm, w_ref)]
-            + [(n, nb.at[i]) for i, n in enumerate((n0, n1, n2, n3))]
+            [(q_hbm, qh), (k_hbm, kh), (v_hbm, vh), (l_hbm, lse), (w_hbm, w_ref), (n_hbm, nb)]
         )
     ]
     for m in moves:
@@ -493,14 +509,14 @@
 
 
 def attn_bwd(ids, blocks, w3, qkvl, douts):
-    span, cc = blocks[0].shape
+    _, span, cc = blocks.shape
     heads, full, hd = qkvl[0].shape
     width = heads * hd
     pp = jax.ShapeDtypeStruct((span, cc), BF16)
     gg = jax.ShapeDtypeStruct(((cc + 1) // 2, 3 * width), BF16)
     return pl.pallas_call(
         attn_bwd_kernel,
-        in_specs=[SMEM] + [HBM] * 9 + [VMEM] * 4,
+        in_specs=[SMEM] + [HBM] * 6 + [VMEM] * 4,
         out_specs=[VMEM] * 6,
         out_shape=[pp, pp, jax.ShapeDtypeStruct((2 * span, cc), BF16), gg, gg, jax.ShapeDtypeStruct((8, 3 * width), F32)],
         scratch_shapes=[
@@ -516,7 +532,7 @@
             pltpu.VMEM((heads, full, hd), BF16),
             pltpu.VMEM((heads, full, hd), BF16),
             pltpu.VMEM((heads, QUAD, span), F32),
-            pltpu.SemaphoreType.DMA((9,)),
+            pltpu.SemaphoreType.DMA((6,)),
         ],
         compiler_params=params(30),
         cost_estimate=cost(
@@ -524,7 +540,7 @@
             8 * full * cc,
             heads * full * full,
         ),
-    )(ids, *blocks, w3, *qkvl, *douts)
+    )(ids, blocks, w3, *qkvl, *douts)
 
 
 def input_kernel(part, r0, r1, dmid, x, pv, dx, gg):
@@ -892,8 +908,8 @@
     e2 = e1 + lens[2]
     e3 = e2 + lens[3]
     ids = jnp.stack([c, s, e0, e1, e2, e3, c, s]).astype(jnp.int32)
-    x = rows_in(ids, layer_in)
-    x, w_qkv = tied(x, w_qkv)
+    cs = jnp.stack([c, s]).astype(jnp.int32)
+    x = rows_in(cs, layer_in)
 
     def row(v, n=ff):
         return jnp.pad(v, ((0, 0), (0, n - v.shape[-1])))
@@ -922,9 +938,9 @@
     squares = []
     for l in range(2):
         blocks = quad_gather(normed)
-        qh, kh, vh, lse, *att = attn_fwd(l == 0, ids, blocks, w3[l], pv[l], heads, hd)
-        if l == 0:
-            att, blocks = att[:QUAD], att[QUAD:]
+        if l == 1:
+            blocks, df = tied(blocks, rows_in(cs, cotangent))
+        qh, kh, vh, lse, blocks, *att = attn_fwd(l == 0, ids, blocks, w3[l], pv[l], heads, hd)
         att = [att[0]] + [to_quad(att[k], k) for k in (1, 2, 3)]
         mid, u, xout, normed, sq, astk = mlp_fwd(
             l, ids, x, att, wo[l], pv[l], pv[min(l + 1, 1)], up, dn
@@ -978,10 +994,7 @@
     def add_first(a, b):
         return add_low(a, b[:span])
 
-    df = rows_in(ids, cotangent)
-    out_got = to_core(jnp.where(mine, outs[1], outs[0]))
     lr1, rr1, dmid1, g1, douts1 = first_part(1, df)
-    out_got = wait(out_got)
 
     far1 = to_core(send(1, (3, 2), lr1, rr1))
     douts1 = wait(*douts1)
@@ -993,9 +1006,10 @@
     p0, p1, _, _, gk1, gb1, pr, gs_got = attention(1, douts1)
     x1a, near1 = wait(x1a, near1)
 
+    out_got = to_core(run(lambda a, b: jnp.where(mine, a, b), outs[1], outs[0]))
     near1 = keep(1, (1, 0), lr1, rr1, near1)
     half1 = run(add_low, near1[0], x1a)
-    pr, gs_got = wait(pr, gs_got)
+    pr, gs_got, out_got = wait(pr, gs_got, out_got)
 
     q = to_second(run(add_first, p1, pr))
     q = wait(q)
@@ -1096,21 +1110,23 @@
     have0[1], have0[2], qkv_rest0 = wait(have0[1], have0[2], qkv_rest0)
 
     have0.append(to_first(have0[1]))
-    got0 += [to_owner(0, have0[1]), to_owner(0, have0[2])]
     qkv0 = run(lambda a, b: jnp.concatenate([a, b]), qkv_pair0, qkv_rest0)
-    got0[1], got0[2] = wait(got0[1], got0[2])
+    have0[1], have0[2] = wait(have0[1], have0[2])
+    got0.append(to_owner(0, have0[1]))
     qkv0_got, qkv1_got = to_owner(0, qkv0), to_owner(1, qkv1)
+    got0[1] = wait(got0[1])
     outs_w = place((1,), outs_w)
+    got0.append(to_owner(0, wait(have0[2])))
     qkv0_got, qkv1_got = wait(qkv0_got, qkv1_got)
-    outs_w = place((2,), outs_w)
+    grad_qkv = run(lambda *v: qkv_out(ids, v, cc), qkv0, qkv0_got, qkv1_got, qkv1)
     count = micro * dp_count * span * QUAD
     vectors = run(
         lambda *v: vectors_out(ids, v, count, cc, ff, model), qkv0, qkv0_got, qkv1_got, qkv1
     )
-    have0[3] = wait(have0[3])
+    have0[3], got0[2] = wait(have0[3], got0[2])
 
     got0.append(to_owner(0, have0[3]))
-    grad_qkv = run(lambda *v: qkv_out(ids, v, cc), qkv0, qkv0_got, qkv1_got, qkv1)
+    outs_w = place((2,), outs_w)
     got0[3] = wait(got0[3])
     grad_down, grad_up, grad_out = place_rows(
         (3,), order_of.token, [v[3] for v in (have0, got0, got1, have1)], outs_w, cc, ff, model

time: 495 us -> 479 us (0.968)
  starting transfers between devices: 103 us -> 92.6 us
  Pallas kernels: 148 us -> 141 us
    ppermute x10, starting transfers between devices: 17.4 us -> 10.7 us  [to_second(): return lax.ppermute(v, ('section', 'seq'), pairs)]
    ppermute x16, starting transfers between devices: 40.4 us -> 33.6 us  [dp_partner(): return lax.ppermute(v, 'dp', [(i, i ^ step) for i in range(n)])]
    ppermute x10, waiting for transfers between devices: 41.4 us -> 47.2 us  [to_second(): return lax.ppermute(v, ('section', 'seq'), pairs)]
    ppermute x10, waiting for transfers between devices: 5.54 us -> 0.03 us  [to_owner(): return lax.ppermute(v, 'section', [(1 - l, l)])]
    unnamed x232 -> x216, local copies, waits for them, and re-layouts: 27.7 us -> 23.8 us
  transfers between devices with their start and end apart: 77 -> 77, of which waited for: 37 -> 32; matrix products, arithmetic and copies ran while one was open for 7% -> 7% of each run, Pallas kernels for 23% -> 20%
where the time goes in v6:
time: 479 us; the launch traced here: 473 us
  waiting for transfers between devices  174 us (36%)
  Pallas kernels  141 us (29%)
  starting transfers between devices  92.6 us (19%)
  local copies, waits for them, and re-layouts  35.9 us (7%)
  other arithmetic  24.7 us (5%)
  between operations  5.37 us (1%)
    ppermute x16, waiting for transfers between devices, to_first(): return lax.ppermute(v, ('section', 'seq'), pairs)  73.2 us
    ppermute x10, waiting for transfers between devices, to_second(): return lax.ppermute(v, ('section', 'seq'), pairs)  47.2 us
    ppermute x16, waiting for transfers between devices, dp_partner(): return lax.ppermute(v, 'dp', [(i, i ^ step) for i in range(n)])  40.3 us
    ppermute x16, starting transfers between devices, dp_partner(): return lax.ppermute(v, 'dp', [(i, i ^ step) for i in range(n)])  33.6 us
    pallas_call x2, Pallas kernels, attn_bwd(): pl.pallas_call(attn_bwd_kernel, in_specs=[SMEM] + [HBM] * 6 + [VMEM] * 4,...  25.4 us
    unnamed x216, local copies, waits for them, and re-layouts  23.8 us
    pallas_call x2, Pallas kernels, attn_fwd(): pl.pallas_call(functools.partial(attn_fwd_kernel, raw), in_specs=[SMEM] +...  22.8 us
    pallas_call x2, Pallas kernels, mlp_bwd(): pl.pallas_call(functools.partial(mlp_bwd_kernel, layer), grid_spec=grid,...  20.1 us
  transfers between devices with their start and end apart: 77, of which 32 were waited for; matrix products, arithmetic and copies ran while one was open for 7% of the time, Pallas kernels for 20%

profile of v6, /device:TPU:0, one launch (start us, length us, event | category | flops | bytes accessed | tf_op | source)
XLA Modules:
  0.0 473.1 jit_solution(7218425619946642175)
XLA Ops:
  1.3 2.8 dynamic-slice_bitcast_fusion.2
  9.9 2.7 collective-permute-start
  21.7 2.0 broadcast_select_fusion.2
  23.7 2.0 collective-permute-done.1.n2
  25.7 4.2 collective-permute-done.2.n3
  31.8 11.6 %shard_map.229 = (bf16[3,1024,64]{2,1,0:T(8,128)(2,1)S(1)}, bf16[3,1024,64]{2,1,0:T(8,128)(2,1)S(1)}, bf16[3,1024,64]{2,1,0:T(8,128)(2,1)S(1)}, f32[3,4,256]{2,1...) custom-call(s32[8]{0:T(128)S(1)} %stack.144.ids, ...), custom_call_target="tpu_custom_call" | custom-call | flops 3320709120 | bytes 3141632 | tf_op jit(solution)/shard_map/pallas_call | solution.py:194
  48.6 2.9 collective-permute-done.6.a2
  51.5 8.3 %shard_map.230 = (f32[256,767]{1,0:T(8,128)S(1)}, f32[256,3072]{1,0:T(8,128)S(1)}, bf16[256,767]{1,0:T(8,128)(2,1)S(1)}, bf16[256,767]{1,0:T(8,128)(2,1)S(1)}, f...) custom-call(s32[8]{0:T(128)S(1)} %stack.144.ids, bf16[256,767]{1,0:T(8,128)(2,1)S(1)} %shard_map.228.n0.x, ...), custom_call_target="tpu_custom_call" | custom-call | flops 3619160064 | bytes 12570624 | tf_op jit(solution)/shard_map/pallas_call | solution.py:292
  62.0 9.3 %collective-permute-done.11.n1 = bf16[256,767]{1,0:T(8,128)(2,1)S(1)} collective-permute-done((bf16[256,767]{1,0:T(8,128)(2,1)S(1)}, bf16[256,767]{1,0:T(8,128)(2,1)S(1)}, u32[]{:S(2)}, u32[]{:S(2)}) %collective-permute-start.11) | collective-permute-done | bytes 392736 | tf_op jit(solution)/shard_map/ppermute | solution.py:795
  71.3 1.8 collective-permute-start.13
  73.1 2.0 shard_map.231.df
  75.1 3.9 collective-permute-done.13.n3
  79.1 11.2 %shard_map.232 = (bf16[3,1024,64]{2,1,0:T(8,128)(2,1)S(1)}, bf16[3,1024,64]{2,1,0:T(8,128)(2,1)S(1)}, bf16[3,1024,64]{2,1,0:T(8,128)(2,1)S(1)}, f32[3,4,256]{2,1...) custom-call(s32[8]{0:T(128)S(1)} %stack.144.ids, ...), custom_call_target="tpu_custom_call" | custom-call | flops 3320709120 | bytes 3141632 | tf_op jit(solution)/shard_map/pallas_call | solution.py:194
  92.3 1.8 collective-permute-start.14
  97.0 2.9 collective-permute-done.15.a2
  99.9 9.4 %shard_map.233 = (f32[256,767]{1,0:T(8,128)S(1)}, f32[256,3072]{1,0:T(8,128)S(1)}, bf16[256,767]{1,0:T(8,128)(2,1)S(1)}, bf16[256,767]{1,0:T(8,128)(2,1)}, f32[8...) custom-call(s32[8]{0:T(128)S(1)} %stack.144.ids, bf16[256,767]{1,0:T(8,128)(2,1)S(1)} %get-tuple-element.930.x, ...), custom_call_target="tpu_custom_call" | custom-call | flops 3619160064 | bytes 12570624 | tf_op jit(solution)/shard_map/pallas_call | solution.py:292
  109.2 10.0 %shard_map.234 = (bf16[2,256,3072]{2,1,0:T(8,128)(2,1)S(1)}, bf16[3,4,256,192]{3,2,1,0:T(8,128)(2,1)S(1)}, f32[256,767]{1,0:T(8,128)S(1)}, f32[8,3072]{1,0:T(8,1...) custom-call(s32[8]{0:T(128)S(1)} %stack.144.ids, ...), custom_call_target="tpu_custom_call" | custom-call | flops 3619160064 | bytes 15716352 | tf_op jit(solution)/shard_map/pallas_call | solution.py:395
  121.8 1.9 collective-permute-start.17
  127.1 3.6 collective-permute-done.18.d2
  132.3 2.7 shard_map.237
  135.6 12.2 %shard_map.238 = (bf16[256,767]{1,0:T(8,128)(2,1)S(1)}, bf16[256,767]{1,0:T(8,128)(2,1)S(1)}, bf16[512,767]{1,0:T(8,128)(2,1)S(1)}, bf16[384,576]{1,0:T(8,128)(2...) custom-call(s32[8]{0:T(128)S(1)} %stack.144.ids, bf16[4,256,767]{2,1,0:T(8,128)(2,1)S(1)} %copy-done.78, ...), custom_call_target="tpu_custom_call" | custom-call | flops 7849377792 | bytes 6283264 | tf_op jit(solution)/shard_map/pallas_call | solution.py:517
  149.3 3.5 collective-permute-done.23
  156.1 5.2 %collective-permute-done.21.r0 = bf16[512,767]{1,0:T(8,128)(2,1)S(1)} collective-permute-done((bf16[512,767]{1,0:T(8,128)(2,1)S(1)}, bf16[512,767]{1,0:T(8,128)(2,1)S(1)}, u32[]{:S(2)}, u32[]{:S(2)}) %collective-permute-start.21) | collective-permute-done | bytes 785440 | tf_op jit(solution)/shard_map/ppermute | solution.py:790
  162.0 7.2 %collective-permute-done.26.r1 = bf16[256,767]{1,0:T(8,128)(2,1)S(1)} collective-permute-done((bf16[256,767]{1,0:T(8,128)(2,1)S(1)}, bf16[256,767]{1,0:T(8,128)(2,1)S(1)}, u32[]{:S(2)}, u32[]{:S(2)}) %collective-permute-start.26) | collective-permute-done | bytes 392736 | tf_op jit(solution)/shard_map/ppermute | solution.py:795
  172.7 10.0 %shard_map.241 = (bf16[2,256,3072]{2,1,0:T(8,128)(2,1)S(1)}, bf16[3,4,256,192]{3,2,1,0:T(8,128)(2,1)S(1)}, f32[256,767]{1,0:T(8,128)S(1)}, f32[8,3072]{1,0:T(8,1...) custom-call(s32[8]{0:T(128)S(1)} %stack.144.ids, ...), custom_call_target="tpu_custom_call" | custom-call | flops 3619160064 | bytes 15716352 | tf_op jit(solution)/shard_map/pallas_call | solution.py:395
  182.9 3.1 shard_map.242
  188.5 3.0 shard_map.243
  193.6 8.0 %collective-permute-done.31 = bf16[192,3456]{1,0:T(8,128)(2,1)} collective-permute-done((bf16[192,3456]{1,0:T(8,128)(2,1)}, bf16[192,3456]{1,0:T(8,128)(2,1)}, u32[]{:S(2)}, u32[]{:S(2)}) %collective-permute-start.31) | collective-permute-done | bytes 1327136 | tf_op jit(solution)/shard_map/ppermute | solution.py:790
  203.1 2.2 add_convert_fusion.3
  207.4 3.5 shard_map.244
  224.8 13.2 %shard_map.245 = (bf16[256,767]{1,0:T(8,128)(2,1)S(1)}, bf16[256,767]{1,0:T(8,128)(2,1)S(1)}, bf16[512,767]{1,0:T(8,128)(2,1)}, bf16[384,576]{1,0:T(8,128)(2,1)}...) custom-call(s32[8]{0:T(128)S(1)} %stack.144.ids, bf16[4,256,767]{2,1,0:T(8,128)(2,1)S(1)} %copy-done.76, ...), custom_call_target="tpu_custom_call" | custom-call | flops 7849377792 | bytes 6283264 | tf_op jit(solution)/shard_map/pallas_call | solution.py:517
  240.8 2.8 shard_map.246
  243.7 3.3 add_convert_fusion.2
  253.6 2.6 collective-permute-start.42
  256.1 3.2 collective-permute-done.39.r1
  261.1 5.8 %collective-permute-done.36 = bf16[2,104,576]{2,1,0:T(8,128)(2,1)S(1)} collective-permute-done((bf16[2,104,576]{2,1,0:T(8,128)(2,1)S(1)}, bf16[2,104,576]{2,1,0:T(8,128)(2,1)S(1)}, u32[]{:S(2)}, u32[]{:S(2)}) %collective-permute-start.36) | collective-permute-done | bytes 239648 | tf_op jit(solution)/shard_map/ppermute | solution.py:808
  270.5 2.9 collective-permute-start.40
  273.5 11.3 %collective-permute-done.41 = bf16[192,3456]{1,0:T(8,128)(2,1)S(1)} collective-permute-done((bf16[192,3456]{1,0:T(8,128)(2,1)S(1)}, bf16[192,3456]{1,0:T(8,128)(2,1)S(1)}, u32[]{:S(2)}, u32[]{:S(2)}) %collective-permute-start.41) | collective-permute-done | bytes 1327136 | tf_op jit(solution)/shard_map/ppermute | solution.py:790
  288.4 5.6 %collective-permute-start.46 = (bf16[2,48,3456]{2,1,0:T(8,128)(2,1)S(1)}, bf16[2,48,3456]{2,1,0:T(8,128)(2,1)S(1)}, u32[]{:S(2)}, u32[]{:S(2)}) collective-permute-start(bf16[2,48,3456]{2,1,0:T(8,128)(2,1)S(1)} %maximum_select_fusion.2), channel_id=1, source_target_pairs={{0,4},{4,0},{8,12},{12,8},{1,5},{5,1},{9,13},{13,9},{2,6},{6,2},{1... | collective-permute-start | bytes 1990664 | tf_op jit(solution)/shard_map/ppermute | solution.py:808
  297.0 3.0 collective-permute-start.44
  300.1 4.5 collective-permute-done.45
  304.5 5.3 %collective-permute-done.46 = bf16[2,48,3456]{2,1,0:T(8,128)(2,1)S(1)} collective-permute-done((bf16[2,48,3456]{2,1,0:T(8,128)(2,1)S(1)}, bf16[2,48,3456]{2,1,0:T(8,128)(2,1)S(1)}, u32[]{:S(2)}, u32[]{:S(2)}) %collective-permute-start.46) | collective-permute-done | bytes 663584 | tf_op jit(solution)/shard_map/ppermute | solution.py:808
  318.8 11.3 %collective-permute-done.50 = bf16[2,48,3456]{2,1,0:T(8,128)(2,1)S(1)} collective-permute-done((bf16[2,48,3456]{2,1,0:T(8,128)(2,1)S(1)}, bf16[2,48,3456]{2,1,0:T(8,128)(2,1)S(1)}, u32[]{:S(2)}, u32[]{:S(2)}) %collective-permute-start.50) | collective-permute-done | bytes 663584 | tf_op jit(solution)/shard_map/ppermute | solution.py:808
  330.2 4.7 collective-permute-start.54
  335.0 7.4 %collective-permute-done.48.refs_3_ = bf16[192,3456]{1,0:T(8,128)(2,1)S(1)} collective-permute-done((bf16[192,3456]{1,0:T(8,128)(2,1)S(1)}, bf16[192,3456]{1,0:T(8,128)(2,1)S(1)}, u32[]{:S(2)}, u32[]{:S(2)}) %collective-permute-start.48) | collective-permute-done | bytes 1327136 | tf_op jit(solution)/shard_map/ppermute | solution.py:795
  342.4 5.7 %collective-permute-start.58 = (bf16[1,48,3456]{2,1,0:T(8,128)(2,1)S(1)}, bf16[1,48,3456]{2,1,0:T(8,128)(2,1)S(1)}, u32[]{:S(2)}, u32[]{:S(2)}) collective-permute-start(bf16[1,48,3456]{2,1,0:T(8,128)(2,1)S(1)} %get-tuple-element.877), channel_id=1, source_target_pairs={{0,8},{4,12},{8,0},{12,4},{1,9},{5,13},{9,1},{13,5},{2,10},{6,14},... | collective-permute-start | bytes 995336 | tf_op jit(solution)/shard_map/ppermute | solution.py:808
  351.2 11.3 %collective-permute-done.58 = bf16[1,48,3456]{2,1,0:T(8,128)(2,1)S(1)} collective-permute-done((bf16[1,48,3456]{2,1,0:T(8,128)(2,1)S(1)}, bf16[1,48,3456]{2,1,0:T(8,128)(2,1)S(1)}, u32[]{:S(2)}, u32[]{:S(2)}) %collective-permute-start.58) | collective-permute-done | bytes 331808 | tf_op jit(solution)/shard_map/ppermute | solution.py:808
  362.6 3.0 collective-permute-start.62
  367.3 1.8 collective-permute-done.55
  369.2 8.3 %collective-permute-done.52 = bf16[416,576]{1,0:T(8,128)(2,1)S(1)} collective-permute-done((bf16[416,576]{1,0:T(8,128)(2,1)S(1)}, bf16[416,576]{1,0:T(8,128)(2,1)S(1)}, u32[]{:S(2)}, u32[]{:S(2)}) %collective-permute-start.52) | collective-permute-done | bytes 479264 | tf_op jit(solution)/shard_map/ppermute | solution.py:795
  377.6 2.0 collective-permute-start.61
  380.5 3.7 collective-permute-done.61
  386.3 7.4 %collective-permute-done.63 = bf16[416,576]{1,0:T(8,128)(2,1)S(1)} collective-permute-done((bf16[416,576]{1,0:T(8,128)(2,1)S(1)}, bf16[416,576]{1,0:T(8,128)(2,1)S(1)}, u32[]{:S(2)}, u32[]{:S(2)}) %collective-permute-start.63) | collective-permute-done | bytes 479264 | tf_op jit(solution)/shard_map/ppermute | solution.py:795
  401.4 2.3 shard_map.248
  403.7 3.7 shard_map.249
  407.4 2.5 shard_map.250
  409.9 30.2 %collective-permute-done.70 = bf16[2,416,576]{2,1,0:T(8,128)(2,1)S(1)} collective-permute-done((bf16[2,416,576]{2,1,0:T(8,128)(2,1)S(1)}, bf16[2,416,576]{2,1,0:T(8,128)(2,1)S(1)}, u32[]{:S(2)}, u32[]{:S(2)}) %collective-permute-start.70) | collective-permute-done | bytes 958496 | tf_op jit(solution)/shard_map/ppermute | solution.py:790
  441.7 3.2 collective-permute-start.72
  446.9 3.7 shard_map.251
  451.9 7.8 %shard_map.252 = f32[767,1,2304]{2,1,0:T(1,128)} custom-call(s32[8]{0:T(128)S(1)} %stack.144.ids, bf16[4,416,576]{2,1,0:T(8,128)(2,1)S(1)} %pad_maximum_fusion.1.refs_0_, bf16[4,416,576]{2,1,0:T(8,128)(2,1)S(1)} %collective-permute-done.71.refs_1_, bf16[4,416,576]{2,1,0:T(8,128)(2,1)S(1)} %collective-permute-done.72.refs_2_, ...), custom_call_target="tpu_custom_call" | custom-call | bytes 10603008 | tf_op jit(solution)/shard_map/pallas_call | solution.py:708
  459.7 1.8 shard_map.253
  461.5 2.7 collective-permute-done.74.refs_0_
  465.4 3.7 shard_map.254
  469.1 3.7 shard_map.255
  (439 shorter events, 117.8 us)
Async XLA Ops:
  0.7 50.8 %collective-permute-start.10 = (bf16[1,3072,767]{2,1,0:T(8,128)(2,1)}, bf16[1,3072,767]{2,1,0:T(8,128)(2,1)}, u32[]{:S(2)}, u32[]{:S(2)}) collective-permute-start(bf16[1,3072,767]{2,1,0:T(8,128)(2,1)} %dno.7), channel_id=1, source_target_pairs={{0,16},{16,0},{1,17},{17,1},{2,18},{18,2},{3,19},{19,3},{4,20},{20... | collective-permute-start | bytes 14137352 | tf_op jit(solution)/shard_map/ppermute | solution.py:803
  1.2 50.3 %collective-permute-start.9 = (bf16[1,767,3072]{2,1,0:T(8,128)(2,1)}, bf16[1,767,3072]{2,1,0:T(8,128)(2,1)}, u32[]{:S(2)}, u32[]{:S(2)}) collective-permute-start(bf16[1,767,3072]{2,1,0:T(8,128)(2,1)} %upo.7), channel_id=1, source_target_pairs={{0,16},{16,0},{1,17},{17,1},{2,18},{18,2},{3,19},{19,3},{4,20},{20... | collective-permute-start | bytes 14137352 | tf_op jit(solution)/shard_map/ppermute | solution.py:803
  7.6 11.6 %collective-permute-start.3 = (bf16[767,576]{0,1:T(8,128)(2,1)}, bf16[767,576]{0,1:T(8,128)(2,1)S(1)}, u32[]{:S(2)}, u32[]{:S(2)}) collective-permute-start(bf16[767,576]{0,1:T(8,128)(2,1)} %copy.51), channel_id=1, source_target_pairs={{0,16},{16,0},{1,17},{17,1},{2,18},{18,2},{3,19},{19,3},{4,20},{20... | collective-permute-start | bytes 2650760 | tf_op jit(solution)/shard_map/ppermute | solution.py:803
  9.9 9.3 %collective-permute-start = (bf16[256,767]{1,0:T(8,128)(2,1)S(1)}, bf16[256,767]{1,0:T(8,128)(2,1)S(1)}, u32[]{:S(2)}, u32[]{:S(2)}) collective-permute-start(bf16[256,767]{1,0:T(8,128)(2,1)S(1)} %shard_map.228.n0.x), channel_id=1, source_target_pairs={{0,2},{1,3},{2,0},{3,1},{16,17},{17,16},{18,19},{19,18},{4,6},{5,7... | collective-permute-start | bytes 1178120 | tf_op jit(solution)/shard_map/ppermute | solution.py:795
  17.9 7.8 %collective-permute-start.1 = (bf16[256,767]{1,0:T(8,128)(2,1)S(1)}, bf16[256,767]{1,0:T(8,128)(2,1)S(1)}, u32[]{:S(2)}, u32[]{:S(2)}) collective-permute-start(bf16[256,767]{1,0:T(8,128)(2,1)S(1)} %shard_map.228.n0.x), channel_id=1, source_target_pairs={{0,1},{1,0},{2,3},{3,2},{16,18},{17,19},{18,16},{19,17},{4,5},{5,4... | collective-permute-start | bytes 1178120 | tf_op jit(solution)/shard_map/ppermute | solution.py:790
  19.3 26.5 %collective-permute-start.8 = (bf16[768,767]{1,0:T(8,128)(2,1)}, bf16[768,767]{1,0:T(8,128)(2,1)}, u32[]{:S(2)}, u32[]{:S(2)}) collective-permute-start(bf16[768,767]{1,0:T(8,128)(2,1)} %bitcast.177), channel_id=1, source_target_pairs={{0,16},{16,0},{1,17},{17,1},{2,18},{18,2},{3,19},{19,3},{4,20},{20... | collective-permute-start | bytes 3534344 | tf_op jit(solution)/shard_map/ppermute | solution.py:803
  19.3 10.6 %collective-permute-start.2 = (bf16[256,767]{1,0:T(8,128)(2,1)S(1)}, bf16[256,767]{1,0:T(8,128)(2,1)S(1)}, u32[]{:S(2)}, u32[]{:S(2)}) collective-permute-start(bf16[256,767]{1,0:T(8,128)(2,1)S(1)} %collective-permute-done.n1), channel_id=1, source_target_pairs={{0,1},{1,0},{2,3},{3,2},{16,18},{17,19},{18,16},{19,17},{4,5},{5,4... | collective-permute-start | bytes 1178120 | tf_op jit(solution)/shard_map/ppermute | solution.py:790
  59.9 11.4 %collective-permute-start.11 = (bf16[256,767]{1,0:T(8,128)(2,1)S(1)}, bf16[256,767]{1,0:T(8,128)(2,1)S(1)}, u32[]{:S(2)}, u32[]{:S(2)}) collective-permute-start(bf16[256,767]{1,0:T(8,128)(2,1)S(1)} %get-tuple-element.537.n0), channel_id=1, source_target_pairs={{0,2},{1,3},{2,0},{3,1},{16,17},{17,16},{18,19},{19,18},{4,6},{5,7... | collective-permute-start | bytes 1178120 | tf_op jit(solution)/shard_map/ppermute | solution.py:795
  61.0 14.1 %collective-permute-start.12 = (bf16[256,767]{1,0:T(8,128)(2,1)S(1)}, bf16[256,767]{1,0:T(8,128)(2,1)S(1)}, u32[]{:S(2)}, u32[]{:S(2)}) collective-permute-start(bf16[256,767]{1,0:T(8,128)(2,1)S(1)} %get-tuple-element.537.n0), channel_id=1, source_target_pairs={{0,1},{1,0},{2,3},{3,2},{16,18},{17,19},{18,16},{19,17},{4,5},{5,4... | collective-permute-start | bytes 1178120 | tf_op jit(solution)/shard_map/ppermute | solution.py:790
  71.3 7.8 %collective-permute-start.13 = (bf16[256,767]{1,0:T(8,128)(2,1)S(1)}, bf16[256,767]{1,0:T(8,128)(2,1)S(1)}, u32[]{:S(2)}, u32[]{:S(2)}) collective-permute-start(bf16[256,767]{1,0:T(8,128)(2,1)S(1)} %collective-permute-done.11.n1), channel_id=1, source_target_pairs={{0,1},{1,0},{2,3},{3,2},{16,18},{17,19},{18,16},{19,17},{4,5},{5,4... | collective-permute-start | bytes 1178120 | tf_op jit(solution)/shard_map/ppermute | solution.py:790
  121.7 10.6 %collective-permute-start.20 = (bf16[2,192,3456]{2,1,0:T(8,128)(2,1)S(1)}, bf16[2,192,3456]{2,1,0:T(8,128)(2,1)S(1)}, u32[]{:S(2)}, u32[]{:S(2)}) collective-permute-start(bf16[2,192,3456]{2,1,0:T(8,128)(2,1)S(1)} %shard_map.235), channel_id=1, source_target_pairs={{0,16},{16,0},{1,17},{17,1},{2,18},{18,2},{3,19},{19,3},{4,20},{20... | collective-permute-start | bytes 7962632 | tf_op jit(solution)/shard_map/ppermute | solution.py:803
  123.7 7.0 %collective-permute-start.18 = (bf16[192,256]{1,0:T(8,128)(2,1)S(1)}, bf16[192,256]{1,0:T(8,128)(2,1)S(1)}, u32[]{:S(2)}, u32[]{:S(2)}) collective-permute-start(bf16[192,256]{1,0:T(8,128)(2,1)S(1)} %get-tuple-element.566), channel_id=1, source_target_pairs={{0,2},{1,3},{2,0},{3,1},{4,6},{5,7},{6,4},{7,5},{8,10},{9,11},{10,... | collective-permute-start | bytes 294920 | tf_op jit(solution)/shard_map/ppermute | solution.py:799
  123.9 6.7 %collective-permute-start.19 = (bf16[192,256]{1,0:T(8,128)(2,1)S(1)}, bf16[192,256]{1,0:T(8,128)(2,1)S(1)}, u32[]{:S(2)}, u32[]{:S(2)}) collective-permute-start(bf16[192,256]{1,0:T(8,128)(2,1)S(1)} %get-tuple-element.567), channel_id=1, source_target_pairs={{0,3},{1,2},{2,1},{3,0},{4,7},{5,6},{6,5},{7,4},{8,11},{9,10},{10,... | collective-permute-start | bytes 294920 | tf_op jit(solution)/shard_map/ppermute | solution.py:799
  132.2 17.1 %collective-permute-start.24 = (bf16[2,192,3456]{2,1,0:T(8,128)(2,1)S(1)}, bf16[2,192,3456]{2,1,0:T(8,128)(2,1)S(1)}, u32[]{:S(2)}, u32[]{:S(2)}) collective-permute-start(bf16[2,192,3456]{2,1,0:T(8,128)(2,1)S(1)} %shard_map.236), channel_id=1, source_target_pairs={{0,16},{16,0},{1,17},{17,1},{2,18},{18,2},{3,19},{19,3},{4,20},{20... | collective-permute-start | bytes 7962632 | tf_op jit(solution)/shard_map/ppermute | solution.py:803
  135.0 17.8 %collective-permute-start.23 = (bf16[192,3456]{1,0:T(8,128)(2,1)S(1)}, bf16[192,3456]{1,0:T(8,128)(2,1)S(1)}, u32[]{:S(2)}, u32[]{:S(2)}) collective-permute-start(bf16[192,3456]{1,0:T(8,128)(2,1)S(1)} %get-tuple-element.608), channel_id=1, source_target_pairs={{0,1},{1,0},{2,3},{3,2},{16,18},{17,19},{18,16},{19,17},{4,5},{5,4... | collective-permute-start | bytes 3981320 | tf_op jit(solution)/shard_map/ppermute | solution.py:790
  147.8 13.4 %collective-permute-start.21 = (bf16[512,767]{1,0:T(8,128)(2,1)S(1)}, bf16[512,767]{1,0:T(8,128)(2,1)S(1)}, u32[]{:S(2)}, u32[]{:S(2)}) collective-permute-start(bf16[512,767]{1,0:T(8,128)(2,1)S(1)} %get-tuple-element.606), channel_id=1, source_target_pairs={{0,1},{1,0},{2,3},{3,2},{16,18},{17,19},{18,16},{19,17},{4,5},{5,4... | collective-permute-start | bytes 2356232 | tf_op jit(solution)/shard_map/ppermute | solution.py:790
  149.3 6.7 %collective-permute-start.22 = (bf16[384,576]{1,0:T(8,128)(2,1)S(1)}, bf16[384,576]{1,0:T(8,128)(2,1)S(1)}, u32[]{:S(2)}, u32[]{:S(2)}) collective-permute-start(bf16[384,576]{1,0:T(8,128)(2,1)S(1)} %get-tuple-element.607), channel_id=1, source_target_pairs={{0,16},{16,0},{1,17},{17,1},{2,18},{18,2},{3,19},{19,3},{4,20},{20... | collective-permute-start | bytes 1327112 | tf_op jit(solution)/shard_map/ppermute | solution.py:803
  154.5 6.7 %collective-permute-start.25 = (bf16[256,767]{1,0:T(8,128)(2,1)S(1)}, bf16[256,767]{1,0:T(8,128)(2,1)S(1)}, u32[]{:S(2)}, u32[]{:S(2)}) collective-permute-start(bf16[256,767]{1,0:T(8,128)(2,1)S(1)} %broadcast_select_fusion.7), channel_id=1, source_target_pairs={{0,16},{16,0},{1,17},{17,1},{2,18},{18,2},{3,19},{19,3},{4,20},{20... | collective-permute-start | bytes 1178120 | tf_op jit(solution)/shard_map/ppermute | solution.py:803
  161.4 7.8 %collective-permute-start.26 = (bf16[256,767]{1,0:T(8,128)(2,1)S(1)}, bf16[256,767]{1,0:T(8,128)(2,1)S(1)}, u32[]{:S(2)}, u32[]{:S(2)}) collective-permute-start(bf16[256,767]{1,0:T(8,128)(2,1)S(1)} %add_convert_fusion.11), channel_id=1, source_target_pairs={{0,2},{1,3},{2,0},{3,1},{16,17},{17,16},{18,19},{19,18},{4,6},{5,7... | collective-permute-start | bytes 1178120 | tf_op jit(solution)/shard_map/ppermute | solution.py:795
  169.2 32.4 %collective-permute-start.31 = (bf16[192,3456]{1,0:T(8,128)(2,1)}, bf16[192,3456]{1,0:T(8,128)(2,1)}, u32[]{:S(2)}, u32[]{:S(2)}) collective-permute-start(bf16[192,3456]{1,0:T(8,128)(2,1)} %get-tuple-element.686), channel_id=1, source_target_pairs={{0,1},{1,0},{2,3},{3,2},{16,18},{17,19},{18,16},{19,17},{4,5},{5,4... | collective-permute-start | bytes 3981320 | tf_op jit(solution)/shard_map/ppermute | solution.py:790
  169.8 33.3 %collective-permute-start.32 = (bf16[192,3456]{1,0:T(8,128)(2,1)}, bf16[192,3456]{1,0:T(8,128)(2,1)}, u32[]{:S(2)}, u32[]{:S(2)}) collective-permute-start(bf16[192,3456]{1,0:T(8,128)(2,1)} %add_convert_fusion.5), channel_id=1, source_target_pairs={{0,2},{1,3},{2,0},{3,1},{16,17},{17,16},{18,19},{19,18},{4,6},{5,7... | collective-permute-start | bytes 3981320 | tf_op jit(solution)/shard_map/ppermute | solution.py:795
  186.0 21.1 %collective-permute-start.27 = (bf16[2,192,3456]{2,1,0:T(8,128)(2,1)}, bf16[2,192,3456]{2,1,0:T(8,128)(2,1)}, u32[]{:S(2)}, u32[]{:S(2)}) collective-permute-start(bf16[2,192,3456]{2,1,0:T(8,128)(2,1)} %shard_map.242), channel_id=1, source_target_pairs={{0,16},{16,0},{1,17},{17,1},{2,18},{18,2},{3,19},{19,3},{4,20},{20... | collective-permute-start | bytes 7962632 | tf_op jit(solution)/shard_map/ppermute | solution.py:803
  191.6 15.0 %collective-permute-start.28 = (bf16[192,256]{1,0:T(8,128)(2,1)S(1)}, bf16[192,256]{1,0:T(8,128)(2,1)S(1)}, u32[]{:S(2)}, u32[]{:S(2)}) collective-permute-start(bf16[192,256]{1,0:T(8,128)(2,1)S(1)} %copy-done.74), channel_id=1, source_target_pairs={{0,1},{1,0},{2,3},{3,2},{4,5},{5,4},{6,7},{7,6},{8,9},{9,8},{10,11... | collective-permute-start | bytes 294920 | tf_op jit(solution)/shard_map/ppermute | solution.py:799
  192.1 14.5 %collective-permute-start.29 = (bf16[192,256]{1,0:T(8,128)(2,1)S(1)}, bf16[192,256]{1,0:T(8,128)(2,1)S(1)}, u32[]{:S(2)}, u32[]{:S(2)}) collective-permute-start(bf16[192,256]{1,0:T(8,128)(2,1)S(1)} %copy-done.72), channel_id=1, source_target_pairs={{0,2},{1,3},{2,0},{3,1},{4,6},{5,7},{6,4},{7,5},{8,10},{9,11},{10,... | collective-permute-start | bytes 294920 | tf_op jit(solution)/shard_map/ppermute | solution.py:799
  203.1 36.6 %collective-permute-start.34 = (bf16[2,192,3456]{2,1,0:T(8,128)(2,1)}, bf16[2,192,3456]{2,1,0:T(8,128)(2,1)}, u32[]{:S(2)}, u32[]{:S(2)}) collective-permute-start(bf16[2,192,3456]{2,1,0:T(8,128)(2,1)} %shard_map.243), channel_id=1, source_target_pairs={{0,16},{16,0},{1,17},{17,1},{2,18},{18,2},{3,19},{19,3},{4,20},{20... | collective-permute-start | bytes 7962632 | tf_op jit(solution)/shard_map/ppermute | solution.py:803
  211.9 27.8 %collective-permute-start.33 = (bf16[192,3456]{1,0:T(8,128)(2,1)}, bf16[192,3456]{1,0:T(8,128)(2,1)}, u32[]{:S(2)}, u32[]{:S(2)}) collective-permute-start(bf16[192,3456]{1,0:T(8,128)(2,1)} %get-tuple-element.709), channel_id=1, source_target_pairs={{0,1},{1,0},{2,3},{3,2},{16,18},{17,19},{18,16},{19,17},{4,5},{5,4... | collective-permute-start | bytes 3981320 | tf_op jit(solution)/shard_map/ppermute | solution.py:790
  212.9 26.8 %collective-permute-start.35 = (bf16[2,48,3456]{2,1,0:T(8,128)(2,1)}, bf16[2,48,3456]{2,1,0:T(8,128)(2,1)S(1)}, u32[]{:S(2)}, u32[]{:S(2)}) collective-permute-start(bf16[2,48,3456]{2,1,0:T(8,128)(2,1)} %get-tuple-element.735), channel_id=1, source_target_pairs={{0,4},{4,0},{8,12},{12,8},{1,5},{5,1},{9,13},{13,9},{2,6},{6,2},{1... | collective-permute-start | bytes 1990664 | tf_op jit(solution)/shard_map/ppermute | solution.py:808
  238.1 12.4 %collective-permute-start.37 = (bf16[512,767]{1,0:T(8,128)(2,1)}, bf16[512,767]{1,0:T(8,128)(2,1)}, u32[]{:S(2)}, u32[]{:S(2)}) collective-permute-start(bf16[512,767]{1,0:T(8,128)(2,1)} %get-tuple-element.764), channel_id=1, source_target_pairs={{0,1},{1,0},{2,3},{3,2},{16,18},{17,19},{18,16},{19,17},{4,5},{5,4... | collective-permute-start | bytes 2356232 | tf_op jit(solution)/shard_map/ppermute | solution.py:790
  239.7 9.7 %collective-permute-start.38 = (bf16[384,576]{1,0:T(8,128)(2,1)}, bf16[384,576]{1,0:T(8,128)(2,1)}, u32[]{:S(2)}, u32[]{:S(2)}) collective-permute-start(bf16[384,576]{1,0:T(8,128)(2,1)} %get-tuple-element.765), channel_id=1, source_target_pairs={{0,16},{16,0},{1,17},{17,1},{2,18},{18,2},{3,19},{19,3},{4,20},{20... | collective-permute-start | bytes 1327112 | tf_op jit(solution)/shard_map/ppermute | solution.py:803
  251.5 7.8 %collective-permute-start.39 = (bf16[256,767]{1,0:T(8,128)(2,1)S(1)}, bf16[256,767]{1,0:T(8,128)(2,1)S(1)}, u32[]{:S(2)}, u32[]{:S(2)}) collective-permute-start(bf16[256,767]{1,0:T(8,128)(2,1)S(1)} %add_convert_fusion.10), channel_id=1, source_target_pairs={{0,2},{1,3},{2,0},{3,1},{16,17},{17,16},{18,19},{19,18},{4,6},{5,7... | collective-permute-start | bytes 1178120 | tf_op jit(solution)/shard_map/ppermute | solution.py:795
  253.1 13.8 %collective-permute-start.36 = (bf16[2,104,576]{2,1,0:T(8,128)(2,1)S(1)}, bf16[2,104,576]{2,1,0:T(8,128)(2,1)S(1)}, u32[]{:S(2)}, u32[]{:S(2)}) collective-permute-start(bf16[2,104,576]{2,1,0:T(8,128)(2,1)S(1)} %get-tuple-element.762), channel_id=1, source_target_pairs={{0,4},{4,0},{8,12},{12,8},{1,5},{5,1},{9,13},{13,9},{2,6},{6,2},{1... | collective-permute-start | bytes 718856 | tf_op jit(solution)/shard_map/ppermute | solution.py:808
  253.6 16.3 %collective-permute-start.42 = (bf16[1,48,3456]{2,1,0:T(8,128)(2,1)S(1)}, bf16[1,48,3456]{2,1,0:T(8,128)(2,1)S(1)}, u32[]{:S(2)}, u32[]{:S(2)}) collective-permute-start(bf16[1,48,3456]{2,1,0:T(8,128)(2,1)S(1)} %copy-done.98), channel_id=1, source_target_pairs={{0,8},{4,12},{8,0},{12,4},{1,9},{5,13},{9,1},{13,5},{2,10},{6,14},... | collective-permute-start | bytes 995336 | tf_op jit(solution)/shard_map/ppermute | solution.py:808
  267.0 17.8 %collective-permute-start.41 = (bf16[192,3456]{1,0:T(8,128)(2,1)S(1)}, bf16[192,3456]{1,0:T(8,128)(2,1)S(1)}, u32[]{:S(2)}, u32[]{:S(2)}) collective-permute-start(bf16[192,3456]{1,0:T(8,128)(2,1)S(1)} %copy-done.58), channel_id=1, source_target_pairs={{0,1},{1,0},{2,3},{3,2},{16,18},{17,19},{18,16},{19,17},{4,5},{5,4... | collective-permute-start | bytes 3981320 | tf_op jit(solution)/shard_map/ppermute | solution.py:790
  270.0 14.8 %collective-permute-start.43 = (bf16[1,48,3456]{2,1,0:T(8,128)(2,1)S(1)}, bf16[1,48,3456]{2,1,0:T(8,128)(2,1)S(1)}, u32[]{:S(2)}, u32[]{:S(2)}) collective-permute-start(bf16[1,48,3456]{2,1,0:T(8,128)(2,1)S(1)} %add_convert_fusion.13), channel_id=1, source_target_pairs={{0,8},{4,12},{8,0},{12,4},{1,9},{5,13},{9,1},{13,5},{2,10},{6,14},... | collective-permute-start | bytes 995336 | tf_op jit(solution)/shard_map/ppermute | solution.py:808
  270.5 24.8 %collective-permute-start.40 = (bf16[1,104,576]{2,1,0:T(8,128)(2,1)}, bf16[1,104,576]{2,1,0:T(8,128)(2,1)}, u32[]{:S(2)}, u32[]{:S(2)}) collective-permute-start(bf16[1,104,576]{2,1,0:T(8,128)(2,1)} %get-tuple-element.792), channel_id=1, source_target_pairs={{0,8},{4,12},{8,0},{12,4},{1,9},{5,13},{9,1},{13,5},{2,10},{6,14},... | collective-permute-start | bytes 359432 | tf_op jit(solution)/shard_map/ppermute | solution.py:808
  286.4 18.2 %collective-permute-start.45 = (bf16[192,3456]{1,0:T(8,128)(2,1)}, bf16[192,3456]{1,0:T(8,128)(2,1)}, u32[]{:S(2)}, u32[]{:S(2)}) collective-permute-start(bf16[192,3456]{1,0:T(8,128)(2,1)} %add_convert_fusion.2), channel_id=1, source_target_pairs={{0,2},{1,3},{2,0},{3,1},{16,17},{17,16},{18,19},{19,18},{4,6},{5,7... | collective-permute-start | bytes 3981320 | tf_op jit(solution)/shard_map/ppermute | solution.py:795
  288.4 21.4 %collective-permute-start.46 = (bf16[2,48,3456]{2,1,0:T(8,128)(2,1)S(1)}, bf16[2,48,3456]{2,1,0:T(8,128)(2,1)S(1)}, u32[]{:S(2)}, u32[]{:S(2)}) collective-permute-start(bf16[2,48,3456]{2,1,0:T(8,128)(2,1)S(1)} %maximum_select_fusion.2), channel_id=1, source_target_pairs={{0,4},{4,0},{8,12},{12,8},{1,5},{5,1},{9,13},{13,9},{2,6},{6,2},{1... | collective-permute-start | bytes 1990664 | tf_op jit(solution)/shard_map/ppermute | solution.py:808
  297.0 18.6 %collective-permute-start.44 = (bf16[1,104,576]{2,1,0:T(8,128)(2,1)S(1)}, bf16[1,104,576]{2,1,0:T(8,128)(2,1)S(1)}, u32[]{:S(2)}, u32[]{:S(2)}) collective-permute-start(bf16[1,104,576]{2,1,0:T(8,128)(2,1)S(1)} %add_convert_fusion.17), channel_id=1, source_target_pairs={{0,8},{4,12},{8,0},{12,4},{1,9},{5,13},{9,1},{13,5},{2,10},{6,14},... | collective-permute-start | bytes 359432 | tf_op jit(solution)/shard_map/ppermute | solution.py:808
  300.0 17.1 %collective-permute-start.51 = (bf16[2,104,576]{2,1,0:T(8,128)(2,1)S(1)}, bf16[2,104,576]{2,1,0:T(8,128)(2,1)S(1)}, u32[]{:S(2)}, u32[]{:S(2)}) collective-permute-start(bf16[2,104,576]{2,1,0:T(8,128)(2,1)S(1)} %fusion.11), channel_id=1, source_target_pairs={{0,4},{4,0},{8,12},{12,8},{1,5},{5,1},{9,13},{13,9},{2,6},{6,2},{1... | collective-permute-start | bytes 718856 | tf_op jit(solution)/shard_map/ppermute | solution.py:808
  313.2 17.0 %collective-permute-start.50 = (bf16[2,48,3456]{2,1,0:T(8,128)(2,1)S(1)}, bf16[2,48,3456]{2,1,0:T(8,128)(2,1)S(1)}, u32[]{:S(2)}, u32[]{:S(2)}) collective-permute-start(bf16[2,48,3456]{2,1,0:T(8,128)(2,1)S(1)} %fusion.5), channel_id=1, source_target_pairs={{0,4},{4,0},{8,12},{12,8},{1,5},{5,1},{9,13},{13,9},{2,6},{6,2},{1... | collective-permute-start | bytes 1990664 | tf_op jit(solution)/shard_map/ppermute | solution.py:808
  313.6 28.8 %collective-permute-start.48 = (bf16[192,3456]{1,0:T(8,128)(2,1)S(1)}, bf16[192,3456]{1,0:T(8,128)(2,1)S(1)}, u32[]{:S(2)}, u32[]{:S(2)}) collective-permute-start(bf16[192,3456]{1,0:T(8,128)(2,1)S(1)} %bitcast.151), channel_id=1, source_target_pairs={{0,2},{1,3},{2,0},{3,1},{16,17},{17,16},{18,19},{19,18},{4,6},{5,7... | collective-permute-start | bytes 3981320 | tf_op jit(solution)/shard_map/ppermute | solution.py:795
  314.5 33.6 %collective-permute-start.49 = (bf16[192,3456]{1,0:T(8,128)(2,1)S(1)}, bf16[192,3456]{1,0:T(8,128)(2,1)S(1)}, u32[]{:S(2)}, u32[]{:S(2)}) collective-permute-start(bf16[192,3456]{1,0:T(8,128)(2,1)S(1)} %bitcast.152), channel_id=1, source_target_pairs={{0,1},{1,0},{2,3},{3,2},{16,18},{17,19},{18,16},{19,17},{4,5},{5,4... | collective-permute-start | bytes 3981320 | tf_op jit(solution)/shard_map/ppermute | solution.py:790
  315.7 46.9 %collective-permute-start.57 = (bf16[192,3456]{1,0:T(8,128)(2,1)S(1)}, bf16[192,3456]{1,0:T(8,128)(2,1)S(1)}, u32[]{:S(2)}, u32[]{:S(2)}) collective-permute-start(bf16[192,3456]{1,0:T(8,128)(2,1)S(1)} %bitcast.153), channel_id=1, source_target_pairs={{0,16},{1,17},{2,18},{3,19},{4,20},{5,21},{6,22},{7,23},{8,24},{9,... | collective-permute-start | bytes 3981320 | tf_op jit(solution)/shard_map/ppermute | solution.py:812
  317.3 32.3 %collective-permute-start.47 = (bf16[2,104,576]{2,1,0:T(8,128)(2,1)S(1)}, bf16[2,104,576]{2,1,0:T(8,128)(2,1)S(1)}, u32[]{:S(2)}, u32[]{:S(2)}) collective-permute-start(bf16[2,104,576]{2,1,0:T(8,128)(2,1)S(1)} %maximum_select_fusion.6), channel_id=1, source_target_pairs={{0,4},{4,0},{8,12},{12,8},{1,5},{5,1},{9,13},{13,9},{2,6},{6,2},{1... | collective-permute-start | bytes 718856 | tf_op jit(solution)/shard_map/ppermute | solution.py:808
  330.2 21.0 %collective-permute-start.54 = (bf16[1,104,576]{2,1,0:T(8,128)(2,1)S(1)}, bf16[1,104,576]{2,1,0:T(8,128)(2,1)S(1)}, u32[]{:S(2)}, u32[]{:S(2)}) collective-permute-start(bf16[1,104,576]{2,1,0:T(8,128)(2,1)S(1)} %get-tuple-element.870), channel_id=1, source_target_pairs={{0,8},{4,12},{8,0},{12,4},{1,9},{5,13},{9,1},{13,5},{2,10},{6,14},... | collective-permute-start | bytes 359432 | tf_op jit(solution)/shard_map/ppermute | solution.py:808
  342.4 20.1 %collective-permute-start.58 = (bf16[1,48,3456]{2,1,0:T(8,128)(2,1)S(1)}, bf16[1,48,3456]{2,1,0:T(8,128)(2,1)S(1)}, u32[]{:S(2)}, u32[]{:S(2)}) collective-permute-start(bf16[1,48,3456]{2,1,0:T(8,128)(2,1)S(1)} %get-tuple-element.877), channel_id=1, source_target_pairs={{0,8},{4,12},{8,0},{12,4},{1,9},{5,13},{9,1},{13,5},{2,10},{6,14},... | collective-permute-start | bytes 995336 | tf_op jit(solution)/shard_map/ppermute | solution.py:808
  348.1 17.8 %collective-permute-start.56 = (bf16[192,3456]{1,0:T(8,128)(2,1)S(1)}, bf16[192,3456]{1,0:T(8,128)(2,1)S(1)}, u32[]{:S(2)}, u32[]{:S(2)}) collective-permute-start(bf16[192,3456]{1,0:T(8,128)(2,1)S(1)} %collective-permute-done.48.refs_3_), channel_id=1, source_target_pairs={{0,1},{1,0},{2,3},{3,2},{16,18},{17,19},{18,16},{19,17},{4,5},{5,4... | collective-permute-start | bytes 3981320 | tf_op jit(solution)/shard_map/ppermute | solution.py:790
  349.6 27.9 %collective-permute-start.53 = (bf16[192,3456]{1,0:T(8,128)(2,1)S(1)}, bf16[192,3456]{1,0:T(8,128)(2,1)S(1)}, u32[]{:S(2)}, u32[]{:S(2)}) collective-permute-start(bf16[192,3456]{1,0:T(8,128)(2,1)S(1)} %collective-permute-done.48.refs_3_), channel_id=1, source_target_pairs={{0,16},{1,17},{2,18},{3,19},{4,20},{5,21},{6,22},{7,23},{8,24},{9,... | collective-permute-start | bytes 3981320 | tf_op jit(solution)/shard_map/ppermute | solution.py:812
  362.5 6.6 %collective-permute-start.55 = (bf16[1,104,576]{2,1,0:T(8,128)(2,1)S(1)}, bf16[1,104,576]{2,1,0:T(8,128)(2,1)S(1)}, u32[]{:S(2)}, u32[]{:S(2)}) collective-permute-start(bf16[1,104,576]{2,1,0:T(8,128)(2,1)S(1)} %add_convert_fusion.16), channel_id=1, source_target_pairs={{0,8},{4,12},{8,0},{12,4},{1,9},{5,13},{9,1},{13,5},{2,10},{6,14},... | collective-permute-start | bytes 359432 | tf_op jit(solution)/shard_map/ppermute | solution.py:808
  362.5 14.9 %collective-permute-start.52 = (bf16[416,576]{1,0:T(8,128)(2,1)S(1)}, bf16[416,576]{1,0:T(8,128)(2,1)S(1)}, u32[]{:S(2)}, u32[]{:S(2)}) collective-permute-start(bf16[416,576]{1,0:T(8,128)(2,1)S(1)} %bitcast.172), channel_id=1, source_target_pairs={{0,2},{1,3},{2,0},{3,1},{16,17},{17,16},{18,19},{19,18},{4,6},{5,7... | collective-permute-start | bytes 1437704 | tf_op jit(solution)/shard_map/ppermute | solution.py:795
  362.6 15.0 %collective-permute-start.62 = (bf16[1,48,3456]{2,1,0:T(8,128)(2,1)S(1)}, bf16[1,48,3456]{2,1,0:T(8,128)(2,1)S(1)}, u32[]{:S(2)}, u32[]{:S(2)}) collective-permute-start(bf16[1,48,3456]{2,1,0:T(8,128)(2,1)S(1)} %add_convert_fusion.12), channel_id=1, source_target_pairs={{0,8},{4,12},{8,0},{12,4},{1,9},{5,13},{9,1},{13,5},{2,10},{6,14},... | collective-permute-start | bytes 995336 | tf_op jit(solution)/shard_map/ppermute | solution.py:808
  365.9 20.4 %collective-permute-start.60 = (bf16[192,3456]{1,0:T(8,128)(2,1)S(1)}, bf16[192,3456]{1,0:T(8,128)(2,1)S(1)}, u32[]{:S(2)}, u32[]{:S(2)}) collective-permute-start(bf16[192,3456]{1,0:T(8,128)(2,1)S(1)} %collective-permute-done.49.refs_3_), channel_id=1, source_target_pairs={{0,16},{1,17},{2,18},{3,19},{4,20},{5,21},{6,22},{7,23},{8,24},{9,... | collective-permute-start | bytes 3981320 | tf_op jit(solution)/shard_map/ppermute | solution.py:812
  379.6 15.0 %collective-permute-start.59 = (bf16[2,416,576]{2,1,0:T(8,128)(2,1)S(1)}, bf16[2,416,576]{2,1,0:T(8,128)(2,1)S(1)}, u32[]{:S(2)}, u32[]{:S(2)}) collective-permute-start(bf16[2,416,576]{2,1,0:T(8,128)(2,1)S(1)} %pad_maximum_fusion.2), channel_id=1, source_target_pairs={{0,1},{1,0},{2,3},{3,2},{16,18},{17,19},{18,16},{19,17},{4,5},{5,4... | collective-permute-start | bytes 2875400 | tf_op jit(solution)/shard_map/ppermute | solution.py:790
  380.3 14.3 %collective-permute-start.65 = (bf16[2,48,3456]{2,1,0:T(8,128)(2,1)S(1)}, bf16[2,48,3456]{2,1,0:T(8,128)(2,1)S(1)}, u32[]{:S(2)}, u32[]{:S(2)}) collective-permute-start(bf16[2,48,3456]{2,1,0:T(8,128)(2,1)S(1)} %maximum_select_fusion.3), channel_id=1, source_target_pairs={{0,4},{4,0},{8,12},{12,8},{1,5},{5,1},{9,13},{13,9},{2,6},{6,2},{1... | collective-permute-start | bytes 1990664 | tf_op jit(solution)/shard_map/ppermute | solution.py:808
  384.3 9.3 %collective-permute-start.63 = (bf16[416,576]{1,0:T(8,128)(2,1)S(1)}, bf16[416,576]{1,0:T(8,128)(2,1)S(1)}, u32[]{:S(2)}, u32[]{:S(2)}) collective-permute-start(bf16[416,576]{1,0:T(8,128)(2,1)S(1)} %bitcast.174), channel_id=1, source_target_pairs={{0,2},{1,3},{2,0},{3,1},{16,17},{17,16},{18,19},{19,18},{4,6},{5,7... | collective-permute-start | bytes 1437704 | tf_op jit(solution)/shard_map/ppermute | solution.py:795
  384.9 14.4 %collective-permute-start.64 = (bf16[192,3456]{1,0:T(8,128)(2,1)S(1)}, bf16[192,3456]{1,0:T(8,128)(2,1)S(1)}, u32[]{:S(2)}, u32[]{:S(2)}) collective-permute-start(bf16[192,3456]{1,0:T(8,128)(2,1)S(1)} %collective-permute-done.56.refs_3_), channel_id=1, source_target_pairs={{0,16},{1,17},{2,18},{3,19},{4,20},{5,21},{6,22},{7,23},{8,24},{9,... | collective-permute-start | bytes 3981320 | tf_op jit(solution)/shard_map/ppermute | solution.py:812
  395.0 8.7 %collective-permute-start.66 = (bf16[192,3456]{1,0:T(8,128)(2,1)S(1)}, bf16[192,3456]{1,0:T(8,128)(2,1)S(1)}, u32[]{:S(2)}, u32[]{:S(2)}) collective-permute-start(bf16[192,3456]{1,0:T(8,128)(2,1)S(1)} %bitcast.155), channel_id=1, source_target_pairs={{16,0},{17,1},{18,2},{19,3},{20,4},{21,5},{22,6},{23,7},{24,8},{25... | collective-permute-start | bytes 3981320 | tf_op jit(solution)/shard_map/ppermute | solution.py:812
  396.4 43.7 %collective-permute-start.68 = (bf16[192,3456]{1,0:T(8,128)(2,1)S(1)}, bf16[192,3456]{1,0:T(8,128)(2,1)S(1)}, u32[]{:S(2)}, u32[]{:S(2)}) collective-permute-start(bf16[192,3456]{1,0:T(8,128)(2,1)S(1)} %bitcast.156), channel_id=1, source_target_pairs={{0,2},{1,3},{2,0},{3,1},{16,17},{17,16},{18,19},{19,18},{4,6},{5,7... | collective-permute-start | bytes 3981320 | tf_op jit(solution)/shard_map/ppermute | solution.py:795
  397.1 43.0 %collective-permute-start.69 = (bf16[192,3456]{1,0:T(8,128)(2,1)S(1)}, bf16[192,3456]{1,0:T(8,128)(2,1)S(1)}, u32[]{:S(2)}, u32[]{:S(2)}) collective-permute-start(bf16[192,3456]{1,0:T(8,128)(2,1)S(1)} %bitcast.157), channel_id=1, source_target_pairs={{0,1},{1,0},{2,3},{3,2},{16,18},{17,19},{18,16},{19,17},{4,5},{5,4... | collective-permute-start | bytes 3981320 | tf_op jit(solution)/shard_map/ppermute | solution.py:790
  398.7 41.4 %collective-permute-start.70 = (bf16[2,416,576]{2,1,0:T(8,128)(2,1)S(1)}, bf16[2,416,576]{2,1,0:T(8,128)(2,1)S(1)}, u32[]{:S(2)}, u32[]{:S(2)}) collective-permute-start(bf16[2,416,576]{2,1,0:T(8,128)(2,1)S(1)} %pad_maximum_fusion.3), channel_id=1, source_target_pairs={{0,1},{1,0},{2,3},{3,2},{16,18},{17,19},{18,16},{19,17},{4,5},{5,4... | collective-permute-start | bytes 2875400 | tf_op jit(solution)/shard_map/ppermute | solution.py:790
  441.7 10.1 %collective-permute-start.72 = (bf16[4,416,576]{2,1,0:T(8,128)(2,1)S(1)}, bf16[4,416,576]{2,1,0:T(8,128)(2,1)S(1)}, u32[]{:S(2)}, u32[]{:S(2)}) collective-permute-start(bf16[4,416,576]{2,1,0:T(8,128)(2,1)S(1)} %pad_maximum_fusion.refs_3_), channel_id=1, source_target_pairs={{0,16},{1,17},{2,18},{3,19},{4,20},{5,21},{6,22},{7,23},{8,24},{9,... | collective-permute-start | bytes 5750792 | tf_op jit(solution)/shard_map/ppermute | solution.py:812
  445.0 6.9 %collective-permute-start.71 = (bf16[4,416,576]{2,1,0:T(8,128)(2,1)S(1)}, bf16[4,416,576]{2,1,0:T(8,128)(2,1)S(1)}, u32[]{:S(2)}, u32[]{:S(2)}) collective-permute-start(bf16[4,416,576]{2,1,0:T(8,128)(2,1)S(1)} %pad_maximum_fusion.1.refs_0_), channel_id=1, source_target_pairs={{16,0},{17,1},{18,2},{19,3},{20,4},{21,5},{22,6},{23,7},{24,8},{25... | collective-permute-start | bytes 5750792 | tf_op jit(solution)/shard_map/ppermute | solution.py:812
  446.3 17.8 %collective-permute-start.74 = (bf16[192,3456]{1,0:T(8,128)(2,1)S(1)}, bf16[192,3456]{1,0:T(8,128)(2,1)S(1)}, u32[]{:S(2)}, u32[]{:S(2)}) collective-permute-start(bf16[192,3456]{1,0:T(8,128)(2,1)S(1)} %collective-permute-done.68.refs_0_), channel_id=1, source_target_pairs={{0,1},{1,0},{2,3},{3,2},{16,18},{17,19},{18,16},{19,17},{4,5},{5,4... | collective-permute-start | bytes 3981320 | tf_op jit(solution)/shard_map/ppermute | solution.py:790
  450.6 13.6 %collective-permute-start.75 = (bf16[192,3456]{1,0:T(8,128)(2,1)S(1)}, bf16[192,3456]{1,0:T(8,128)(2,1)S(1)}, u32[]{:S(2)}, u32[]{:S(2)}) collective-permute-start(bf16[192,3456]{1,0:T(8,128)(2,1)S(1)} %collective-permute-done.69.refs_0_), channel_id=1, source_target_pairs={{16,0},{17,1},{18,2},{19,3},{20,4},{21,5},{22,6},{23,7},{24,8},{25... | collective-permute-start | bytes 3981320 | tf_op jit(solution)/shard_map/ppermute | solution.py:812
  (121 other events, 908.7 us)

commit v7 on v6

--- a/solution.py
+++ b/solution.py
@@ -62,7 +62,9 @@
 
 
 def cost(flops, nbytes, trans=0):
-    return pl.CostEstimate(flops=int(flops), bytes_accessed=int(nbytes), transcendentals=int(trans))
+    return pl.CostEstimate(
+        flops=int(2 * flops), bytes_accessed=int(2 * nbytes), transcendentals=int(2 * trans)
+    )
 
 
 SMEM = pl.BlockSpec(memory_space=pltpu.SMEM)

time: 479 us -> 476 us (level)
  waiting for transfers between devices: 174 us -> 188 us
  starting transfers between devices: 92.6 us -> 82.9 us
  local copies, waits for them, and re-layouts: 35.9 us -> 27.6 us
  Pallas kernels: 141 us -> 146 us
    ppermute x16, waiting for transfers between devices: 40.3 us -> 54.2 us  [dp_partner(): return lax.ppermute(v, 'dp', [(i, i ^ step) for i in range(n)])]
    ppermute x16, starting transfers between devices: 33.6 us -> 25 us  [dp_partner(): return lax.ppermute(v, 'dp', [(i, i ^ step) for i in range(n)])]
    pallas_call x2, Pallas kernels: 25.4 us -> 34 us  [attn_bwd(): pl.pallas_call(attn_bwd_kernel, in_specs=[SMEM] + [HBM] * 6 + [VMEM] * 4,...]
    unnamed x216 -> x202, local copies, waits for them, and re-layouts: 23.8 us -> 15.6 us
    ppermute x10, waiting for transfers between devices: 47.2 us -> 55.1 us  [to_second(): return lax.ppermute(v, ('section', 'seq'), pairs)]
    ppermute x16, waiting for transfers between devices: 73.2 us -> 65.6 us  [to_first(): return lax.ppermute(v, ('section', 'seq'), pairs)]
  transfers between devices with their start and end apart: 77 -> 77, of which waited for: 32 -> 35; matrix products, arithmetic and copies ran while one was open for 7% -> 7% of each run, Pallas kernels for 20% -> 21%
where the time goes in v7:
time: 476 us; the launch traced here: 470 us
  waiting for transfers between devices  188 us (39%)
  Pallas kernels  146 us (31%)
  starting transfers between devices  82.9 us (17%)
  local copies, waits for them, and re-layouts  27.6 us (6%)
  other arithmetic  20.8 us (4%)
  between operations  5.45 us (1%)
    ppermute x16, waiting for transfers between devices, to_first(): return lax.ppermute(v, ('section', 'seq'), pairs)  65.6 us
    ppermute x10, waiting for transfers between devices, to_second(): return lax.ppermute(v, ('section', 'seq'), pairs)  55.1 us
    ppermute x16, waiting for transfers between devices, dp_partner(): return lax.ppermute(v, 'dp', [(i, i ^ step) for i in range(n)])  54.2 us
    pallas_call x2, Pallas kernels, attn_bwd(): pl.pallas_call(attn_bwd_kernel, in_specs=[SMEM] + [HBM] * 6 + [VMEM] * 4,...  34 us
    ppermute x16, starting transfers between devices, dp_partner(): return lax.ppermute(v, 'dp', [(i, i ^ step) for i in range(n)])  25 us
    pallas_call x2, Pallas kernels, attn_fwd(): pl.pallas_call(functools.partial(attn_fwd_kernel, raw), in_specs=[SMEM] +...  22.9 us
    pallas_call x2, Pallas kernels, mlp_bwd(): pl.pallas_call(functools.partial(mlp_bwd_kernel, layer), grid_spec=grid,...  20.1 us
    pallas_call x2, Pallas kernels, mlp_fwd(): pl.pallas_call(functools.partial(mlp_fwd_kernel, layer), grid_spec=grid,...  17.7 us
  transfers between devices with their start and end apart: 77, of which 35 were waited for; matrix products, arithmetic and copies ran while one was open for 7% of the time, Pallas kernels for 21%

profile of v7, /device:TPU:0, one launch (start us, length us, event | category | flops | bytes accessed | tf_op | source)
XLA Modules:
  0.0 470.4 jit_solution(17414800387065471649)
XLA Ops:
  1.3 2.0 dynamic-slice_bitcast_fusion.2
  6.9 2.7 collective-permute-start
  15.7 2.9 collective-permute-start.1
  20.1 2.3 copy.52
  22.4 2.1 broadcast_select_fusion.2
  24.5 4.1 collective-permute-done.2.n3
  28.6 11.6 %shard_map.229 = (bf16[3,1024,64]{2,1,0:T(8,128)(2,1)S(1)}, bf16[3,1024,64]{2,1,0:T(8,128)(2,1)S(1)}, bf16[3,1024,64]{2,1,0:T(8,128)(2,1)S(1)}, f32[3,4,256]{2,1...) custom-call(s32[8]{0:T(128)S(1)} %stack.144.ids, ...), custom_call_target="tpu_custom_call" | custom-call | flops 6641418240 | bytes 6283264 | tf_op jit(solution)/shard_map/pallas_call | solution.py:196
  40.3 2.1 collective-permute-start.5
  45.4 2.6 collective-permute-done.6.a2
  49.5 8.3 %shard_map.230 = (f32[256,767]{1,0:T(8,128)S(1)}, f32[256,3072]{1,0:T(8,128)S(1)}, bf16[256,767]{1,0:T(8,128)(2,1)S(1)}, bf16[256,767]{1,0:T(8,128)(2,1)S(1)}, f...) custom-call(s32[8]{0:T(128)S(1)} %stack.144.ids, bf16[256,767]{1,0:T(8,128)(2,1)S(1)} %shard_map.228.n0.x, ...), custom_call_target="tpu_custom_call" | custom-call | flops 7238320128 | bytes 25141248 | tf_op jit(solution)/shard_map/pallas_call | solution.py:294
  59.0 10.1 %collective-permute-done.11.n1 = bf16[256,767]{1,0:T(8,128)(2,1)S(1)} collective-permute-done((bf16[256,767]{1,0:T(8,128)(2,1)S(1)}, bf16[256,767]{1,0:T(8,128)(2,1)S(1)}, u32[]{:S(2)}, u32[]{:S(2)}) %collective-permute-start.11) | collective-permute-done | bytes 392736 | tf_op jit(solution)/shard_map/ppermute | solution.py:797
  71.6 5.2 %collective-permute-done.13.n3 = bf16[256,767]{1,0:T(8,128)(2,1)S(1)} collective-permute-done((bf16[256,767]{1,0:T(8,128)(2,1)S(1)}, bf16[256,767]{1,0:T(8,128)(2,1)S(1)}, u32[]{:S(2)}, u32[]{:S(2)}) %collective-permute-start.13) | collective-permute-done | bytes 392736 | tf_op jit(solution)/shard_map/ppermute | solution.py:792
  76.8 11.2 %shard_map.232 = (bf16[3,1024,64]{2,1,0:T(8,128)(2,1)S(1)}, bf16[3,1024,64]{2,1,0:T(8,128)(2,1)S(1)}, bf16[3,1024,64]{2,1,0:T(8,128)(2,1)S(1)}, f32[3,4,256]{2,1...) custom-call(s32[8]{0:T(128)S(1)} %stack.144.ids, ...), custom_call_target="tpu_custom_call" | custom-call | flops 6641418240 | bytes 6283264 | tf_op jit(solution)/shard_map/pallas_call | solution.py:196
  91.2 2.4 collective-permute-start.16
  96.7 9.4 %shard_map.233 = (f32[256,767]{1,0:T(8,128)S(1)}, f32[256,3072]{1,0:T(8,128)S(1)}, bf16[256,767]{1,0:T(8,128)(2,1)S(1)}, bf16[256,767]{1,0:T(8,128)(2,1)}, f32[8...) custom-call(s32[8]{0:T(128)S(1)} %stack.144.ids, bf16[256,767]{1,0:T(8,128)(2,1)S(1)} %get-tuple-element.930.x, ...), custom_call_target="tpu_custom_call" | custom-call | flops 7238320128 | bytes 25141248 | tf_op jit(solution)/shard_map/pallas_call | solution.py:294
  107.8 2.0 copy-done.56
  109.9 10.1 %shard_map.234 = (bf16[2,256,3072]{2,1,0:T(8,128)(2,1)S(1)}, bf16[3,4,256,192]{3,2,1,0:T(8,128)(2,1)S(1)}, f32[256,767]{1,0:T(8,128)S(1)}, f32[8,3072]{1,0:T(8,1...) custom-call(s32[8]{0:T(128)S(1)} %stack.144.ids, ...), custom_call_target="tpu_custom_call" | custom-call | flops 7238320128 | bytes 31432704 | tf_op jit(solution)/shard_map/pallas_call | solution.py:397
  126.8 2.3 collective-permute-done.18.d2
  131.8 2.6 shard_map.237
  135.6 20.8 %shard_map.238 = (bf16[256,767]{1,0:T(8,128)(2,1)S(1)}, bf16[256,767]{1,0:T(8,128)(2,1)S(1)}, bf16[512,767]{1,0:T(8,128)(2,1)S(1)}, bf16[384,576]{1,0:T(8,128)(2...) custom-call(s32[8]{0:T(128)S(1)} %stack.144.ids, bf16[4,256,767]{2,1,0:T(8,128)(2,1)S(1)} %copy-done.64, ...), custom_call_target="tpu_custom_call" | custom-call | flops 15698755584 | bytes 12566528 | tf_op jit(solution)/shard_map/pallas_call | solution.py:519
  161.0 7.4 %collective-permute-done.21.r0 = bf16[512,767]{1,0:T(8,128)(2,1)S(1)} collective-permute-done((bf16[512,767]{1,0:T(8,128)(2,1)S(1)}, bf16[512,767]{1,0:T(8,128)(2,1)S(1)}, u32[]{:S(2)}, u32[]{:S(2)}) %collective-permute-start.21) | collective-permute-done | bytes 785440 | tf_op jit(solution)/shard_map/ppermute | solution.py:792
  169.8 6.7 %collective-permute-done.26.r1 = bf16[256,767]{1,0:T(8,128)(2,1)S(1)} collective-permute-done((bf16[256,767]{1,0:T(8,128)(2,1)S(1)}, bf16[256,767]{1,0:T(8,128)(2,1)S(1)}, u32[]{:S(2)}, u32[]{:S(2)}) %collective-permute-start.26) | collective-permute-done | bytes 392736 | tf_op jit(solution)/shard_map/ppermute | solution.py:797
  180.2 2.3 copy-done.46
  182.6 10.0 %shard_map.241 = (bf16[2,256,3072]{2,1,0:T(8,128)(2,1)S(1)}, bf16[3,4,256,192]{3,2,1,0:T(8,128)(2,1)S(1)}, f32[256,767]{1,0:T(8,128)S(1)}, f32[8,3072]{1,0:T(8,1...) custom-call(s32[8]{0:T(128)S(1)} %stack.144.ids, ...), custom_call_target="tpu_custom_call" | custom-call | flops 7238320128 | bytes 31432704 | tf_op jit(solution)/shard_map/pallas_call | solution.py:397
  192.7 3.0 shard_map.242
  202.2 8.1 %collective-permute-done.31 = bf16[192,3456]{1,0:T(8,128)(2,1)} collective-permute-done((bf16[192,3456]{1,0:T(8,128)(2,1)}, bf16[192,3456]{1,0:T(8,128)(2,1)}, u32[]{:S(2)}, u32[]{:S(2)}) %collective-permute-start.31) | collective-permute-done | bytes 1327136 | tf_op jit(solution)/shard_map/ppermute | solution.py:792
  210.3 1.8 collective-permute-start.30
  212.0 2.2 add_convert_fusion.3
  214.5 1.8 collective-permute-start.35
  216.4 2.8 shard_map.244
  221.1 13.2 %shard_map.245 = (bf16[256,767]{1,0:T(8,128)(2,1)S(1)}, bf16[256,767]{1,0:T(8,128)(2,1)S(1)}, bf16[512,767]{1,0:T(8,128)(2,1)}, bf16[384,576]{1,0:T(8,128)(2,1)}...) custom-call(s32[8]{0:T(128)S(1)} %stack.144.ids, bf16[4,256,767]{2,1,0:T(8,128)(2,1)S(1)} %copy-done.62, ...), custom_call_target="tpu_custom_call" | custom-call | flops 15698755584 | bytes 12566528 | tf_op jit(solution)/shard_map/pallas_call | solution.py:519
  235.7 2.4 collective-permute-done.33
  244.7 2.1 collective-permute-done.37.r0
  248.9 1.8 collective-permute-start.36
  250.6 2.5 collective-permute-start.42
  253.2 2.5 collective-permute-done.39.r1
  257.4 4.4 collective-permute-done.36
  263.9 9.8 %collective-permute-done.42 = bf16[1,48,3456]{2,1,0:T(8,128)(2,1)S(1)} collective-permute-done((bf16[1,48,3456]{2,1,0:T(8,128)(2,1)S(1)}, bf16[1,48,3456]{2,1,0:T(8,128)(2,1)S(1)}, u32[]{:S(2)}, u32[]{:S(2)}) %collective-permute-start.42) | collective-permute-done | bytes 331808 | tf_op jit(solution)/shard_map/ppermute | solution.py:810
  274.3 2.9 collective-permute-start.40
  277.3 2.4 collective-permute-done.41
  279.6 6.1 %collective-permute-done.43 = bf16[1,48,3456]{2,1,0:T(8,128)(2,1)S(1)} collective-permute-done((bf16[1,48,3456]{2,1,0:T(8,128)(2,1)S(1)}, bf16[1,48,3456]{2,1,0:T(8,128)(2,1)S(1)}, u32[]{:S(2)}, u32[]{:S(2)}) %collective-permute-start.43) | collective-permute-done | bytes 331808 | tf_op jit(solution)/shard_map/ppermute | solution.py:810
  293.1 2.9 collective-permute-start.44
  296.1 9.5 %collective-permute-done.45 = bf16[192,3456]{1,0:T(8,128)(2,1)} collective-permute-done((bf16[192,3456]{1,0:T(8,128)(2,1)}, bf16[192,3456]{1,0:T(8,128)(2,1)}, u32[]{:S(2)}, u32[]{:S(2)}) %collective-permute-start.45) | collective-permute-done | bytes 1327136 | tf_op jit(solution)/shard_map/ppermute | solution.py:797
  305.6 2.0 collective-permute-done.46
  314.8 13.6 %collective-permute-done.50 = bf16[2,48,3456]{2,1,0:T(8,128)(2,1)S(1)} collective-permute-done((bf16[2,48,3456]{2,1,0:T(8,128)(2,1)S(1)}, bf16[2,48,3456]{2,1,0:T(8,128)(2,1)S(1)}, u32[]{:S(2)}, u32[]{:S(2)}) %collective-permute-start.50) | collective-permute-done | bytes 663584 | tf_op jit(solution)/shard_map/ppermute | solution.py:810
  329.7 10.7 %collective-permute-done.48.refs_3_ = bf16[192,3456]{1,0:T(8,128)(2,1)S(1)} collective-permute-done((bf16[192,3456]{1,0:T(8,128)(2,1)S(1)}, bf16[192,3456]{1,0:T(8,128)(2,1)S(1)}, u32[]{:S(2)}, u32[]{:S(2)}) %collective-permute-start.48) | collective-permute-done | bytes 1327136 | tf_op jit(solution)/shard_map/ppermute | solution.py:797
  340.4 2.8 collective-permute-start.58
  346.2 12.8 %collective-permute-done.58 = bf16[1,48,3456]{2,1,0:T(8,128)(2,1)S(1)} collective-permute-done((bf16[1,48,3456]{2,1,0:T(8,128)(2,1)S(1)}, bf16[1,48,3456]{2,1,0:T(8,128)(2,1)S(1)}, u32[]{:S(2)}, u32[]{:S(2)}) %collective-permute-start.58) | collective-permute-done | bytes 331808 | tf_op jit(solution)/shard_map/ppermute | solution.py:810
  360.0 3.0 collective-permute-start.62
  366.2 7.8 %collective-permute-done.52 = bf16[416,576]{1,0:T(8,128)(2,1)S(1)} collective-permute-done((bf16[416,576]{1,0:T(8,128)(2,1)S(1)}, bf16[416,576]{1,0:T(8,128)(2,1)S(1)}, u32[]{:S(2)}, u32[]{:S(2)}) %collective-permute-start.52) | collective-permute-done | bytes 479264 | tf_op jit(solution)/shard_map/ppermute | solution.py:797
  374.1 3.0 collective-permute-start.61
  377.9 3.6 collective-permute-done.61
  383.2 7.8 %collective-permute-done.63 = bf16[416,576]{1,0:T(8,128)(2,1)S(1)} collective-permute-done((bf16[416,576]{1,0:T(8,128)(2,1)S(1)}, bf16[416,576]{1,0:T(8,128)(2,1)S(1)}, u32[]{:S(2)}, u32[]{:S(2)}) %collective-permute-start.63) | collective-permute-done | bytes 479264 | tf_op jit(solution)/shard_map/ppermute | solution.py:797
  398.5 2.3 shard_map.248
  400.8 3.7 shard_map.249
  404.5 2.5 shard_map.250
  407.1 30.4 %collective-permute-done.70 = bf16[2,416,576]{2,1,0:T(8,128)(2,1)S(1)} collective-permute-done((bf16[2,416,576]{2,1,0:T(8,128)(2,1)S(1)}, bf16[2,416,576]{2,1,0:T(8,128)(2,1)S(1)}, u32[]{:S(2)}, u32[]{:S(2)}) %collective-permute-start.70) | collective-permute-done | bytes 958496 | tf_op jit(solution)/shard_map/ppermute | solution.py:792
  439.0 3.2 collective-permute-start.72
  444.3 3.7 shard_map.251
  449.3 7.8 %shard_map.252 = f32[767,1,2304]{2,1,0:T(1,128)} custom-call(s32[8]{0:T(128)S(1)} %stack.144.ids, bf16[4,416,576]{2,1,0:T(8,128)(2,1)S(1)} %pad_maximum_fusion.1.refs_0_, bf16[4,416,576]{2,1,0:T(8,128)(2,1)S(1)} %collective-permute-done.71.refs_1_, bf16[4,416,576]{2,1,0:T(8,128)(2,1)S(1)} %collective-permute-done.72.refs_2_, ...), custom_call_target="tpu_custom_call" | custom-call | bytes 21206016 | tf_op jit(solution)/shard_map/pallas_call | solution.py:710
  457.1 1.8 shard_map.253
  458.9 2.5 collective-permute-done.74.refs_0_
  462.7 3.7 shard_map.254
  466.4 3.7 shard_map.255
  (427 shorter events, 107.1 us)
Async XLA Ops:
  0.7 48.8 %collective-permute-start.10 = (bf16[1,3072,767]{2,1,0:T(8,128)(2,1)}, bf16[1,3072,767]{2,1,0:T(8,128)(2,1)}, u32[]{:S(2)}, u32[]{:S(2)}) collective-permute-start(bf16[1,3072,767]{2,1,0:T(8,128)(2,1)} %dno.7), channel_id=1, source_target_pairs={{0,16},{16,0},{1,17},{17,1},{2,18},{18,2},{3,19},{19,3},{4,20},{20... | collective-permute-start | bytes 14137352 | tf_op jit(solution)/shard_map/ppermute | solution.py:805
  1.2 48.3 %collective-permute-start.9 = (bf16[1,767,3072]{2,1,0:T(8,128)(2,1)}, bf16[1,767,3072]{2,1,0:T(8,128)(2,1)}, u32[]{:S(2)}, u32[]{:S(2)}) collective-permute-start(bf16[1,767,3072]{2,1,0:T(8,128)(2,1)} %upo.7), channel_id=1, source_target_pairs={{0,16},{16,0},{1,17},{17,1},{2,18},{18,2},{3,19},{19,3},{4,20},{20... | collective-permute-start | bytes 14137352 | tf_op jit(solution)/shard_map/ppermute | solution.py:805
  4.9 13.7 %collective-permute-start.3 = (bf16[767,576]{0,1:T(8,128)(2,1)}, bf16[767,576]{0,1:T(8,128)(2,1)}, u32[]{:S(2)}, u32[]{:S(2)}) collective-permute-start(bf16[767,576]{0,1:T(8,128)(2,1)} %copy.51), channel_id=1, source_target_pairs={{0,16},{16,0},{1,17},{17,1},{2,18},{18,2},{3,19},{19,3},{4,20},{20... | collective-permute-start | bytes 2650760 | tf_op jit(solution)/shard_map/ppermute | solution.py:805
  6.9 11.7 %collective-permute-start = (bf16[256,767]{1,0:T(8,128)(2,1)S(1)}, bf16[256,767]{1,0:T(8,128)(2,1)S(1)}, u32[]{:S(2)}, u32[]{:S(2)}) collective-permute-start(bf16[256,767]{1,0:T(8,128)(2,1)S(1)} %shard_map.228.n0.x), channel_id=1, source_target_pairs={{0,2},{1,3},{2,0},{3,1},{16,17},{17,16},{18,19},{19,18},{4,6},{5,7... | collective-permute-start | bytes 1178120 | tf_op jit(solution)/shard_map/ppermute | solution.py:797
  15.7 8.8 %collective-permute-start.1 = (bf16[256,767]{1,0:T(8,128)(2,1)S(1)}, bf16[256,767]{1,0:T(8,128)(2,1)S(1)}, u32[]{:S(2)}, u32[]{:S(2)}) collective-permute-start(bf16[256,767]{1,0:T(8,128)(2,1)S(1)} %shard_map.228.n0.x), channel_id=1, source_target_pairs={{0,1},{1,0},{2,3},{3,2},{16,18},{17,19},{18,16},{19,17},{4,5},{5,4... | collective-permute-start | bytes 1178120 | tf_op jit(solution)/shard_map/ppermute | solution.py:792
  18.6 25.3 %collective-permute-start.8 = (bf16[768,767]{1,0:T(8,128)(2,1)}, bf16[768,767]{1,0:T(8,128)(2,1)}, u32[]{:S(2)}, u32[]{:S(2)}) collective-permute-start(bf16[768,767]{1,0:T(8,128)(2,1)} %bitcast.181), channel_id=1, source_target_pairs={{0,16},{16,0},{1,17},{17,1},{2,18},{18,2},{3,19},{19,3},{4,20},{20... | collective-permute-start | bytes 3534344 | tf_op jit(solution)/shard_map/ppermute | solution.py:805
  18.6 10.0 %collective-permute-start.2 = (bf16[256,767]{1,0:T(8,128)(2,1)S(1)}, bf16[256,767]{1,0:T(8,128)(2,1)S(1)}, u32[]{:S(2)}, u32[]{:S(2)}) collective-permute-start(bf16[256,767]{1,0:T(8,128)(2,1)S(1)} %collective-permute-done.n1), channel_id=1, source_target_pairs={{0,1},{1,0},{2,3},{3,2},{16,18},{17,19},{18,16},{19,17},{4,5},{5,4... | collective-permute-start | bytes 1178120 | tf_op jit(solution)/shard_map/ppermute | solution.py:792
  57.9 11.2 %collective-permute-start.11 = (bf16[256,767]{1,0:T(8,128)(2,1)S(1)}, bf16[256,767]{1,0:T(8,128)(2,1)S(1)}, u32[]{:S(2)}, u32[]{:S(2)}) collective-permute-start(bf16[256,767]{1,0:T(8,128)(2,1)S(1)} %get-tuple-element.537.n0), channel_id=1, source_target_pairs={{0,2},{1,3},{2,0},{3,1},{16,17},{17,16},{18,19},{19,18},{4,6},{5,7... | collective-permute-start | bytes 1178120 | tf_op jit(solution)/shard_map/ppermute | solution.py:797
  58.4 13.2 %collective-permute-start.12 = (bf16[256,767]{1,0:T(8,128)(2,1)S(1)}, bf16[256,767]{1,0:T(8,128)(2,1)S(1)}, u32[]{:S(2)}, u32[]{:S(2)}) collective-permute-start(bf16[256,767]{1,0:T(8,128)(2,1)S(1)} %get-tuple-element.537.n0), channel_id=1, source_target_pairs={{0,1},{1,0},{2,3},{3,2},{16,18},{17,19},{18,16},{19,17},{4,5},{5,4... | collective-permute-start | bytes 1178120 | tf_op jit(solution)/shard_map/ppermute | solution.py:792
  69.0 7.8 %collective-permute-start.13 = (bf16[256,767]{1,0:T(8,128)(2,1)S(1)}, bf16[256,767]{1,0:T(8,128)(2,1)S(1)}, u32[]{:S(2)}, u32[]{:S(2)}) collective-permute-start(bf16[256,767]{1,0:T(8,128)(2,1)S(1)} %collective-permute-done.11.n1), channel_id=1, source_target_pairs={{0,1},{1,0},{2,3},{3,2},{16,18},{17,19},{18,16},{19,17},{4,5},{5,4... | collective-permute-start | bytes 1178120 | tf_op jit(solution)/shard_map/ppermute | solution.py:792
  121.5 10.3 %collective-permute-start.20 = (bf16[2,192,3456]{2,1,0:T(8,128)(2,1)S(1)}, bf16[2,192,3456]{2,1,0:T(8,128)(2,1)S(1)}, u32[]{:S(2)}, u32[]{:S(2)}) collective-permute-start(bf16[2,192,3456]{2,1,0:T(8,128)(2,1)S(1)} %shard_map.235), channel_id=1, source_target_pairs={{0,16},{16,0},{1,17},{17,1},{2,18},{18,2},{3,19},{19,3},{4,20},{20... | collective-permute-start | bytes 7962632 | tf_op jit(solution)/shard_map/ppermute | solution.py:805
  122.9 6.2 %collective-permute-start.18 = (bf16[192,256]{1,0:T(8,128)(2,1)S(1)}, bf16[192,256]{1,0:T(8,128)(2,1)S(1)}, u32[]{:S(2)}, u32[]{:S(2)}) collective-permute-start(bf16[192,256]{1,0:T(8,128)(2,1)S(1)} %get-tuple-element.566), channel_id=1, source_target_pairs={{0,2},{1,3},{2,0},{3,1},{4,6},{5,7},{6,4},{7,5},{8,10},{9,11},{10,... | collective-permute-start | bytes 294920 | tf_op jit(solution)/shard_map/ppermute | solution.py:801
  131.7 25.6 %collective-permute-start.24 = (bf16[2,192,3456]{2,1,0:T(8,128)(2,1)S(1)}, bf16[2,192,3456]{2,1,0:T(8,128)(2,1)S(1)}, u32[]{:S(2)}, u32[]{:S(2)}) collective-permute-start(bf16[2,192,3456]{2,1,0:T(8,128)(2,1)S(1)} %shard_map.236), channel_id=1, source_target_pairs={{0,16},{16,0},{1,17},{17,1},{2,18},{18,2},{3,19},{19,3},{4,20},{20... | collective-permute-start | bytes 7962632 | tf_op jit(solution)/shard_map/ppermute | solution.py:805
  134.4 22.9 %collective-permute-start.23 = (bf16[192,3456]{1,0:T(8,128)(2,1)S(1)}, bf16[192,3456]{1,0:T(8,128)(2,1)S(1)}, u32[]{:S(2)}, u32[]{:S(2)}) collective-permute-start(bf16[192,3456]{1,0:T(8,128)(2,1)S(1)} %get-tuple-element.608), channel_id=1, source_target_pairs={{0,1},{1,0},{2,3},{3,2},{16,18},{17,19},{18,16},{19,17},{4,5},{5,4... | collective-permute-start | bytes 3981320 | tf_op jit(solution)/shard_map/ppermute | solution.py:792
  156.4 12.1 %collective-permute-start.21 = (bf16[512,767]{1,0:T(8,128)(2,1)S(1)}, bf16[512,767]{1,0:T(8,128)(2,1)S(1)}, u32[]{:S(2)}, u32[]{:S(2)}) collective-permute-start(bf16[512,767]{1,0:T(8,128)(2,1)S(1)} %get-tuple-element.606), channel_id=1, source_target_pairs={{0,1},{1,0},{2,3},{3,2},{16,18},{17,19},{18,16},{19,17},{4,5},{5,4... | collective-permute-start | bytes 2356232 | tf_op jit(solution)/shard_map/ppermute | solution.py:792
  159.0 9.5 %collective-permute-start.25 = (bf16[256,767]{1,0:T(8,128)(2,1)S(1)}, bf16[256,767]{1,0:T(8,128)(2,1)S(1)}, u32[]{:S(2)}, u32[]{:S(2)}) collective-permute-start(bf16[256,767]{1,0:T(8,128)(2,1)S(1)} %broadcast_select_fusion.7), channel_id=1, source_target_pairs={{0,16},{16,0},{1,17},{17,1},{2,18},{18,2},{3,19},{19,3},{4,20},{20... | collective-permute-start | bytes 1178120 | tf_op jit(solution)/shard_map/ppermute | solution.py:805
  168.6 7.8 %collective-permute-start.26 = (bf16[256,767]{1,0:T(8,128)(2,1)S(1)}, bf16[256,767]{1,0:T(8,128)(2,1)S(1)}, u32[]{:S(2)}, u32[]{:S(2)}) collective-permute-start(bf16[256,767]{1,0:T(8,128)(2,1)S(1)} %add_convert_fusion.11), channel_id=1, source_target_pairs={{0,2},{1,3},{2,0},{3,1},{16,17},{17,16},{18,19},{19,18},{4,6},{5,7... | collective-permute-start | bytes 1178120 | tf_op jit(solution)/shard_map/ppermute | solution.py:797
  177.9 32.4 %collective-permute-start.31 = (bf16[192,3456]{1,0:T(8,128)(2,1)}, bf16[192,3456]{1,0:T(8,128)(2,1)}, u32[]{:S(2)}, u32[]{:S(2)}) collective-permute-start(bf16[192,3456]{1,0:T(8,128)(2,1)} %get-tuple-element.686), channel_id=1, source_target_pairs={{0,1},{1,0},{2,3},{3,2},{16,18},{17,19},{18,16},{19,17},{4,5},{5,4... | collective-permute-start | bytes 3981320 | tf_op jit(solution)/shard_map/ppermute | solution.py:792
  178.8 33.3 %collective-permute-start.32 = (bf16[192,3456]{1,0:T(8,128)(2,1)}, bf16[192,3456]{1,0:T(8,128)(2,1)}, u32[]{:S(2)}, u32[]{:S(2)}) collective-permute-start(bf16[192,3456]{1,0:T(8,128)(2,1)} %add_convert_fusion.5), channel_id=1, source_target_pairs={{0,2},{1,3},{2,0},{3,1},{16,17},{17,16},{18,19},{19,18},{4,6},{5,7... | collective-permute-start | bytes 3981320 | tf_op jit(solution)/shard_map/ppermute | solution.py:797
  195.8 20.6 %collective-permute-start.27 = (bf16[2,192,3456]{2,1,0:T(8,128)(2,1)}, bf16[2,192,3456]{2,1,0:T(8,128)(2,1)}, u32[]{:S(2)}, u32[]{:S(2)}) collective-permute-start(bf16[2,192,3456]{2,1,0:T(8,128)(2,1)} %shard_map.242), channel_id=1, source_target_pairs={{0,16},{16,0},{1,17},{17,1},{2,18},{18,2},{3,19},{19,3},{4,20},{20... | collective-permute-start | bytes 7962632 | tf_op jit(solution)/shard_map/ppermute | solution.py:805
  200.4 14.2 %collective-permute-start.28 = (bf16[192,256]{1,0:T(8,128)(2,1)S(1)}, bf16[192,256]{1,0:T(8,128)(2,1)S(1)}, u32[]{:S(2)}, u32[]{:S(2)}) collective-permute-start(bf16[192,256]{1,0:T(8,128)(2,1)S(1)} %copy-done.54), channel_id=1, source_target_pairs={{0,1},{1,0},{2,3},{3,2},{4,5},{5,4},{6,7},{7,6},{8,9},{9,8},{10,11... | collective-permute-start | bytes 294920 | tf_op jit(solution)/shard_map/ppermute | solution.py:801
  201.2 15.1 %collective-permute-start.29 = (bf16[192,256]{1,0:T(8,128)(2,1)S(1)}, bf16[192,256]{1,0:T(8,128)(2,1)S(1)}, u32[]{:S(2)}, u32[]{:S(2)}) collective-permute-start(bf16[192,256]{1,0:T(8,128)(2,1)S(1)} %copy-done.52), channel_id=1, source_target_pairs={{0,2},{1,3},{2,0},{3,1},{4,6},{5,7},{6,4},{7,5},{8,10},{9,11},{10,... | collective-permute-start | bytes 294920 | tf_op jit(solution)/shard_map/ppermute | solution.py:801
  212.0 23.6 %collective-permute-start.34 = (bf16[2,192,3456]{2,1,0:T(8,128)(2,1)S(1)}, bf16[2,192,3456]{2,1,0:T(8,128)(2,1)S(1)}, u32[]{:S(2)}, u32[]{:S(2)}) collective-permute-start(bf16[2,192,3456]{2,1,0:T(8,128)(2,1)S(1)} %shard_map.243), channel_id=1, source_target_pairs={{0,16},{16,0},{1,17},{17,1},{2,18},{18,2},{3,19},{19,3},{4,20},{20... | collective-permute-start | bytes 7962632 | tf_op jit(solution)/shard_map/ppermute | solution.py:805
  214.5 23.5 %collective-permute-start.35 = (bf16[2,48,3456]{2,1,0:T(8,128)(2,1)S(1)}, bf16[2,48,3456]{2,1,0:T(8,128)(2,1)S(1)}, u32[]{:S(2)}, u32[]{:S(2)}) collective-permute-start(bf16[2,48,3456]{2,1,0:T(8,128)(2,1)S(1)} %get-tuple-element.735), channel_id=1, source_target_pairs={{0,4},{4,0},{8,12},{12,8},{1,5},{5,1},{9,13},{13,9},{2,6},{6,2},{1... | collective-permute-start | bytes 1990664 | tf_op jit(solution)/shard_map/ppermute | solution.py:810
  220.3 17.8 %collective-permute-start.33 = (bf16[192,3456]{1,0:T(8,128)(2,1)S(1)}, bf16[192,3456]{1,0:T(8,128)(2,1)S(1)}, u32[]{:S(2)}, u32[]{:S(2)}) collective-permute-start(bf16[192,3456]{1,0:T(8,128)(2,1)S(1)} %get-tuple-element.709), channel_id=1, source_target_pairs={{0,1},{1,0},{2,3},{3,2},{16,18},{17,19},{18,16},{19,17},{4,5},{5,4... | collective-permute-start | bytes 3981320 | tf_op jit(solution)/shard_map/ppermute | solution.py:792
  234.4 12.4 %collective-permute-start.37 = (bf16[512,767]{1,0:T(8,128)(2,1)}, bf16[512,767]{1,0:T(8,128)(2,1)}, u32[]{:S(2)}, u32[]{:S(2)}) collective-permute-start(bf16[512,767]{1,0:T(8,128)(2,1)} %get-tuple-element.764), channel_id=1, source_target_pairs={{0,1},{1,0},{2,3},{3,2},{16,18},{17,19},{18,16},{19,17},{4,5},{5,4... | collective-permute-start | bytes 2356232 | tf_op jit(solution)/shard_map/ppermute | solution.py:792
  235.7 9.0 %collective-permute-start.38 = (bf16[384,576]{1,0:T(8,128)(2,1)}, bf16[384,576]{1,0:T(8,128)(2,1)}, u32[]{:S(2)}, u32[]{:S(2)}) collective-permute-start(bf16[384,576]{1,0:T(8,128)(2,1)} %get-tuple-element.765), channel_id=1, source_target_pairs={{0,16},{16,0},{1,17},{17,1},{2,18},{18,2},{3,19},{19,3},{4,20},{20... | collective-permute-start | bytes 1327112 | tf_op jit(solution)/shard_map/ppermute | solution.py:805
  247.8 7.8 %collective-permute-start.39 = (bf16[256,767]{1,0:T(8,128)(2,1)S(1)}, bf16[256,767]{1,0:T(8,128)(2,1)S(1)}, u32[]{:S(2)}, u32[]{:S(2)}) collective-permute-start(bf16[256,767]{1,0:T(8,128)(2,1)S(1)} %add_convert_fusion.10), channel_id=1, source_target_pairs={{0,2},{1,3},{2,0},{3,1},{16,17},{17,16},{18,19},{19,18},{4,6},{5,7... | collective-permute-start | bytes 1178120 | tf_op jit(solution)/shard_map/ppermute | solution.py:797
  248.9 13.0 %collective-permute-start.36 = (bf16[2,104,576]{2,1,0:T(8,128)(2,1)S(1)}, bf16[2,104,576]{2,1,0:T(8,128)(2,1)S(1)}, u32[]{:S(2)}, u32[]{:S(2)}) collective-permute-start(bf16[2,104,576]{2,1,0:T(8,128)(2,1)S(1)} %get-tuple-element.762), channel_id=1, source_target_pairs={{0,4},{4,0},{8,12},{12,8},{1,5},{5,1},{9,13},{13,9},{2,6},{6,2},{1... | collective-permute-start | bytes 718856 | tf_op jit(solution)/shard_map/ppermute | solution.py:810
  250.6 23.0 %collective-permute-start.42 = (bf16[1,48,3456]{2,1,0:T(8,128)(2,1)S(1)}, bf16[1,48,3456]{2,1,0:T(8,128)(2,1)S(1)}, u32[]{:S(2)}, u32[]{:S(2)}) collective-permute-start(bf16[1,48,3456]{2,1,0:T(8,128)(2,1)S(1)} %copy-done.87), channel_id=1, source_target_pairs={{0,8},{4,12},{8,0},{12,4},{1,9},{5,13},{9,1},{13,5},{2,10},{6,14},... | collective-permute-start | bytes 995336 | tf_op jit(solution)/shard_map/ppermute | solution.py:810
  261.8 17.8 %collective-permute-start.41 = (bf16[192,3456]{1,0:T(8,128)(2,1)S(1)}, bf16[192,3456]{1,0:T(8,128)(2,1)S(1)}, u32[]{:S(2)}, u32[]{:S(2)}) collective-permute-start(bf16[192,3456]{1,0:T(8,128)(2,1)S(1)} %copy-done.48), channel_id=1, source_target_pairs={{0,1},{1,0},{2,3},{3,2},{16,18},{17,19},{18,16},{19,17},{4,5},{5,4... | collective-permute-start | bytes 3981320 | tf_op jit(solution)/shard_map/ppermute | solution.py:792
  273.7 12.0 %collective-permute-start.43 = (bf16[1,48,3456]{2,1,0:T(8,128)(2,1)S(1)}, bf16[1,48,3456]{2,1,0:T(8,128)(2,1)S(1)}, u32[]{:S(2)}, u32[]{:S(2)}) collective-permute-start(bf16[1,48,3456]{2,1,0:T(8,128)(2,1)S(1)} %add_convert_fusion.13), channel_id=1, source_target_pairs={{0,8},{4,12},{8,0},{12,4},{1,9},{5,13},{9,1},{13,5},{2,10},{6,14},... | collective-permute-start | bytes 995336 | tf_op jit(solution)/shard_map/ppermute | solution.py:810
  274.3 17.1 %collective-permute-start.40 = (bf16[1,104,576]{2,1,0:T(8,128)(2,1)}, bf16[1,104,576]{2,1,0:T(8,128)(2,1)}, u32[]{:S(2)}, u32[]{:S(2)}) collective-permute-start(bf16[1,104,576]{2,1,0:T(8,128)(2,1)} %get-tuple-element.792), channel_id=1, source_target_pairs={{0,8},{4,12},{8,0},{12,4},{1,9},{5,13},{9,1},{13,5},{2,10},{6,14},... | collective-permute-start | bytes 359432 | tf_op jit(solution)/shard_map/ppermute | solution.py:810
  287.4 18.2 %collective-permute-start.45 = (bf16[192,3456]{1,0:T(8,128)(2,1)}, bf16[192,3456]{1,0:T(8,128)(2,1)}, u32[]{:S(2)}, u32[]{:S(2)}) collective-permute-start(bf16[192,3456]{1,0:T(8,128)(2,1)} %add_convert_fusion.2), channel_id=1, source_target_pairs={{0,2},{1,3},{2,0},{3,1},{16,17},{17,16},{18,19},{19,18},{4,6},{5,7... | collective-permute-start | bytes 3981320 | tf_op jit(solution)/shard_map/ppermute | solution.py:797
  288.5 19.1 %collective-permute-start.46 = (bf16[2,48,3456]{2,1,0:T(8,128)(2,1)S(1)}, bf16[2,48,3456]{2,1,0:T(8,128)(2,1)S(1)}, u32[]{:S(2)}, u32[]{:S(2)}) collective-permute-start(bf16[2,48,3456]{2,1,0:T(8,128)(2,1)S(1)} %maximum_select_fusion.2), channel_id=1, source_target_pairs={{0,4},{4,0},{8,12},{12,8},{1,5},{5,1},{9,13},{13,9},{2,6},{6,2},{1... | collective-permute-start | bytes 1990664 | tf_op jit(solution)/shard_map/ppermute | solution.py:810
  293.1 18.7 %collective-permute-start.44 = (bf16[1,104,576]{2,1,0:T(8,128)(2,1)S(1)}, bf16[1,104,576]{2,1,0:T(8,128)(2,1)S(1)}, u32[]{:S(2)}, u32[]{:S(2)}) collective-permute-start(bf16[1,104,576]{2,1,0:T(8,128)(2,1)S(1)} %add_convert_fusion.17), channel_id=1, source_target_pairs={{0,8},{4,12},{8,0},{12,4},{1,9},{5,13},{9,1},{13,5},{2,10},{6,14},... | collective-permute-start | bytes 359432 | tf_op jit(solution)/shard_map/ppermute | solution.py:810
  296.0 17.3 %collective-permute-start.51 = (bf16[2,104,576]{2,1,0:T(8,128)(2,1)S(1)}, bf16[2,104,576]{2,1,0:T(8,128)(2,1)S(1)}, u32[]{:S(2)}, u32[]{:S(2)}) collective-permute-start(bf16[2,104,576]{2,1,0:T(8,128)(2,1)S(1)} %fusion.11), channel_id=1, source_target_pairs={{0,4},{4,0},{8,12},{12,8},{1,5},{5,1},{9,13},{13,9},{2,6},{6,2},{1... | collective-permute-start | bytes 718856 | tf_op jit(solution)/shard_map/ppermute | solution.py:810
  310.9 17.5 %collective-permute-start.50 = (bf16[2,48,3456]{2,1,0:T(8,128)(2,1)S(1)}, bf16[2,48,3456]{2,1,0:T(8,128)(2,1)S(1)}, u32[]{:S(2)}, u32[]{:S(2)}) collective-permute-start(bf16[2,48,3456]{2,1,0:T(8,128)(2,1)S(1)} %fusion.5), channel_id=1, source_target_pairs={{0,4},{4,0},{8,12},{12,8},{1,5},{5,1},{9,13},{13,9},{2,6},{6,2},{1... | collective-permute-start | bytes 1990664 | tf_op jit(solution)/shard_map/ppermute | solution.py:810
  311.0 29.4 %collective-permute-start.48 = (bf16[192,3456]{1,0:T(8,128)(2,1)S(1)}, bf16[192,3456]{1,0:T(8,128)(2,1)S(1)}, u32[]{:S(2)}, u32[]{:S(2)}) collective-permute-start(bf16[192,3456]{1,0:T(8,128)(2,1)S(1)} %bitcast.147), channel_id=1, source_target_pairs={{0,2},{1,3},{2,0},{3,1},{16,17},{17,16},{18,19},{19,18},{4,6},{5,7... | collective-permute-start | bytes 3981320 | tf_op jit(solution)/shard_map/ppermute | solution.py:797
  311.1 32.1 %collective-permute-start.49 = (bf16[192,3456]{1,0:T(8,128)(2,1)S(1)}, bf16[192,3456]{1,0:T(8,128)(2,1)S(1)}, u32[]{:S(2)}, u32[]{:S(2)}) collective-permute-start(bf16[192,3456]{1,0:T(8,128)(2,1)S(1)} %bitcast.148), channel_id=1, source_target_pairs={{0,1},{1,0},{2,3},{3,2},{16,18},{17,19},{18,16},{19,17},{4,5},{5,4... | collective-permute-start | bytes 3981320 | tf_op jit(solution)/shard_map/ppermute | solution.py:792
  311.8 48.2 %collective-permute-start.57 = (bf16[192,3456]{1,0:T(8,128)(2,1)S(1)}, bf16[192,3456]{1,0:T(8,128)(2,1)S(1)}, u32[]{:S(2)}, u32[]{:S(2)}) collective-permute-start(bf16[192,3456]{1,0:T(8,128)(2,1)S(1)} %bitcast.149), channel_id=1, source_target_pairs={{0,16},{1,17},{2,18},{3,19},{4,20},{5,21},{6,22},{7,23},{8,24},{9,... | collective-permute-start | bytes 3981320 | tf_op jit(solution)/shard_map/ppermute | solution.py:814
  313.4 31.1 %collective-permute-start.47 = (bf16[2,104,576]{2,1,0:T(8,128)(2,1)S(1)}, bf16[2,104,576]{2,1,0:T(8,128)(2,1)S(1)}, u32[]{:S(2)}, u32[]{:S(2)}) collective-permute-start(bf16[2,104,576]{2,1,0:T(8,128)(2,1)S(1)} %maximum_select_fusion.6), channel_id=1, source_target_pairs={{0,4},{4,0},{8,12},{12,8},{1,5},{5,1},{9,13},{13,9},{2,6},{6,2},{1... | collective-permute-start | bytes 718856 | tf_op jit(solution)/shard_map/ppermute | solution.py:810
  328.4 17.7 %collective-permute-start.54 = (bf16[1,104,576]{2,1,0:T(8,128)(2,1)S(1)}, bf16[1,104,576]{2,1,0:T(8,128)(2,1)S(1)}, u32[]{:S(2)}, u32[]{:S(2)}) collective-permute-start(bf16[1,104,576]{2,1,0:T(8,128)(2,1)S(1)} %get-tuple-element.870), channel_id=1, source_target_pairs={{0,8},{4,12},{8,0},{12,4},{1,9},{5,13},{9,1},{13,5},{2,10},{6,14},... | collective-permute-start | bytes 359432 | tf_op jit(solution)/shard_map/ppermute | solution.py:810
  340.4 18.6 %collective-permute-start.58 = (bf16[1,48,3456]{2,1,0:T(8,128)(2,1)S(1)}, bf16[1,48,3456]{2,1,0:T(8,128)(2,1)S(1)}, u32[]{:S(2)}, u32[]{:S(2)}) collective-permute-start(bf16[1,48,3456]{2,1,0:T(8,128)(2,1)S(1)} %get-tuple-element.877), channel_id=1, source_target_pairs={{0,8},{4,12},{8,0},{12,4},{1,9},{5,13},{9,1},{13,5},{2,10},{6,14},... | collective-permute-start | bytes 995336 | tf_op jit(solution)/shard_map/ppermute | solution.py:810
  343.2 19.8 %collective-permute-start.56 = (bf16[192,3456]{1,0:T(8,128)(2,1)S(1)}, bf16[192,3456]{1,0:T(8,128)(2,1)S(1)}, u32[]{:S(2)}, u32[]{:S(2)}) collective-permute-start(bf16[192,3456]{1,0:T(8,128)(2,1)S(1)} %collective-permute-done.48.refs_3_), channel_id=1, source_target_pairs={{0,1},{1,0},{2,3},{3,2},{16,18},{17,19},{18,16},{19,17},{4,5},{5,4... | collective-permute-start | bytes 3981320 | tf_op jit(solution)/shard_map/ppermute | solution.py:792
  344.6 29.4 %collective-permute-start.53 = (bf16[192,3456]{1,0:T(8,128)(2,1)S(1)}, bf16[192,3456]{1,0:T(8,128)(2,1)S(1)}, u32[]{:S(2)}, u32[]{:S(2)}) collective-permute-start(bf16[192,3456]{1,0:T(8,128)(2,1)S(1)} %collective-permute-done.48.refs_3_), channel_id=1, source_target_pairs={{0,16},{1,17},{2,18},{3,19},{4,20},{5,21},{6,22},{7,23},{8,24},{9,... | collective-permute-start | bytes 3981320 | tf_op jit(solution)/shard_map/ppermute | solution.py:814
  359.0 7.1 %collective-permute-start.55 = (bf16[1,104,576]{2,1,0:T(8,128)(2,1)S(1)}, bf16[1,104,576]{2,1,0:T(8,128)(2,1)S(1)}, u32[]{:S(2)}, u32[]{:S(2)}) collective-permute-start(bf16[1,104,576]{2,1,0:T(8,128)(2,1)S(1)} %add_convert_fusion.16), channel_id=1, source_target_pairs={{0,8},{4,12},{8,0},{12,4},{1,9},{5,13},{9,1},{13,5},{2,10},{6,14},... | collective-permute-start | bytes 359432 | tf_op jit(solution)/shard_map/ppermute | solution.py:810
  359.0 14.9 %collective-permute-start.52 = (bf16[416,576]{1,0:T(8,128)(2,1)S(1)}, bf16[416,576]{1,0:T(8,128)(2,1)S(1)}, u32[]{:S(2)}, u32[]{:S(2)}) collective-permute-start(bf16[416,576]{1,0:T(8,128)(2,1)S(1)} %bitcast.176), channel_id=1, source_target_pairs={{0,2},{1,3},{2,0},{3,1},{16,17},{17,16},{18,19},{19,18},{4,6},{5,7... | collective-permute-start | bytes 1437704 | tf_op jit(solution)/shard_map/ppermute | solution.py:797
  360.0 14.2 %collective-permute-start.62 = (bf16[1,48,3456]{2,1,0:T(8,128)(2,1)S(1)}, bf16[1,48,3456]{2,1,0:T(8,128)(2,1)S(1)}, u32[]{:S(2)}, u32[]{:S(2)}) collective-permute-start(bf16[1,48,3456]{2,1,0:T(8,128)(2,1)S(1)} %add_convert_fusion.12), channel_id=1, source_target_pairs={{0,8},{4,12},{8,0},{12,4},{1,9},{5,13},{9,1},{13,5},{2,10},{6,14},... | collective-permute-start | bytes 995336 | tf_op jit(solution)/shard_map/ppermute | solution.py:810
  363.0 20.2 %collective-permute-start.60 = (bf16[192,3456]{1,0:T(8,128)(2,1)S(1)}, bf16[192,3456]{1,0:T(8,128)(2,1)S(1)}, u32[]{:S(2)}, u32[]{:S(2)}) collective-permute-start(bf16[192,3456]{1,0:T(8,128)(2,1)S(1)} %collective-permute-done.49.refs_3_), channel_id=1, source_target_pairs={{0,16},{1,17},{2,18},{3,19},{4,20},{5,21},{6,22},{7,23},{8,24},{9,... | collective-permute-start | bytes 3981320 | tf_op jit(solution)/shard_map/ppermute | solution.py:814
  374.1 7.4 %collective-permute-start.61 = (bf16[2,104,576]{2,1,0:T(8,128)(2,1)S(1)}, bf16[2,104,576]{2,1,0:T(8,128)(2,1)S(1)}, u32[]{:S(2)}, u32[]{:S(2)}) collective-permute-start(bf16[2,104,576]{2,1,0:T(8,128)(2,1)S(1)} %maximum_select_fusion.7), channel_id=1, source_target_pairs={{0,4},{4,0},{8,12},{12,8},{1,5},{5,1},{9,13},{13,9},{2,6},{6,2},{1... | collective-permute-start | bytes 718856 | tf_op jit(solution)/shard_map/ppermute | solution.py:810
  377.1 15.0 %collective-permute-start.59 = (bf16[2,416,576]{2,1,0:T(8,128)(2,1)S(1)}, bf16[2,416,576]{2,1,0:T(8,128)(2,1)S(1)}, u32[]{:S(2)}, u32[]{:S(2)}) collective-permute-start(bf16[2,416,576]{2,1,0:T(8,128)(2,1)S(1)} %pad_maximum_fusion.2), channel_id=1, source_target_pairs={{0,1},{1,0},{2,3},{3,2},{16,18},{17,19},{18,16},{19,17},{4,5},{5,4... | collective-permute-start | bytes 2875400 | tf_op jit(solution)/shard_map/ppermute | solution.py:792
  377.8 14.3 %collective-permute-start.65 = (bf16[2,48,3456]{2,1,0:T(8,128)(2,1)S(1)}, bf16[2,48,3456]{2,1,0:T(8,128)(2,1)S(1)}, u32[]{:S(2)}, u32[]{:S(2)}) collective-permute-start(bf16[2,48,3456]{2,1,0:T(8,128)(2,1)S(1)} %maximum_select_fusion.3), channel_id=1, source_target_pairs={{0,4},{4,0},{8,12},{12,8},{1,5},{5,1},{9,13},{13,9},{2,6},{6,2},{1... | collective-permute-start | bytes 1990664 | tf_op jit(solution)/shard_map/ppermute | solution.py:810
  381.7 9.3 %collective-permute-start.63 = (bf16[416,576]{1,0:T(8,128)(2,1)S(1)}, bf16[416,576]{1,0:T(8,128)(2,1)S(1)}, u32[]{:S(2)}, u32[]{:S(2)}) collective-permute-start(bf16[416,576]{1,0:T(8,128)(2,1)S(1)} %bitcast.178), channel_id=1, source_target_pairs={{0,2},{1,3},{2,0},{3,1},{16,17},{17,16},{18,19},{19,18},{4,6},{5,7... | collective-permute-start | bytes 1437704 | tf_op jit(solution)/shard_map/ppermute | solution.py:797
  381.8 14.5 %collective-permute-start.64 = (bf16[192,3456]{1,0:T(8,128)(2,1)S(1)}, bf16[192,3456]{1,0:T(8,128)(2,1)S(1)}, u32[]{:S(2)}, u32[]{:S(2)}) collective-permute-start(bf16[192,3456]{1,0:T(8,128)(2,1)S(1)} %collective-permute-done.56.refs_3_), channel_id=1, source_target_pairs={{0,16},{1,17},{2,18},{3,19},{4,20},{5,21},{6,22},{7,23},{8,24},{9,... | collective-permute-start | bytes 3981320 | tf_op jit(solution)/shard_map/ppermute | solution.py:814
  392.4 8.4 %collective-permute-start.66 = (bf16[192,3456]{1,0:T(8,128)(2,1)S(1)}, bf16[192,3456]{1,0:T(8,128)(2,1)S(1)}, u32[]{:S(2)}, u32[]{:S(2)}) collective-permute-start(bf16[192,3456]{1,0:T(8,128)(2,1)S(1)} %bitcast.151), channel_id=1, source_target_pairs={{16,0},{17,1},{18,2},{19,3},{20,4},{21,5},{22,6},{23,7},{24,8},{25... | collective-permute-start | bytes 3981320 | tf_op jit(solution)/shard_map/ppermute | solution.py:814
  393.9 43.6 %collective-permute-start.68 = (bf16[192,3456]{1,0:T(8,128)(2,1)S(1)}, bf16[192,3456]{1,0:T(8,128)(2,1)S(1)}, u32[]{:S(2)}, u32[]{:S(2)}) collective-permute-start(bf16[192,3456]{1,0:T(8,128)(2,1)S(1)} %bitcast.152), channel_id=1, source_target_pairs={{0,2},{1,3},{2,0},{3,1},{16,17},{17,16},{18,19},{19,18},{4,6},{5,7... | collective-permute-start | bytes 3981320 | tf_op jit(solution)/shard_map/ppermute | solution.py:797
  394.0 43.5 %collective-permute-start.69 = (bf16[192,3456]{1,0:T(8,128)(2,1)S(1)}, bf16[192,3456]{1,0:T(8,128)(2,1)S(1)}, u32[]{:S(2)}, u32[]{:S(2)}) collective-permute-start(bf16[192,3456]{1,0:T(8,128)(2,1)S(1)} %bitcast.153), channel_id=1, source_target_pairs={{0,1},{1,0},{2,3},{3,2},{16,18},{17,19},{18,16},{19,17},{4,5},{5,4... | collective-permute-start | bytes 3981320 | tf_op jit(solution)/shard_map/ppermute | solution.py:792
  395.0 42.4 %collective-permute-start.70 = (bf16[2,416,576]{2,1,0:T(8,128)(2,1)S(1)}, bf16[2,416,576]{2,1,0:T(8,128)(2,1)S(1)}, u32[]{:S(2)}, u32[]{:S(2)}) collective-permute-start(bf16[2,416,576]{2,1,0:T(8,128)(2,1)S(1)} %pad_maximum_fusion.3), channel_id=1, source_target_pairs={{0,1},{1,0},{2,3},{3,2},{16,18},{17,19},{18,16},{19,17},{4,5},{5,4... | collective-permute-start | bytes 2875400 | tf_op jit(solution)/shard_map/ppermute | solution.py:792
  437.7 6.6 %collective-permute-start.73 = (bf16[192,3456]{1,0:T(8,128)(2,1)S(1)}, bf16[192,3456]{1,0:T(8,128)(2,1)S(1)}, u32[]{:S(2)}, u32[]{:S(2)}) collective-permute-start(bf16[192,3456]{1,0:T(8,128)(2,1)S(1)} %collective-permute-done.68.refs_0_), channel_id=1, source_target_pairs={{16,0},{17,1},{18,2},{19,3},{20,4},{21,5},{22,6},{23,7},{24,8},{25... | collective-permute-start | bytes 3981320 | tf_op jit(solution)/shard_map/ppermute | solution.py:814
  439.0 10.3 %collective-permute-start.72 = (bf16[4,416,576]{2,1,0:T(8,128)(2,1)S(1)}, bf16[4,416,576]{2,1,0:T(8,128)(2,1)S(1)}, u32[]{:S(2)}, u32[]{:S(2)}) collective-permute-start(bf16[4,416,576]{2,1,0:T(8,128)(2,1)S(1)} %pad_maximum_fusion.refs_3_), channel_id=1, source_target_pairs={{0,16},{1,17},{2,18},{3,19},{4,20},{5,21},{6,22},{7,23},{8,24},{9,... | collective-permute-start | bytes 5750792 | tf_op jit(solution)/shard_map/ppermute | solution.py:814
  442.3 7.0 %collective-permute-start.71 = (bf16[4,416,576]{2,1,0:T(8,128)(2,1)S(1)}, bf16[4,416,576]{2,1,0:T(8,128)(2,1)S(1)}, u32[]{:S(2)}, u32[]{:S(2)}) collective-permute-start(bf16[4,416,576]{2,1,0:T(8,128)(2,1)S(1)} %pad_maximum_fusion.1.refs_0_), channel_id=1, source_target_pairs={{16,0},{17,1},{18,2},{19,3},{20,4},{21,5},{22,6},{23,7},{24,8},{25... | collective-permute-start | bytes 5750792 | tf_op jit(solution)/shard_map/ppermute | solution.py:814
  443.6 17.8 %collective-permute-start.74 = (bf16[192,3456]{1,0:T(8,128)(2,1)S(1)}, bf16[192,3456]{1,0:T(8,128)(2,1)S(1)}, u32[]{:S(2)}, u32[]{:S(2)}) collective-permute-start(bf16[192,3456]{1,0:T(8,128)(2,1)S(1)} %collective-permute-done.68.refs_0_), channel_id=1, source_target_pairs={{0,1},{1,0},{2,3},{3,2},{16,18},{17,19},{18,16},{19,17},{4,5},{5,4... | collective-permute-start | bytes 3981320 | tf_op jit(solution)/shard_map/ppermute | solution.py:792
  448.0 13.4 %collective-permute-start.75 = (bf16[192,3456]{1,0:T(8,128)(2,1)S(1)}, bf16[192,3456]{1,0:T(8,128)(2,1)S(1)}, u32[]{:S(2)}, u32[]{:S(2)}) collective-permute-start(bf16[192,3456]{1,0:T(8,128)(2,1)S(1)} %collective-permute-done.69.refs_0_), channel_id=1, source_target_pairs={{16,0},{17,1},{18,2},{19,3},{20,4},{21,5},{22,6},{23,7},{24,8},{25... | collective-permute-start | bytes 3981320 | tf_op jit(solution)/shard_map/ppermute | solution.py:814
  (114 other events, 1076.0 us)

commit v8 on v7

--- a/solution.py
+++ b/solution.py
@@ -205,7 +205,7 @@
             pltpu.VMEM((full, span), F32),
             pltpu.SemaphoreType.DMA((8,)),
         ],
-        compiler_params=params(22),
+        compiler_params=params(18),
         cost_estimate=cost(
             2 * full * width * 3 * heads * hd + 3 * 4 * full * full * hd * heads,
             4 * full * width,
@@ -302,7 +302,7 @@
             jax.ShapeDtypeStruct((8, 128), F32),
             jax.ShapeDtypeStruct((QUAD, span, rows), BF16),
         ],
-        compiler_params=params(32, dimension_semantics=("arbitrary",)),
+        compiler_params=params(26, dimension_semantics=("arbitrary",)),
         cost_estimate=cost(6 * span * cc * ff, 4 * cc * ff + 4 * span * ff, span * ff),
     )(ids, x, *att, wo, pv, pvn, pv, up[0], up[1], dn[0], dn[1])
 
@@ -404,7 +404,7 @@
             jax.ShapeDtypeStruct((8, ff), F32),
             dd, dd, dd, dd,
         ],
-        compiler_params=params(32, dimension_semantics=("arbitrary",)),
+        compiler_params=params(26, dimension_semantics=("arbitrary",)),
         cost_estimate=cost(6 * span * cc * ff, 4 * cc * ff + 8 * span * ff, span * ff),
     )(ids, df, u, mid, wo, pv, up[0], up[1], dn[0], dn[1])
 
@@ -439,7 +439,7 @@
         out_shape=jax.ShapeDtypeStruct((len(places), quarter, cols), BF16)
         if send
         else [jax.ShapeDtypeStruct((quarter, cols), BF16)] * len(places),
-        compiler_params=params(22),
+        compiler_params=params(18),
         cost_estimate=cost(2 * span * quarter * cols * len(places), 2 * 4 * quarter * cols * len(places)),
     )(ids, lr, rr, att, *got)
 
@@ -536,7 +536,7 @@
             pltpu.VMEM((heads, QUAD, span), F32),
             pltpu.SemaphoreType.DMA((6,)),
         ],
-        compiler_params=params(30),
+        compiler_params=params(26),
         cost_estimate=cost(
             4 * full * cc * 3 * width + 3 * 10 * full * full * hd * heads,
             8 * full * cc,

time: 476 us -> 465 us (0.977)
  starting transfers between devices: 82.9 us -> 104 us
  waiting for transfers between devices: 188 us -> 169 us
  Pallas kernels: 146 us -> 136 us
    ppermute x16, waiting for transfers between devices: 54.2 us -> 38.8 us  [dp_partner(): return lax.ppermute(v, 'dp', [(i, i ^ step) for i in range(n)])]
    ppermute x16, starting transfers between devices: 25 us -> 36.8 us  [dp_partner(): return lax.ppermute(v, 'dp', [(i, i ^ step) for i in range(n)])]
    ppermute x10, waiting for transfers between devices: 55.1 us -> 44.8 us  [to_second(): return lax.ppermute(v, ('section', 'seq'), pairs)]
    pallas_call x2, Pallas kernels: 34 us -> 25.4 us  [attn_bwd(): pl.pallas_call(attn_bwd_kernel, in_specs=[SMEM] + [HBM] * 6 + [VMEM] * 4,...]
    ppermute x10, starting transfers between devices: 8.07 us -> 15.9 us  [to_second(): return lax.ppermute(v, ('section', 'seq'), pairs)]
    ppermute x16, waiting for transfers between devices: 65.6 us -> 73.1 us  [to_first(): return lax.ppermute(v, ('section', 'seq'), pairs)]
    unnamed x202 -> x194, local copies, waits for them, and re-layouts: 15.6 us -> 11.9 us
  transfers between devices with their start and end apart: 77 -> 77, of which waited for: 35 -> 34; matrix products, arithmetic and copies ran while one was open for 7% -> 7% of each run, Pallas kernels for 21% -> 20%
where the time goes in v8:
time: 465 us; the launch traced here: 460 us
  waiting for transfers between devices  169 us (36%)
  Pallas kernels  136 us (29%)
  starting transfers between devices  104 us (22%)
  local copies, waits for them, and re-layouts  23.9 us (5%)
  other arithmetic  22.4 us (5%)
  between operations  5.38 us (1%)
    ppermute x16, waiting for transfers between devices, to_first(): return lax.ppermute(v, ('section', 'seq'), pairs)  73.1 us
    ppermute x10, waiting for transfers between devices, to_second(): return lax.ppermute(v, ('section', 'seq'), pairs)  44.8 us
    ppermute x16, waiting for transfers between devices, dp_partner(): return lax.ppermute(v, 'dp', [(i, i ^ step) for i in range(n)])  38.8 us
    ppermute x16, starting transfers between devices, dp_partner(): return lax.ppermute(v, 'dp', [(i, i ^ step) for i in range(n)])  36.8 us
    pallas_call x2, Pallas kernels, attn_bwd(): pl.pallas_call(attn_bwd_kernel, in_specs=[SMEM] + [HBM] * 6 + [VMEM] * 4,...  25.4 us
    pallas_call x2, Pallas kernels, attn_fwd(): pl.pallas_call(functools.partial(attn_fwd_kernel, raw), in_specs=[SMEM] +...  22.7 us
    ppermute x16, starting transfers between devices, to_first(): return lax.ppermute(v, ('section', 'seq'), pairs)  19.4 us
    pallas_call x2, Pallas kernels, mlp_bwd(): pl.pallas_call(functools.partial(mlp_bwd_kernel, layer), grid_spec=grid,...  19.4 us
  transfers between devices with their start and end apart: 77, of which 34 were waited for; matrix products, arithmetic and copies ran while one was open for 7% of the time, Pallas kernels for 20%

profile of v8, /device:TPU:0, one launch (start us, length us, event | category | flops | bytes accessed | tf_op | source)
XLA Modules:
  0.0 460.4 jit_solution(570803582989441127)
XLA Ops:
  1.3 2.8 dynamic-slice_bitcast_fusion.2
  9.2 2.7 collective-permute-start
  17.2 2.6 collective-permute-start.1
  22.5 2.1 broadcast_select_fusion.2
  25.5 4.2 collective-permute-done.2.n3
  29.7 11.5 %shard_map.229 = (bf16[3,1024,64]{2,1,0:T(8,128)(2,1)S(1)}, bf16[3,1024,64]{2,1,0:T(8,128)(2,1)S(1)}, bf16[3,1024,64]{2,1,0:T(8,128)(2,1)S(1)}, f32[3,4,256]{2,1...) custom-call(s32[8]{0:T(128)S(1)} %stack.144.ids, ...), custom_call_target="tpu_custom_call" | custom-call | flops 6641418240 | bytes 6283264 | tf_op jit(solution)/shard_map/pallas_call | solution.py:196
  41.3 2.1 collective-permute-start.5
  46.8 2.3 collective-permute-done.6.a2
  50.5 8.3 %shard_map.230 = (f32[256,767]{1,0:T(8,128)S(1)}, f32[256,3072]{1,0:T(8,128)S(1)}, bf16[256,767]{1,0:T(8,128)(2,1)S(1)}, bf16[256,767]{1,0:T(8,128)(2,1)S(1)}, f...) custom-call(s32[8]{0:T(128)S(1)} %stack.144.ids, bf16[256,767]{1,0:T(8,128)(2,1)S(1)} %shard_map.228.n0.x, ...), custom_call_target="tpu_custom_call" | custom-call | flops 7238320128 | bytes 25141248 | tf_op jit(solution)/shard_map/pallas_call | solution.py:294
  61.6 10.0 %collective-permute-done.11.n1 = bf16[256,767]{1,0:T(8,128)(2,1)S(1)} collective-permute-done((bf16[256,767]{1,0:T(8,128)(2,1)S(1)}, bf16[256,767]{1,0:T(8,128)(2,1)S(1)}, u32[]{:S(2)}, u32[]{:S(2)}) %collective-permute-start.11) | collective-permute-done | bytes 392736 | tf_op jit(solution)/shard_map/ppermute | solution.py:797
  72.5 1.9 shard_map.231.df
  74.4 5.0 %collective-permute-done.13.n3 = bf16[256,767]{1,0:T(8,128)(2,1)S(1)} collective-permute-done((bf16[256,767]{1,0:T(8,128)(2,1)S(1)}, bf16[256,767]{1,0:T(8,128)(2,1)S(1)}, u32[]{:S(2)}, u32[]{:S(2)}) %collective-permute-start.13) | collective-permute-done | bytes 392736 | tf_op jit(solution)/shard_map/ppermute | solution.py:792
  79.4 11.2 %shard_map.232 = (bf16[3,1024,64]{2,1,0:T(8,128)(2,1)S(1)}, bf16[3,1024,64]{2,1,0:T(8,128)(2,1)S(1)}, bf16[3,1024,64]{2,1,0:T(8,128)(2,1)S(1)}, f32[3,4,256]{2,1...) custom-call(s32[8]{0:T(128)S(1)} %stack.144.ids, ...), custom_call_target="tpu_custom_call" | custom-call | flops 6641418240 | bytes 6283264 | tf_op jit(solution)/shard_map/pallas_call | solution.py:196
  94.7 2.3 collective-permute-start.16
  100.3 9.3 %shard_map.233 = (f32[256,767]{1,0:T(8,128)S(1)}, f32[256,3072]{1,0:T(8,128)S(1)}, bf16[256,767]{1,0:T(8,128)(2,1)S(1)}, bf16[256,767]{1,0:T(8,128)(2,1)}, f32[8...) custom-call(s32[8]{0:T(128)S(1)} %stack.144.ids, bf16[256,767]{1,0:T(8,128)(2,1)S(1)} %get-tuple-element.930.x, ...), custom_call_target="tpu_custom_call" | custom-call | flops 7238320128 | bytes 25141248 | tf_op jit(solution)/shard_map/pallas_call | solution.py:294
  109.5 9.7 %shard_map.234 = (bf16[2,256,3072]{2,1,0:T(8,128)(2,1)S(1)}, bf16[3,4,256,192]{3,2,1,0:T(8,128)(2,1)S(1)}, f32[256,767]{1,0:T(8,128)S(1)}, f32[8,3072]{1,0:T(8,1...) custom-call(s32[8]{0:T(128)S(1)} %stack.144.ids, ...), custom_call_target="tpu_custom_call" | custom-call | flops 7238320128 | bytes 31432704 | tf_op jit(solution)/shard_map/pallas_call | solution.py:397
  126.1 2.2 collective-permute-done.18.d2
  131.0 2.6 shard_map.237
  134.8 12.2 %shard_map.238 = (bf16[256,767]{1,0:T(8,128)(2,1)S(1)}, bf16[256,767]{1,0:T(8,128)(2,1)S(1)}, bf16[512,767]{1,0:T(8,128)(2,1)S(1)}, bf16[384,576]{1,0:T(8,128)(2...) custom-call(s32[8]{0:T(128)S(1)} %stack.144.ids, bf16[4,256,767]{2,1,0:T(8,128)(2,1)S(1)} %copy-done.61, ...), custom_call_target="tpu_custom_call" | custom-call | flops 15698755584 | bytes 12566528 | tf_op jit(solution)/shard_map/pallas_call | solution.py:519
  148.0 3.4 collective-permute-done.23
  154.6 5.2 %collective-permute-done.21.r0 = bf16[512,767]{1,0:T(8,128)(2,1)S(1)} collective-permute-done((bf16[512,767]{1,0:T(8,128)(2,1)S(1)}, bf16[512,767]{1,0:T(8,128)(2,1)S(1)}, u32[]{:S(2)}, u32[]{:S(2)}) %collective-permute-start.21) | collective-permute-done | bytes 785440 | tf_op jit(solution)/shard_map/ppermute | solution.py:792
  161.4 6.4 %collective-permute-done.26.r1 = bf16[256,767]{1,0:T(8,128)(2,1)S(1)} collective-permute-done((bf16[256,767]{1,0:T(8,128)(2,1)S(1)}, bf16[256,767]{1,0:T(8,128)(2,1)S(1)}, u32[]{:S(2)}, u32[]{:S(2)}) %collective-permute-start.26) | collective-permute-done | bytes 392736 | tf_op jit(solution)/shard_map/ppermute | solution.py:797
  171.1 9.7 %shard_map.241 = (bf16[2,256,3072]{2,1,0:T(8,128)(2,1)S(1)}, bf16[3,4,256,192]{3,2,1,0:T(8,128)(2,1)S(1)}, f32[256,767]{1,0:T(8,128)S(1)}, f32[8,3072]{1,0:T(8,1...) custom-call(s32[8]{0:T(128)S(1)} %stack.144.ids, ...), custom_call_target="tpu_custom_call" | custom-call | flops 7238320128 | bytes 31432704 | tf_op jit(solution)/shard_map/pallas_call | solution.py:397
  180.9 3.0 shard_map.242
  190.5 10.6 %collective-permute-done.31 = bf16[192,3456]{1,0:T(8,128)(2,1)} collective-permute-done((bf16[192,3456]{1,0:T(8,128)(2,1)}, bf16[192,3456]{1,0:T(8,128)(2,1)}, u32[]{:S(2)}, u32[]{:S(2)}) %collective-permute-start.31) | collective-permute-done | bytes 1327136 | tf_op jit(solution)/shard_map/ppermute | solution.py:792
  202.9 2.2 add_convert_fusion.3
  207.2 2.8 shard_map.244
  212.3 13.2 %shard_map.245 = (bf16[256,767]{1,0:T(8,128)(2,1)S(1)}, bf16[256,767]{1,0:T(8,128)(2,1)S(1)}, bf16[512,767]{1,0:T(8,128)(2,1)}, bf16[384,576]{1,0:T(8,128)(2,1)}...) custom-call(s32[8]{0:T(128)S(1)} %stack.144.ids, bf16[4,256,767]{2,1,0:T(8,128)(2,1)S(1)} %copy-done.59, ...), custom_call_target="tpu_custom_call" | custom-call | flops 15698755584 | bytes 12566528 | tf_op jit(solution)/shard_map/pallas_call | solution.py:519
  226.5 2.4 collective-permute-done.33
  235.5 2.4 collective-permute-done.37.r0
  241.6 2.6 collective-permute-start.42
  244.2 2.7 collective-permute-done.39.r1
  248.6 4.4 collective-permute-done.36
  254.7 5.0 %collective-permute-done.42 = bf16[1,48,3456]{2,1,0:T(8,128)(2,1)S(1)} collective-permute-done((bf16[1,48,3456]{2,1,0:T(8,128)(2,1)S(1)}, bf16[1,48,3456]{2,1,0:T(8,128)(2,1)S(1)}, u32[]{:S(2)}, u32[]{:S(2)}) %collective-permute-start.42) | collective-permute-done | bytes 331808 | tf_op jit(solution)/shard_map/ppermute | solution.py:810
  260.5 2.9 collective-permute-start.40
  263.4 7.5 %collective-permute-done.41 = bf16[192,3456]{1,0:T(8,128)(2,1)S(1)} collective-permute-done((bf16[192,3456]{1,0:T(8,128)(2,1)S(1)}, bf16[192,3456]{1,0:T(8,128)(2,1)S(1)}, u32[]{:S(2)}, u32[]{:S(2)}) %collective-permute-start.41) | collective-permute-done | bytes 1327136 | tf_op jit(solution)/shard_map/ppermute | solution.py:792
  275.7 5.6 %collective-permute-start.46 = (bf16[2,48,3456]{2,1,0:T(8,128)(2,1)S(1)}, bf16[2,48,3456]{2,1,0:T(8,128)(2,1)S(1)}, u32[]{:S(2)}, u32[]{:S(2)}) collective-permute-start(bf16[2,48,3456]{2,1,0:T(8,128)(2,1)S(1)} %maximum_select_fusion.2), channel_id=1, source_target_pairs={{0,4},{4,0},{8,12},{12,8},{1,5},{5,1},{9,13},{13,9},{2,6},{6,2},{1... | collective-permute-start | bytes 1990664 | tf_op jit(solution)/shard_map/ppermute | solution.py:810
  284.4 3.0 collective-permute-start.44
  287.4 4.3 collective-permute-done.45
  291.7 5.3 %collective-permute-done.46 = bf16[2,48,3456]{2,1,0:T(8,128)(2,1)S(1)} collective-permute-done((bf16[2,48,3456]{2,1,0:T(8,128)(2,1)S(1)}, bf16[2,48,3456]{2,1,0:T(8,128)(2,1)S(1)}, u32[]{:S(2)}, u32[]{:S(2)}) %collective-permute-start.46) | collective-permute-done | bytes 663584 | tf_op jit(solution)/shard_map/ppermute | solution.py:810
  301.7 2.5 collective-permute-start.49
  305.8 2.0 collective-permute-start.47
  307.8 9.5 %collective-permute-done.50 = bf16[2,48,3456]{2,1,0:T(8,128)(2,1)S(1)} collective-permute-done((bf16[2,48,3456]{2,1,0:T(8,128)(2,1)S(1)}, bf16[2,48,3456]{2,1,0:T(8,128)(2,1)S(1)}, u32[]{:S(2)}, u32[]{:S(2)}) %collective-permute-start.50) | collective-permute-done | bytes 663584 | tf_op jit(solution)/shard_map/ppermute | solution.py:810
  317.3 4.7 %collective-permute-start.54 = (bf16[1,104,576]{2,1,0:T(8,128)(2,1)S(1)}, bf16[1,104,576]{2,1,0:T(8,128)(2,1)S(1)}, u32[]{:S(2)}, u32[]{:S(2)}) collective-permute-start(bf16[1,104,576]{2,1,0:T(8,128)(2,1)S(1)} %get-tuple-element.870), channel_id=1, source_target_pairs={{0,8},{4,12},{8,0},{12,4},{1,9},{5,13},{9,1},{13,5},{2,10},{6,14},... | collective-permute-start | bytes 359432 | tf_op jit(solution)/shard_map/ppermute | solution.py:810
  322.3 7.0 %collective-permute-done.48.refs_3_ = bf16[192,3456]{1,0:T(8,128)(2,1)S(1)} collective-permute-done((bf16[192,3456]{1,0:T(8,128)(2,1)S(1)}, bf16[192,3456]{1,0:T(8,128)(2,1)S(1)}, u32[]{:S(2)}, u32[]{:S(2)}) %collective-permute-start.48) | collective-permute-done | bytes 1327136 | tf_op jit(solution)/shard_map/ppermute | solution.py:797
  329.3 6.4 %collective-permute-start.58 = (bf16[1,48,3456]{2,1,0:T(8,128)(2,1)S(1)}, bf16[1,48,3456]{2,1,0:T(8,128)(2,1)S(1)}, u32[]{:S(2)}, u32[]{:S(2)}) collective-permute-start(bf16[1,48,3456]{2,1,0:T(8,128)(2,1)S(1)} %get-tuple-element.877), channel_id=1, source_target_pairs={{0,8},{4,12},{8,0},{12,4},{1,9},{5,13},{9,1},{13,5},{2,10},{6,14},... | collective-permute-start | bytes 995336 | tf_op jit(solution)/shard_map/ppermute | solution.py:810
  337.3 11.0 %collective-permute-done.58 = bf16[1,48,3456]{2,1,0:T(8,128)(2,1)S(1)} collective-permute-done((bf16[1,48,3456]{2,1,0:T(8,128)(2,1)S(1)}, bf16[1,48,3456]{2,1,0:T(8,128)(2,1)S(1)}, u32[]{:S(2)}, u32[]{:S(2)}) %collective-permute-start.58) | collective-permute-done | bytes 331808 | tf_op jit(solution)/shard_map/ppermute | solution.py:810
  348.3 2.8 collective-permute-start.52
  351.2 3.0 collective-permute-start.62
  355.6 8.4 %collective-permute-done.52 = bf16[416,576]{1,0:T(8,128)(2,1)S(1)} collective-permute-done((bf16[416,576]{1,0:T(8,128)(2,1)S(1)}, bf16[416,576]{1,0:T(8,128)(2,1)S(1)}, u32[]{:S(2)}, u32[]{:S(2)}) %collective-permute-start.52) | collective-permute-done | bytes 479264 | tf_op jit(solution)/shard_map/ppermute | solution.py:797
  364.2 2.7 collective-permute-start.61
  368.8 2.5 collective-permute-done.61
  371.5 2.1 collective-permute-start.63
  375.0 5.9 %collective-permute-done.63 = bf16[416,576]{1,0:T(8,128)(2,1)S(1)} collective-permute-done((bf16[416,576]{1,0:T(8,128)(2,1)S(1)}, bf16[416,576]{1,0:T(8,128)(2,1)S(1)}, u32[]{:S(2)}, u32[]{:S(2)}) %collective-permute-start.63) | collective-permute-done | bytes 479264 | tf_op jit(solution)/shard_map/ppermute | solution.py:797
  383.7 2.1 collective-permute-start.68
  390.1 2.3 shard_map.248
  392.4 3.7 shard_map.249
  396.1 2.5 shard_map.250
  398.6 28.8 %collective-permute-done.70 = bf16[2,416,576]{2,1,0:T(8,128)(2,1)S(1)} collective-permute-done((bf16[2,416,576]{2,1,0:T(8,128)(2,1)S(1)}, bf16[2,416,576]{2,1,0:T(8,128)(2,1)S(1)}, u32[]{:S(2)}, u32[]{:S(2)}) %collective-permute-start.70) | collective-permute-done | bytes 958496 | tf_op jit(solution)/shard_map/ppermute | solution.py:792
  429.0 3.2 collective-permute-start.72
  435.2 3.7 shard_map.251
  440.2 7.8 %shard_map.252 = f32[767,1,2304]{2,1,0:T(1,128)} custom-call(s32[8]{0:T(128)S(1)} %stack.144.ids, bf16[4,416,576]{2,1,0:T(8,128)(2,1)S(1)} %pad_maximum_fusion.1.refs_0_, bf16[4,416,576]{2,1,0:T(8,128)(2,1)S(1)} %collective-permute-done.71.refs_1_, bf16[4,416,576]{2,1,0:T(8,128)(2,1)S(1)} %collective-permute-done.72.refs_2_, ...), custom_call_target="tpu_custom_call" | custom-call | bytes 21206016 | tf_op jit(solution)/shard_map/pallas_call | solution.py:710
  452.7 3.7 shard_map.254
  456.4 3.7 shard_map.255
  (419 shorter events, 113.3 us)
Async XLA Ops:
  0.7 49.8 %collective-permute-start.10 = (bf16[1,3072,767]{2,1,0:T(8,128)(2,1)}, bf16[1,3072,767]{2,1,0:T(8,128)(2,1)}, u32[]{:S(2)}, u32[]{:S(2)}) collective-permute-start(bf16[1,3072,767]{2,1,0:T(8,128)(2,1)} %dno.7), channel_id=1, source_target_pairs={{0,16},{16,0},{1,17},{17,1},{2,18},{18,2},{3,19},{19,3},{4,20},{20... | collective-permute-start | bytes 14137352 | tf_op jit(solution)/shard_map/ppermute | solution.py:805
  1.2 49.2 %collective-permute-start.9 = (bf16[1,767,3072]{2,1,0:T(8,128)(2,1)}, bf16[1,767,3072]{2,1,0:T(8,128)(2,1)}, u32[]{:S(2)}, u32[]{:S(2)}) collective-permute-start(bf16[1,767,3072]{2,1,0:T(8,128)(2,1)} %upo.7), channel_id=1, source_target_pairs={{0,16},{16,0},{1,17},{17,1},{2,18},{18,2},{3,19},{19,3},{4,20},{20... | collective-permute-start | bytes 14137352 | tf_op jit(solution)/shard_map/ppermute | solution.py:805
  7.0 12.7 %collective-permute-start.3 = (bf16[767,576]{0,1:T(8,128)(2,1)}, bf16[767,576]{0,1:T(8,128)(2,1)S(1)}, u32[]{:S(2)}, u32[]{:S(2)}) collective-permute-start(bf16[767,576]{0,1:T(8,128)(2,1)} %copy.51), channel_id=1, source_target_pairs={{0,16},{16,0},{1,17},{17,1},{2,18},{18,2},{3,19},{19,3},{4,20},{20... | collective-permute-start | bytes 2650760 | tf_op jit(solution)/shard_map/ppermute | solution.py:805
  9.2 10.5 %collective-permute-start = (bf16[256,767]{1,0:T(8,128)(2,1)S(1)}, bf16[256,767]{1,0:T(8,128)(2,1)S(1)}, u32[]{:S(2)}, u32[]{:S(2)}) collective-permute-start(bf16[256,767]{1,0:T(8,128)(2,1)S(1)} %shard_map.228.n0.x), channel_id=1, source_target_pairs={{0,2},{1,3},{2,0},{3,1},{16,17},{17,16},{18,19},{19,18},{4,6},{5,7... | collective-permute-start | bytes 1178120 | tf_op jit(solution)/shard_map/ppermute | solution.py:797
  17.2 8.3 %collective-permute-start.1 = (bf16[256,767]{1,0:T(8,128)(2,1)S(1)}, bf16[256,767]{1,0:T(8,128)(2,1)S(1)}, u32[]{:S(2)}, u32[]{:S(2)}) collective-permute-start(bf16[256,767]{1,0:T(8,128)(2,1)S(1)} %shard_map.228.n0.x), channel_id=1, source_target_pairs={{0,1},{1,0},{2,3},{3,2},{16,18},{17,19},{18,16},{19,17},{4,5},{5,4... | collective-permute-start | bytes 1178120 | tf_op jit(solution)/shard_map/ppermute | solution.py:792
  19.7 25.2 %collective-permute-start.8 = (bf16[768,767]{1,0:T(8,128)(2,1)}, bf16[768,767]{1,0:T(8,128)(2,1)}, u32[]{:S(2)}, u32[]{:S(2)}) collective-permute-start(bf16[768,767]{1,0:T(8,128)(2,1)} %bitcast.11), channel_id=1, source_target_pairs={{0,16},{16,0},{1,17},{17,1},{2,18},{18,2},{3,19},{19,3},{4,20},{20... | collective-permute-start | bytes 3534344 | tf_op jit(solution)/shard_map/ppermute | solution.py:805
  19.7 10.0 %collective-permute-start.2 = (bf16[256,767]{1,0:T(8,128)(2,1)S(1)}, bf16[256,767]{1,0:T(8,128)(2,1)S(1)}, u32[]{:S(2)}, u32[]{:S(2)}) collective-permute-start(bf16[256,767]{1,0:T(8,128)(2,1)S(1)} %collective-permute-done.n1), channel_id=1, source_target_pairs={{0,1},{1,0},{2,3},{3,2},{16,18},{17,19},{18,16},{19,17},{4,5},{5,4... | collective-permute-start | bytes 1178120 | tf_op jit(solution)/shard_map/ppermute | solution.py:792
  60.5 11.1 %collective-permute-start.11 = (bf16[256,767]{1,0:T(8,128)(2,1)S(1)}, bf16[256,767]{1,0:T(8,128)(2,1)S(1)}, u32[]{:S(2)}, u32[]{:S(2)}) collective-permute-start(bf16[256,767]{1,0:T(8,128)(2,1)S(1)} %get-tuple-element.537.n0), channel_id=1, source_target_pairs={{0,2},{1,3},{2,0},{3,1},{16,17},{17,16},{18,19},{19,18},{4,6},{5,7... | collective-permute-start | bytes 1178120 | tf_op jit(solution)/shard_map/ppermute | solution.py:797
  61.0 13.4 %collective-permute-start.12 = (bf16[256,767]{1,0:T(8,128)(2,1)S(1)}, bf16[256,767]{1,0:T(8,128)(2,1)S(1)}, u32[]{:S(2)}, u32[]{:S(2)}) collective-permute-start(bf16[256,767]{1,0:T(8,128)(2,1)S(1)} %get-tuple-element.537.n0), channel_id=1, source_target_pairs={{0,1},{1,0},{2,3},{3,2},{16,18},{17,19},{18,16},{19,17},{4,5},{5,4... | collective-permute-start | bytes 1178120 | tf_op jit(solution)/shard_map/ppermute | solution.py:792
  71.6 7.8 %collective-permute-start.13 = (bf16[256,767]{1,0:T(8,128)(2,1)S(1)}, bf16[256,767]{1,0:T(8,128)(2,1)S(1)}, u32[]{:S(2)}, u32[]{:S(2)}) collective-permute-start(bf16[256,767]{1,0:T(8,128)(2,1)S(1)} %collective-permute-done.11.n1), channel_id=1, source_target_pairs={{0,1},{1,0},{2,3},{3,2},{16,18},{17,19},{18,16},{19,17},{4,5},{5,4... | collective-permute-start | bytes 1178120 | tf_op jit(solution)/shard_map/ppermute | solution.py:792
  120.8 10.3 %collective-permute-start.20 = (bf16[2,192,3456]{2,1,0:T(8,128)(2,1)S(1)}, bf16[2,192,3456]{2,1,0:T(8,128)(2,1)S(1)}, u32[]{:S(2)}, u32[]{:S(2)}) collective-permute-start(bf16[2,192,3456]{2,1,0:T(8,128)(2,1)S(1)} %shard_map.235), channel_id=1, source_target_pairs={{0,16},{16,0},{1,17},{17,1},{2,18},{18,2},{3,19},{19,3},{4,20},{20... | collective-permute-start | bytes 7962632 | tf_op jit(solution)/shard_map/ppermute | solution.py:805
  131.0 17.0 %collective-permute-start.24 = (bf16[2,192,3456]{2,1,0:T(8,128)(2,1)S(1)}, bf16[2,192,3456]{2,1,0:T(8,128)(2,1)S(1)}, u32[]{:S(2)}, u32[]{:S(2)}) collective-permute-start(bf16[2,192,3456]{2,1,0:T(8,128)(2,1)S(1)} %shard_map.236), channel_id=1, source_target_pairs={{0,16},{16,0},{1,17},{17,1},{2,18},{18,2},{3,19},{19,3},{4,20},{20... | collective-permute-start | bytes 7962632 | tf_op jit(solution)/shard_map/ppermute | solution.py:805
  133.7 17.8 %collective-permute-start.23 = (bf16[192,3456]{1,0:T(8,128)(2,1)S(1)}, bf16[192,3456]{1,0:T(8,128)(2,1)S(1)}, u32[]{:S(2)}, u32[]{:S(2)}) collective-permute-start(bf16[192,3456]{1,0:T(8,128)(2,1)S(1)} %get-tuple-element.608), channel_id=1, source_target_pairs={{0,1},{1,0},{2,3},{3,2},{16,18},{17,19},{18,16},{19,17},{4,5},{5,4... | collective-permute-start | bytes 3981320 | tf_op jit(solution)/shard_map/ppermute | solution.py:792
  147.0 12.8 %collective-permute-start.21 = (bf16[512,767]{1,0:T(8,128)(2,1)S(1)}, bf16[512,767]{1,0:T(8,128)(2,1)S(1)}, u32[]{:S(2)}, u32[]{:S(2)}) collective-permute-start(bf16[512,767]{1,0:T(8,128)(2,1)S(1)} %get-tuple-element.606), channel_id=1, source_target_pairs={{0,1},{1,0},{2,3},{3,2},{16,18},{17,19},{18,16},{19,17},{4,5},{5,4... | collective-permute-start | bytes 2356232 | tf_op jit(solution)/shard_map/ppermute | solution.py:792
  148.0 6.6 %collective-permute-start.22 = (bf16[384,576]{1,0:T(8,128)(2,1)S(1)}, bf16[384,576]{1,0:T(8,128)(2,1)S(1)}, u32[]{:S(2)}, u32[]{:S(2)}) collective-permute-start(bf16[384,576]{1,0:T(8,128)(2,1)S(1)} %get-tuple-element.607), channel_id=1, source_target_pairs={{0,16},{16,0},{1,17},{17,1},{2,18},{18,2},{3,19},{19,3},{4,20},{20... | collective-permute-start | bytes 1327112 | tf_op jit(solution)/shard_map/ppermute | solution.py:805
  153.1 6.8 %collective-permute-start.25 = (bf16[256,767]{1,0:T(8,128)(2,1)S(1)}, bf16[256,767]{1,0:T(8,128)(2,1)S(1)}, u32[]{:S(2)}, u32[]{:S(2)}) collective-permute-start(bf16[256,767]{1,0:T(8,128)(2,1)S(1)} %broadcast_select_fusion.7), channel_id=1, source_target_pairs={{0,16},{16,0},{1,17},{17,1},{2,18},{18,2},{3,19},{19,3},{4,20},{20... | collective-permute-start | bytes 1178120 | tf_op jit(solution)/shard_map/ppermute | solution.py:805
  160.0 7.8 %collective-permute-start.26 = (bf16[256,767]{1,0:T(8,128)(2,1)S(1)}, bf16[256,767]{1,0:T(8,128)(2,1)S(1)}, u32[]{:S(2)}, u32[]{:S(2)}) collective-permute-start(bf16[256,767]{1,0:T(8,128)(2,1)S(1)} %add_convert_fusion.11), channel_id=1, source_target_pairs={{0,2},{1,3},{2,0},{3,1},{16,17},{17,16},{18,19},{19,18},{4,6},{5,7... | collective-permute-start | bytes 1178120 | tf_op jit(solution)/shard_map/ppermute | solution.py:797
  168.7 32.4 %collective-permute-start.31 = (bf16[192,3456]{1,0:T(8,128)(2,1)}, bf16[192,3456]{1,0:T(8,128)(2,1)}, u32[]{:S(2)}, u32[]{:S(2)}) collective-permute-start(bf16[192,3456]{1,0:T(8,128)(2,1)} %get-tuple-element.686), channel_id=1, source_target_pairs={{0,1},{1,0},{2,3},{3,2},{16,18},{17,19},{18,16},{19,17},{4,5},{5,4... | collective-permute-start | bytes 3981320 | tf_op jit(solution)/shard_map/ppermute | solution.py:792
  169.9 33.0 %collective-permute-start.32 = (bf16[192,3456]{1,0:T(8,128)(2,1)}, bf16[192,3456]{1,0:T(8,128)(2,1)}, u32[]{:S(2)}, u32[]{:S(2)}) collective-permute-start(bf16[192,3456]{1,0:T(8,128)(2,1)} %add_convert_fusion.5), channel_id=1, source_target_pairs={{0,2},{1,3},{2,0},{3,1},{16,17},{17,16},{18,19},{19,18},{4,6},{5,7... | collective-permute-start | bytes 3981320 | tf_op jit(solution)/shard_map/ppermute | solution.py:797
  184.0 23.2 %collective-permute-start.27 = (bf16[2,192,3456]{2,1,0:T(8,128)(2,1)}, bf16[2,192,3456]{2,1,0:T(8,128)(2,1)}, u32[]{:S(2)}, u32[]{:S(2)}) collective-permute-start(bf16[2,192,3456]{2,1,0:T(8,128)(2,1)} %shard_map.242), channel_id=1, source_target_pairs={{0,16},{16,0},{1,17},{17,1},{2,18},{18,2},{3,19},{19,3},{4,20},{20... | collective-permute-start | bytes 7962632 | tf_op jit(solution)/shard_map/ppermute | solution.py:805
  188.6 16.8 %collective-permute-start.28 = (bf16[192,256]{1,0:T(8,128)(2,1)S(1)}, bf16[192,256]{1,0:T(8,128)(2,1)S(1)}, u32[]{:S(2)}, u32[]{:S(2)}) collective-permute-start(bf16[192,256]{1,0:T(8,128)(2,1)S(1)} %copy-done.53), channel_id=1, source_target_pairs={{0,1},{1,0},{2,3},{3,2},{4,5},{5,4},{6,7},{7,6},{8,9},{9,8},{10,11... | collective-permute-start | bytes 294920 | tf_op jit(solution)/shard_map/ppermute | solution.py:801
  189.8 17.3 %collective-permute-start.29 = (bf16[192,256]{1,0:T(8,128)(2,1)S(1)}, bf16[192,256]{1,0:T(8,128)(2,1)S(1)}, u32[]{:S(2)}, u32[]{:S(2)}) collective-permute-start(bf16[192,256]{1,0:T(8,128)(2,1)S(1)} %copy-done.51), channel_id=1, source_target_pairs={{0,2},{1,3},{2,0},{3,1},{4,6},{5,7},{6,4},{7,5},{8,10},{9,11},{10,... | collective-permute-start | bytes 294920 | tf_op jit(solution)/shard_map/ppermute | solution.py:801
  202.9 23.6 %collective-permute-start.34 = (bf16[2,192,3456]{2,1,0:T(8,128)(2,1)S(1)}, bf16[2,192,3456]{2,1,0:T(8,128)(2,1)S(1)}, u32[]{:S(2)}, u32[]{:S(2)}) collective-permute-start(bf16[2,192,3456]{2,1,0:T(8,128)(2,1)S(1)} %shard_map.243), channel_id=1, source_target_pairs={{0,16},{16,0},{1,17},{17,1},{2,18},{18,2},{3,19},{19,3},{4,20},{20... | collective-permute-start | bytes 7962632 | tf_op jit(solution)/shard_map/ppermute | solution.py:805
  205.4 23.5 %collective-permute-start.35 = (bf16[2,48,3456]{2,1,0:T(8,128)(2,1)S(1)}, bf16[2,48,3456]{2,1,0:T(8,128)(2,1)S(1)}, u32[]{:S(2)}, u32[]{:S(2)}) collective-permute-start(bf16[2,48,3456]{2,1,0:T(8,128)(2,1)S(1)} %get-tuple-element.735), channel_id=1, source_target_pairs={{0,4},{4,0},{8,12},{12,8},{1,5},{5,1},{9,13},{13,9},{2,6},{6,2},{1... | collective-permute-start | bytes 1990664 | tf_op jit(solution)/shard_map/ppermute | solution.py:810
  211.1 17.8 %collective-permute-start.33 = (bf16[192,3456]{1,0:T(8,128)(2,1)S(1)}, bf16[192,3456]{1,0:T(8,128)(2,1)S(1)}, u32[]{:S(2)}, u32[]{:S(2)}) collective-permute-start(bf16[192,3456]{1,0:T(8,128)(2,1)S(1)} %get-tuple-element.709), channel_id=1, source_target_pairs={{0,1},{1,0},{2,3},{3,2},{16,18},{17,19},{18,16},{19,17},{4,5},{5,4... | collective-permute-start | bytes 3981320 | tf_op jit(solution)/shard_map/ppermute | solution.py:792
  225.6 12.4 %collective-permute-start.37 = (bf16[512,767]{1,0:T(8,128)(2,1)}, bf16[512,767]{1,0:T(8,128)(2,1)}, u32[]{:S(2)}, u32[]{:S(2)}) collective-permute-start(bf16[512,767]{1,0:T(8,128)(2,1)} %get-tuple-element.764), channel_id=1, source_target_pairs={{0,1},{1,0},{2,3},{3,2},{16,18},{17,19},{18,16},{19,17},{4,5},{5,4... | collective-permute-start | bytes 2356232 | tf_op jit(solution)/shard_map/ppermute | solution.py:792
  226.5 9.0 %collective-permute-start.38 = (bf16[384,576]{1,0:T(8,128)(2,1)}, bf16[384,576]{1,0:T(8,128)(2,1)}, u32[]{:S(2)}, u32[]{:S(2)}) collective-permute-start(bf16[384,576]{1,0:T(8,128)(2,1)} %get-tuple-element.765), channel_id=1, source_target_pairs={{0,16},{16,0},{1,17},{17,1},{2,18},{18,2},{3,19},{19,3},{4,20},{20... | collective-permute-start | bytes 1327112 | tf_op jit(solution)/shard_map/ppermute | solution.py:805
  239.0 7.8 %collective-permute-start.39 = (bf16[256,767]{1,0:T(8,128)(2,1)S(1)}, bf16[256,767]{1,0:T(8,128)(2,1)S(1)}, u32[]{:S(2)}, u32[]{:S(2)}) collective-permute-start(bf16[256,767]{1,0:T(8,128)(2,1)S(1)} %add_convert_fusion.10), channel_id=1, source_target_pairs={{0,2},{1,3},{2,0},{3,1},{16,17},{17,16},{18,19},{19,18},{4,6},{5,7... | collective-permute-start | bytes 1178120 | tf_op jit(solution)/shard_map/ppermute | solution.py:797
  239.8 13.3 %collective-permute-start.36 = (bf16[2,104,576]{2,1,0:T(8,128)(2,1)S(1)}, bf16[2,104,576]{2,1,0:T(8,128)(2,1)S(1)}, u32[]{:S(2)}, u32[]{:S(2)}) collective-permute-start(bf16[2,104,576]{2,1,0:T(8,128)(2,1)S(1)} %get-tuple-element.762), channel_id=1, source_target_pairs={{0,4},{4,0},{8,12},{12,8},{1,5},{5,1},{9,13},{13,9},{2,6},{6,2},{1... | collective-permute-start | bytes 718856 | tf_op jit(solution)/shard_map/ppermute | solution.py:810
  241.6 18.2 %collective-permute-start.42 = (bf16[1,48,3456]{2,1,0:T(8,128)(2,1)S(1)}, bf16[1,48,3456]{2,1,0:T(8,128)(2,1)S(1)}, u32[]{:S(2)}, u32[]{:S(2)}) collective-permute-start(bf16[1,48,3456]{2,1,0:T(8,128)(2,1)S(1)} %copy-done.83), channel_id=1, source_target_pairs={{0,8},{4,12},{8,0},{12,4},{1,9},{5,13},{9,1},{13,5},{2,10},{6,14},... | collective-permute-start | bytes 995336 | tf_op jit(solution)/shard_map/ppermute | solution.py:810
  253.1 17.8 %collective-permute-start.41 = (bf16[192,3456]{1,0:T(8,128)(2,1)S(1)}, bf16[192,3456]{1,0:T(8,128)(2,1)S(1)}, u32[]{:S(2)}, u32[]{:S(2)}) collective-permute-start(bf16[192,3456]{1,0:T(8,128)(2,1)S(1)} %copy-done.47), channel_id=1, source_target_pairs={{0,1},{1,0},{2,3},{3,2},{16,18},{17,19},{18,16},{19,17},{4,5},{5,4... | collective-permute-start | bytes 3981320 | tf_op jit(solution)/shard_map/ppermute | solution.py:792
  259.9 12.0 %collective-permute-start.43 = (bf16[1,48,3456]{2,1,0:T(8,128)(2,1)S(1)}, bf16[1,48,3456]{2,1,0:T(8,128)(2,1)S(1)}, u32[]{:S(2)}, u32[]{:S(2)}) collective-permute-start(bf16[1,48,3456]{2,1,0:T(8,128)(2,1)S(1)} %add_convert_fusion.13), channel_id=1, source_target_pairs={{0,8},{4,12},{8,0},{12,4},{1,9},{5,13},{9,1},{13,5},{2,10},{6,14},... | collective-permute-start | bytes 995336 | tf_op jit(solution)/shard_map/ppermute | solution.py:810
  260.5 22.2 %collective-permute-start.40 = (bf16[1,104,576]{2,1,0:T(8,128)(2,1)}, bf16[1,104,576]{2,1,0:T(8,128)(2,1)}, u32[]{:S(2)}, u32[]{:S(2)}) collective-permute-start(bf16[1,104,576]{2,1,0:T(8,128)(2,1)} %get-tuple-element.792), channel_id=1, source_target_pairs={{0,8},{4,12},{8,0},{12,4},{1,9},{5,13},{9,1},{13,5},{2,10},{6,14},... | collective-permute-start | bytes 359432 | tf_op jit(solution)/shard_map/ppermute | solution.py:810
  273.5 18.2 %collective-permute-start.45 = (bf16[192,3456]{1,0:T(8,128)(2,1)}, bf16[192,3456]{1,0:T(8,128)(2,1)}, u32[]{:S(2)}, u32[]{:S(2)}) collective-permute-start(bf16[192,3456]{1,0:T(8,128)(2,1)} %add_convert_fusion.2), channel_id=1, source_target_pairs={{0,2},{1,3},{2,0},{3,1},{16,17},{17,16},{18,19},{19,18},{4,6},{5,7... | collective-permute-start | bytes 3981320 | tf_op jit(solution)/shard_map/ppermute | solution.py:797
  275.7 21.2 %collective-permute-start.46 = (bf16[2,48,3456]{2,1,0:T(8,128)(2,1)S(1)}, bf16[2,48,3456]{2,1,0:T(8,128)(2,1)S(1)}, u32[]{:S(2)}, u32[]{:S(2)}) collective-permute-start(bf16[2,48,3456]{2,1,0:T(8,128)(2,1)S(1)} %maximum_select_fusion.2), channel_id=1, source_target_pairs={{0,4},{4,0},{8,12},{12,8},{1,5},{5,1},{9,13},{13,9},{2,6},{6,2},{1... | collective-permute-start | bytes 1990664 | tf_op jit(solution)/shard_map/ppermute | solution.py:810
  284.4 19.9 %collective-permute-start.44 = (bf16[1,104,576]{2,1,0:T(8,128)(2,1)S(1)}, bf16[1,104,576]{2,1,0:T(8,128)(2,1)S(1)}, u32[]{:S(2)}, u32[]{:S(2)}) collective-permute-start(bf16[1,104,576]{2,1,0:T(8,128)(2,1)S(1)} %add_convert_fusion.17), channel_id=1, source_target_pairs={{0,8},{4,12},{8,0},{12,4},{1,9},{5,13},{9,1},{13,5},{2,10},{6,14},... | collective-permute-start | bytes 359432 | tf_op jit(solution)/shard_map/ppermute | solution.py:810
  287.3 18.4 %collective-permute-start.51 = (bf16[2,104,576]{2,1,0:T(8,128)(2,1)S(1)}, bf16[2,104,576]{2,1,0:T(8,128)(2,1)S(1)}, u32[]{:S(2)}, u32[]{:S(2)}) collective-permute-start(bf16[2,104,576]{2,1,0:T(8,128)(2,1)S(1)} %fusion.11), channel_id=1, source_target_pairs={{0,4},{4,0},{8,12},{12,8},{1,5},{5,1},{9,13},{13,9},{2,6},{6,2},{1... | collective-permute-start | bytes 718856 | tf_op jit(solution)/shard_map/ppermute | solution.py:810
  300.3 17.0 %collective-permute-start.50 = (bf16[2,48,3456]{2,1,0:T(8,128)(2,1)S(1)}, bf16[2,48,3456]{2,1,0:T(8,128)(2,1)S(1)}, u32[]{:S(2)}, u32[]{:S(2)}) collective-permute-start(bf16[2,48,3456]{2,1,0:T(8,128)(2,1)S(1)} %fusion.5), channel_id=1, source_target_pairs={{0,4},{4,0},{8,12},{12,8},{1,5},{5,1},{9,13},{13,9},{2,6},{6,2},{1... | collective-permute-start | bytes 1990664 | tf_op jit(solution)/shard_map/ppermute | solution.py:810
  300.5 28.8 %collective-permute-start.48 = (bf16[192,3456]{1,0:T(8,128)(2,1)S(1)}, bf16[192,3456]{1,0:T(8,128)(2,1)S(1)}, u32[]{:S(2)}, u32[]{:S(2)}) collective-permute-start(bf16[192,3456]{1,0:T(8,128)(2,1)S(1)} %bitcast.147), channel_id=1, source_target_pairs={{0,2},{1,3},{2,0},{3,1},{16,17},{17,16},{18,19},{19,18},{4,6},{5,7... | collective-permute-start | bytes 3981320 | tf_op jit(solution)/shard_map/ppermute | solution.py:797
  301.7 33.9 %collective-permute-start.49 = (bf16[192,3456]{1,0:T(8,128)(2,1)S(1)}, bf16[192,3456]{1,0:T(8,128)(2,1)S(1)}, u32[]{:S(2)}, u32[]{:S(2)}) collective-permute-start(bf16[192,3456]{1,0:T(8,128)(2,1)S(1)} %bitcast.148), channel_id=1, source_target_pairs={{0,1},{1,0},{2,3},{3,2},{16,18},{17,19},{18,16},{19,17},{4,5},{5,4... | collective-permute-start | bytes 3981320 | tf_op jit(solution)/shard_map/ppermute | solution.py:792
  304.2 46.9 %collective-permute-start.57 = (bf16[192,3456]{1,0:T(8,128)(2,1)S(1)}, bf16[192,3456]{1,0:T(8,128)(2,1)S(1)}, u32[]{:S(2)}, u32[]{:S(2)}) collective-permute-start(bf16[192,3456]{1,0:T(8,128)(2,1)S(1)} %bitcast.149), channel_id=1, source_target_pairs={{0,16},{1,17},{2,18},{3,19},{4,20},{5,21},{6,22},{7,23},{8,24},{9,... | collective-permute-start | bytes 3981320 | tf_op jit(solution)/shard_map/ppermute | solution.py:814
  305.8 29.8 %collective-permute-start.47 = (bf16[2,104,576]{2,1,0:T(8,128)(2,1)S(1)}, bf16[2,104,576]{2,1,0:T(8,128)(2,1)S(1)}, u32[]{:S(2)}, u32[]{:S(2)}) collective-permute-start(bf16[2,104,576]{2,1,0:T(8,128)(2,1)S(1)} %maximum_select_fusion.6), channel_id=1, source_target_pairs={{0,4},{4,0},{8,12},{12,8},{1,5},{5,1},{9,13},{13,9},{2,6},{6,2},{1... | collective-permute-start | bytes 718856 | tf_op jit(solution)/shard_map/ppermute | solution.py:810
  317.3 19.9 %collective-permute-start.54 = (bf16[1,104,576]{2,1,0:T(8,128)(2,1)S(1)}, bf16[1,104,576]{2,1,0:T(8,128)(2,1)S(1)}, u32[]{:S(2)}, u32[]{:S(2)}) collective-permute-start(bf16[1,104,576]{2,1,0:T(8,128)(2,1)S(1)} %get-tuple-element.870), channel_id=1, source_target_pairs={{0,8},{4,12},{8,0},{12,4},{1,9},{5,13},{9,1},{13,5},{2,10},{6,14},... | collective-permute-start | bytes 359432 | tf_op jit(solution)/shard_map/ppermute | solution.py:810
  329.3 19.0 %collective-permute-start.58 = (bf16[1,48,3456]{2,1,0:T(8,128)(2,1)S(1)}, bf16[1,48,3456]{2,1,0:T(8,128)(2,1)S(1)}, u32[]{:S(2)}, u32[]{:S(2)}) collective-permute-start(bf16[1,48,3456]{2,1,0:T(8,128)(2,1)S(1)} %get-tuple-element.877), channel_id=1, source_target_pairs={{0,8},{4,12},{8,0},{12,4},{1,9},{5,13},{9,1},{13,5},{2,10},{6,14},... | collective-permute-start | bytes 995336 | tf_op jit(solution)/shard_map/ppermute | solution.py:810
  335.7 18.5 %collective-permute-start.56 = (bf16[192,3456]{1,0:T(8,128)(2,1)S(1)}, bf16[192,3456]{1,0:T(8,128)(2,1)S(1)}, u32[]{:S(2)}, u32[]{:S(2)}) collective-permute-start(bf16[192,3456]{1,0:T(8,128)(2,1)S(1)} %collective-permute-done.48.refs_3_), channel_id=1, source_target_pairs={{0,1},{1,0},{2,3},{3,2},{16,18},{17,19},{18,16},{19,17},{4,5},{5,4... | collective-permute-start | bytes 3981320 | tf_op jit(solution)/shard_map/ppermute | solution.py:792
  335.7 28.4 %collective-permute-start.53 = (bf16[192,3456]{1,0:T(8,128)(2,1)S(1)}, bf16[192,3456]{1,0:T(8,128)(2,1)S(1)}, u32[]{:S(2)}, u32[]{:S(2)}) collective-permute-start(bf16[192,3456]{1,0:T(8,128)(2,1)S(1)} %collective-permute-done.48.refs_3_), channel_id=1, source_target_pairs={{0,16},{1,17},{2,18},{3,19},{4,20},{5,21},{6,22},{7,23},{8,24},{9,... | collective-permute-start | bytes 3981320 | tf_op jit(solution)/shard_map/ppermute | solution.py:814
  348.3 7.2 %collective-permute-start.55 = (bf16[1,104,576]{2,1,0:T(8,128)(2,1)S(1)}, bf16[1,104,576]{2,1,0:T(8,128)(2,1)S(1)}, u32[]{:S(2)}, u32[]{:S(2)}) collective-permute-start(bf16[1,104,576]{2,1,0:T(8,128)(2,1)S(1)} %add_convert_fusion.16), channel_id=1, source_target_pairs={{0,8},{4,12},{8,0},{12,4},{1,9},{5,13},{9,1},{13,5},{2,10},{6,14},... | collective-permute-start | bytes 359432 | tf_op jit(solution)/shard_map/ppermute | solution.py:810
  348.3 15.7 %collective-permute-start.52 = (bf16[416,576]{1,0:T(8,128)(2,1)S(1)}, bf16[416,576]{1,0:T(8,128)(2,1)S(1)}, u32[]{:S(2)}, u32[]{:S(2)}) collective-permute-start(bf16[416,576]{1,0:T(8,128)(2,1)S(1)} %bitcast.176), channel_id=1, source_target_pairs={{0,2},{1,3},{2,0},{3,1},{16,17},{17,16},{18,19},{19,18},{4,6},{5,7... | collective-permute-start | bytes 1437704 | tf_op jit(solution)/shard_map/ppermute | solution.py:797
  351.2 13.0 %collective-permute-start.62 = (bf16[1,48,3456]{2,1,0:T(8,128)(2,1)S(1)}, bf16[1,48,3456]{2,1,0:T(8,128)(2,1)S(1)}, u32[]{:S(2)}, u32[]{:S(2)}) collective-permute-start(bf16[1,48,3456]{2,1,0:T(8,128)(2,1)S(1)} %add_convert_fusion.12), channel_id=1, source_target_pairs={{0,8},{4,12},{8,0},{12,4},{1,9},{5,13},{9,1},{13,5},{2,10},{6,14},... | collective-permute-start | bytes 995336 | tf_op jit(solution)/shard_map/ppermute | solution.py:810
  354.2 20.8 %collective-permute-start.60 = (bf16[192,3456]{1,0:T(8,128)(2,1)S(1)}, bf16[192,3456]{1,0:T(8,128)(2,1)S(1)}, u32[]{:S(2)}, u32[]{:S(2)}) collective-permute-start(bf16[192,3456]{1,0:T(8,128)(2,1)S(1)} %collective-permute-done.49.refs_3_), channel_id=1, source_target_pairs={{0,16},{1,17},{2,18},{3,19},{4,20},{5,21},{6,22},{7,23},{8,24},{9,... | collective-permute-start | bytes 3981320 | tf_op jit(solution)/shard_map/ppermute | solution.py:814
  364.2 7.1 %collective-permute-start.61 = (bf16[2,104,576]{2,1,0:T(8,128)(2,1)S(1)}, bf16[2,104,576]{2,1,0:T(8,128)(2,1)S(1)}, u32[]{:S(2)}, u32[]{:S(2)}) collective-permute-start(bf16[2,104,576]{2,1,0:T(8,128)(2,1)S(1)} %maximum_select_fusion.7), channel_id=1, source_target_pairs={{0,4},{4,0},{8,12},{12,8},{1,5},{5,1},{9,13},{13,9},{2,6},{6,2},{1... | collective-permute-start | bytes 718856 | tf_op jit(solution)/shard_map/ppermute | solution.py:810
  366.9 15.0 %collective-permute-start.59 = (bf16[2,416,576]{2,1,0:T(8,128)(2,1)S(1)}, bf16[2,416,576]{2,1,0:T(8,128)(2,1)S(1)}, u32[]{:S(2)}, u32[]{:S(2)}) collective-permute-start(bf16[2,416,576]{2,1,0:T(8,128)(2,1)S(1)} %pad_maximum_fusion.2), channel_id=1, source_target_pairs={{0,1},{1,0},{2,3},{3,2},{16,18},{17,19},{18,16},{19,17},{4,5},{5,4... | collective-permute-start | bytes 2875400 | tf_op jit(solution)/shard_map/ppermute | solution.py:792
  368.6 13.3 %collective-permute-start.65 = (bf16[2,48,3456]{2,1,0:T(8,128)(2,1)S(1)}, bf16[2,48,3456]{2,1,0:T(8,128)(2,1)S(1)}, u32[]{:S(2)}, u32[]{:S(2)}) collective-permute-start(bf16[2,48,3456]{2,1,0:T(8,128)(2,1)S(1)} %maximum_select_fusion.3), channel_id=1, source_target_pairs={{0,4},{4,0},{8,12},{12,8},{1,5},{5,1},{9,13},{13,9},{2,6},{6,2},{1... | collective-permute-start | bytes 1990664 | tf_op jit(solution)/shard_map/ppermute | solution.py:810
  371.5 9.3 %collective-permute-start.63 = (bf16[416,576]{1,0:T(8,128)(2,1)S(1)}, bf16[416,576]{1,0:T(8,128)(2,1)S(1)}, u32[]{:S(2)}, u32[]{:S(2)}) collective-permute-start(bf16[416,576]{1,0:T(8,128)(2,1)S(1)} %bitcast.178), channel_id=1, source_target_pairs={{0,2},{1,3},{2,0},{3,1},{16,17},{17,16},{18,19},{19,18},{4,6},{5,7... | collective-permute-start | bytes 1437704 | tf_op jit(solution)/shard_map/ppermute | solution.py:797
  373.6 14.4 %collective-permute-start.64 = (bf16[192,3456]{1,0:T(8,128)(2,1)S(1)}, bf16[192,3456]{1,0:T(8,128)(2,1)S(1)}, u32[]{:S(2)}, u32[]{:S(2)}) collective-permute-start(bf16[192,3456]{1,0:T(8,128)(2,1)S(1)} %collective-permute-done.56.refs_3_), channel_id=1, source_target_pairs={{0,16},{1,17},{2,18},{3,19},{4,20},{5,21},{6,22},{7,23},{8,24},{9,... | collective-permute-start | bytes 3981320 | tf_op jit(solution)/shard_map/ppermute | solution.py:814
  382.3 10.1 %collective-permute-start.66 = (bf16[192,3456]{1,0:T(8,128)(2,1)S(1)}, bf16[192,3456]{1,0:T(8,128)(2,1)S(1)}, u32[]{:S(2)}, u32[]{:S(2)}) collective-permute-start(bf16[192,3456]{1,0:T(8,128)(2,1)S(1)} %bitcast.151), channel_id=1, source_target_pairs={{16,0},{17,1},{18,2},{19,3},{20,4},{21,5},{22,6},{23,7},{24,8},{25... | collective-permute-start | bytes 3981320 | tf_op jit(solution)/shard_map/ppermute | solution.py:814
  383.7 43.7 %collective-permute-start.68 = (bf16[192,3456]{1,0:T(8,128)(2,1)S(1)}, bf16[192,3456]{1,0:T(8,128)(2,1)S(1)}, u32[]{:S(2)}, u32[]{:S(2)}) collective-permute-start(bf16[192,3456]{1,0:T(8,128)(2,1)S(1)} %bitcast.152), channel_id=1, source_target_pairs={{0,2},{1,3},{2,0},{3,1},{16,17},{17,16},{18,19},{19,18},{4,6},{5,7... | collective-permute-start | bytes 3981320 | tf_op jit(solution)/shard_map/ppermute | solution.py:797
  385.8 41.6 %collective-permute-start.69 = (bf16[192,3456]{1,0:T(8,128)(2,1)S(1)}, bf16[192,3456]{1,0:T(8,128)(2,1)S(1)}, u32[]{:S(2)}, u32[]{:S(2)}) collective-permute-start(bf16[192,3456]{1,0:T(8,128)(2,1)S(1)} %bitcast.153), channel_id=1, source_target_pairs={{0,1},{1,0},{2,3},{3,2},{16,18},{17,19},{18,16},{19,17},{4,5},{5,4... | collective-permute-start | bytes 3981320 | tf_op jit(solution)/shard_map/ppermute | solution.py:792
  387.5 39.9 %collective-permute-start.70 = (bf16[2,416,576]{2,1,0:T(8,128)(2,1)S(1)}, bf16[2,416,576]{2,1,0:T(8,128)(2,1)S(1)}, u32[]{:S(2)}, u32[]{:S(2)}) collective-permute-start(bf16[2,416,576]{2,1,0:T(8,128)(2,1)S(1)} %pad_maximum_fusion.3), channel_id=1, source_target_pairs={{0,1},{1,0},{2,3},{3,2},{16,18},{17,19},{18,16},{19,17},{4,5},{5,4... | collective-permute-start | bytes 2875400 | tf_op jit(solution)/shard_map/ppermute | solution.py:792
  427.7 7.5 %collective-permute-start.73 = (bf16[192,3456]{1,0:T(8,128)(2,1)S(1)}, bf16[192,3456]{1,0:T(8,128)(2,1)S(1)}, u32[]{:S(2)}, u32[]{:S(2)}) collective-permute-start(bf16[192,3456]{1,0:T(8,128)(2,1)S(1)} %collective-permute-done.68.refs_0_), channel_id=1, source_target_pairs={{16,0},{17,1},{18,2},{19,3},{20,4},{21,5},{22,6},{23,7},{24,8},{25... | collective-permute-start | bytes 3981320 | tf_op jit(solution)/shard_map/ppermute | solution.py:814
  429.0 11.2 %collective-permute-start.72 = (bf16[4,416,576]{2,1,0:T(8,128)(2,1)S(1)}, bf16[4,416,576]{2,1,0:T(8,128)(2,1)S(1)}, u32[]{:S(2)}, u32[]{:S(2)}) collective-permute-start(bf16[4,416,576]{2,1,0:T(8,128)(2,1)S(1)} %pad_maximum_fusion.refs_3_), channel_id=1, source_target_pairs={{0,16},{1,17},{2,18},{3,19},{4,20},{5,21},{6,22},{7,23},{8,24},{9,... | collective-permute-start | bytes 5750792 | tf_op jit(solution)/shard_map/ppermute | solution.py:814
  432.3 7.9 %collective-permute-start.71 = (bf16[4,416,576]{2,1,0:T(8,128)(2,1)S(1)}, bf16[4,416,576]{2,1,0:T(8,128)(2,1)S(1)}, u32[]{:S(2)}, u32[]{:S(2)}) collective-permute-start(bf16[4,416,576]{2,1,0:T(8,128)(2,1)S(1)} %pad_maximum_fusion.1.refs_0_), channel_id=1, source_target_pairs={{16,0},{17,1},{18,2},{19,3},{20,4},{21,5},{22,6},{23,7},{24,8},{25... | collective-permute-start | bytes 5750792 | tf_op jit(solution)/shard_map/ppermute | solution.py:814
  433.6 17.8 %collective-permute-start.74 = (bf16[192,3456]{1,0:T(8,128)(2,1)S(1)}, bf16[192,3456]{1,0:T(8,128)(2,1)S(1)}, u32[]{:S(2)}, u32[]{:S(2)}) collective-permute-start(bf16[192,3456]{1,0:T(8,128)(2,1)S(1)} %collective-permute-done.68.refs_0_), channel_id=1, source_target_pairs={{0,1},{1,0},{2,3},{3,2},{16,18},{17,19},{18,16},{19,17},{4,5},{5,4... | collective-permute-start | bytes 3981320 | tf_op jit(solution)/shard_map/ppermute | solution.py:792
  438.9 12.5 %collective-permute-start.75 = (bf16[192,3456]{1,0:T(8,128)(2,1)S(1)}, bf16[192,3456]{1,0:T(8,128)(2,1)S(1)}, u32[]{:S(2)}, u32[]{:S(2)}) collective-permute-start(bf16[192,3456]{1,0:T(8,128)(2,1)S(1)} %collective-permute-done.69.refs_0_), channel_id=1, source_target_pairs={{16,0},{17,1},{18,2},{19,3},{20,4},{21,5},{22,6},{23,7},{24,8},{25... | collective-permute-start | bytes 3981320 | tf_op jit(solution)/shard_map/ppermute | solution.py:814
  (110 other events, 1002.7 us)

commit v9 on v8

--- a/solution.py
+++ b/solution.py
@@ -205,7 +205,7 @@
             pltpu.VMEM((full, span), F32),
             pltpu.SemaphoreType.DMA((8,)),
         ],
-        compiler_params=params(18),
+        compiler_params=params(15),
         cost_estimate=cost(
             2 * full * width * 3 * heads * hd + 3 * 4 * full * full * hd * heads,
             4 * full * width,
@@ -302,7 +302,7 @@
             jax.ShapeDtypeStruct((8, 128), F32),
             jax.ShapeDtypeStruct((QUAD, span, rows), BF16),
         ],
-        compiler_params=params(26, dimension_semantics=("arbitrary",)),
+        compiler_params=params(23, dimension_semantics=("arbitrary",)),
         cost_estimate=cost(6 * span * cc * ff, 4 * cc * ff + 4 * span * ff, span * ff),
     )(ids, x, *att, wo, pv, pvn, pv, up[0], up[1], dn[0], dn[1])
 
@@ -404,7 +404,7 @@
             jax.ShapeDtypeStruct((8, ff), F32),
             dd, dd, dd, dd,
         ],
-        compiler_params=params(26, dimension_semantics=("arbitrary",)),
+        compiler_params=params(23, dimension_semantics=("arbitrary",)),
         cost_estimate=cost(6 * span * cc * ff, 4 * cc * ff + 8 * span * ff, span * ff),
     )(ids, df, u, mid, wo, pv, up[0], up[1], dn[0], dn[1])
 
@@ -439,7 +439,7 @@
         out_shape=jax.ShapeDtypeStruct((len(places), quarter, cols), BF16)
         if send
         else [jax.ShapeDtypeStruct((quarter, cols), BF16)] * len(places),
-        compiler_params=params(18),
+        compiler_params=params(15),
         cost_estimate=cost(2 * span * quarter * cols * len(places), 2 * 4 * quarter * cols * len(places)),
     )(ids, lr, rr, att, *got)
 
@@ -536,7 +536,7 @@
             pltpu.VMEM((heads, QUAD, span), F32),
             pltpu.SemaphoreType.DMA((6,)),
         ],
-        compiler_params=params(26),
+        compiler_params=params(24),
         cost_estimate=cost(
             4 * full * cc * 3 * width + 3 * 10 * full * full * hd * heads,
             8 * full * cc,
@@ -718,7 +718,7 @@
             pltpu.VMEM((2, half // 2, 1, QUAD * cols), F32),
             pltpu.SemaphoreType.DMA((2, 2 * QUAD)),
         ],
-        compiler_params=params(18),
+        compiler_params=params(15),
         cost_estimate=cost(0, 6 * cc * QUAD * cols),
     )(ids, *srcs)
 

time: 465 us -> 462 us (level)
  starting transfers between devices: 104 us -> 98.4 us
    unnamed x194 -> x190, local copies, waits for them, and re-layouts: 11.9 us -> 13.7 us
where the time goes in v9:
time: 462 us; the launch traced here: 457 us
  waiting for transfers between devices  169 us (37%)
  Pallas kernels  136 us (29%)
  starting transfers between devices  98.4 us (21%)
  local copies, waits for them, and re-layouts  25.7 us (6%)
  other arithmetic  22.1 us (5%)
  between operations  5.33 us (1%)
    ppermute x16, waiting for transfers between devices, to_first(): return lax.ppermute(v, ('section', 'seq'), pairs)  70.2 us
    ppermute x10, waiting for transfers between devices, to_second(): return lax.ppermute(v, ('section', 'seq'), pairs)  45.6 us
    ppermute x16, waiting for transfers between devices, dp_partner(): return lax.ppermute(v, 'dp', [(i, i ^ step) for i in range(n)])  41.1 us
    ppermute x16, starting transfers between devices, dp_partner(): return lax.ppermute(v, 'dp', [(i, i ^ step) for i in range(n)])  35.4 us
    pallas_call x2, Pallas kernels, attn_bwd(): pl.pallas_call(attn_bwd_kernel, in_specs=[SMEM] + [HBM] * 6 + [VMEM] * 4,...  25.4 us
    pallas_call x2, Pallas kernels, attn_fwd(): pl.pallas_call(functools.partial(attn_fwd_kernel, raw), in_specs=[SMEM] +...  22.7 us
    pallas_call x2, Pallas kernels, mlp_bwd(): pl.pallas_call(functools.partial(mlp_bwd_kernel, layer), grid_spec=grid,...  19.3 us
    pallas_call x2, Pallas kernels, mlp_fwd(): pl.pallas_call(functools.partial(mlp_fwd_kernel, layer), grid_spec=grid,...  17.6 us
  transfers between devices with their start and end apart: 77, of which 34 were waited for; matrix products, arithmetic and copies ran while one was open for 7% of the time, Pallas kernels for 20%

profile of v9, /device:TPU:0, one launch (start us, length us, event | category | flops | bytes accessed | tf_op | source)
XLA Modules:
  0.0 457.0 jit_solution(2219991301173991622)
XLA Ops:
  1.3 2.8 dynamic-slice_bitcast_fusion.2
  9.2 2.7 collective-permute-start
  17.2 2.6 collective-permute-start.1
  22.5 2.1 broadcast_select_fusion.2
  25.5 4.2 collective-permute-done.2.n3
  29.7 11.5 %shard_map.229 = (bf16[3,1024,64]{2,1,0:T(8,128)(2,1)S(1)}, bf16[3,1024,64]{2,1,0:T(8,128)(2,1)S(1)}, bf16[3,1024,64]{2,1,0:T(8,128)(2,1)S(1)}, f32[3,4,256]{2,1...) custom-call(s32[8]{0:T(128)S(1)} %stack.144.ids, ...), custom_call_target="tpu_custom_call" | custom-call | flops 6641418240 | bytes 6283264 | tf_op jit(solution)/shard_map/pallas_call | solution.py:196
  42.4 2.1 collective-permute-start.5
  47.5 2.6 collective-permute-done.6.a2
  51.6 8.3 %shard_map.230 = (f32[256,767]{1,0:T(8,128)S(1)}, f32[256,3072]{1,0:T(8,128)S(1)}, bf16[256,767]{1,0:T(8,128)(2,1)S(1)}, bf16[256,767]{1,0:T(8,128)(2,1)S(1)}, f...) custom-call(s32[8]{0:T(128)S(1)} %stack.144.ids, bf16[256,767]{1,0:T(8,128)(2,1)S(1)} %shard_map.228.n0.x, ...), custom_call_target="tpu_custom_call" | custom-call | flops 7238320128 | bytes 25141248 | tf_op jit(solution)/shard_map/pallas_call | solution.py:294
  61.1 10.0 %collective-permute-done.11.n1 = bf16[256,767]{1,0:T(8,128)(2,1)S(1)} collective-permute-done((bf16[256,767]{1,0:T(8,128)(2,1)S(1)}, bf16[256,767]{1,0:T(8,128)(2,1)S(1)}, u32[]{:S(2)}, u32[]{:S(2)}) %collective-permute-start.11) | collective-permute-done | bytes 392736 | tf_op jit(solution)/shard_map/ppermute | solution.py:797
  72.0 1.9 shard_map.231.df
  73.9 5.1 %collective-permute-done.13.n3 = bf16[256,767]{1,0:T(8,128)(2,1)S(1)} collective-permute-done((bf16[256,767]{1,0:T(8,128)(2,1)S(1)}, bf16[256,767]{1,0:T(8,128)(2,1)S(1)}, u32[]{:S(2)}, u32[]{:S(2)}) %collective-permute-start.13) | collective-permute-done | bytes 392736 | tf_op jit(solution)/shard_map/ppermute | solution.py:792
  78.9 11.2 %shard_map.232 = (bf16[3,1024,64]{2,1,0:T(8,128)(2,1)S(1)}, bf16[3,1024,64]{2,1,0:T(8,128)(2,1)S(1)}, bf16[3,1024,64]{2,1,0:T(8,128)(2,1)S(1)}, f32[3,4,256]{2,1...) custom-call(s32[8]{0:T(128)S(1)} %stack.144.ids, ...), custom_call_target="tpu_custom_call" | custom-call | flops 6641418240 | bytes 6283264 | tf_op jit(solution)/shard_map/pallas_call | solution.py:196
  91.3 2.4 collective-permute-start.16
  96.8 9.3 %shard_map.233 = (f32[256,767]{1,0:T(8,128)S(1)}, f32[256,3072]{1,0:T(8,128)S(1)}, bf16[256,767]{1,0:T(8,128)(2,1)S(1)}, bf16[256,767]{1,0:T(8,128)(2,1)}, f32[8...) custom-call(s32[8]{0:T(128)S(1)} %stack.144.ids, bf16[256,767]{1,0:T(8,128)(2,1)S(1)} %get-tuple-element.930.x, ...), custom_call_target="tpu_custom_call" | custom-call | flops 7238320128 | bytes 25141248 | tf_op jit(solution)/shard_map/pallas_call | solution.py:294
  106.1 9.7 %shard_map.234 = (bf16[2,256,3072]{2,1,0:T(8,128)(2,1)S(1)}, bf16[3,4,256,192]{3,2,1,0:T(8,128)(2,1)S(1)}, f32[256,767]{1,0:T(8,128)S(1)}, f32[8,3072]{1,0:T(8,1...) custom-call(s32[8]{0:T(128)S(1)} %stack.144.ids, ...), custom_call_target="tpu_custom_call" | custom-call | flops 7238320128 | bytes 31432704 | tf_op jit(solution)/shard_map/pallas_call | solution.py:397
  122.6 2.3 collective-permute-done.18.d2
  127.6 2.6 shard_map.237
  131.4 12.2 %shard_map.238 = (bf16[256,767]{1,0:T(8,128)(2,1)S(1)}, bf16[256,767]{1,0:T(8,128)(2,1)S(1)}, bf16[512,767]{1,0:T(8,128)(2,1)S(1)}, bf16[384,576]{1,0:T(8,128)(2...) custom-call(s32[8]{0:T(128)S(1)} %stack.144.ids, bf16[4,256,767]{2,1,0:T(8,128)(2,1)S(1)} %get-tuple-element.546.n_hbm, ...), custom_call_target="tpu_custom_call" | custom-call | flops 15698755584 | bytes 12566528 | tf_op jit(solution)/shard_map/pallas_call | solution.py:519
  144.5 3.5 collective-permute-done.23
  152.1 4.3 collective-permute-done.21.r0
  158.1 6.3 %collective-permute-done.26.r1 = bf16[256,767]{1,0:T(8,128)(2,1)S(1)} collective-permute-done((bf16[256,767]{1,0:T(8,128)(2,1)S(1)}, bf16[256,767]{1,0:T(8,128)(2,1)S(1)}, u32[]{:S(2)}, u32[]{:S(2)}) %collective-permute-start.26) | collective-permute-done | bytes 392736 | tf_op jit(solution)/shard_map/ppermute | solution.py:797
  168.2 2.3 copy-done.48
  170.5 9.7 %shard_map.241 = (bf16[2,256,3072]{2,1,0:T(8,128)(2,1)S(1)}, bf16[3,4,256,192]{3,2,1,0:T(8,128)(2,1)S(1)}, f32[256,767]{1,0:T(8,128)S(1)}, f32[8,3072]{1,0:T(8,1...) custom-call(s32[8]{0:T(128)S(1)} %stack.144.ids, ...), custom_call_target="tpu_custom_call" | custom-call | flops 7238320128 | bytes 31432704 | tf_op jit(solution)/shard_map/pallas_call | solution.py:397
  180.3 3.0 shard_map.242
  189.8 8.3 %collective-permute-done.31 = bf16[192,3456]{1,0:T(8,128)(2,1)} collective-permute-done((bf16[192,3456]{1,0:T(8,128)(2,1)}, bf16[192,3456]{1,0:T(8,128)(2,1)}, u32[]{:S(2)}, u32[]{:S(2)}) %collective-permute-start.31) | collective-permute-done | bytes 1327136 | tf_op jit(solution)/shard_map/ppermute | solution.py:792
  200.0 2.2 add_convert_fusion.3
  204.3 2.8 shard_map.244
  209.5 13.2 %shard_map.245 = (bf16[256,767]{1,0:T(8,128)(2,1)S(1)}, bf16[256,767]{1,0:T(8,128)(2,1)S(1)}, bf16[512,767]{1,0:T(8,128)(2,1)}, bf16[384,576]{1,0:T(8,128)(2,1)}...) custom-call(s32[8]{0:T(128)S(1)} %stack.144.ids, bf16[4,256,767]{2,1,0:T(8,128)(2,1)S(1)} %copy-done.64, ...), custom_call_target="tpu_custom_call" | custom-call | flops 15698755584 | bytes 12566528 | tf_op jit(solution)/shard_map/pallas_call | solution.py:519
  223.6 2.4 collective-permute-done.33
  238.7 2.6 collective-permute-start.42
  241.3 2.7 collective-permute-done.39.r1
  245.8 4.4 collective-permute-done.36
  251.8 5.2 %collective-permute-done.42 = bf16[1,48,3456]{2,1,0:T(8,128)(2,1)S(1)} collective-permute-done((bf16[1,48,3456]{2,1,0:T(8,128)(2,1)S(1)}, bf16[1,48,3456]{2,1,0:T(8,128)(2,1)S(1)}, u32[]{:S(2)}, u32[]{:S(2)}) %collective-permute-start.42) | collective-permute-done | bytes 331808 | tf_op jit(solution)/shard_map/ppermute | solution.py:810
  257.7 2.9 collective-permute-start.40
  260.6 7.4 %collective-permute-done.41 = bf16[192,3456]{1,0:T(8,128)(2,1)S(1)} collective-permute-done((bf16[192,3456]{1,0:T(8,128)(2,1)S(1)}, bf16[192,3456]{1,0:T(8,128)(2,1)S(1)}, u32[]{:S(2)}, u32[]{:S(2)}) %collective-permute-start.41) | collective-permute-done | bytes 1327136 | tf_op jit(solution)/shard_map/ppermute | solution.py:792
  272.9 5.6 %collective-permute-start.46 = (bf16[2,48,3456]{2,1,0:T(8,128)(2,1)S(1)}, bf16[2,48,3456]{2,1,0:T(8,128)(2,1)S(1)}, u32[]{:S(2)}, u32[]{:S(2)}) collective-permute-start(bf16[2,48,3456]{2,1,0:T(8,128)(2,1)S(1)} %maximum_select_fusion.2), channel_id=1, source_target_pairs={{0,4},{4,0},{8,12},{12,8},{1,5},{5,1},{9,13},{13,9},{2,6},{6,2},{1... | collective-permute-start | bytes 1990664 | tf_op jit(solution)/shard_map/ppermute | solution.py:810
  281.5 2.9 collective-permute-start.44
  284.4 4.4 collective-permute-done.45
  288.8 5.4 %collective-permute-done.46 = bf16[2,48,3456]{2,1,0:T(8,128)(2,1)S(1)} collective-permute-done((bf16[2,48,3456]{2,1,0:T(8,128)(2,1)S(1)}, bf16[2,48,3456]{2,1,0:T(8,128)(2,1)S(1)}, u32[]{:S(2)}, u32[]{:S(2)}) %collective-permute-start.46) | collective-permute-done | bytes 663584 | tf_op jit(solution)/shard_map/ppermute | solution.py:810
  301.7 2.0 collective-permute-start.47
  303.7 10.9 %collective-permute-done.50 = bf16[2,48,3456]{2,1,0:T(8,128)(2,1)S(1)} collective-permute-done((bf16[2,48,3456]{2,1,0:T(8,128)(2,1)S(1)}, bf16[2,48,3456]{2,1,0:T(8,128)(2,1)S(1)}, u32[]{:S(2)}, u32[]{:S(2)}) %collective-permute-start.50) | collective-permute-done | bytes 663584 | tf_op jit(solution)/shard_map/ppermute | solution.py:810
  314.5 4.6 %collective-permute-start.54 = (bf16[1,104,576]{2,1,0:T(8,128)(2,1)S(1)}, bf16[1,104,576]{2,1,0:T(8,128)(2,1)S(1)}, u32[]{:S(2)}, u32[]{:S(2)}) collective-permute-start(bf16[1,104,576]{2,1,0:T(8,128)(2,1)S(1)} %get-tuple-element.870), channel_id=1, source_target_pairs={{0,8},{4,12},{8,0},{12,4},{1,9},{5,13},{9,1},{13,5},{2,10},{6,14},... | collective-permute-start | bytes 359432 | tf_op jit(solution)/shard_map/ppermute | solution.py:810
  319.4 7.7 %collective-permute-done.48.refs_3_ = bf16[192,3456]{1,0:T(8,128)(2,1)S(1)} collective-permute-done((bf16[192,3456]{1,0:T(8,128)(2,1)S(1)}, bf16[192,3456]{1,0:T(8,128)(2,1)S(1)}, u32[]{:S(2)}, u32[]{:S(2)}) %collective-permute-start.48) | collective-permute-done | bytes 1327136 | tf_op jit(solution)/shard_map/ppermute | solution.py:797
  327.1 5.7 %collective-permute-start.58 = (bf16[1,48,3456]{2,1,0:T(8,128)(2,1)S(1)}, bf16[1,48,3456]{2,1,0:T(8,128)(2,1)S(1)}, u32[]{:S(2)}, u32[]{:S(2)}) collective-permute-start(bf16[1,48,3456]{2,1,0:T(8,128)(2,1)S(1)} %get-tuple-element.877), channel_id=1, source_target_pairs={{0,8},{4,12},{8,0},{12,4},{1,9},{5,13},{9,1},{13,5},{2,10},{6,14},... | collective-permute-start | bytes 995336 | tf_op jit(solution)/shard_map/ppermute | solution.py:810
  334.4 10.8 %collective-permute-done.58 = bf16[1,48,3456]{2,1,0:T(8,128)(2,1)S(1)} collective-permute-done((bf16[1,48,3456]{2,1,0:T(8,128)(2,1)S(1)}, bf16[1,48,3456]{2,1,0:T(8,128)(2,1)S(1)}, u32[]{:S(2)}, u32[]{:S(2)}) %collective-permute-start.58) | collective-permute-done | bytes 331808 | tf_op jit(solution)/shard_map/ppermute | solution.py:810
  345.2 3.0 collective-permute-start.52
  348.2 3.0 collective-permute-start.62
  352.7 8.3 %collective-permute-done.52 = bf16[416,576]{1,0:T(8,128)(2,1)S(1)} collective-permute-done((bf16[416,576]{1,0:T(8,128)(2,1)S(1)}, bf16[416,576]{1,0:T(8,128)(2,1)S(1)}, u32[]{:S(2)}, u32[]{:S(2)}) %collective-permute-start.52) | collective-permute-done | bytes 479264 | tf_op jit(solution)/shard_map/ppermute | solution.py:797
  361.2 2.3 collective-permute-start.61
  364.6 3.3 collective-permute-done.61
  368.1 1.9 collective-permute-start.63
  371.4 6.1 %collective-permute-done.63 = bf16[416,576]{1,0:T(8,128)(2,1)S(1)} collective-permute-done((bf16[416,576]{1,0:T(8,128)(2,1)S(1)}, bf16[416,576]{1,0:T(8,128)(2,1)S(1)}, u32[]{:S(2)}, u32[]{:S(2)}) %collective-permute-start.63) | collective-permute-done | bytes 479264 | tf_op jit(solution)/shard_map/ppermute | solution.py:797
  386.2 2.3 shard_map.248
  388.5 3.7 shard_map.249
  392.2 2.5 shard_map.250
  394.8 29.3 %collective-permute-done.70 = bf16[2,416,576]{2,1,0:T(8,128)(2,1)S(1)} collective-permute-done((bf16[2,416,576]{2,1,0:T(8,128)(2,1)S(1)}, bf16[2,416,576]{2,1,0:T(8,128)(2,1)S(1)}, u32[]{:S(2)}, u32[]{:S(2)}) %collective-permute-start.70) | collective-permute-done | bytes 958496 | tf_op jit(solution)/shard_map/ppermute | solution.py:792
  425.6 3.2 collective-permute-start.72
  431.1 3.7 shard_map.251
  436.0 7.8 %shard_map.252 = f32[767,1,2304]{2,1,0:T(1,128)} custom-call(s32[8]{0:T(128)S(1)} %stack.144.ids, bf16[4,416,576]{2,1,0:T(8,128)(2,1)S(1)} %pad_maximum_fusion.1.refs_0_, bf16[4,416,576]{2,1,0:T(8,128)(2,1)S(1)} %collective-permute-done.71.refs_1_, bf16[4,416,576]{2,1,0:T(8,128)(2,1)S(1)} %collective-permute-done.72.refs_2_, ...), custom_call_target="tpu_custom_call" | custom-call | bytes 21206016 | tf_op jit(solution)/shard_map/pallas_call | solution.py:710
  443.8 1.8 shard_map.253
  445.6 2.4 collective-permute-done.74.refs_0_
  449.3 3.7 shard_map.254
  453.0 3.7 shard_map.255
  (415 shorter events, 111.0 us)
Async XLA Ops:
  0.7 50.9 %collective-permute-start.10 = (bf16[1,3072,767]{2,1,0:T(8,128)(2,1)}, bf16[1,3072,767]{2,1,0:T(8,128)(2,1)}, u32[]{:S(2)}, u32[]{:S(2)}) collective-permute-start(bf16[1,3072,767]{2,1,0:T(8,128)(2,1)} %dno.7), channel_id=1, source_target_pairs={{0,16},{16,0},{1,17},{17,1},{2,18},{18,2},{3,19},{19,3},{4,20},{20... | collective-permute-start | bytes 14137352 | tf_op jit(solution)/shard_map/ppermute | solution.py:805
  1.2 50.3 %collective-permute-start.9 = (bf16[1,767,3072]{2,1,0:T(8,128)(2,1)}, bf16[1,767,3072]{2,1,0:T(8,128)(2,1)}, u32[]{:S(2)}, u32[]{:S(2)}) collective-permute-start(bf16[1,767,3072]{2,1,0:T(8,128)(2,1)} %upo.7), channel_id=1, source_target_pairs={{0,16},{16,0},{1,17},{17,1},{2,18},{18,2},{3,19},{19,3},{4,20},{20... | collective-permute-start | bytes 14137352 | tf_op jit(solution)/shard_map/ppermute | solution.py:805
  7.0 12.7 %collective-permute-start.3 = (bf16[767,576]{0,1:T(8,128)(2,1)}, bf16[767,576]{0,1:T(8,128)(2,1)S(1)}, u32[]{:S(2)}, u32[]{:S(2)}) collective-permute-start(bf16[767,576]{0,1:T(8,128)(2,1)} %copy.51), channel_id=1, source_target_pairs={{0,16},{16,0},{1,17},{17,1},{2,18},{18,2},{3,19},{19,3},{4,20},{20... | collective-permute-start | bytes 2650760 | tf_op jit(solution)/shard_map/ppermute | solution.py:805
  9.2 10.5 %collective-permute-start = (bf16[256,767]{1,0:T(8,128)(2,1)S(1)}, bf16[256,767]{1,0:T(8,128)(2,1)S(1)}, u32[]{:S(2)}, u32[]{:S(2)}) collective-permute-start(bf16[256,767]{1,0:T(8,128)(2,1)S(1)} %shard_map.228.n0.x), channel_id=1, source_target_pairs={{0,2},{1,3},{2,0},{3,1},{16,17},{17,16},{18,19},{19,18},{4,6},{5,7... | collective-permute-start | bytes 1178120 | tf_op jit(solution)/shard_map/ppermute | solution.py:797
  17.2 8.3 %collective-permute-start.1 = (bf16[256,767]{1,0:T(8,128)(2,1)S(1)}, bf16[256,767]{1,0:T(8,128)(2,1)S(1)}, u32[]{:S(2)}, u32[]{:S(2)}) collective-permute-start(bf16[256,767]{1,0:T(8,128)(2,1)S(1)} %shard_map.228.n0.x), channel_id=1, source_target_pairs={{0,1},{1,0},{2,3},{3,2},{16,18},{17,19},{18,16},{19,17},{4,5},{5,4... | collective-permute-start | bytes 1178120 | tf_op jit(solution)/shard_map/ppermute | solution.py:792
  19.7 26.3 %collective-permute-start.8 = (bf16[768,767]{1,0:T(8,128)(2,1)}, bf16[768,767]{1,0:T(8,128)(2,1)}, u32[]{:S(2)}, u32[]{:S(2)}) collective-permute-start(bf16[768,767]{1,0:T(8,128)(2,1)} %bitcast.181), channel_id=1, source_target_pairs={{0,16},{16,0},{1,17},{17,1},{2,18},{18,2},{3,19},{19,3},{4,20},{20... | collective-permute-start | bytes 3534344 | tf_op jit(solution)/shard_map/ppermute | solution.py:805
  19.7 10.0 %collective-permute-start.2 = (bf16[256,767]{1,0:T(8,128)(2,1)S(1)}, bf16[256,767]{1,0:T(8,128)(2,1)S(1)}, u32[]{:S(2)}, u32[]{:S(2)}) collective-permute-start(bf16[256,767]{1,0:T(8,128)(2,1)S(1)} %collective-permute-done.n1), channel_id=1, source_target_pairs={{0,1},{1,0},{2,3},{3,2},{16,18},{17,19},{18,16},{19,17},{4,5},{5,4... | collective-permute-start | bytes 1178120 | tf_op jit(solution)/shard_map/ppermute | solution.py:792
  60.0 11.2 %collective-permute-start.11 = (bf16[256,767]{1,0:T(8,128)(2,1)S(1)}, bf16[256,767]{1,0:T(8,128)(2,1)S(1)}, u32[]{:S(2)}, u32[]{:S(2)}) collective-permute-start(bf16[256,767]{1,0:T(8,128)(2,1)S(1)} %get-tuple-element.537.n0), channel_id=1, source_target_pairs={{0,2},{1,3},{2,0},{3,1},{16,17},{17,16},{18,19},{19,18},{4,6},{5,7... | collective-permute-start | bytes 1178120 | tf_op jit(solution)/shard_map/ppermute | solution.py:797
  60.6 13.3 %collective-permute-start.12 = (bf16[256,767]{1,0:T(8,128)(2,1)S(1)}, bf16[256,767]{1,0:T(8,128)(2,1)S(1)}, u32[]{:S(2)}, u32[]{:S(2)}) collective-permute-start(bf16[256,767]{1,0:T(8,128)(2,1)S(1)} %get-tuple-element.537.n0), channel_id=1, source_target_pairs={{0,1},{1,0},{2,3},{3,2},{16,18},{17,19},{18,16},{19,17},{4,5},{5,4... | collective-permute-start | bytes 1178120 | tf_op jit(solution)/shard_map/ppermute | solution.py:792
  71.2 7.8 %collective-permute-start.13 = (bf16[256,767]{1,0:T(8,128)(2,1)S(1)}, bf16[256,767]{1,0:T(8,128)(2,1)S(1)}, u32[]{:S(2)}, u32[]{:S(2)}) collective-permute-start(bf16[256,767]{1,0:T(8,128)(2,1)S(1)} %collective-permute-done.11.n1), channel_id=1, source_target_pairs={{0,1},{1,0},{2,3},{3,2},{16,18},{17,19},{18,16},{19,17},{4,5},{5,4... | collective-permute-start | bytes 1178120 | tf_op jit(solution)/shard_map/ppermute | solution.py:792
  117.3 10.2 %collective-permute-start.20 = (bf16[2,192,3456]{2,1,0:T(8,128)(2,1)S(1)}, bf16[2,192,3456]{2,1,0:T(8,128)(2,1)S(1)}, u32[]{:S(2)}, u32[]{:S(2)}) collective-permute-start(bf16[2,192,3456]{2,1,0:T(8,128)(2,1)S(1)} %shard_map.235), channel_id=1, source_target_pairs={{0,16},{16,0},{1,17},{17,1},{2,18},{18,2},{3,19},{19,3},{4,20},{20... | collective-permute-start | bytes 7962632 | tf_op jit(solution)/shard_map/ppermute | solution.py:805
  118.7 6.2 %collective-permute-start.18 = (bf16[192,256]{1,0:T(8,128)(2,1)S(1)}, bf16[192,256]{1,0:T(8,128)(2,1)S(1)}, u32[]{:S(2)}, u32[]{:S(2)}) collective-permute-start(bf16[192,256]{1,0:T(8,128)(2,1)S(1)} %get-tuple-element.566), channel_id=1, source_target_pairs={{0,2},{1,3},{2,0},{3,1},{4,6},{5,7},{6,4},{7,5},{8,10},{9,11},{10,... | collective-permute-start | bytes 294920 | tf_op jit(solution)/shard_map/ppermute | solution.py:801
  127.5 17.0 %collective-permute-start.24 = (bf16[2,192,3456]{2,1,0:T(8,128)(2,1)S(1)}, bf16[2,192,3456]{2,1,0:T(8,128)(2,1)S(1)}, u32[]{:S(2)}, u32[]{:S(2)}) collective-permute-start(bf16[2,192,3456]{2,1,0:T(8,128)(2,1)S(1)} %shard_map.236), channel_id=1, source_target_pairs={{0,16},{16,0},{1,17},{17,1},{2,18},{18,2},{3,19},{19,3},{4,20},{20... | collective-permute-start | bytes 7962632 | tf_op jit(solution)/shard_map/ppermute | solution.py:805
  130.2 17.8 %collective-permute-start.23 = (bf16[192,3456]{1,0:T(8,128)(2,1)S(1)}, bf16[192,3456]{1,0:T(8,128)(2,1)S(1)}, u32[]{:S(2)}, u32[]{:S(2)}) collective-permute-start(bf16[192,3456]{1,0:T(8,128)(2,1)S(1)} %get-tuple-element.608), channel_id=1, source_target_pairs={{0,1},{1,0},{2,3},{3,2},{16,18},{17,19},{18,16},{19,17},{4,5},{5,4... | collective-permute-start | bytes 3981320 | tf_op jit(solution)/shard_map/ppermute | solution.py:792
  143.6 12.8 %collective-permute-start.21 = (bf16[512,767]{1,0:T(8,128)(2,1)S(1)}, bf16[512,767]{1,0:T(8,128)(2,1)S(1)}, u32[]{:S(2)}, u32[]{:S(2)}) collective-permute-start(bf16[512,767]{1,0:T(8,128)(2,1)S(1)} %get-tuple-element.606), channel_id=1, source_target_pairs={{0,1},{1,0},{2,3},{3,2},{16,18},{17,19},{18,16},{19,17},{4,5},{5,4... | collective-permute-start | bytes 2356232 | tf_op jit(solution)/shard_map/ppermute | solution.py:792
  144.5 7.6 %collective-permute-start.22 = (bf16[384,576]{1,0:T(8,128)(2,1)S(1)}, bf16[384,576]{1,0:T(8,128)(2,1)S(1)}, u32[]{:S(2)}, u32[]{:S(2)}) collective-permute-start(bf16[384,576]{1,0:T(8,128)(2,1)S(1)} %get-tuple-element.607), channel_id=1, source_target_pairs={{0,16},{16,0},{1,17},{17,1},{2,18},{18,2},{3,19},{19,3},{4,20},{20... | collective-permute-start | bytes 1327112 | tf_op jit(solution)/shard_map/ppermute | solution.py:805
  156.6 7.8 %collective-permute-start.26 = (bf16[256,767]{1,0:T(8,128)(2,1)S(1)}, bf16[256,767]{1,0:T(8,128)(2,1)S(1)}, u32[]{:S(2)}, u32[]{:S(2)}) collective-permute-start(bf16[256,767]{1,0:T(8,128)(2,1)S(1)} %add_convert_fusion.11), channel_id=1, source_target_pairs={{0,2},{1,3},{2,0},{3,1},{16,17},{17,16},{18,19},{19,18},{4,6},{5,7... | collective-permute-start | bytes 1178120 | tf_op jit(solution)/shard_map/ppermute | solution.py:797
  165.8 32.3 %collective-permute-start.31 = (bf16[192,3456]{1,0:T(8,128)(2,1)}, bf16[192,3456]{1,0:T(8,128)(2,1)}, u32[]{:S(2)}, u32[]{:S(2)}) collective-permute-start(bf16[192,3456]{1,0:T(8,128)(2,1)} %get-tuple-element.686), channel_id=1, source_target_pairs={{0,1},{1,0},{2,3},{3,2},{16,18},{17,19},{18,16},{19,17},{4,5},{5,4... | collective-permute-start | bytes 3981320 | tf_op jit(solution)/shard_map/ppermute | solution.py:792
  167.0 32.9 %collective-permute-start.32 = (bf16[192,3456]{1,0:T(8,128)(2,1)}, bf16[192,3456]{1,0:T(8,128)(2,1)}, u32[]{:S(2)}, u32[]{:S(2)}) collective-permute-start(bf16[192,3456]{1,0:T(8,128)(2,1)} %add_convert_fusion.5), channel_id=1, source_target_pairs={{0,2},{1,3},{2,0},{3,1},{16,17},{17,16},{18,19},{19,18},{4,6},{5,7... | collective-permute-start | bytes 3981320 | tf_op jit(solution)/shard_map/ppermute | solution.py:797
  183.4 20.8 %collective-permute-start.27 = (bf16[2,192,3456]{2,1,0:T(8,128)(2,1)}, bf16[2,192,3456]{2,1,0:T(8,128)(2,1)}, u32[]{:S(2)}, u32[]{:S(2)}) collective-permute-start(bf16[2,192,3456]{2,1,0:T(8,128)(2,1)} %shard_map.242), channel_id=1, source_target_pairs={{0,16},{16,0},{1,17},{17,1},{2,18},{18,2},{3,19},{19,3},{4,20},{20... | collective-permute-start | bytes 7962632 | tf_op jit(solution)/shard_map/ppermute | solution.py:805
  188.0 14.4 %collective-permute-start.28 = (bf16[192,256]{1,0:T(8,128)(2,1)S(1)}, bf16[192,256]{1,0:T(8,128)(2,1)S(1)}, u32[]{:S(2)}, u32[]{:S(2)}) collective-permute-start(bf16[192,256]{1,0:T(8,128)(2,1)S(1)} %copy-done.56), channel_id=1, source_target_pairs={{0,1},{1,0},{2,3},{3,2},{4,5},{5,4},{6,7},{7,6},{8,9},{9,8},{10,11... | collective-permute-start | bytes 294920 | tf_op jit(solution)/shard_map/ppermute | solution.py:801
  189.3 14.9 %collective-permute-start.29 = (bf16[192,256]{1,0:T(8,128)(2,1)S(1)}, bf16[192,256]{1,0:T(8,128)(2,1)S(1)}, u32[]{:S(2)}, u32[]{:S(2)}) collective-permute-start(bf16[192,256]{1,0:T(8,128)(2,1)S(1)} %copy-done.54), channel_id=1, source_target_pairs={{0,2},{1,3},{2,0},{3,1},{4,6},{5,7},{6,4},{7,5},{8,10},{9,11},{10,... | collective-permute-start | bytes 294920 | tf_op jit(solution)/shard_map/ppermute | solution.py:801
  200.0 23.6 %collective-permute-start.34 = (bf16[2,192,3456]{2,1,0:T(8,128)(2,1)S(1)}, bf16[2,192,3456]{2,1,0:T(8,128)(2,1)S(1)}, u32[]{:S(2)}, u32[]{:S(2)}) collective-permute-start(bf16[2,192,3456]{2,1,0:T(8,128)(2,1)S(1)} %shard_map.243), channel_id=1, source_target_pairs={{0,16},{16,0},{1,17},{17,1},{2,18},{18,2},{3,19},{19,3},{4,20},{20... | collective-permute-start | bytes 7962632 | tf_op jit(solution)/shard_map/ppermute | solution.py:805
  202.5 23.5 %collective-permute-start.35 = (bf16[2,48,3456]{2,1,0:T(8,128)(2,1)S(1)}, bf16[2,48,3456]{2,1,0:T(8,128)(2,1)S(1)}, u32[]{:S(2)}, u32[]{:S(2)}) collective-permute-start(bf16[2,48,3456]{2,1,0:T(8,128)(2,1)S(1)} %get-tuple-element.735), channel_id=1, source_target_pairs={{0,4},{4,0},{8,12},{12,8},{1,5},{5,1},{9,13},{13,9},{2,6},{6,2},{1... | collective-permute-start | bytes 1990664 | tf_op jit(solution)/shard_map/ppermute | solution.py:810
  208.2 17.8 %collective-permute-start.33 = (bf16[192,3456]{1,0:T(8,128)(2,1)S(1)}, bf16[192,3456]{1,0:T(8,128)(2,1)S(1)}, u32[]{:S(2)}, u32[]{:S(2)}) collective-permute-start(bf16[192,3456]{1,0:T(8,128)(2,1)S(1)} %get-tuple-element.709), channel_id=1, source_target_pairs={{0,1},{1,0},{2,3},{3,2},{16,18},{17,19},{18,16},{19,17},{4,5},{5,4... | collective-permute-start | bytes 3981320 | tf_op jit(solution)/shard_map/ppermute | solution.py:792
  222.7 12.4 %collective-permute-start.37 = (bf16[512,767]{1,0:T(8,128)(2,1)}, bf16[512,767]{1,0:T(8,128)(2,1)}, u32[]{:S(2)}, u32[]{:S(2)}) collective-permute-start(bf16[512,767]{1,0:T(8,128)(2,1)} %get-tuple-element.764), channel_id=1, source_target_pairs={{0,1},{1,0},{2,3},{3,2},{16,18},{17,19},{18,16},{19,17},{4,5},{5,4... | collective-permute-start | bytes 2356232 | tf_op jit(solution)/shard_map/ppermute | solution.py:792
  223.6 10.0 %collective-permute-start.38 = (bf16[384,576]{1,0:T(8,128)(2,1)}, bf16[384,576]{1,0:T(8,128)(2,1)}, u32[]{:S(2)}, u32[]{:S(2)}) collective-permute-start(bf16[384,576]{1,0:T(8,128)(2,1)} %get-tuple-element.765), channel_id=1, source_target_pairs={{0,16},{16,0},{1,17},{17,1},{2,18},{18,2},{3,19},{19,3},{4,20},{20... | collective-permute-start | bytes 1327112 | tf_op jit(solution)/shard_map/ppermute | solution.py:805
  236.2 7.8 %collective-permute-start.39 = (bf16[256,767]{1,0:T(8,128)(2,1)S(1)}, bf16[256,767]{1,0:T(8,128)(2,1)S(1)}, u32[]{:S(2)}, u32[]{:S(2)}) collective-permute-start(bf16[256,767]{1,0:T(8,128)(2,1)S(1)} %add_convert_fusion.10), channel_id=1, source_target_pairs={{0,2},{1,3},{2,0},{3,1},{16,17},{17,16},{18,19},{19,18},{4,6},{5,7... | collective-permute-start | bytes 1178120 | tf_op jit(solution)/shard_map/ppermute | solution.py:797
  236.9 13.3 %collective-permute-start.36 = (bf16[2,104,576]{2,1,0:T(8,128)(2,1)S(1)}, bf16[2,104,576]{2,1,0:T(8,128)(2,1)S(1)}, u32[]{:S(2)}, u32[]{:S(2)}) collective-permute-start(bf16[2,104,576]{2,1,0:T(8,128)(2,1)S(1)} %get-tuple-element.762), channel_id=1, source_target_pairs={{0,4},{4,0},{8,12},{12,8},{1,5},{5,1},{9,13},{13,9},{2,6},{6,2},{1... | collective-permute-start | bytes 718856 | tf_op jit(solution)/shard_map/ppermute | solution.py:810
  238.7 18.3 %collective-permute-start.42 = (bf16[1,48,3456]{2,1,0:T(8,128)(2,1)S(1)}, bf16[1,48,3456]{2,1,0:T(8,128)(2,1)S(1)}, u32[]{:S(2)}, u32[]{:S(2)}) collective-permute-start(bf16[1,48,3456]{2,1,0:T(8,128)(2,1)S(1)} %copy-done.81), channel_id=1, source_target_pairs={{0,8},{4,12},{8,0},{12,4},{1,9},{5,13},{9,1},{13,5},{2,10},{6,14},... | collective-permute-start | bytes 995336 | tf_op jit(solution)/shard_map/ppermute | solution.py:810
  250.2 17.8 %collective-permute-start.41 = (bf16[192,3456]{1,0:T(8,128)(2,1)S(1)}, bf16[192,3456]{1,0:T(8,128)(2,1)S(1)}, u32[]{:S(2)}, u32[]{:S(2)}) collective-permute-start(bf16[192,3456]{1,0:T(8,128)(2,1)S(1)} %copy-done.50), channel_id=1, source_target_pairs={{0,1},{1,0},{2,3},{3,2},{16,18},{17,19},{18,16},{19,17},{4,5},{5,4... | collective-permute-start | bytes 3981320 | tf_op jit(solution)/shard_map/ppermute | solution.py:792
  257.1 12.0 %collective-permute-start.43 = (bf16[1,48,3456]{2,1,0:T(8,128)(2,1)S(1)}, bf16[1,48,3456]{2,1,0:T(8,128)(2,1)S(1)}, u32[]{:S(2)}, u32[]{:S(2)}) collective-permute-start(bf16[1,48,3456]{2,1,0:T(8,128)(2,1)S(1)} %add_convert_fusion.13), channel_id=1, source_target_pairs={{0,8},{4,12},{8,0},{12,4},{1,9},{5,13},{9,1},{13,5},{2,10},{6,14},... | collective-permute-start | bytes 995336 | tf_op jit(solution)/shard_map/ppermute | solution.py:810
  257.7 22.1 %collective-permute-start.40 = (bf16[1,104,576]{2,1,0:T(8,128)(2,1)}, bf16[1,104,576]{2,1,0:T(8,128)(2,1)}, u32[]{:S(2)}, u32[]{:S(2)}) collective-permute-start(bf16[1,104,576]{2,1,0:T(8,128)(2,1)} %get-tuple-element.792), channel_id=1, source_target_pairs={{0,8},{4,12},{8,0},{12,4},{1,9},{5,13},{9,1},{13,5},{2,10},{6,14},... | collective-permute-start | bytes 359432 | tf_op jit(solution)/shard_map/ppermute | solution.py:810
  270.7 18.2 %collective-permute-start.45 = (bf16[192,3456]{1,0:T(8,128)(2,1)}, bf16[192,3456]{1,0:T(8,128)(2,1)}, u32[]{:S(2)}, u32[]{:S(2)}) collective-permute-start(bf16[192,3456]{1,0:T(8,128)(2,1)} %add_convert_fusion.2), channel_id=1, source_target_pairs={{0,2},{1,3},{2,0},{3,1},{16,17},{17,16},{18,19},{19,18},{4,6},{5,7... | collective-permute-start | bytes 3981320 | tf_op jit(solution)/shard_map/ppermute | solution.py:797
  272.9 21.4 %collective-permute-start.46 = (bf16[2,48,3456]{2,1,0:T(8,128)(2,1)S(1)}, bf16[2,48,3456]{2,1,0:T(8,128)(2,1)S(1)}, u32[]{:S(2)}, u32[]{:S(2)}) collective-permute-start(bf16[2,48,3456]{2,1,0:T(8,128)(2,1)S(1)} %maximum_select_fusion.2), channel_id=1, source_target_pairs={{0,4},{4,0},{8,12},{12,8},{1,5},{5,1},{9,13},{13,9},{2,6},{6,2},{1... | collective-permute-start | bytes 1990664 | tf_op jit(solution)/shard_map/ppermute | solution.py:810
  281.5 18.6 %collective-permute-start.44 = (bf16[1,104,576]{2,1,0:T(8,128)(2,1)S(1)}, bf16[1,104,576]{2,1,0:T(8,128)(2,1)S(1)}, u32[]{:S(2)}, u32[]{:S(2)}) collective-permute-start(bf16[1,104,576]{2,1,0:T(8,128)(2,1)S(1)} %add_convert_fusion.17), channel_id=1, source_target_pairs={{0,8},{4,12},{8,0},{12,4},{1,9},{5,13},{9,1},{13,5},{2,10},{6,14},... | collective-permute-start | bytes 359432 | tf_op jit(solution)/shard_map/ppermute | solution.py:810
  284.4 17.1 %collective-permute-start.51 = (bf16[2,104,576]{2,1,0:T(8,128)(2,1)S(1)}, bf16[2,104,576]{2,1,0:T(8,128)(2,1)S(1)}, u32[]{:S(2)}, u32[]{:S(2)}) collective-permute-start(bf16[2,104,576]{2,1,0:T(8,128)(2,1)S(1)} %fusion.11), channel_id=1, source_target_pairs={{0,4},{4,0},{8,12},{12,8},{1,5},{5,1},{9,13},{13,9},{2,6},{6,2},{1... | collective-permute-start | bytes 718856 | tf_op jit(solution)/shard_map/ppermute | solution.py:810
  297.6 16.9 %collective-permute-start.50 = (bf16[2,48,3456]{2,1,0:T(8,128)(2,1)S(1)}, bf16[2,48,3456]{2,1,0:T(8,128)(2,1)S(1)}, u32[]{:S(2)}, u32[]{:S(2)}) collective-permute-start(bf16[2,48,3456]{2,1,0:T(8,128)(2,1)S(1)} %fusion.5), channel_id=1, source_target_pairs={{0,4},{4,0},{8,12},{12,8},{1,5},{5,1},{9,13},{13,9},{2,6},{6,2},{1... | collective-permute-start | bytes 1990664 | tf_op jit(solution)/shard_map/ppermute | solution.py:810
  297.7 29.4 %collective-permute-start.48 = (bf16[192,3456]{1,0:T(8,128)(2,1)S(1)}, bf16[192,3456]{1,0:T(8,128)(2,1)S(1)}, u32[]{:S(2)}, u32[]{:S(2)}) collective-permute-start(bf16[192,3456]{1,0:T(8,128)(2,1)S(1)} %bitcast.147), channel_id=1, source_target_pairs={{0,2},{1,3},{2,0},{3,1},{16,17},{17,16},{18,19},{19,18},{4,6},{5,7... | collective-permute-start | bytes 3981320 | tf_op jit(solution)/shard_map/ppermute | solution.py:797
  298.9 33.8 %collective-permute-start.49 = (bf16[192,3456]{1,0:T(8,128)(2,1)S(1)}, bf16[192,3456]{1,0:T(8,128)(2,1)S(1)}, u32[]{:S(2)}, u32[]{:S(2)}) collective-permute-start(bf16[192,3456]{1,0:T(8,128)(2,1)S(1)} %bitcast.148), channel_id=1, source_target_pairs={{0,1},{1,0},{2,3},{3,2},{16,18},{17,19},{18,16},{19,17},{4,5},{5,4... | collective-permute-start | bytes 3981320 | tf_op jit(solution)/shard_map/ppermute | solution.py:792
  300.1 48.1 %collective-permute-start.57 = (bf16[192,3456]{1,0:T(8,128)(2,1)S(1)}, bf16[192,3456]{1,0:T(8,128)(2,1)S(1)}, u32[]{:S(2)}, u32[]{:S(2)}) collective-permute-start(bf16[192,3456]{1,0:T(8,128)(2,1)S(1)} %bitcast.149), channel_id=1, source_target_pairs={{0,16},{1,17},{2,18},{3,19},{4,20},{5,21},{6,22},{7,23},{8,24},{9,... | collective-permute-start | bytes 3981320 | tf_op jit(solution)/shard_map/ppermute | solution.py:814
  301.7 31.1 %collective-permute-start.47 = (bf16[2,104,576]{2,1,0:T(8,128)(2,1)S(1)}, bf16[2,104,576]{2,1,0:T(8,128)(2,1)S(1)}, u32[]{:S(2)}, u32[]{:S(2)}) collective-permute-start(bf16[2,104,576]{2,1,0:T(8,128)(2,1)S(1)} %maximum_select_fusion.6), channel_id=1, source_target_pairs={{0,4},{4,0},{8,12},{12,8},{1,5},{5,1},{9,13},{13,9},{2,6},{6,2},{1... | collective-permute-start | bytes 718856 | tf_op jit(solution)/shard_map/ppermute | solution.py:810
  314.5 19.8 %collective-permute-start.54 = (bf16[1,104,576]{2,1,0:T(8,128)(2,1)S(1)}, bf16[1,104,576]{2,1,0:T(8,128)(2,1)S(1)}, u32[]{:S(2)}, u32[]{:S(2)}) collective-permute-start(bf16[1,104,576]{2,1,0:T(8,128)(2,1)S(1)} %get-tuple-element.870), channel_id=1, source_target_pairs={{0,8},{4,12},{8,0},{12,4},{1,9},{5,13},{9,1},{13,5},{2,10},{6,14},... | collective-permute-start | bytes 359432 | tf_op jit(solution)/shard_map/ppermute | solution.py:810
  327.1 18.1 %collective-permute-start.58 = (bf16[1,48,3456]{2,1,0:T(8,128)(2,1)S(1)}, bf16[1,48,3456]{2,1,0:T(8,128)(2,1)S(1)}, u32[]{:S(2)}, u32[]{:S(2)}) collective-permute-start(bf16[1,48,3456]{2,1,0:T(8,128)(2,1)S(1)} %get-tuple-element.877), channel_id=1, source_target_pairs={{0,8},{4,12},{8,0},{12,4},{1,9},{5,13},{9,1},{13,5},{2,10},{6,14},... | collective-permute-start | bytes 995336 | tf_op jit(solution)/shard_map/ppermute | solution.py:810
  332.7 18.5 %collective-permute-start.56 = (bf16[192,3456]{1,0:T(8,128)(2,1)S(1)}, bf16[192,3456]{1,0:T(8,128)(2,1)S(1)}, u32[]{:S(2)}, u32[]{:S(2)}) collective-permute-start(bf16[192,3456]{1,0:T(8,128)(2,1)S(1)} %collective-permute-done.48.refs_3_), channel_id=1, source_target_pairs={{0,1},{1,0},{2,3},{3,2},{16,18},{17,19},{18,16},{19,17},{4,5},{5,4... | collective-permute-start | bytes 3981320 | tf_op jit(solution)/shard_map/ppermute | solution.py:792
  332.7 28.3 %collective-permute-start.53 = (bf16[192,3456]{1,0:T(8,128)(2,1)S(1)}, bf16[192,3456]{1,0:T(8,128)(2,1)S(1)}, u32[]{:S(2)}, u32[]{:S(2)}) collective-permute-start(bf16[192,3456]{1,0:T(8,128)(2,1)S(1)} %collective-permute-done.48.refs_3_), channel_id=1, source_target_pairs={{0,16},{1,17},{2,18},{3,19},{4,20},{5,21},{6,22},{7,23},{8,24},{9,... | collective-permute-start | bytes 3981320 | tf_op jit(solution)/shard_map/ppermute | solution.py:814
  345.2 7.4 %collective-permute-start.55 = (bf16[1,104,576]{2,1,0:T(8,128)(2,1)S(1)}, bf16[1,104,576]{2,1,0:T(8,128)(2,1)S(1)}, u32[]{:S(2)}, u32[]{:S(2)}) collective-permute-start(bf16[1,104,576]{2,1,0:T(8,128)(2,1)S(1)} %add_convert_fusion.16), channel_id=1, source_target_pairs={{0,8},{4,12},{8,0},{12,4},{1,9},{5,13},{9,1},{13,5},{2,10},{6,14},... | collective-permute-start | bytes 359432 | tf_op jit(solution)/shard_map/ppermute | solution.py:810
  345.2 15.8 %collective-permute-start.52 = (bf16[416,576]{1,0:T(8,128)(2,1)S(1)}, bf16[416,576]{1,0:T(8,128)(2,1)S(1)}, u32[]{:S(2)}, u32[]{:S(2)}) collective-permute-start(bf16[416,576]{1,0:T(8,128)(2,1)S(1)} %bitcast.176), channel_id=1, source_target_pairs={{0,2},{1,3},{2,0},{3,1},{16,17},{17,16},{18,19},{19,18},{4,6},{5,7... | collective-permute-start | bytes 1437704 | tf_op jit(solution)/shard_map/ppermute | solution.py:797
  348.2 13.0 %collective-permute-start.62 = (bf16[1,48,3456]{2,1,0:T(8,128)(2,1)S(1)}, bf16[1,48,3456]{2,1,0:T(8,128)(2,1)S(1)}, u32[]{:S(2)}, u32[]{:S(2)}) collective-permute-start(bf16[1,48,3456]{2,1,0:T(8,128)(2,1)S(1)} %add_convert_fusion.12), channel_id=1, source_target_pairs={{0,8},{4,12},{8,0},{12,4},{1,9},{5,13},{9,1},{13,5},{2,10},{6,14},... | collective-permute-start | bytes 995336 | tf_op jit(solution)/shard_map/ppermute | solution.py:810
  351.2 20.1 %collective-permute-start.60 = (bf16[192,3456]{1,0:T(8,128)(2,1)S(1)}, bf16[192,3456]{1,0:T(8,128)(2,1)S(1)}, u32[]{:S(2)}, u32[]{:S(2)}) collective-permute-start(bf16[192,3456]{1,0:T(8,128)(2,1)S(1)} %collective-permute-done.49.refs_3_), channel_id=1, source_target_pairs={{0,16},{1,17},{2,18},{3,19},{4,20},{5,21},{6,22},{7,23},{8,24},{9,... | collective-permute-start | bytes 3981320 | tf_op jit(solution)/shard_map/ppermute | solution.py:814
  361.2 6.7 %collective-permute-start.61 = (bf16[2,104,576]{2,1,0:T(8,128)(2,1)S(1)}, bf16[2,104,576]{2,1,0:T(8,128)(2,1)S(1)}, u32[]{:S(2)}, u32[]{:S(2)}) collective-permute-start(bf16[2,104,576]{2,1,0:T(8,128)(2,1)S(1)} %maximum_select_fusion.7), channel_id=1, source_target_pairs={{0,4},{4,0},{8,12},{12,8},{1,5},{5,1},{9,13},{13,9},{2,6},{6,2},{1... | collective-permute-start | bytes 718856 | tf_op jit(solution)/shard_map/ppermute | solution.py:810
  363.5 15.0 %collective-permute-start.59 = (bf16[2,416,576]{2,1,0:T(8,128)(2,1)S(1)}, bf16[2,416,576]{2,1,0:T(8,128)(2,1)S(1)}, u32[]{:S(2)}, u32[]{:S(2)}) collective-permute-start(bf16[2,416,576]{2,1,0:T(8,128)(2,1)S(1)} %pad_maximum_fusion.2), channel_id=1, source_target_pairs={{0,1},{1,0},{2,3},{3,2},{16,18},{17,19},{18,16},{19,17},{4,5},{5,4... | collective-permute-start | bytes 2875400 | tf_op jit(solution)/shard_map/ppermute | solution.py:792
  364.5 14.0 %collective-permute-start.65 = (bf16[2,48,3456]{2,1,0:T(8,128)(2,1)S(1)}, bf16[2,48,3456]{2,1,0:T(8,128)(2,1)S(1)}, u32[]{:S(2)}, u32[]{:S(2)}) collective-permute-start(bf16[2,48,3456]{2,1,0:T(8,128)(2,1)S(1)} %maximum_select_fusion.3), channel_id=1, source_target_pairs={{0,4},{4,0},{8,12},{12,8},{1,5},{5,1},{9,13},{13,9},{2,6},{6,2},{1... | collective-permute-start | bytes 1990664 | tf_op jit(solution)/shard_map/ppermute | solution.py:810
  368.1 9.3 %collective-permute-start.63 = (bf16[416,576]{1,0:T(8,128)(2,1)S(1)}, bf16[416,576]{1,0:T(8,128)(2,1)S(1)}, u32[]{:S(2)}, u32[]{:S(2)}) collective-permute-start(bf16[416,576]{1,0:T(8,128)(2,1)S(1)} %bitcast.178), channel_id=1, source_target_pairs={{0,2},{1,3},{2,0},{3,1},{16,17},{17,16},{18,19},{19,18},{4,6},{5,7... | collective-permute-start | bytes 1437704 | tf_op jit(solution)/shard_map/ppermute | solution.py:797
  370.0 14.2 %collective-permute-start.64 = (bf16[192,3456]{1,0:T(8,128)(2,1)S(1)}, bf16[192,3456]{1,0:T(8,128)(2,1)S(1)}, u32[]{:S(2)}, u32[]{:S(2)}) collective-permute-start(bf16[192,3456]{1,0:T(8,128)(2,1)S(1)} %collective-permute-done.56.refs_3_), channel_id=1, source_target_pairs={{0,16},{1,17},{2,18},{3,19},{4,20},{5,21},{6,22},{7,23},{8,24},{9,... | collective-permute-start | bytes 3981320 | tf_op jit(solution)/shard_map/ppermute | solution.py:814
  378.9 9.6 %collective-permute-start.66 = (bf16[192,3456]{1,0:T(8,128)(2,1)S(1)}, bf16[192,3456]{1,0:T(8,128)(2,1)S(1)}, u32[]{:S(2)}, u32[]{:S(2)}) collective-permute-start(bf16[192,3456]{1,0:T(8,128)(2,1)S(1)} %bitcast.151), channel_id=1, source_target_pairs={{16,0},{17,1},{18,2},{19,3},{20,4},{21,5},{22,6},{23,7},{24,8},{25... | collective-permute-start | bytes 3981320 | tf_op jit(solution)/shard_map/ppermute | solution.py:814
  380.3 43.7 %collective-permute-start.68 = (bf16[192,3456]{1,0:T(8,128)(2,1)S(1)}, bf16[192,3456]{1,0:T(8,128)(2,1)S(1)}, u32[]{:S(2)}, u32[]{:S(2)}) collective-permute-start(bf16[192,3456]{1,0:T(8,128)(2,1)S(1)} %bitcast.152), channel_id=1, source_target_pairs={{0,2},{1,3},{2,0},{3,1},{16,17},{17,16},{18,19},{19,18},{4,6},{5,7... | collective-permute-start | bytes 3981320 | tf_op jit(solution)/shard_map/ppermute | solution.py:797
  381.9 42.1 %collective-permute-start.69 = (bf16[192,3456]{1,0:T(8,128)(2,1)S(1)}, bf16[192,3456]{1,0:T(8,128)(2,1)S(1)}, u32[]{:S(2)}, u32[]{:S(2)}) collective-permute-start(bf16[192,3456]{1,0:T(8,128)(2,1)S(1)} %bitcast.153), channel_id=1, source_target_pairs={{0,1},{1,0},{2,3},{3,2},{16,18},{17,19},{18,16},{19,17},{4,5},{5,4... | collective-permute-start | bytes 3981320 | tf_op jit(solution)/shard_map/ppermute | solution.py:792
  382.9 41.2 %collective-permute-start.70 = (bf16[2,416,576]{2,1,0:T(8,128)(2,1)S(1)}, bf16[2,416,576]{2,1,0:T(8,128)(2,1)S(1)}, u32[]{:S(2)}, u32[]{:S(2)}) collective-permute-start(bf16[2,416,576]{2,1,0:T(8,128)(2,1)S(1)} %pad_maximum_fusion.3), channel_id=1, source_target_pairs={{0,1},{1,0},{2,3},{3,2},{16,18},{17,19},{18,16},{19,17},{4,5},{5,4... | collective-permute-start | bytes 2875400 | tf_op jit(solution)/shard_map/ppermute | solution.py:792
  424.3 6.7 %collective-permute-start.73 = (bf16[192,3456]{1,0:T(8,128)(2,1)S(1)}, bf16[192,3456]{1,0:T(8,128)(2,1)S(1)}, u32[]{:S(2)}, u32[]{:S(2)}) collective-permute-start(bf16[192,3456]{1,0:T(8,128)(2,1)S(1)} %collective-permute-done.68.refs_0_), channel_id=1, source_target_pairs={{16,0},{17,1},{18,2},{19,3},{20,4},{21,5},{22,6},{23,7},{24,8},{25... | collective-permute-start | bytes 3981320 | tf_op jit(solution)/shard_map/ppermute | solution.py:814
  425.6 10.4 %collective-permute-start.72 = (bf16[4,416,576]{2,1,0:T(8,128)(2,1)S(1)}, bf16[4,416,576]{2,1,0:T(8,128)(2,1)S(1)}, u32[]{:S(2)}, u32[]{:S(2)}) collective-permute-start(bf16[4,416,576]{2,1,0:T(8,128)(2,1)S(1)} %pad_maximum_fusion.refs_3_), channel_id=1, source_target_pairs={{0,16},{1,17},{2,18},{3,19},{4,20},{5,21},{6,22},{7,23},{8,24},{9,... | collective-permute-start | bytes 5750792 | tf_op jit(solution)/shard_map/ppermute | solution.py:814
  428.9 7.1 %collective-permute-start.71 = (bf16[4,416,576]{2,1,0:T(8,128)(2,1)S(1)}, bf16[4,416,576]{2,1,0:T(8,128)(2,1)S(1)}, u32[]{:S(2)}, u32[]{:S(2)}) collective-permute-start(bf16[4,416,576]{2,1,0:T(8,128)(2,1)S(1)} %pad_maximum_fusion.1.refs_0_), channel_id=1, source_target_pairs={{16,0},{17,1},{18,2},{19,3},{20,4},{21,5},{22,6},{23,7},{24,8},{25... | collective-permute-start | bytes 5750792 | tf_op jit(solution)/shard_map/ppermute | solution.py:814
  430.2 17.8 %collective-permute-start.74 = (bf16[192,3456]{1,0:T(8,128)(2,1)S(1)}, bf16[192,3456]{1,0:T(8,128)(2,1)S(1)}, u32[]{:S(2)}, u32[]{:S(2)}) collective-permute-start(bf16[192,3456]{1,0:T(8,128)(2,1)S(1)} %collective-permute-done.68.refs_0_), channel_id=1, source_target_pairs={{0,1},{1,0},{2,3},{3,2},{16,18},{17,19},{18,16},{19,17},{4,5},{5,4... | collective-permute-start | bytes 3981320 | tf_op jit(solution)/shard_map/ppermute | solution.py:792
  434.7 13.3 %collective-permute-start.75 = (bf16[192,3456]{1,0:T(8,128)(2,1)S(1)}, bf16[192,3456]{1,0:T(8,128)(2,1)S(1)}, u32[]{:S(2)}, u32[]{:S(2)}) collective-permute-start(bf16[192,3456]{1,0:T(8,128)(2,1)S(1)} %collective-permute-done.69.refs_0_), channel_id=1, source_target_pairs={{16,0},{17,1},{18,2},{19,3},{20,4},{21,5},{22,6},{23,7},{24,8},{25... | collective-permute-start | bytes 3981320 | tf_op jit(solution)/shard_map/ppermute | solution.py:814
  (108 other events, 1089.7 us)
